TPU v7x, 32 devices: a whole 2x2x4 slice. The times are simulated.
32 devices in a mesh: dp: 16 (over z, x, core), tensor: 2 (over y).
Axes of the slice: x: 2, y: 2, z: 4, core: 2. Of those that a mesh axis runs over, the one named last changes fastest.
Arguments:
- inputs: bfloat16 [2048, 4096], P('dp'), may hold values from -6 to 6
- w_key: bfloat16 [4096, 1024], P(None, 'tensor'), may hold values from -0.09375 to 0.09375
- values: bfloat16 [2048, 1024], P('dp', 'tensor'), may hold values from -6 to 6
- queries: bfloat16 [2048, 4096], P('dp', 'tensor'), may hold values from -200 to 200
- d_out: bfloat16 [2048, 4096], P('dp', 'tensor'), may hold values from -6 to 6
- doc_lens: int32 [4], replicated, may hold values from 1 to 1024, 2048 in all
- block_pos: int32 [32], P('dp'), may hold values from 0 to 31, as said below
Outputs:
- d_query: bfloat16 [2048, 4096], P('dp', 'tensor')
- d_value: bfloat16 [2048, 1024], P('dp', 'tensor')
- d_input: bfloat16 [2048, 4096], P('dp', 'tensor')
- d_wkey: float32 [4096, 1024], P('dp', 'tensor')
Inputs may be any that keep to these rules, and one draw needn't show every extreme that they name: `block_pos`: each stored block holds one block of 64 rows of the pack; every pack block is held once. `doc_lens`: lengths of the 4 documents in pack order; they sum to 2048.
All inputs are finite; a program needn't handle non-finite values.
Results may differ from a plain program's by a relative error of at most 0.023.
The roundings to bfloat16 on the way count: a program that leaves them out, or rounds other values in their place, can miss the bound.
Values may be sent and summed in bfloat16 or wider, within the bound.
No kernel may reach another device: no remote copies, remote signals or barrier semaphores. Data moves between devices by JAX's collectives and lax.ppermute only.
A program may use at most 64 MiB of HBM per device.

v0:
```python
import math

import jax
import jax.numpy as jnp
from jax import lax
from jax.sharding import PartitionSpec as P

HD = 128
BLK = 64


masked_fill = -1e30


def row_positions(block_pos):
    within = jnp.tile(jnp.arange(BLK, dtype=jnp.int32), block_pos.shape[0])
    return jnp.repeat(block_pos, BLK) * BLK + within


def documents(positions, doc_lens):
    starts = jnp.cumsum(doc_lens) - doc_lens
    return jnp.sum((positions[:, None] >= starts[None, :]).astype(jnp.int32), axis=1) - 1


def split_heads(block_rows, kv_heads):
    return block_rows.reshape(block_rows.shape[0], kv_heads, HD)


def scored(query_heads, key_block, score_scale):
    key_split = split_heads(key_block, query_heads.shape[1])
    return (
        jnp.einsum("qcgd,kcd->cgqk", query_heads, key_split, preferred_element_type=jnp.float32)
        * score_scale
    )


def contributions(
    query_heads, grad_heads, key_block, value_block, allowed, row_max, row_sum, delta, score_scale
):
    kv_heads = query_heads.shape[1]
    key_split = split_heads(key_block, kv_heads)
    value_split = split_heads(value_block, kv_heads)
    scores = scored(query_heads, key_block, score_scale)
    mask_full = allowed[None, None]
    probabilities = (
        jnp.where(mask_full, jnp.exp(scores - row_max[..., None]), 0.0) / row_sum[..., None]
    )
    d_prob = jnp.einsum(
        "qcgd,kcd->cgqk", grad_heads, value_split, preferred_element_type=jnp.float32
    )
    d_score = probabilities * (d_prob - delta[..., None])
    prob_bf = probabilities.astype(jnp.bfloat16)
    score_bf = d_score.astype(jnp.bfloat16)
    query_part = score_scale * jnp.einsum(
        "cgqk,kcd->qcgd", score_bf, key_split, preferred_element_type=jnp.float32
    )
    key_part = score_scale * jnp.einsum(
        "cgqk,qcgd->kcd", score_bf, query_heads, preferred_element_type=jnp.float32
    )
    value_part = jnp.einsum(
        "cgqk,qcgd->kcd", prob_bf, grad_heads, preferred_element_type=jnp.float32
    )
    width_rows = key_block.shape[0]
    partial_value = jnp.concatenate(
        [key_part.reshape(width_rows, -1), value_part.reshape(width_rows, -1)], axis=1
    )
    return (query_part, partial_value)


def on_device(inputs, w_key, values, queries, d_out, doc_lens, block_pos):
    local_rows = inputs.shape[0]
    kv_heads = values.shape[1] // HD
    group_size = queries.shape[1] // (kv_heads * HD)
    kv_columns = kv_heads * HD
    score_scale = 1.0 / math.sqrt(HD)
    key_rows = jnp.dot(inputs, w_key, preferred_element_type=jnp.float32).astype(jnp.bfloat16)
    all_keys, all_values, all_blocks = (
        lax.all_gather(key_rows, "dp", axis=0, tiled=True),
        lax.all_gather(values, "dp", axis=0, tiled=True),
        lax.all_gather(block_pos, "dp", axis=0, tiled=True),
    )
    key_pos = row_positions(all_blocks)
    key_doc = documents(key_pos, doc_lens)
    query_pos = row_positions(block_pos)
    query_doc = documents(query_pos, doc_lens)
    query_heads = queries.reshape(local_rows, kv_heads, group_size, HD)
    grad_heads = d_out.reshape(local_rows, kv_heads, group_size, HD)
    total_rows = all_keys.shape[0]
    key_width = math.gcd(512, total_rows)
    stat_shape = (kv_heads, group_size, local_rows)

    def mask_for(first_row, width_rows):
        pos_here = lax.dynamic_slice_in_dim(key_pos, first_row, width_rows, 0)
        doc_here = lax.dynamic_slice_in_dim(key_doc, first_row, width_rows, 0)
        return (query_doc[:, None] == doc_here[None, :]) & (pos_here[None, :] <= query_pos[:, None])

    def visit_stats(block_index, running):
        first_row = block_index * key_width
        key_block = lax.dynamic_slice_in_dim(all_keys, first_row, key_width, 0)
        value_block = lax.dynamic_slice_in_dim(all_values, first_row, key_width, 0)
        allowed = mask_for(first_row, key_width)

        def visit_compute_live(state_now):
            row_max, row_sum, weighted = state_now
            scores = scored(query_heads, key_block, score_scale)
            mask_full = allowed[None, None]
            new_max = jnp.maximum(
                row_max, jnp.max(jnp.where(mask_full, scores, masked_fill), axis=3)
            )
            exp_terms = jnp.where(mask_full, jnp.exp(scores - new_max[..., None]), 0.0)
            d_prob = jnp.einsum(
                "qcgd,kcd->cgqk",
                grad_heads,
                split_heads(value_block, kv_heads),
                preferred_element_type=jnp.float32,
            )
            shrink = jnp.exp(row_max - new_max)
            return (
                new_max,
                row_sum * shrink + jnp.sum(exp_terms, axis=3),
                weighted * shrink + jnp.sum(exp_terms * d_prob, axis=3),
            )

        return lax.cond(jnp.any(allowed), visit_compute_live, lambda state_now: state_now, running)

    start_state = (
        jnp.full(stat_shape, masked_fill, jnp.float32),
        jnp.zeros(stat_shape, jnp.float32),
        jnp.zeros(stat_shape, jnp.float32),
    )
    row_max, row_sum, weighted = lax.fori_loop(0, total_rows // key_width, visit_stats, start_state)
    delta = weighted / row_sum

    def block_work(key_block, value_block, allowed):
        width_rows = key_block.shape[0]

        def block_compute_live(operands):
            return contributions(
                query_heads,
                grad_heads,
                operands[0],
                operands[1],
                operands[2],
                row_max,
                row_sum,
                delta,
                score_scale,
            )

        def dead_block(operands):
            return (
                jnp.zeros((local_rows, kv_heads, group_size, HD), jnp.float32),
                jnp.zeros((width_rows, 2 * kv_columns), jnp.float32),
            )

        return lax.cond(
            jnp.any(allowed), block_compute_live, dead_block, (key_block, value_block, allowed)
        )

    query_start = jnp.zeros((local_rows, kv_heads, group_size, HD), jnp.float32)

    def visit_block(block_index, running):
        query_sum, buffer_rows = running
        first_row = block_index * key_width
        key_block = lax.dynamic_slice_in_dim(all_keys, first_row, key_width, 0)
        value_block = lax.dynamic_slice_in_dim(all_values, first_row, key_width, 0)
        query_part, partial_value = block_work(
            key_block, value_block, mask_for(first_row, key_width)
        )
        return (
            query_sum + query_part,
            lax.dynamic_update_slice_in_dim(buffer_rows, partial_value, first_row, 0),
        )

    empty_buffer = jnp.zeros((total_rows, 2 * kv_columns), jnp.float32)
    query_sum, buffer_rows = lax.fori_loop(
        0, total_rows // key_width, visit_block, (query_start, empty_buffer)
    )
    arrived = lax.all_to_all(
        buffer_rows.astype(jnp.bfloat16), "dp", split_axis=0, concat_axis=0, tiled=True
    ).astype(buffer_rows.dtype)
    own_sums = jnp.sum(arrived.reshape(-1, local_rows, 2 * kv_columns), axis=0)
    d_query = query_sum.astype(jnp.bfloat16).reshape(local_rows, kv_columns * group_size)
    key_grad = own_sums[:, :kv_columns].astype(jnp.bfloat16)
    d_value = own_sums[:, kv_columns:].astype(jnp.bfloat16)
    d_wkey = lax.psum_scatter(
        lax.dot_general(
            inputs, key_grad, (((0,), (0,)), ((), ())), preferred_element_type=jnp.float32
        ),
        "dp",
        scatter_dimension=0,
        tiled=True,
    )
    partial_input = lax.dot_general(
        key_grad, w_key, (((1,), (1,)), ((), ())), preferred_element_type=jnp.float32
    )
    d_input = lax.psum_scatter(
        partial_input.astype(jnp.bfloat16), "tensor", scatter_dimension=1, tiled=True
    )
    return (d_query, d_value, d_input, d_wkey)


def solution(mesh):
    return jax.shard_map(
        on_device,
        mesh=mesh,
        in_specs=(
            P("dp", None),
            P(None, "tensor"),
            P("dp", "tensor"),
            P("dp", "tensor"),
            P("dp", "tensor"),
            P(),
            P("dp"),
        ),
        out_specs=(P("dp", "tensor"), P("dp", "tensor"), P("dp", "tensor"), P("dp", "tensor")),
        check_vma=False,
    )
```

profile of v0, /device:TPU:0, one launch (start us, length us, event | category | flops | bytes accessed | tf_op | source)
XLA Modules:
  0.0 438.0 jit_solution(4649805849938709478)
XLA Ops:
  8.5 3.6 convolution_convert_fusion.1
  14.5 13.7 %all-reduce = s32[32]{0:T(128)S(1)} all-reduce(s32[32]{0:T(128)S(1)} %dynamic-update-slice), channel_id=1, replica_groups=mesh['dp'=16,'tensor'=2] {'dp'}, use_global_device_ids=true, to_apply=%add | all-reduce | flops 32 | bytes 256
  31.8 24.5 %all-gather.3.cloned.1.call-done = bf16[2048,512]{1,0:T(8,128)(2,1)} async-done(((bf16[128,512]{1,0:T(8,128)(2,1)}), bf16[2048,512]{1,0:T(8,128)(2,1)}) %all-gather.3.cloned.1.call-update) | async-done | bytes 2097168 | tf_op jit(solution)/shard_map/all_gather | solution.py:78
  56.3 4.0 copy.101
  60.3 38.8 %all-gather.5.cloned.1.call-done = bf16[2048,512]{0,1:T(8,128)(2,1)} async-done(((bf16[128,512]{0,1:T(8,128)(2,1)}), bf16[2048,512]{0,1:T(8,128)(2,1)}) %all-gather.5.cloned.1.call-update) | async-done | bytes 2097168 | tf_op jit(solution)/shard_map/all_gather | solution.py:79
  99.1 20.6 %while.34 = (s32[]{:T(128)}, f32[4,4,128]{2,1,0:T(4,128)S(1)}, f32[4,4,128]{2,1,0:T(4,128)S(1)}, f32[4,4,128]{2,1,0:T(4,128)S(1)}, s32[128]{0:T(128)S(1)}, /*ind...) while((s32[]{:T(128)}, f32[4,4,128]{2,1,0:T(4,128)S(1)}, ...), condition=%wide.region_10.11_spmd.clone, body=%wide.region_3.10_spmd.clone.sunk | while | flops 549722240 | bytes 17202012 | solution.py:131
  100.9 4.4 %conditional.6 = ((f32[4,4,128]{2,1,0:T(4,128)S(1)}, f32[4,4,128]{2,1,0:T(4,128)S(1)}, f32[4,4,128]{2,1,0:T(4,128)S(1)})) conditional(s32[]{:T(128)} %convert_element_type.66, (f32[4,4,128]{2,1,0:T(4,128)S(1)}, f32[4,4,128]{2,1,0:T(4,128)S(1)}, f32[4,4,128]{2,1,0:T(4,128)S(1)}) %tuple.116, (pred[128,512]{0,1:T(8,128)(4,1)S(1)}, ...), branch_computations={%region_5.5_spmd, %region_6.9_spmd} | conditional | flops 549459968 | bytes 17121316 | solution.py:124
  107.2 4.4 %conditional.6 = ((f32[4,4,128]{2,1,0:T(4,128)S(1)}, f32[4,4,128]{2,1,0:T(4,128)S(1)}, f32[4,4,128]{2,1,0:T(4,128)S(1)})) conditional(s32[]{:T(128)} %convert_element_type.66, (f32[4,4,128]{2,1,0:T(4,128)S(1)}, f32[4,4,128]{2,1,0:T(4,128)S(1)}, f32[4,4,128]{2,1,0:T(4,128)S(1)}) %tuple.116, (pred[128,512]{0,1:T(8,128)(4,1)S(1)}, ...), branch_computations={%region_5.5_spmd, %region_6.9_spmd} | conditional | flops 549459968 | bytes 17121316 | solution.py:124
  113.4 4.4 %conditional.6 = ((f32[4,4,128]{2,1,0:T(4,128)S(1)}, f32[4,4,128]{2,1,0:T(4,128)S(1)}, f32[4,4,128]{2,1,0:T(4,128)S(1)})) conditional(s32[]{:T(128)} %convert_element_type.66, (f32[4,4,128]{2,1,0:T(4,128)S(1)}, f32[4,4,128]{2,1,0:T(4,128)S(1)}, f32[4,4,128]{2,1,0:T(4,128)S(1)}) %tuple.116, (pred[128,512]{0,1:T(8,128)(4,1)S(1)}, ...), branch_computations={%region_5.5_spmd, %region_6.9_spmd} | conditional | flops 549459968 | bytes 17121316 | solution.py:124
  119.7 2.5 broadcast_in_dim.82.clone
  122.2 57.7 %while.35 = (s32[]{:T(128)}, f32[128,4,4,128]{3,0,2,1:T(8,128)}, bf16[2048,1024]{1,0:T(8,128)(2,1)}, s32[128]{0:T(128)S(1)}, s32[2048]{0:T(1024)S(1)}, /*index=5...) while((s32[]{:T(128)}, f32[128,4,4,128]{3,0,2,1:T(8,128)}, ...), condition=%wide.region_15.16_spmd.clone, body=%wide.region_11.15_spmd.clone.sunk | while | flops 1354236032 | bytes 42638724 | solution.py:176
  124.0 9.3 %conditional.7 = (f32[128,4,4,128]{3,0,2,1:T(8,128)S(1)}, bf16[512,1024]{0,1:T(8,128)(2,1)S(1)}) conditional(s32[]{:T(128)} %convert_element_type.67, () %tuple.120, (pred[128,512]{0,1:T(8,128)(4,1)S(1)}, bf16[2048,512]{0,1:T(8,128)(2,1)}, s32[]{:T(128)}, bf16[128,4,4,128]{0,3,2,1:T(8,128)(2,1)}, f32[4,4,128]{2,1,0:T(4,128)S(1)}, ...), branch_computations={%region_13.13_spmd, %region_14.14_spmd} | conditional | flops 1353449472 | bytes 31023152 | solution.py:156
  139.7 9.3 %conditional.7 = (f32[128,4,4,128]{3,0,2,1:T(8,128)S(1)}, bf16[512,1024]{0,1:T(8,128)(2,1)S(1)}) conditional(s32[]{:T(128)} %convert_element_type.67, () %tuple.120, (pred[128,512]{0,1:T(8,128)(4,1)S(1)}, bf16[2048,512]{0,1:T(8,128)(2,1)}, s32[]{:T(128)}, bf16[128,4,4,128]{0,3,2,1:T(8,128)(2,1)}, f32[4,4,128]{2,1,0:T(4,128)S(1)}, ...), branch_computations={%region_13.13_spmd, %region_14.14_spmd} | conditional | flops 1353449472 | bytes 31023152 | solution.py:156
  152.6 2.4 select_add_fusion.2
  156.8 9.3 %conditional.7 = (f32[128,4,4,128]{3,0,2,1:T(8,128)S(1)}, bf16[512,1024]{0,1:T(8,128)(2,1)S(1)}) conditional(s32[]{:T(128)} %convert_element_type.67, () %tuple.120, (pred[128,512]{0,1:T(8,128)(4,1)S(1)}, bf16[2048,512]{0,1:T(8,128)(2,1)}, s32[]{:T(128)}, bf16[128,4,4,128]{0,3,2,1:T(8,128)(2,1)}, f32[4,4,128]{2,1,0:T(4,128)S(1)}, ...), branch_computations={%region_13.13_spmd, %region_14.14_spmd} | conditional | flops 1353449472 | bytes 31023152 | solution.py:156
  169.6 2.4 select_add_fusion.2
  177.5 2.4 select_add_fusion.2
  179.9 6.4 %copy.104 = bf16[16,128,1024]{1,2,0:T(8,128)(2,1)} copy(bf16[16,128,1024]{2,1,0:T(8,128)(2,1)} %bitcast.107) | data formatting | bytes 8388608 | tf_op jit(solution)/shard_map/all_to_all | solution.py:179
  186.3 109.5 %all_to_all.9 = bf16[16,128,1024]{1,2,0:T(8,128)(2,1)} all-to-all(bf16[16,128,1024]{1,2,0:T(8,128)(2,1)} %copy.104), channel_id=1, replica_groups=mesh['dp'=16,'tensor'=2] {'dp'}, dimensions={0} | all-to-all | bytes 8388608 | tf_op jit(solution)/shard_map/all_to_all | solution.py:179
  295.8 2.9 reduce
  298.7 4.5 %convolution_bitcast_fusion.1 = f32[4096,512]{0,1:T(8,128)} fusion(bf16[128,4096]{1,0:T(8,128)(2,1)S(1)} %copy-done, bf16[128,1024]{0,1:T(8,128)(2,1)S(1)} %reduce), kind=kOutput, calls=%fused_computation.37 | convolution fusion | flops 536870912 | bytes 9568256 | tf_op jit(solution)/shard_map/dot_general | solution.py:187
  303.2 4.7 %convolution_convert_fusion = bf16[128,4096]{1,0:T(8,128)(2,1)} fusion(bf16[4096,512]{1,0:T(8,128)(2,1)} %param.16, bf16[128,1024]{0,1:T(8,128)(2,1)S(1)} %reduce), kind=kOutput, calls=%fused_computation.38 | convolution fusion | flops 537395200 | bytes 5373952 | tf_op jit(solution)/shard_map/dot_general | solution.py:194
  310.4 98.3 %reduce-scatter.5.cloned.1.call-done = f32[256,512]{0,1:T(8,128)} async-done(((f32[4096,512]{0,1:T(8,128)}), f32[256,512]{0,1:T(8,128)}) %reduce-scatter.5.cloned.1.call-update) | async-done | bytes 524304 | tf_op jit(solution)/shard_map/reduce_scatter | solution.py:186
  410.8 20.7 %reduce-scatter.3.cloned.1.call-done = bf16[128,2048]{1,0:T(8,128)(2,1)} async-done(((bf16[128,4096]{1,0:T(8,128)(2,1)}), bf16[128,2048]{1,0:T(8,128)(2,1)}) %reduce-scatter.3.cloned.1.call-update) | async-done | bytes 524304 | tf_op jit(solution)/shard_map/reduce_scatter | solution.py:197
  (166 shorter events, 76.6 us)
Async XLA Ops:
  7.2 1.3 copy-start
  7.2 5.8 %copy-start.10 = (u32[32]{0:T(128)S(1)}, u32[32]{0:T(128)}, u32[]{:S(2)}) copy-start(u32[32]{0:T(128)} %constant.136) | copy-start | bytes 388
  7.2 4.9 %copy-start.7 = (bf16[128,512]{1,0:T(8,128)(2,1)S(1)}, bf16[128,512]{1,0:T(8,128)(2,1)}, u32[]{:S(2)}) copy-start(bf16[128,512]{1,0:T(8,128)(2,1)} %param.17) | copy-start | bytes 393220
  7.2 7.0 %copy-start.8 = (s32[2]{0:T(128)S(1)}, s32[2]{0:T(128)}, u32[]{:S(2)}) copy-start(s32[2]{0:T(128)} %param.21) | copy-start | bytes 28
  7.2 21.2 %copy-start.9 = (s32[4]{0:T(128)S(1)}, s32[4]{0:T(128)}, u32[]{:S(2)}) copy-start(s32[4]{0:T(128)} %param.20) | copy-start | bytes 52
  7.2 21.5 %copy-start.5 = (bf16[128,2048]{1,0:T(8,128)(2,1)S(1)}, bf16[128,2048]{1,0:T(8,128)(2,1)}, u32[]{:S(2)}) copy-start(bf16[128,2048]{1,0:T(8,128)(2,1)} %param.19) | copy-start | bytes 1572868
  7.2 23.8 %copy-start.6 = (bf16[128,2048]{1,0:T(8,128)(2,1)S(1)}, bf16[128,2048]{1,0:T(8,128)(2,1)}, u32[]{:S(2)}) copy-start(bf16[128,2048]{1,0:T(8,128)(2,1)} %param.18) | copy-start | bytes 1572868
  7.2 49.1 %all-gather.3.cloned.1.call-start = ((), (), s32[]{:S(2)}) async-start(), calls=%async_computation.3 | async-start | bytes 2228224 | tf_op jit(solution)/shard_map/all_gather | solution.py:78
  12.1 87.0 %all-gather.5.cloned.1.call-start = ((), (), s32[]{:S(2)}) async-start(), calls=%async_computation.4 | async-start | bytes 2228224 | tf_op jit(solution)/shard_map/all_gather | solution.py:79
  12.9 395.8 %reduce-scatter.5.cloned.1.call-start = ((), (), s32[]{:S(2)}) async-start(), calls=%async_computation.6 | async-start | bytes 8912896 | tf_op jit(solution)/shard_map/reduce_scatter | solution.py:186
  31.3 67.7 %copy-start.3 = (bf16[128,2048]{0,1:T(8,128)(2,1)}, bf16[128,2048]{0,1:T(8,128)(2,1)S(1)}, u32[]{:S(2)}) copy-start(bf16[128,2048]{0,1:T(8,128)(2,1)S(1)} %copy.95) | copy-start | bytes 1572868
  127.6 1.9 copy-start.4
  133.2 1.0 copy-start.1
  143.4 1.9 copy-start.4
  149.0 1.0 copy-start.1
  160.4 1.9 copy-start.4
  166.1 1.0 copy-start.1
  174.0 1.0 copy-start.1
  303.1 4.8 %copy-start.2 = (f32[128,4,4,128]{3,0,2,1:T(8,128)S(1)}, f32[128,4,4,128]{3,0,2,1:T(8,128)}, u32[]{:S(2)}) copy-start(f32[128,4,4,128]{3,0,2,1:T(8,128)} %get-tuple-element.599) | copy-start | bytes 3145732
  303.1 128.3 %reduce-scatter.3.cloned.1.call-start = ((), (), s32[]{:S(2)}) async-start(), calls=%async_computation.5 | async-start | bytes 1572864 | tf_op jit(solution)/shard_map/reduce_scatter | solution.py:197
Sparse Core Ops, SparseCore 0:
  12.2 44.1 all-gather.2
  59.1 39.9 all-gather.4
  303.3 105.4 reduce-scatter.4
  411.4 20.0 reduce-scatter.2
where the time goes:
time: 440 us; the launch traced here: 438 us
  waiting for transfers between devices  182 us (41%)
  blocking collectives  123 us (28%)
  local copies, waits for them, and re-layouts  46.9 us (11%)
  matrix products  42.9 us (10%)
  other arithmetic  21.9 us (5%)
  between operations  14.7 us (3%)
  loops' own time  5.87 us (1%)
    all_to_all x1, blocking collectives, on_device(): lax.all_to_all(buffer_rows.astype(jnp.bfloat16), 'dp', split_axis=0, conc...  109 us
    reduce_scatter x1, waiting for transfers between devices, on_device(): lax.psum_scatter(lax.dot_general(inputs, key_grad, (((0,), (0,)), ((), ()...  98.3 us
    all_gather x1, waiting for transfers between devices, on_device(): lax.all_gather(values, 'dp', axis=0, tiled=True)  38.8 us
    all_gather x1, waiting for transfers between devices, on_device(): lax.all_gather(key_rows, 'dp', axis=0, tiled=True)  24.5 us
    reduce_scatter x1, waiting for transfers between devices, on_device(): lax.psum_scatter(partial_input.astype(jnp.bfloat16), 'tensor', scatter_di...  20.7 us
    unnamed x1, blocking collectives  13.7 us
    unnamed x29, local copies, waits for them, and re-layouts  12.4 us
    dynamic_update_slice x8, local copies, waits for them, and re-layouts, visit_block(): lax.dynamic_update_slice_in_dim(buffer_rows, partial_value, first_row, 0)  10.2 us
  transfers between devices with their start and end apart: 4, of which 4 were waited for; matrix products, arithmetic and copies ran while one was open for 4% of the time, Pallas kernels for 0%

commit v1 on v0

--- a/solution.py
+++ b/solution.py
@@ -3,6 +3,8 @@
 import jax
 import jax.numpy as jnp
 from jax import lax
+from jax.experimental import pallas as pl
+from jax.experimental.pallas import tpu as pltpu
 from jax.sharding import PartitionSpec as P
 
 HD = 128
@@ -200,9 +202,387 @@
     return (d_query, d_value, d_input, d_wkey)
 
 
+CORE, Z_HI = 1, 8
+GROUP = 4
+ROWS = 128
+TILE = 256
+Q_BLOCKS = GROUP * ROWS // BLK
+SMEM = pltpu.SMEM
+VMEM = pltpu.VMEM
+
+
+def swap(array, mask):
+    return lax.ppermute(array, "dp", [(i, i ^ mask) for i in range(16)])
+
+
+def swap_tensor(array):
+    return lax.ppermute(array, "tensor", [(0, 1), (1, 0)])
+
+
+def own_head():
+    return (lax.axis_index("dp") >> 1) & 3
+
+
+def columns(index, width):
+    return pl.ds(pl.multiple_of(index * width, width), width)
+
+
+def whole_spec(space=VMEM):
+    return pl.BlockSpec(memory_space=space)
+
+
+def pack_rows(queries_ref, grads_ref, *out_refs):
+    head = own_head()
+    for m, out_ref in enumerate(out_refs):
+        span = columns(head ^ m, GROUP * HD)
+        out_ref[:, : GROUP * HD] = queries_ref[:, span]
+        out_ref[:, GROUP * HD :] = grads_ref[:, span]
+
+
+def project_keys(inputs_ref, values_ref, w_ref, *refs):
+    pair_refs, feature_refs, total = refs[:GROUP], refs[GROUP : 2 * GROUP], refs[-1]
+    step = pl.program_id(0)
+    head = own_head()
+
+    @pl.when(step == 0)
+    def _():
+        total[...] = jnp.zeros_like(total)
+        chip = lax.axis_index("dp") >> 1
+        side = lax.axis_index("tensor")
+        for m in range(GROUP):
+            pair_refs[m][:, HD:] = values_ref[:, columns(head ^ m, HD)]
+            for far in range(2):
+                target = chip ^ (m + GROUP * far)
+                feature_refs[m][far] = inputs_ref[:, columns(2 * target + side, 256)]
+
+    total[...] += jnp.dot(
+        inputs_ref[:, columns(step, 512)], w_ref[...], preferred_element_type=jnp.float32
+    )
+
+    @pl.when(step == pl.num_programs(0) - 1)
+    def _():
+        for m in range(GROUP):
+            pair_refs[m][:, :HD] = total[:, columns(head ^ m, HD)].astype(jnp.bfloat16)
+
+
+def dot_nt(left, right):
+    return lax.dot_general(
+        left, right, (((1,), (1,)), ((), ())), preferred_element_type=jnp.float32
+    )
+
+
+def folded(array, reduce):
+    return reduce(array.reshape(-1, 8, array.shape[-1]), axis=0)
+
+
+def attend(pos_ref, lens_ref, *refs):
+    row_refs, pair_refs, refs = refs[:GROUP], refs[GROUP : 2 * GROUP], refs[2 * GROUP :]
+    dq_ref, dk_keep, dk_send, dv_keep, dv_send = refs[:5]
+    q_rows, g_rows, keys, keys_t, values, dk, dv, scores, d_prob = refs[5:]
+    score_scale = 1.0 / math.sqrt(HD)
+    base_two = score_scale * math.log2(math.e)
+
+    for block in range(Q_BLOCKS):
+        here = pl.ds(block % 2 * BLK, BLK)
+        for h in range(GROUP):
+            there = pl.ds(h * BLK, BLK)
+            q_rows[block, there] = row_refs[block // 2][here, h * HD : (h + 1) * HD]
+            g_rows[block, there] = row_refs[block // 2][
+                here, (GROUP + h) * HD : (GROUP + h + 1) * HD
+            ]
+    for block in range(4 * Q_BLOCKS):
+        here = pl.ds(block % Q_BLOCKS * BLK, BLK)
+        there = pl.ds(pl.multiple_of(pos_ref[block] * BLK, BLK), BLK)
+        keys[there] = pair_refs[block // Q_BLOCKS][here, :HD]
+        values[there] = pair_refs[block // Q_BLOCKS][here, HD:]
+    for tile in range(keys.shape[0] // TILE):
+        here = pl.ds(tile * TILE, TILE)
+        keys_t[:, here] = keys[here].astype(jnp.float32).T.astype(jnp.bfloat16)
+    dk[...] = jnp.zeros_like(dk)
+    dv[...] = jnp.zeros_like(dv)
+    starts = [lens_ref[0]]
+    for k in (1, 2):
+        starts.append(starts[-1] + lens_ref[k])
+
+    def document_start(position):
+        found = jnp.zeros_like(position)
+        for start in starts:
+            found = jnp.where(start <= position, start, found)
+        return found
+
+    @pl.loop(0, Q_BLOCKS)
+    def _(block):
+        first = pos_ref[block] * BLK
+        lanes = lax.broadcasted_iota(jnp.int32, (1, GROUP * BLK), 1)
+        position = first + (lanes & (BLK - 1))
+        start = document_start(position)
+        low = document_start(first) // TILE
+        high = (first + BLK - 1) // TILE + 1
+        query = q_rows[block]
+        grad = g_rows[block]
+        folded_shape = (8, GROUP * BLK)
+
+        def visit_scores(tile, row_max):
+            here = columns(tile, TILE)
+            raw = dot_nt(keys[here], query)
+            key_position = tile * TILE + lax.broadcasted_iota(jnp.int32, raw.shape, 0)
+            allowed = (key_position <= position) & (key_position >= start)
+            raw = jnp.where(allowed, raw, masked_fill)
+            scores[here] = raw
+            d_prob[here] = dot_nt(values[here], grad)
+            return jnp.maximum(row_max, folded(raw, jnp.max))
+
+        row_max = lax.fori_loop(
+            low, high, visit_scores, jnp.full(folded_shape, masked_fill, jnp.float32)
+        )
+        row_max = jnp.max(row_max, axis=0, keepdims=True)
+
+        def visit_sums(tile, running):
+            here = columns(tile, TILE)
+            terms = jnp.exp2((scores[here] - row_max) * base_two)
+            scores[here] = terms
+            return (
+                running[0] + folded(terms, jnp.sum),
+                running[1] + folded(terms * d_prob[here], jnp.sum),
+            )
+
+        zeros = jnp.zeros(folded_shape, jnp.float32)
+        row_sum, weighted = lax.fori_loop(low, high, visit_sums, (zeros, zeros))
+        inverse = 1.0 / jnp.sum(row_sum, axis=0, keepdims=True)
+        delta = jnp.sum(weighted, axis=0, keepdims=True) * inverse
+
+        def visit_grads(tile, dq):
+            here = columns(tile, TILE)
+            prob = scores[here] * inverse
+            score_bf = (prob * (d_prob[here] - delta)).astype(jnp.bfloat16)
+            dk[here] += jnp.dot(score_bf, query, preferred_element_type=jnp.float32)
+            dv[here] += jnp.dot(
+                prob.astype(jnp.bfloat16), grad, preferred_element_type=jnp.float32
+            )
+            return dq + jnp.dot(keys_t[:, here], score_bf, preferred_element_type=jnp.float32)
+
+        dq = lax.fori_loop(
+            low, high, visit_grads, jnp.zeros((HD, GROUP * BLK), jnp.float32)
+        )
+        dq = (dq * score_scale).T.astype(jnp.bfloat16)
+        for h in range(GROUP):
+            dq_ref[block, :, h * HD : (h + 1) * HD] = dq[h * BLK : (h + 1) * BLK]
+
+    for block in range(4 * Q_BLOCKS):
+        quarter = block // Q_BLOCKS
+        here = pl.ds(quarter // 2 * Q_BLOCKS * BLK + block % Q_BLOCKS * BLK, BLK)
+        there = pl.ds(pl.multiple_of(pos_ref[block] * BLK, BLK), BLK)
+        (dk_send if quarter % 2 else dk_keep)[here] = dk[there] * score_scale
+        (dv_send if quarter % 2 else dv_keep)[here] = dv[there]
+
+
+def weight_grad(own_ref, other_ref, *refs):
+    grad_refs, out_ref, grads = refs[:GROUP], refs[GROUP], refs[GROUP + 1]
+    head = own_head()
+    for k, grad_ref in enumerate(grad_refs):
+        for far in range(2):
+            for m in range(GROUP):
+                here = pl.ds((far * GROUP + m) * ROWS, ROWS)
+                there = pl.ds((far * GROUP + (m ^ k)) * ROWS, ROWS)
+                grads[here, columns(head ^ k, HD)] = grad_ref[there]
+    slot = (lax.axis_index("dp") & 1) ^ lax.axis_index("tensor")
+    out_ref[slot] = jnp.dot(own_ref[...], grads[...], preferred_element_type=jnp.float32)
+    out_ref[1 - slot] = jnp.dot(other_ref[...], grads[...], preferred_element_type=jnp.float32)
+
+
+def input_grad(ids_ref, own_ref, other_ref, w_own, w_near, w_far, out_ref, own_all, other_all):
+    step = pl.program_id(0)
+    head = ids_ref[0]
+
+    @pl.when(step == 0)
+    def _():
+        for k in range(GROUP):
+            own_all[:, columns(head ^ k, HD)] = own_ref[k]
+            other_all[:, columns(head ^ k, HD)] = other_ref[k]
+
+    part = dot_nt(own_all[...], w_own[...])
+
+    @pl.when(step < 2)
+    def _():
+        out_ref[...] = (part + dot_nt(other_all[...], w_near[...])).astype(jnp.bfloat16)
+
+    @pl.when(step >= 2)
+    def _():
+        out_ref[...] = (part + dot_nt(other_all[...], w_far[...])).astype(jnp.bfloat16)
+
+
+def place_rows(*refs):
+    dq_refs, dv_refs = refs[:GROUP], refs[GROUP : 2 * GROUP]
+    dq_out, dv_out = refs[2 * GROUP :]
+    head = own_head()
+    for m in range(GROUP):
+        dq_out[:, columns(head ^ m, GROUP * HD)] = dq_refs[m][...]
+        dv_out[:, columns(head ^ m, HD)] = dv_refs[m][...]
+
+
+def shaped(shape, dtype=jnp.bfloat16):
+    return jax.ShapeDtypeStruct(shape, dtype)
+
+
+def limits(mebibytes):
+    return pltpu.CompilerParams(vmem_limit_bytes=mebibytes << 20)
+
+
+def on_device_by_heads(inputs, w_key, values, queries, d_out, doc_lens, block_pos):
+    features = inputs.shape[1]
+    kv_columns = values.shape[1]
+    total_rows = 16 * ROWS
+    index = lax.axis_index("dp")
+    side = lax.axis_index("tensor")
+    core = index & 1
+    vmem, smem = whole_spec(), whole_spec(SMEM)
+
+    packed_rows = pl.pallas_call(
+        pack_rows,
+        out_shape=[shaped((ROWS, 2 * GROUP * HD))] * GROUP,
+        in_specs=[vmem] * 2,
+        out_specs=[vmem] * GROUP,
+        compiler_params=limits(16),
+        name="pack_rows",
+    )(queries, d_out)
+    rows = [packed_rows[0]] + [swap(packed_rows[m], 2 * m) for m in (1, 2, 3)]
+
+    steps = features // 512
+    projected = pl.pallas_call(
+        project_keys,
+        out_shape=[shaped((ROWS, 2 * HD))] * GROUP + [shaped((2, ROWS, 256))] * GROUP,
+        grid=(steps,),
+        in_specs=[
+            pl.BlockSpec((ROWS, features), lambda k: (0, 0)),
+            pl.BlockSpec((ROWS, kv_columns), lambda k: (0, 0)),
+            pl.BlockSpec((512, kv_columns), lambda k: (k, 0)),
+        ],
+        out_specs=[pl.BlockSpec((ROWS, 2 * HD), lambda k: (0, 0))] * GROUP
+        + [pl.BlockSpec((2, ROWS, 256), lambda k: (0, 0, 0))] * GROUP,
+        scratch_shapes=[VMEM((ROWS, kv_columns), jnp.float32)],
+        compiler_params=limits(24),
+        cost_estimate=pl.CostEstimate(
+            flops=2 * ROWS * features * kv_columns,
+            bytes_accessed=features * kv_columns * 2,
+            transcendentals=0,
+        ),
+        name="project_keys",
+    )(inputs, values, w_key)
+    pairs, feature_parts = projected[:GROUP], projected[GROUP:]
+
+    own_pairs = jnp.concatenate([pairs[0]] + [swap(pairs[m], 2 * m) for m in (1, 2, 3)], axis=0)
+    far_pairs = swap(own_pairs, Z_HI)
+    core_pairs = swap(own_pairs, CORE)
+    far_core_pairs = swap(far_pairs, CORE)
+
+    own_pos = jnp.concatenate([block_pos] + [swap(block_pos, 2 * m) for m in (1, 2, 3)])
+    far_pos = swap(own_pos, Z_HI)
+    positions = jnp.concatenate([own_pos, swap(own_pos, CORE), far_pos, swap(far_pos, CORE)])
+
+    half = total_rows // 2
+    d_rows, dk_keep, dk_send, dv_keep, dv_send = pl.pallas_call(
+        attend,
+        out_shape=[shaped((Q_BLOCKS, BLK, GROUP * HD))] + [shaped((half, HD), jnp.float32)] * 4,
+        in_specs=[smem] * 2 + [vmem] * (2 * GROUP),
+        out_specs=[vmem] * 5,
+        scratch_shapes=[
+            VMEM((Q_BLOCKS, GROUP * BLK, HD), jnp.bfloat16),
+            VMEM((Q_BLOCKS, GROUP * BLK, HD), jnp.bfloat16),
+            VMEM((total_rows, HD), jnp.bfloat16),
+            VMEM((HD, total_rows), jnp.bfloat16),
+            VMEM((total_rows, HD), jnp.bfloat16),
+            VMEM((total_rows, HD), jnp.float32),
+            VMEM((total_rows, HD), jnp.float32),
+            VMEM((total_rows, GROUP * BLK), jnp.float32),
+            VMEM((total_rows, GROUP * BLK), jnp.float32),
+        ],
+        compiler_params=limits(40),
+        cost_estimate=pl.CostEstimate(
+            flops=4 * 10 * 512 * 512 * HD,
+            bytes_accessed=6 << 20,
+            transcendentals=512 * 2048,
+        ),
+        name="attend",
+    )(positions, doc_lens, *rows, own_pairs, core_pairs, far_pairs, far_core_pairs)
+
+    dk_sum = dk_keep + swap(dk_send, CORE)
+    dk_far = swap(dk_sum.astype(jnp.bfloat16), Z_HI)
+    quarter = half // 2
+    dk_far = jnp.concatenate([dk_far[quarter:], dk_far[:quarter]], axis=0)
+    key_grad = (dk_sum + dk_far.astype(jnp.float32)).astype(jnp.bfloat16)
+    key_grads = [key_grad] + [swap(key_grad, 2 * m) for m in (1, 2, 3)]
+    own_key_grad = jnp.stack([key_grads[m][m * ROWS : (m + 1) * ROWS] for m in range(GROUP)])
+    other_key_grad = swap_tensor(own_key_grad)
+
+    arrived = [feature_parts[0]] + [swap(feature_parts[m], 2 * m) for m in (1, 2, 3)]
+    near = jnp.concatenate([part[0] for part in arrived], axis=0)
+    beyond = swap(jnp.concatenate([part[1] for part in arrived], axis=0), Z_HI)
+    own_features = jnp.concatenate([near, beyond], axis=0).T
+    other_features = swap_tensor(own_features)
+
+    partial = pl.pallas_call(
+        weight_grad,
+        out_shape=shaped((2, 256, kv_columns), jnp.float32),
+        in_specs=[vmem] * (2 + GROUP),
+        out_specs=vmem,
+        scratch_shapes=[VMEM((half, kv_columns), jnp.bfloat16)],
+        compiler_params=limits(24),
+        cost_estimate=pl.CostEstimate(
+            flops=4 * 256 * half * kv_columns, bytes_accessed=4 << 20, transcendentals=0
+        ),
+        name="weight_grad",
+    )(own_features, other_features, *key_grads)
+    d_wkey = partial[0] + swap(partial[1], CORE)
+
+    leaving = lax.dynamic_slice_in_dim(w_key, (1 - side) * 2048 + core * 1024, 1024, 0)
+    w_near = swap_tensor(leaving)
+    w_far = swap(w_near, CORE)
+    ids = jnp.stack([(index >> 1) & 3, core, side]).astype(jnp.int32)
+    d_input = pl.pallas_call(
+        input_grad,
+        out_shape=shaped((ROWS, features // 2)),
+        grid_spec=pltpu.PrefetchScalarGridSpec(
+            num_scalar_prefetch=1,
+            grid=(4,),
+            in_specs=[
+                pl.BlockSpec((GROUP, ROWS, HD), lambda k, ids: (0, 0, 0)),
+                pl.BlockSpec((GROUP, ROWS, HD), lambda k, ids: (0, 0, 0)),
+                pl.BlockSpec((512, kv_columns), lambda k, ids: (ids[2] * 4 + (k ^ (2 * ids[1])), 0)),
+                pl.BlockSpec((512, kv_columns), lambda k, ids: (jnp.minimum(k, 1), 0)),
+                pl.BlockSpec((512, kv_columns), lambda k, ids: (jnp.maximum(k - 2, 0), 0)),
+            ],
+            out_specs=pl.BlockSpec((ROWS, 512), lambda k, ids: (0, k ^ (2 * ids[1]))),
+            scratch_shapes=[VMEM((ROWS, kv_columns), jnp.bfloat16)] * 2,
+        ),
+        compiler_params=limits(24),
+        cost_estimate=pl.CostEstimate(
+            flops=4 * ROWS * 2048 * kv_columns, bytes_accessed=5 << 20, transcendentals=0
+        ),
+        name="input_grad",
+    )(ids, own_key_grad, other_key_grad, w_key, w_near, w_far)
+
+    dv_sum = dv_keep + swap(dv_send, CORE)
+    dv_far = swap(dv_sum[quarter:].astype(jnp.bfloat16), Z_HI)
+    value_grad = (dv_sum[:quarter] + dv_far.astype(jnp.float32)).astype(jnp.bfloat16)
+    value_grads = [value_grad[m * ROWS : (m + 1) * ROWS] for m in range(GROUP)]
+    value_grads = [value_grads[0]] + [swap(value_grads[m], 2 * m) for m in (1, 2, 3)]
+    row_grads = d_rows.reshape(GROUP, ROWS, GROUP * HD)
+    row_grads = [row_grads[0]] + [swap(row_grads[m], 2 * m) for m in (1, 2, 3)]
+    d_query, d_value = pl.pallas_call(
+        place_rows,
+        out_shape=[shaped(queries.shape), shaped(values.shape)],
+        in_specs=[vmem] * (2 * GROUP),
+        out_specs=[vmem] * 2,
+        compiler_params=limits(16),
+        name="place_rows",
+    )(*row_grads, *value_grads)
+    return (d_query, d_value, d_input, d_wkey)
+
+
 def solution(mesh):
+    by_heads = mesh.shape["dp"] == 16 and mesh.shape["tensor"] == 2
     return jax.shard_map(
-        on_device,
+        on_device_by_heads if by_heads else on_device,
         mesh=mesh,
         in_specs=(
             P("dp", None),

time: 440 us -> 143 us (0.33)
  blocking collectives: 123 us -> 0 us
  waiting for transfers between devices: 182 us -> 60.5 us
  matrix products: 42.9 us -> 0 us
  starting transfers between devices: 0.16 us -> 38 us
  local copies, waits for them, and re-layouts: 46.9 us -> 20.9 us
  Pallas kernels: 0 us -> 20.2 us
  other arithmetic: 21.9 us -> 2.33 us
  between operations: 14.7 us -> 0.98 us
  loops' own time: 5.87 us -> 0 us
    reduce_scatter x2 -> x0, waiting for transfers between devices: 119 us -> none  [the longest x1 98.3 us: on_device(): lax.psum_scatter(lax.dot_general(inputs, key_grad, (((0,), (0,)), ((), ()...]
    all_to_all x1 -> x0, blocking collectives: 109 us -> none  [on_device(): lax.all_to_all(buffer_rows.astype(jnp.bfloat16), 'dp', split_axis=0, conc...]
    all_gather x2 -> x0, waiting for transfers between devices: 63.3 us -> none  [the longest x1 38.8 us: on_device(): lax.all_gather(values, 'dp', axis=0, tiled=True)]
    ppermute x0 -> x37, waiting for transfers between devices: none -> 60.5 us  [the longest x34 60.5 us: swap(): return lax.ppermute(array, 'dp', [(i, i ^ mask) for i in range(16)])]
    dot_general x24 -> x0, matrix products: 42.9 us -> none  [the longest x6 9.66 us: scored(): jnp.einsum('qcgd,kcd->cgqk', query_heads, key_split, preferred_element_ty...]
    ppermute x0 -> x37, starting transfers between devices: none -> 38 us  [the longest x34 35.3 us: swap(): return lax.ppermute(array, 'dp', [(i, i ^ mask) for i in range(16)])]
    pallas_call x0 -> x6, Pallas kernels: none -> 20.2 us  [the longest x1 11.5 us: on_device_by_heads(): pl.pallas_call(attend, out_shape=[shaped((Q_BLOCKS, BLK, GROUP * HD))] +...]
    unnamed x1 -> x0, blocking collectives: 13.7 us -> none
  transfers between devices with their start and end apart: 4 -> 37, of which waited for: 4 -> 13; matrix products, arithmetic and copies ran while one was open for 4% -> 7% of each run, Pallas kernels for 0% -> 14%
where the time goes in v1:
time: 143 us
  waiting for transfers between devices  60.5 us (42%)
  starting transfers between devices  38 us (27%)
  local copies, waits for them, and re-layouts  20.9 us (15%)
  Pallas kernels  20.2 us (14%)
  other arithmetic  2.33 us (2%)
    ppermute x34, waiting for transfers between devices, swap(): return lax.ppermute(array, 'dp', [(i, i ^ mask) for i in range(16)])  60.5 us
    ppermute x34, starting transfers between devices, swap(): return lax.ppermute(array, 'dp', [(i, i ^ mask) for i in range(16)])  35.3 us
    unnamed x41, local copies, waits for them, and re-layouts  13.2 us
    pallas_call x1, Pallas kernels, on_device_by_heads(): pl.pallas_call(attend, out_shape=[shaped((Q_BLOCKS, BLK, GROUP * HD))] +...  11.5 us
    pallas_call x1, Pallas kernels, on_device_by_heads(): pl.pallas_call(input_grad, out_shape=shaped((ROWS, features // 2)), grid_...  3.82 us
  transfers between devices with their start and end apart: 37, of which 13 were waited for; matrix products, arithmetic and copies ran while one was open for 7% of the time, Pallas kernels for 14%

profile of v1, /device:TPU:0, one launch (start us, length us, event | category | flops | bytes accessed | tf_op | source)
XLA Modules:
  0.0 143.0 jit_solution(14070144685984606145)
XLA Ops:
  0.6 3.0 %collective-permute-start = (s32[2]{0:T(128)}, s32[2]{0:T(128)S(1)}, u32[]{:S(2)}, u32[]{:S(2)}) collective-permute-start(s32[2]{0:T(128)} %param.13), channel_id=1, source_target_pairs={{0,4},{2,6},{4,0},{6,2},{8,12},{10,14},{12,8},{14,10},{16,20},{18,... | collective-permute-start | bytes 32 | tf_op jit(solution)/shard_map/ppermute | solution.py:215
  5.2 2.2 %copy-done = bf16[4096,512]{1,0:T(8,128)(2,1)S(1)} copy-done((bf16[4096,512]{1,0:T(8,128)(2,1)S(1)}, bf16[4096,512]{1,0:T(8,128)(2,1)}, u32[]{:S(2)}) %copy-start) | copy-done | bytes 4194328
  9.5 2.2 %project_keys.1 = (bf16[128,256]{1,0:T(8,128)(2,1)S(1)}, bf16[128,256]{1,0:T(8,128)(2,1)S(1)}, bf16[128,256]{1,0:T(8,128)(2,1)S(1)}, bf16[128,256]{1,0:T(8,128)(...) custom-call(bf16[128,4096]{1,0:T(8,128)(2,1)S(1)} %copy-done.2, ...), custom_call_target="tpu_custom_call" | custom-call | flops 536870912 | bytes 4194304 | tf_op jit(solution)/shard_map/project_keys/pallas_call | solution.py:451
  11.7 2.0 %collective-permute-start.9 = (bf16[128,256]{1,0:T(8,128)(2,1)S(1)}, bf16[128,256]{1,0:T(8,128)(2,1)}, u32[]{:S(2)}, u32[]{:S(2)}) collective-permute-start(bf16[128,256]{1,0:T(8,128)(2,1)S(1)} %get-tuple-element.28), channel_id=1, source_target_pairs={{0,4},{2,6},{4,0},{6,2},{8,12},{10,14},{12,8},{14,10},{16,20},{18,... | collective-permute-start | bytes 196616 | tf_op jit(solution)/shard_map/ppermute | solution.py:215
  17.7 2.3 %constant_dynamic-slice_fusion = bf16[1024,512]{1,0:T(8,128)(2,1)} fusion(bf16[4096,512]{1,0:T(8,128)(2,1)} %w_own.1, s32[]{:T(128)S(6)} %select_n.3), kind=kLoop, calls=%fused_computation.32 | loop fusion | bytes 2097156 | tf_op jit(solution)/shard_map/dynamic_slice | solution.py:537
  20.2 1.9 %collective-permute-start.6 = (bf16[128,1024]{1,0:T(8,128)(2,1)S(1)}, bf16[128,1024]{1,0:T(8,128)(2,1)S(1)}, u32[]{:S(2)}, u32[]{:S(2)}) collective-permute-start(bf16[128,1024]{1,0:T(8,128)(2,1)S(1)} %get-tuple-element.24), channel_id=1, source_target_pairs={{0,4},{2,6},{4,0},{6,2},{8,12},{10,14},{12,8},{14,10},{16,20},{18,... | collective-permute-start | bytes 786440 | tf_op jit(solution)/shard_map/ppermute | solution.py:215
  22.2 2.6 %collective-permute-start.4 = (s32[8]{0:T(128)S(1)}, s32[8]{0:T(128)S(1)}, u32[]{:S(2)}, u32[]{:S(2)}) collective-permute-start(s32[8]{0:T(128)S(1)} %pad_add_fusion), channel_id=1, source_target_pairs={{0,16},{2,18},{4,20},{6,22},{8,24},{10,26},{12,28},{14,30},{16,0},... | collective-permute-start | bytes 104 | tf_op jit(solution)/shard_map/ppermute | solution.py:215
  24.8 1.9 %collective-permute-done.4 = s32[8]{0:T(128)S(1)} collective-permute-done((s32[8]{0:T(128)S(1)}, s32[8]{0:T(128)S(1)}, u32[]{:S(2)}, u32[]{:S(2)}) %collective-permute-start.4) | collective-permute-done | bytes 64 | tf_op jit(solution)/shard_map/ppermute | solution.py:215
  32.2 2.8 %collective-permute-start.33 = (bf16[2,128,256]{1,2,0:T(8,128)(2,1)}, bf16[2,128,256]{1,2,0:T(8,128)(2,1)S(1)}, u32[]{:S(2)}, u32[]{:S(2)}) collective-permute-start(bf16[2,128,256]{1,2,0:T(8,128)(2,1)} %copy.14), channel_id=1, source_target_pairs={{0,12},{2,14},{4,8},{6,10},{8,4},{10,6},{12,0},{14,2},{16,28},{18,... | collective-permute-start | bytes 393224 | tf_op jit(solution)/shard_map/ppermute | solution.py:215
  36.4 9.2 %collective-permute-done.33 = bf16[2,128,256]{1,2,0:T(8,128)(2,1)S(1)} collective-permute-done((bf16[2,128,256]{1,2,0:T(8,128)(2,1)}, bf16[2,128,256]{1,2,0:T(8,128)(2,1)S(1)}, u32[]{:S(2)}, u32[]{:S(2)}) %collective-permute-start.33) | collective-permute-done | bytes 131104 | tf_op jit(solution)/shard_map/ppermute | solution.py:215
  47.4 3.2 %collective-permute-done.32 = bf16[2,128,256]{1,2,0:T(8,128)(2,1)S(1)} collective-permute-done((bf16[2,128,256]{1,2,0:T(8,128)(2,1)S(1)}, bf16[2,128,256]{1,2,0:T(8,128)(2,1)S(1)}, u32[]{:S(2)}, u32[]{:S(2)}) %collective-permute-start.32) | collective-permute-done | bytes 131104 | tf_op jit(solution)/shard_map/ppermute | solution.py:215
  50.6 2.8 %collective-permute-start.13 = (bf16[512,256]{1,0:T(8,128)(2,1)S(1)}, bf16[512,256]{1,0:T(8,128)(2,1)S(1)}, u32[]{:S(2)}, u32[]{:S(2)}) collective-permute-start(bf16[512,256]{1,0:T(8,128)(2,1)S(1)} %constant_dynamic-update-slice_fusion.refs_4_), channel_id=1, source_target_pairs={{0,16},{2,18},{4,20},{6,22},{8,24},{10,26},{12,28},{14,30},{16,0},... | collective-permute-start | bytes 786440 | tf_op jit(solution)/shard_map/ppermute | solution.py:215
  53.5 10.2 %collective-permute-done.13.refs_6_ = bf16[512,256]{1,0:T(8,128)(2,1)S(1)} collective-permute-done((bf16[512,256]{1,0:T(8,128)(2,1)S(1)}, bf16[512,256]{1,0:T(8,128)(2,1)S(1)}, u32[]{:S(2)}, u32[]{:S(2)}) %collective-permute-start.13) | collective-permute-done | bytes 262176 | tf_op jit(solution)/shard_map/ppermute | solution.py:215
  65.4 11.5 %attend.1 = (bf16[8,64,512]{2,1,0:T(8,128)(2,1)S(1)}, f32[1024,128]{1,0:T(8,128)S(1)}, f32[1024,128]{1,0:T(8,128)S(1)}, f32[1024,128]{1,0:T(8,128)S(1)}, f32[1024,128]{1,0:T(8,128)S(1)}) custom-call(s32[32]{0:T(128)S(1)} %concatenate.20.pos_ref, s32[4]{0:T(128)S(1)} %copy-done.13, bf16[128,1024]{1,0:T(8,128)(2,1)S(1)} %get-tuple-element.23.refs_0_, ...), custom_call_target="tpu_custom_call" | custom-call | flops 1342177280 | bytes 6291456 | tf_op jit(solution)/shard_map/attend/pallas_call | solution.py:483
  77.5 2.8 %collective-permute-done.34 = bf16[512,256]{0,1:T(8,128)(2,1)S(1)} collective-permute-done((bf16[512,256]{0,1:T(8,128)(2,1)S(1)}, bf16[512,256]{0,1:T(8,128)(2,1)S(1)}, u32[]{:S(2)}, u32[]{:S(2)}) %collective-permute-start.34) | collective-permute-done | bytes 262176 | tf_op jit(solution)/shard_map/ppermute | solution.py:215
  81.0 2.5 %collective-permute-start.24 = (bf16[1024,128]{1,0:T(8,128)(2,1)S(1)}, bf16[1024,128]{1,0:T(8,128)(2,1)S(1)}, u32[]{:S(2)}, u32[]{:S(2)}) collective-permute-start(bf16[1024,128]{1,0:T(8,128)(2,1)S(1)} %get-tuple-element.42), channel_id=1, source_target_pairs={{0,16},{2,18},{4,20},{6,22},{8,24},{10,26},{12,28},{14,30},{16,0},... | collective-permute-start | bytes 786440 | tf_op jit(solution)/shard_map/ppermute | solution.py:215
  85.0 16.4 %collective-permute-done.19 = bf16[512,128]{1,0:T(8,128)(2,1)S(1)} collective-permute-done((bf16[512,128]{1,0:T(8,128)(2,1)S(1)}, bf16[512,128]{1,0:T(8,128)(2,1)S(1)}, u32[]{:S(2)}, u32[]{:S(2)}) %collective-permute-start.19) | collective-permute-done | bytes 131104 | tf_op jit(solution)/shard_map/ppermute | solution.py:215
  107.7 6.1 %collective-permute-done.25.refs_1_ = bf16[1024,128]{1,0:T(8,128)(2,1)S(1)} collective-permute-done((bf16[1024,128]{1,0:T(8,128)(2,1)S(1)}, bf16[1024,128]{1,0:T(8,128)(2,1)S(1)}, u32[]{:S(2)}, u32[]{:S(2)}) %collective-permute-start.25) | collective-permute-done | bytes 262176 | tf_op jit(solution)/shard_map/ppermute | solution.py:215
  113.8 4.2 %collective-permute-done.27.refs_3_ = bf16[1024,128]{1,0:T(8,128)(2,1)S(1)} collective-permute-done((bf16[1024,128]{1,0:T(8,128)(2,1)S(1)}, bf16[1024,128]{1,0:T(8,128)(2,1)S(1)}, u32[]{:S(2)}, u32[]{:S(2)}) %collective-permute-start.27) | collective-permute-done | bytes 262176 | tf_op jit(solution)/shard_map/ppermute | solution.py:215
  128.3 2.3 %collective-permute-done.22.refs_7_ = bf16[128,128]{1,0:T(8,128)(2,1)S(1)} collective-permute-done((bf16[128,128]{1,0:T(8,128)(2,1)}, bf16[128,128]{1,0:T(8,128)(2,1)S(1)}, u32[]{:S(2)}, u32[]{:S(2)}) %collective-permute-start.22) | collective-permute-done | bytes 32800 | tf_op jit(solution)/shard_map/ppermute | solution.py:215
  133.3 1.8 %place_rows.1 = (bf16[128,2048]{1,0:T(8,128)(2,1)}, bf16[128,512]{1,0:T(8,128)(2,1)}) custom-call(bf16[128,512]{1,0:T(8,128)(2,1)S(1)} %bitcast.48, bf16[128,512]{1,0:T(8,128)(2,1)S(1)} %copy-done.8, bf16[128,512]{1,0:T(8,128)(2,1)S(1)} %copy-done.10, bf16[128,512]{1,0:T(8,128)(2,1)} %collective-permute-done.17.refs_3_, bf16[128,128]{1,0:T(8,128)(2,1)S(1)} %copy-done.11, ...), custom_call_target="tpu_custom_call" | custom-call | tf_op jit(solution)/shard_map/place_rows/pallas_call | solution.py:571
  135.1 2.2 %copy-done.1 = bf16[4096,512]{1,0:T(8,128)(2,1)S(1)} copy-done((bf16[4096,512]{1,0:T(8,128)(2,1)S(1)}, bf16[4096,512]{1,0:T(8,128)(2,1)}, u32[]{:S(2)}) %copy-start.1) | copy-done | bytes 4194328
  137.2 3.8 %input_grad.1 = bf16[128,2048]{1,0:T(8,128)(2,1)} custom-call(s32[3]{0:T(128)S(1)} %pad_add_fusion.1.ids_ref, bf16[4,128,128]{2,1,0:T(8,128)(2,1)S(1)} %pad_maximum_fusion.1.own_ref, bf16[4,128,128]{2,1,0:T(8,128)(2,1)S(1)} %collective-permute-done.28.other_ref, bf16[4096,512]{1,0:T(8,128)(2,1)S(1)} %copy-done.1, ...), custom_call_target="tpu_custom_call" | custom-call | flops 536870912 | bytes 5242880 | tf_op jit(solution)/shard_map/input_grad/pallas_call | solution.py:541
  141.1 1.9 %fusion = f32[256,512]{1,0:T(8,128)} fusion(f32[256,512]{1,0:T(8,128)} %collective-permute-done.36, f32[2,256,512]{2,1,0:T(8,128)S(1)} %weight_grad.1), kind=kLoop, calls=%fused_computation.2 | loop fusion | flops 131072 | bytes 1572864 | tf_op jit(solution)/shard_map/add | solution.py:535
  (127 shorter events, 40.3 us)
Async XLA Ops:
  0.6 19.5 %collective-permute-start = (s32[2]{0:T(128)}, s32[2]{0:T(128)S(1)}, u32[]{:S(2)}, u32[]{:S(2)}) collective-permute-start(s32[2]{0:T(128)} %param.13), channel_id=1, source_target_pairs={{0,4},{2,6},{4,0},{6,2},{8,12},{10,14},{12,8},{14,10},{16,20},{18,... | collective-permute-start | bytes 32 | tf_op jit(solution)/shard_map/ppermute | solution.py:215
  3.6 16.6 %collective-permute-start.1 = (s32[2]{0:T(128)}, s32[2]{0:T(128)S(1)}, u32[]{:S(2)}, u32[]{:S(2)}) collective-permute-start(s32[2]{0:T(128)} %param.13), channel_id=1, source_target_pairs={{0,8},{2,10},{4,12},{6,14},{8,0},{10,2},{12,4},{14,6},{16,24},{18,... | collective-permute-start | bytes 32 | tf_op jit(solution)/shard_map/ppermute | solution.py:215
  5.2 16.9 %collective-permute-start.2 = (s32[2]{0:T(128)}, s32[2]{0:T(128)S(1)}, u32[]{:S(2)}, u32[]{:S(2)}) collective-permute-start(s32[2]{0:T(128)} %param.13), channel_id=1, source_target_pairs={{0,12},{2,14},{4,8},{6,10},{8,4},{10,6},{12,0},{14,2},{16,28},{18,... | collective-permute-start | bytes 32 | tf_op jit(solution)/shard_map/ppermute | solution.py:215
  11.7 19.5 %collective-permute-start.9 = (bf16[128,256]{1,0:T(8,128)(2,1)S(1)}, bf16[128,256]{1,0:T(8,128)(2,1)}, u32[]{:S(2)}, u32[]{:S(2)}) collective-permute-start(bf16[128,256]{1,0:T(8,128)(2,1)S(1)} %get-tuple-element.28), channel_id=1, source_target_pairs={{0,4},{2,6},{4,0},{6,2},{8,12},{10,14},{12,8},{14,10},{16,20},{18,... | collective-permute-start | bytes 196616 | tf_op jit(solution)/shard_map/ppermute | solution.py:215
  13.7 18.5 %collective-permute-start.10 = (bf16[128,256]{1,0:T(8,128)(2,1)S(1)}, bf16[128,256]{1,0:T(8,128)(2,1)}, u32[]{:S(2)}, u32[]{:S(2)}) collective-permute-start(bf16[128,256]{1,0:T(8,128)(2,1)S(1)} %get-tuple-element.29), channel_id=1, source_target_pairs={{0,8},{2,10},{4,12},{6,14},{8,0},{10,2},{12,4},{14,6},{16,24},{18,... | collective-permute-start | bytes 196616 | tf_op jit(solution)/shard_map/ppermute | solution.py:215
  20.1 15.7 %collective-permute-start.11 = (bf16[128,256]{1,0:T(8,128)(2,1)S(1)}, bf16[128,256]{1,0:T(8,128)(2,1)S(1)}, u32[]{:S(2)}, u32[]{:S(2)}) collective-permute-start(bf16[128,256]{1,0:T(8,128)(2,1)S(1)} %get-tuple-element.30), channel_id=1, source_target_pairs={{0,12},{2,14},{4,8},{6,10},{8,4},{10,6},{12,0},{14,2},{16,28},{18,... | collective-permute-start | bytes 196616 | tf_op jit(solution)/shard_map/ppermute | solution.py:215
  20.2 43.5 %collective-permute-start.6 = (bf16[128,1024]{1,0:T(8,128)(2,1)S(1)}, bf16[128,1024]{1,0:T(8,128)(2,1)S(1)}, u32[]{:S(2)}, u32[]{:S(2)}) collective-permute-start(bf16[128,1024]{1,0:T(8,128)(2,1)S(1)} %get-tuple-element.24), channel_id=1, source_target_pairs={{0,4},{2,6},{4,0},{6,2},{8,12},{10,14},{12,8},{14,10},{16,20},{18,... | collective-permute-start | bytes 786440 | tf_op jit(solution)/shard_map/ppermute | solution.py:215
  28.9 36.5 %collective-permute-start.7 = (bf16[128,1024]{1,0:T(8,128)(2,1)S(1)}, bf16[128,1024]{1,0:T(8,128)(2,1)S(1)}, u32[]{:S(2)}, u32[]{:S(2)}) collective-permute-start(bf16[128,1024]{1,0:T(8,128)(2,1)S(1)} %get-tuple-element.25), channel_id=1, source_target_pairs={{0,8},{2,10},{4,12},{6,14},{8,0},{10,2},{12,4},{14,6},{16,24},{18,... | collective-permute-start | bytes 786440 | tf_op jit(solution)/shard_map/ppermute | solution.py:215
  31.2 34.2 %collective-permute-start.8 = (bf16[128,1024]{1,0:T(8,128)(2,1)S(1)}, bf16[128,1024]{1,0:T(8,128)(2,1)S(1)}, u32[]{:S(2)}, u32[]{:S(2)}) collective-permute-start(bf16[128,1024]{1,0:T(8,128)(2,1)S(1)} %get-tuple-element.26), channel_id=1, source_target_pairs={{0,12},{2,14},{4,8},{6,10},{8,4},{10,6},{12,0},{14,2},{16,28},{18,... | collective-permute-start | bytes 786440 | tf_op jit(solution)/shard_map/ppermute | solution.py:215
  32.2 13.5 %collective-permute-start.33 = (bf16[2,128,256]{1,2,0:T(8,128)(2,1)}, bf16[2,128,256]{1,2,0:T(8,128)(2,1)S(1)}, u32[]{:S(2)}, u32[]{:S(2)}) collective-permute-start(bf16[2,128,256]{1,2,0:T(8,128)(2,1)} %copy.14), channel_id=1, source_target_pairs={{0,12},{2,14},{4,8},{6,10},{8,4},{10,6},{12,0},{14,2},{16,28},{18,... | collective-permute-start | bytes 393224 | tf_op jit(solution)/shard_map/ppermute | solution.py:215
  35.9 17.5 %collective-permute-start.31 = (bf16[2,128,256]{1,2,0:T(8,128)(2,1)}, bf16[2,128,256]{1,2,0:T(8,128)(2,1)S(1)}, u32[]{:S(2)}, u32[]{:S(2)}) collective-permute-start(bf16[2,128,256]{1,2,0:T(8,128)(2,1)} %copy.12), channel_id=1, source_target_pairs={{0,4},{2,6},{4,0},{6,2},{8,12},{10,14},{12,8},{14,10},{16,20},{18,... | collective-permute-start | bytes 393224 | tf_op jit(solution)/shard_map/ppermute | solution.py:215
  50.6 13.1 %collective-permute-start.13 = (bf16[512,256]{1,0:T(8,128)(2,1)S(1)}, bf16[512,256]{1,0:T(8,128)(2,1)S(1)}, u32[]{:S(2)}, u32[]{:S(2)}) collective-permute-start(bf16[512,256]{1,0:T(8,128)(2,1)S(1)} %constant_dynamic-update-slice_fusion.refs_4_), channel_id=1, source_target_pairs={{0,16},{2,18},{4,20},{6,22},{8,24},{10,26},{12,28},{14,30},{16,0},... | collective-permute-start | bytes 786440 | tf_op jit(solution)/shard_map/ppermute | solution.py:215
  53.4 12.0 %collective-permute-start.12 = (bf16[512,256]{1,0:T(8,128)(2,1)S(1)}, bf16[512,256]{1,0:T(8,128)(2,1)S(1)}, u32[]{:S(2)}, u32[]{:S(2)}) collective-permute-start(bf16[512,256]{1,0:T(8,128)(2,1)S(1)} %constant_dynamic-update-slice_fusion.refs_4_), channel_id=1, source_target_pairs={{0,2},{2,0},{4,6},{6,4},{8,10},{10,8},{12,14},{14,12},{16,18},{18,... | collective-permute-start | bytes 786440 | tf_op jit(solution)/shard_map/ppermute | solution.py:215
  63.8 43.5 %collective-permute-start.29 = (bf16[1024,512]{1,0:T(8,128)(2,1)}, bf16[1024,512]{1,0:T(8,128)(2,1)S(1)}, u32[]{:S(2)}, u32[]{:S(2)}) collective-permute-start(bf16[1024,512]{1,0:T(8,128)(2,1)} %constant_dynamic-slice_fusion), channel_id=1, source_target_pairs={{0,1},{1,0},{2,3},{3,2},{4,5},{5,4},{6,7},{7,6},{8,9},{9,8},{10,11... | collective-permute-start | bytes 3145736 | tf_op jit(solution)/shard_map/ppermute | solution.py:219
  65.3 15.0 %collective-permute-start.34 = (bf16[512,256]{0,1:T(8,128)(2,1)S(1)}, bf16[512,256]{0,1:T(8,128)(2,1)S(1)}, u32[]{:S(2)}, u32[]{:S(2)}) collective-permute-start(bf16[512,256]{0,1:T(8,128)(2,1)S(1)} %pad_maximum_fusion), channel_id=1, source_target_pairs={{0,16},{2,18},{4,20},{6,22},{8,24},{10,26},{12,28},{14,30},{16,0},... | collective-permute-start | bytes 786440 | tf_op jit(solution)/shard_map/ppermute | solution.py:215
  80.3 25.4 %collective-permute-start.35 = (bf16[256,1024]{1,0:T(8,128)(2,1)S(1)}, bf16[256,1024]{1,0:T(8,128)(2,1)S(1)}, u32[]{:S(2)}, u32[]{:S(2)}) collective-permute-start(bf16[256,1024]{1,0:T(8,128)(2,1)S(1)} %bitcast.46), channel_id=1, source_target_pairs={{0,1},{1,0},{2,3},{3,2},{4,5},{5,4},{6,7},{7,6},{8,9},{9,8},{10,11... | collective-permute-start | bytes 1572872 | tf_op jit(solution)/shard_map/ppermute | solution.py:219
  81.0 20.4 %collective-permute-start.24 = (bf16[1024,128]{1,0:T(8,128)(2,1)S(1)}, bf16[1024,128]{1,0:T(8,128)(2,1)S(1)}, u32[]{:S(2)}, u32[]{:S(2)}) collective-permute-start(bf16[1024,128]{1,0:T(8,128)(2,1)S(1)} %get-tuple-element.42), channel_id=1, source_target_pairs={{0,16},{2,18},{4,20},{6,22},{8,24},{10,26},{12,28},{14,30},{16,0},... | collective-permute-start | bytes 786440 | tf_op jit(solution)/shard_map/ppermute | solution.py:215
  83.6 17.8 %collective-permute-start.19 = (bf16[512,128]{1,0:T(8,128)(2,1)S(1)}, bf16[512,128]{1,0:T(8,128)(2,1)S(1)}, u32[]{:S(2)}, u32[]{:S(2)}) collective-permute-start(bf16[512,128]{1,0:T(8,128)(2,1)S(1)} %slice.159), channel_id=1, source_target_pairs={{0,16},{2,18},{4,20},{6,22},{8,24},{10,26},{12,28},{14,30},{16,0},... | collective-permute-start | bytes 393224 | tf_op jit(solution)/shard_map/ppermute | solution.py:215
  101.5 12.3 %collective-permute-start.25 = (bf16[1024,128]{1,0:T(8,128)(2,1)S(1)}, bf16[1024,128]{1,0:T(8,128)(2,1)S(1)}, u32[]{:S(2)}, u32[]{:S(2)}) collective-permute-start(bf16[1024,128]{1,0:T(8,128)(2,1)S(1)} %add_convert_fusion.refs_0_), channel_id=1, source_target_pairs={{0,4},{2,6},{4,0},{6,2},{8,12},{10,14},{12,8},{14,10},{16,20},{18,... | collective-permute-start | bytes 786440 | tf_op jit(solution)/shard_map/ppermute | solution.py:215
  103.5 14.5 %collective-permute-start.27 = (bf16[1024,128]{1,0:T(8,128)(2,1)S(1)}, bf16[1024,128]{1,0:T(8,128)(2,1)S(1)}, u32[]{:S(2)}, u32[]{:S(2)}) collective-permute-start(bf16[1024,128]{1,0:T(8,128)(2,1)S(1)} %add_convert_fusion.refs_0_), channel_id=1, source_target_pairs={{0,12},{2,14},{4,8},{6,10},{8,4},{10,6},{12,0},{14,2},{16,28},{18,... | collective-permute-start | bytes 786440 | tf_op jit(solution)/shard_map/ppermute | solution.py:215
  105.7 15.1 %collective-permute-start.15 = (bf16[128,512]{1,0:T(8,128)(2,1)S(1)}, bf16[128,512]{1,0:T(8,128)(2,1)S(1)}, u32[]{:S(2)}, u32[]{:S(2)}) collective-permute-start(bf16[128,512]{1,0:T(8,128)(2,1)S(1)} %bitcast.50), channel_id=1, source_target_pairs={{0,4},{2,6},{4,0},{6,2},{8,12},{10,14},{12,8},{14,10},{16,20},{18,... | collective-permute-start | bytes 393224 | tf_op jit(solution)/shard_map/ppermute | solution.py:215
  107.3 15.7 %collective-permute-start.16 = (bf16[128,512]{1,0:T(8,128)(2,1)S(1)}, bf16[128,512]{1,0:T(8,128)(2,1)S(1)}, u32[]{:S(2)}, u32[]{:S(2)}) collective-permute-start(bf16[128,512]{1,0:T(8,128)(2,1)S(1)} %bitcast.49), channel_id=1, source_target_pairs={{0,8},{2,10},{4,12},{6,14},{8,0},{10,2},{12,4},{14,6},{16,24},{18,... | collective-permute-start | bytes 393224 | tf_op jit(solution)/shard_map/ppermute | solution.py:215
  113.8 21.3 %collective-permute-start.30 = (bf16[1024,512]{1,0:T(8,128)(2,1)S(1)}, bf16[1024,512]{1,0:T(8,128)(2,1)S(1)}, u32[]{:S(2)}, u32[]{:S(2)}) collective-permute-start(bf16[1024,512]{1,0:T(8,128)(2,1)S(1)} %collective-permute-done.29.w_near), channel_id=1, source_target_pairs={{0,2},{2,0},{4,6},{6,4},{8,10},{10,8},{12,14},{14,12},{16,18},{18,... | collective-permute-start | bytes 3145736 | tf_op jit(solution)/shard_map/ppermute | solution.py:215
  120.7 20.3 %collective-permute-start.36 = (f32[256,512]{1,0:T(8,128)}, f32[256,512]{1,0:T(8,128)}, u32[]{:S(2)}, u32[]{:S(2)}) collective-permute-start(f32[256,512]{1,0:T(8,128)} %slice_bitcast_fusion), channel_id=1, source_target_pairs={{0,2},{2,0},{4,6},{6,4},{8,10},{10,8},{12,14},{14,12},{16,18},{18,... | collective-permute-start | bytes 1572872 | tf_op jit(solution)/shard_map/ppermute | solution.py:215
  (30 other events, 256.5 us)

commit v2 on v1

--- a/solution.py
+++ b/solution.py
@@ -206,9 +206,14 @@
 GROUP = 4
 ROWS = 128
 TILE = 256
+STACK_BYTES = 8 << 20
+PART = 512
+MARKED = ROWS + 16
 Q_BLOCKS = GROUP * ROWS // BLK
 SMEM = pltpu.SMEM
 VMEM = pltpu.VMEM
+HBM = pltpu.HBM
+DMA = pltpu.SemaphoreType.DMA
 
 
 def swap(array, mask):
@@ -231,38 +236,87 @@
     return pl.BlockSpec(memory_space=space)
 
 
-def pack_rows(queries_ref, grads_ref, *out_refs):
+def after(array, *earlier):
+    return lax.optimization_barrier((array,) + earlier)[0]
+
+
+def copy_all(pairs, semaphores):
+    copies = [
+        pltpu.make_async_copy(source, target, semaphores.at[i])
+        for i, (source, target) in enumerate(pairs)
+    ]
+    for copy in copies:
+        copy.start()
+    return copies
+
+
+def project_keys(pos_ref, inputs_ref, values_ref, w_ref, *refs):
+    pair_refs, leaving_ref = refs[:GROUP], refs[GROUP]
+    inputs, weights, total, semaphores = refs[GROUP + 1 :]
     head = own_head()
-    for m, out_ref in enumerate(out_refs):
+    spans = [pl.ds(k * PART, PART) for k in range(weights.shape[0] // PART)]
+    copies = copy_all(
+        [(inputs_ref, inputs)] + [(w_ref.at[span], weights.at[span]) for span in spans],
+        semaphores,
+    )
+    lanes = lax.broadcasted_iota(jnp.int32, (16, 2 * HD), 1)
+    marks = jnp.where(lanes == 0, pos_ref[0], jnp.where(lanes == 1, pos_ref[1], 0))
+    for m in range(GROUP):
+        pair_refs[m][:ROWS, HD:] = values_ref[:, columns(head ^ m, HD)]
+        pair_refs[m][ROWS:] = marks.astype(jnp.float32).astype(jnp.bfloat16)
+    copies[0].wait()
+    for k, span in enumerate(spans):
+        copies[1 + k].wait()
+        part = jnp.dot(inputs[:, span], weights[span], preferred_element_type=jnp.float32)
+        total[...] = part if k == 0 else total[...] + part
+    first = (1 - lax.axis_index("tensor")) * 2 + (lax.axis_index("dp") & 1)
+    leave = pltpu.make_async_copy(
+        weights.at[columns(first, 1024)], leaving_ref, semaphores.at[0]
+    )
+    leave.start()
+    for m in range(GROUP):
+        pair_refs[m][:ROWS, :HD] = total[:, columns(head ^ m, HD)].astype(jnp.bfloat16)
+    leave.wait()
+
+
+def pack_rows(queries_ref, grads_ref, *refs):
+    out_refs, semaphores = refs[:GROUP], refs[GROUP]
+    head = own_head()
+    pairs = []
+    for m in range(GROUP):
         span = columns(head ^ m, GROUP * HD)
-        out_ref[:, : GROUP * HD] = queries_ref[:, span]
-        out_ref[:, GROUP * HD :] = grads_ref[:, span]
-
-
-def project_keys(inputs_ref, values_ref, w_ref, *refs):
-    pair_refs, feature_refs, total = refs[:GROUP], refs[GROUP : 2 * GROUP], refs[-1]
-    step = pl.program_id(0)
-    head = own_head()
-
-    @pl.when(step == 0)
-    def _():
-        total[...] = jnp.zeros_like(total)
-        chip = lax.axis_index("dp") >> 1
-        side = lax.axis_index("tensor")
-        for m in range(GROUP):
-            pair_refs[m][:, HD:] = values_ref[:, columns(head ^ m, HD)]
-            for far in range(2):
-                target = chip ^ (m + GROUP * far)
-                feature_refs[m][far] = inputs_ref[:, columns(2 * target + side, 256)]
-
-    total[...] += jnp.dot(
-        inputs_ref[:, columns(step, 512)], w_ref[...], preferred_element_type=jnp.float32
-    )
-
-    @pl.when(step == pl.num_programs(0) - 1)
-    def _():
-        for m in range(GROUP):
-            pair_refs[m][:, :HD] = total[:, columns(head ^ m, HD)].astype(jnp.bfloat16)
+        pairs.append((queries_ref.at[:, span], out_refs[m].at[:, : GROUP * HD]))
+        pairs.append((grads_ref.at[:, span], out_refs[m].at[:, GROUP * HD :]))
+    for copy in copy_all(pairs, semaphores):
+        copy.wait()
+
+
+def pack_features(inputs_ref, near_ref, far_ref, semaphores):
+    chip = lax.axis_index("dp") >> 1
+    side = lax.axis_index("tensor")
+    pairs = []
+    for m in range(GROUP):
+        span = columns(2 * (chip ^ m) + side, 256)
+        pairs.append((inputs_ref.at[:, span], near_ref.at[m]))
+        span = columns(2 * (chip ^ (m + GROUP)) + side, 256)
+        pairs.append((inputs_ref.at[:, span], far_ref.at[m]))
+    for copy in copy_all(pairs, semaphores):
+        copy.wait()
+
+
+def join_features(near_ref, far_ref, *refs):
+    pairs = []
+    for m, joined_ref in enumerate(refs[:GROUP]):
+        pairs.append((near_ref.at[m], joined_ref.at[0]))
+        pairs.append((far_ref.at[m], joined_ref.at[1]))
+    for copy in copy_all(pairs, refs[GROUP]):
+        copy.wait()
+
+
+def turn_features(*refs):
+    for j in range(2 * GROUP):
+        turned = refs[j % GROUP][j // GROUP].astype(jnp.float32).T
+        refs[-1][:, j * ROWS : (j + 1) * ROWS] = turned.astype(jnp.bfloat16)
 
 
 def dot_nt(left, right):
@@ -275,13 +329,8 @@
     return reduce(array.reshape(-1, 8, array.shape[-1]), axis=0)
 
 
-def attend(pos_ref, lens_ref, *refs):
-    row_refs, pair_refs, refs = refs[:GROUP], refs[GROUP : 2 * GROUP], refs[2 * GROUP :]
-    dq_ref, dk_keep, dk_send, dv_keep, dv_send = refs[:5]
-    q_rows, g_rows, keys, keys_t, values, dk, dv, scores, d_prob = refs[5:]
-    score_scale = 1.0 / math.sqrt(HD)
-    base_two = score_scale * math.log2(math.e)
-
+def stack_rows(*refs):
+    row_refs, (q_rows, g_rows) = refs[:GROUP], refs[GROUP:]
     for block in range(Q_BLOCKS):
         here = pl.ds(block % 2 * BLK, BLK)
         for h in range(GROUP):
@@ -290,9 +339,33 @@
             g_rows[block, there] = row_refs[block // 2][
                 here, (GROUP + h) * HD : (GROUP + h + 1) * HD
             ]
+
+
+def attend(lens_ref, q_rows, g_rows, own_pairs, far_pairs, core_pairs, *refs):
+    reach = GROUP * MARKED
+    pair_refs = [own_pairs, core_pairs.at[:reach], far_pairs, core_pairs.at[reach:]]
+    dq_refs, refs = refs[:GROUP], refs[GROUP:]
+    dk_keep, dk_send, dv_keep, dv_send = refs[:4]
+    keys, keys_t, values, dk, dv, dq_all, scores, d_prob = refs[4:12]
+    marks, positions, semaphore = refs[12:]
+    score_scale = 1.0 / math.sqrt(HD)
+    base_two = score_scale * math.log2(math.e)
+
+    for part in range(4 * GROUP):
+        here = pl.ds(part % GROUP * MARKED + ROWS, 16)
+        row = pair_refs[part // GROUP][here, :HD].astype(jnp.float32).astype(jnp.int32)
+        marks[part : part + 1] = row[:1]
+    to_scalars = pltpu.make_async_copy(marks, positions, semaphore)
+    to_scalars.start()
+    to_scalars.wait()
+
+    def first_row(block):
+        return pl.multiple_of(positions[block // 2, block % 2] * BLK, BLK)
+
     for block in range(4 * Q_BLOCKS):
-        here = pl.ds(block % Q_BLOCKS * BLK, BLK)
-        there = pl.ds(pl.multiple_of(pos_ref[block] * BLK, BLK), BLK)
+        part = block // 2 % GROUP
+        here = pl.ds(part * MARKED + block % 2 * BLK, BLK)
+        there = pl.ds(first_row(block), BLK)
         keys[there] = pair_refs[block // Q_BLOCKS][here, :HD]
         values[there] = pair_refs[block // Q_BLOCKS][here, HD:]
     for tile in range(keys.shape[0] // TILE):
@@ -312,7 +385,7 @@
 
     @pl.loop(0, Q_BLOCKS)
     def _(block):
-        first = pos_ref[block] * BLK
+        first = first_row(block)
         lanes = lax.broadcasted_iota(jnp.int32, (1, GROUP * BLK), 1)
         position = first + (lanes & (BLK - 1))
         start = document_start(position)
@@ -366,18 +439,20 @@
         )
         dq = (dq * score_scale).T.astype(jnp.bfloat16)
         for h in range(GROUP):
-            dq_ref[block, :, h * HD : (h + 1) * HD] = dq[h * BLK : (h + 1) * BLK]
-
+            dq_all[block, :, h * HD : (h + 1) * HD] = dq[h * BLK : (h + 1) * BLK]
+
+    for block in range(Q_BLOCKS):
+        dq_refs[block // 2][pl.ds(block % 2 * BLK, BLK)] = dq_all[block]
     for block in range(4 * Q_BLOCKS):
         quarter = block // Q_BLOCKS
         here = pl.ds(quarter // 2 * Q_BLOCKS * BLK + block % Q_BLOCKS * BLK, BLK)
-        there = pl.ds(pl.multiple_of(pos_ref[block] * BLK, BLK), BLK)
+        there = pl.ds(first_row(block), BLK)
         (dk_send if quarter % 2 else dk_keep)[here] = dk[there] * score_scale
         (dv_send if quarter % 2 else dv_keep)[here] = dv[there]
 
 
 def weight_grad(own_ref, other_ref, *refs):
-    grad_refs, out_ref, grads = refs[:GROUP], refs[GROUP], refs[GROUP + 1]
+    grad_refs, (keep_ref, send_ref, grads) = refs[:GROUP], refs[GROUP:]
     head = own_head()
     for k, grad_ref in enumerate(grad_refs):
         for far in range(2):
@@ -385,39 +460,56 @@
                 here = pl.ds((far * GROUP + m) * ROWS, ROWS)
                 there = pl.ds((far * GROUP + (m ^ k)) * ROWS, ROWS)
                 grads[here, columns(head ^ k, HD)] = grad_ref[there]
-    slot = (lax.axis_index("dp") & 1) ^ lax.axis_index("tensor")
-    out_ref[slot] = jnp.dot(own_ref[...], grads[...], preferred_element_type=jnp.float32)
-    out_ref[1 - slot] = jnp.dot(other_ref[...], grads[...], preferred_element_type=jnp.float32)
-
-
-def input_grad(ids_ref, own_ref, other_ref, w_own, w_near, w_far, out_ref, own_all, other_all):
-    step = pl.program_id(0)
-    head = ids_ref[0]
-
-    @pl.when(step == 0)
+    own = jnp.dot(own_ref[...], grads[...], preferred_element_type=jnp.float32)
+    other = jnp.dot(other_ref[...], grads[...], preferred_element_type=jnp.float32)
+    crossed = (lax.axis_index("dp") & 1) ^ lax.axis_index("tensor")
+
+    @pl.when(crossed == 0)
     def _():
-        for k in range(GROUP):
-            own_all[:, columns(head ^ k, HD)] = own_ref[k]
-            other_all[:, columns(head ^ k, HD)] = other_ref[k]
-
-    part = dot_nt(own_all[...], w_own[...])
-
-    @pl.when(step < 2)
+        keep_ref[...] = own
+        send_ref[...] = other
+
+    @pl.when(crossed == 1)
     def _():
-        out_ref[...] = (part + dot_nt(other_all[...], w_near[...])).astype(jnp.bfloat16)
-
-    @pl.when(step >= 2)
-    def _():
-        out_ref[...] = (part + dot_nt(other_all[...], w_far[...])).astype(jnp.bfloat16)
+        keep_ref[...] = other
+        send_ref[...] = own
+
+
+def input_grad(own_ref, other_ref, w_own, w_near, w_far, out_ref, *refs):
+    own_all, other_all, own_weights, other_weights, semaphores = refs
+    head = own_head()
+    core = lax.axis_index("dp") & 1
+    side = lax.axis_index("tensor")
+    halves = [core, 1 - core]
+    pairs = []
+    for k in range(4):
+        half, span = halves[k // 2], pl.ds(k * PART, PART)
+        pairs.append((w_own.at[columns(side * 4 + half * 2 + k % 2, PART)], own_weights.at[span]))
+        source = (w_near, w_far)[k // 2].at[pl.ds(k % 2 * PART, PART)]
+        pairs.append((source, other_weights.at[span]))
+    copies = copy_all(pairs, semaphores)
+    for k in range(GROUP):
+        own_all[:, columns(head ^ k, HD)] = own_ref[k]
+        other_all[:, columns(head ^ k, HD)] = other_ref[k]
+    for k in range(4):
+        span = pl.ds(k * PART, PART)
+        copies[2 * k].wait()
+        part = dot_nt(own_all[...], own_weights[span])
+        copies[2 * k + 1].wait()
+        part = part + dot_nt(other_all[...], other_weights[span])
+        out_ref[:, columns(halves[k // 2] * 2 + k % 2, PART)] = part.astype(jnp.bfloat16)
+
+
+def finish(keep_ref, arrived_ref, *refs):
+    value_refs, (weight_out, value_out) = refs[:GROUP], refs[GROUP:]
+    weight_out[...] = keep_ref[...] + arrived_ref[...]
+    for m in range(GROUP):
+        value_out[:, columns(own_head() ^ m, HD)] = value_refs[m][...]
 
 
 def place_rows(*refs):
-    dq_refs, dv_refs = refs[:GROUP], refs[GROUP : 2 * GROUP]
-    dq_out, dv_out = refs[2 * GROUP :]
-    head = own_head()
-    for m in range(GROUP):
-        dq_out[:, columns(head ^ m, GROUP * HD)] = dq_refs[m][...]
-        dv_out[:, columns(head ^ m, HD)] = dv_refs[m][...]
+    for m, ref in enumerate(refs[:GROUP]):
+        refs[GROUP][:, columns(own_head() ^ m, GROUP * HD)] = ref[...]
 
 
 def shaped(shape, dtype=jnp.bfloat16):
@@ -426,105 +518,152 @@
 
 def limits(mebibytes):
     return pltpu.CompilerParams(vmem_limit_bytes=mebibytes << 20)
+
+
+def with_partners(arrays):
+    return [arrays[0]] + [swap(arrays[m], 2 * m) for m in (1, 2, 3)]
 
 
 def on_device_by_heads(inputs, w_key, values, queries, d_out, doc_lens, block_pos):
     features = inputs.shape[1]
     kv_columns = values.shape[1]
     total_rows = 16 * ROWS
-    index = lax.axis_index("dp")
-    side = lax.axis_index("tensor")
-    core = index & 1
-    vmem, smem = whole_spec(), whole_spec(SMEM)
-
-    packed_rows = pl.pallas_call(
-        pack_rows,
-        out_shape=[shaped((ROWS, 2 * GROUP * HD))] * GROUP,
-        in_specs=[vmem] * 2,
-        out_specs=[vmem] * GROUP,
-        compiler_params=limits(16),
-        name="pack_rows",
-    )(queries, d_out)
-    rows = [packed_rows[0]] + [swap(packed_rows[m], 2 * m) for m in (1, 2, 3)]
-
-    steps = features // 512
-    projected = pl.pallas_call(
+    half, quarter = total_rows // 2, total_rows // 4
+    vmem, smem, hbm = whole_spec(), whole_spec(SMEM), whole_spec(HBM)
+
+    near_features, far_features = pl.pallas_call(
+        pack_features,
+        out_shape=[shaped((GROUP, ROWS, 256))] * 2,
+        in_specs=[hbm],
+        out_specs=[hbm] * 2,
+        scratch_shapes=[DMA((2 * GROUP,))],
+        compiler_params=limits(60),
+        name="pack_features",
+    )(inputs)
+    far_features = swap(far_features, Z_HI)
+    *pairs, leaving = pl.pallas_call(
         project_keys,
-        out_shape=[shaped((ROWS, 2 * HD))] * GROUP + [shaped((2, ROWS, 256))] * GROUP,
-        grid=(steps,),
-        in_specs=[
-            pl.BlockSpec((ROWS, features), lambda k: (0, 0)),
-            pl.BlockSpec((ROWS, kv_columns), lambda k: (0, 0)),
-            pl.BlockSpec((512, kv_columns), lambda k: (k, 0)),
+        out_shape=[shaped((MARKED, 2 * HD))] * GROUP + [shaped((1024, kv_columns))],
+        in_specs=[smem, hbm, vmem, hbm],
+        out_specs=[vmem] * GROUP + [hbm],
+        scratch_shapes=[
+            VMEM((ROWS, features), jnp.bfloat16),
+            VMEM((features, kv_columns), jnp.bfloat16),
+            VMEM((ROWS, kv_columns), jnp.float32),
+            DMA((1 + features // PART,)),
         ],
-        out_specs=[pl.BlockSpec((ROWS, 2 * HD), lambda k: (0, 0))] * GROUP
-        + [pl.BlockSpec((2, ROWS, 256), lambda k: (0, 0, 0))] * GROUP,
-        scratch_shapes=[VMEM((ROWS, kv_columns), jnp.float32)],
-        compiler_params=limits(24),
+        compiler_params=limits(60),
         cost_estimate=pl.CostEstimate(
             flops=2 * ROWS * features * kv_columns,
             bytes_accessed=features * kv_columns * 2,
             transcendentals=0,
         ),
         name="project_keys",
-    )(inputs, values, w_key)
-    pairs, feature_parts = projected[:GROUP], projected[GROUP:]
-
-    own_pairs = jnp.concatenate([pairs[0]] + [swap(pairs[m], 2 * m) for m in (1, 2, 3)], axis=0)
+    )(block_pos, after(inputs, near_features), values, w_key)
+    packed_rows = pl.pallas_call(
+        pack_rows,
+        out_shape=[shaped((ROWS, 2 * GROUP * HD))] * GROUP,
+        in_specs=[hbm] * 2,
+        out_specs=[hbm] * GROUP,
+        scratch_shapes=[DMA((2 * GROUP,))],
+        compiler_params=limits(60),
+        name="pack_rows",
+    )(after(queries, pairs[0]), d_out)
+    w_near = swap_tensor(leaving)
+    own_pairs = jnp.concatenate(with_partners([after(pairs[0], packed_rows[0], far_features)] + pairs[1:]), axis=0)
     far_pairs = swap(own_pairs, Z_HI)
-    core_pairs = swap(own_pairs, CORE)
-    far_core_pairs = swap(far_pairs, CORE)
-
-    own_pos = jnp.concatenate([block_pos] + [swap(block_pos, 2 * m) for m in (1, 2, 3)])
-    far_pos = swap(own_pos, Z_HI)
-    positions = jnp.concatenate([own_pos, swap(own_pos, CORE), far_pos, swap(far_pos, CORE)])
-
-    half = total_rows // 2
-    d_rows, dk_keep, dk_send, dv_keep, dv_send = pl.pallas_call(
+
+    rows = with_partners(packed_rows)
+    near_pairs = jnp.concatenate([own_pairs, far_pairs], axis=0)
+    core_pairs = swap(after(near_pairs, *rows), CORE)
+
+    feature_parts = pl.pallas_call(
+        join_features,
+        out_shape=[shaped((2, ROWS, 256))] * GROUP,
+        in_specs=[hbm] * 2,
+        out_specs=[hbm] * GROUP,
+        scratch_shapes=[DMA((2 * GROUP,))],
+        compiler_params=limits(60),
+        name="join_features",
+    )(after(near_features, own_pairs), far_features)
+    feature_parts = with_partners(feature_parts)
+
+    stacked = shaped((Q_BLOCKS, GROUP * BLK, HD))
+    q_rows, g_rows = pl.pallas_call(
+        stack_rows,
+        out_shape=[stacked] * 2,
+        in_specs=[vmem] * GROUP,
+        out_specs=[vmem] * 2,
+        compiler_params=limits(16),
+        cost_estimate=pl.CostEstimate(
+            flops=0, bytes_accessed=STACK_BYTES, transcendentals=0
+        ),
+        name="stack_rows",
+    )(*rows)
+    q_rows = after(q_rows, w_near)
+    attended = pl.pallas_call(
         attend,
-        out_shape=[shaped((Q_BLOCKS, BLK, GROUP * HD))] + [shaped((half, HD), jnp.float32)] * 4,
-        in_specs=[smem] * 2 + [vmem] * (2 * GROUP),
-        out_specs=[vmem] * 5,
+        out_shape=[shaped((ROWS, GROUP * HD))] * GROUP + [shaped((half, HD), jnp.float32)] * 4,
+        in_specs=[smem] + [vmem] * 5,
+        out_specs=[vmem] * (GROUP + 4),
         scratch_shapes=[
-            VMEM((Q_BLOCKS, GROUP * BLK, HD), jnp.bfloat16),
-            VMEM((Q_BLOCKS, GROUP * BLK, HD), jnp.bfloat16),
             VMEM((total_rows, HD), jnp.bfloat16),
             VMEM((HD, total_rows), jnp.bfloat16),
             VMEM((total_rows, HD), jnp.bfloat16),
             VMEM((total_rows, HD), jnp.float32),
             VMEM((total_rows, HD), jnp.float32),
+            VMEM((Q_BLOCKS, BLK, GROUP * HD), jnp.bfloat16),
             VMEM((total_rows, GROUP * BLK), jnp.float32),
             VMEM((total_rows, GROUP * BLK), jnp.float32),
+            VMEM((4 * GROUP, HD), jnp.int32),
+            SMEM((4 * GROUP, HD), jnp.int32),
+            DMA,
         ],
-        compiler_params=limits(40),
+        compiler_params=limits(32),
         cost_estimate=pl.CostEstimate(
-            flops=4 * 10 * 512 * 512 * HD,
+            flops=14_000_000_000,
             bytes_accessed=6 << 20,
             transcendentals=512 * 2048,
         ),
         name="attend",
-    )(positions, doc_lens, *rows, own_pairs, core_pairs, far_pairs, far_core_pairs)
-
-    dk_sum = dk_keep + swap(dk_send, CORE)
+    )(doc_lens, q_rows, g_rows, own_pairs, far_pairs, core_pairs)
+    row_grads, (dk_keep, dk_send, dv_keep, dv_send) = attended[:GROUP], attended[GROUP:]
+    dk_send = after(dk_send, *feature_parts)
+
+    own_features = pl.pallas_call(
+        turn_features,
+        out_shape=shaped((256, half)),
+        in_specs=[vmem] * GROUP,
+        out_specs=vmem,
+        compiler_params=limits(16),
+        name="turn_features",
+    )(after(feature_parts[0], dk_keep), *feature_parts[1:])
+    other_features = swap_tensor(own_features)
+    w_far = swap(after(w_near, dk_keep), CORE)
+
+    d_query = pl.pallas_call(
+        place_rows,
+        out_shape=shaped(queries.shape),
+        in_specs=[vmem] * GROUP,
+        out_specs=vmem,
+        compiler_params=limits(16),
+        name="place_rows",
+    )(*with_partners(row_grads))
+
+    dk_sum = after(dk_keep, own_features) + swap(dk_send, CORE)
     dk_far = swap(dk_sum.astype(jnp.bfloat16), Z_HI)
-    quarter = half // 2
     dk_far = jnp.concatenate([dk_far[quarter:], dk_far[:quarter]], axis=0)
     key_grad = (dk_sum + dk_far.astype(jnp.float32)).astype(jnp.bfloat16)
-    key_grads = [key_grad] + [swap(key_grad, 2 * m) for m in (1, 2, 3)]
+    key_grad = after(key_grad, d_query)
+    key_grads = with_partners([key_grad] * GROUP)
     own_key_grad = jnp.stack([key_grads[m][m * ROWS : (m + 1) * ROWS] for m in range(GROUP)])
     other_key_grad = swap_tensor(own_key_grad)
 
-    arrived = [feature_parts[0]] + [swap(feature_parts[m], 2 * m) for m in (1, 2, 3)]
-    near = jnp.concatenate([part[0] for part in arrived], axis=0)
-    beyond = swap(jnp.concatenate([part[1] for part in arrived], axis=0), Z_HI)
-    own_features = jnp.concatenate([near, beyond], axis=0).T
-    other_features = swap_tensor(own_features)
-
-    partial = pl.pallas_call(
+    keep, send = pl.pallas_call(
         weight_grad,
-        out_shape=shaped((2, 256, kv_columns), jnp.float32),
+        out_shape=[shaped((256, kv_columns), jnp.float32)] * 2,
         in_specs=[vmem] * (2 + GROUP),
-        out_specs=vmem,
+        out_specs=[vmem] * 2,
         scratch_shapes=[VMEM((half, kv_columns), jnp.bfloat16)],
         compiler_params=limits(24),
         cost_estimate=pl.CostEstimate(
@@ -532,50 +671,36 @@
         ),
         name="weight_grad",
     )(own_features, other_features, *key_grads)
-    d_wkey = partial[0] + swap(partial[1], CORE)
-
-    leaving = lax.dynamic_slice_in_dim(w_key, (1 - side) * 2048 + core * 1024, 1024, 0)
-    w_near = swap_tensor(leaving)
-    w_far = swap(w_near, CORE)
-    ids = jnp.stack([(index >> 1) & 3, core, side]).astype(jnp.int32)
+    arrived = swap(send, CORE)
+
+    dv_sum = dv_keep + swap(after(dv_send, dk_sum), CORE)
+    dv_far = swap(after(dv_sum[quarter:].astype(jnp.bfloat16), key_grad), Z_HI)
+    value_grad = (dv_sum[:quarter] + dv_far.astype(jnp.float32)).astype(jnp.bfloat16)
+    value_grads = with_partners([value_grad[m * ROWS : (m + 1) * ROWS] for m in range(GROUP)])
+
     d_input = pl.pallas_call(
         input_grad,
         out_shape=shaped((ROWS, features // 2)),
-        grid_spec=pltpu.PrefetchScalarGridSpec(
-            num_scalar_prefetch=1,
-            grid=(4,),
-            in_specs=[
-                pl.BlockSpec((GROUP, ROWS, HD), lambda k, ids: (0, 0, 0)),
-                pl.BlockSpec((GROUP, ROWS, HD), lambda k, ids: (0, 0, 0)),
-                pl.BlockSpec((512, kv_columns), lambda k, ids: (ids[2] * 4 + (k ^ (2 * ids[1])), 0)),
-                pl.BlockSpec((512, kv_columns), lambda k, ids: (jnp.minimum(k, 1), 0)),
-                pl.BlockSpec((512, kv_columns), lambda k, ids: (jnp.maximum(k - 2, 0), 0)),
-            ],
-            out_specs=pl.BlockSpec((ROWS, 512), lambda k, ids: (0, k ^ (2 * ids[1]))),
-            scratch_shapes=[VMEM((ROWS, kv_columns), jnp.bfloat16)] * 2,
-        ),
-        compiler_params=limits(24),
+        in_specs=[vmem] * 2 + [hbm] * 3,
+        out_specs=vmem,
+        scratch_shapes=[VMEM((ROWS, kv_columns), jnp.bfloat16)] * 2
+        + [VMEM((2048, kv_columns), jnp.bfloat16)] * 2
+        + [DMA((8,))],
+        compiler_params=limits(60),
         cost_estimate=pl.CostEstimate(
             flops=4 * ROWS * 2048 * kv_columns, bytes_accessed=5 << 20, transcendentals=0
         ),
         name="input_grad",
-    )(ids, own_key_grad, other_key_grad, w_key, w_near, w_far)
-
-    dv_sum = dv_keep + swap(dv_send, CORE)
-    dv_far = swap(dv_sum[quarter:].astype(jnp.bfloat16), Z_HI)
-    value_grad = (dv_sum[:quarter] + dv_far.astype(jnp.float32)).astype(jnp.bfloat16)
-    value_grads = [value_grad[m * ROWS : (m + 1) * ROWS] for m in range(GROUP)]
-    value_grads = [value_grads[0]] + [swap(value_grads[m], 2 * m) for m in (1, 2, 3)]
-    row_grads = d_rows.reshape(GROUP, ROWS, GROUP * HD)
-    row_grads = [row_grads[0]] + [swap(row_grads[m], 2 * m) for m in (1, 2, 3)]
-    d_query, d_value = pl.pallas_call(
-        place_rows,
-        out_shape=[shaped(queries.shape), shaped(values.shape)],
-        in_specs=[vmem] * (2 * GROUP),
+    )(after(own_key_grad, send), other_key_grad, w_key, w_near, w_far)
+
+    d_wkey, d_value = pl.pallas_call(
+        finish,
+        out_shape=[shaped((256, kv_columns), jnp.float32), shaped(values.shape)],
+        in_specs=[vmem] * (2 + GROUP),
         out_specs=[vmem] * 2,
         compiler_params=limits(16),
-        name="place_rows",
-    )(*row_grads, *value_grads)
+        name="finish",
+    )(keep, arrived, *value_grads)
     return (d_query, d_value, d_input, d_wkey)
 
 

time: 143 us -> 176 us (1.23)
  Pallas kernels: 20.2 us -> 95.3 us
  local copies, waits for them, and re-layouts: 20.9 us -> 2.72 us
  waiting for transfers between devices: 60.5 us -> 45.8 us
  starting transfers between devices: 38 us -> 32.1 us
  other arithmetic: 2.33 us -> 0.23 us
    pallas_call x5 -> x10, Pallas kernels: 20.1 us -> 62.4 us  [the longest x1 17.1 us: on_device_by_heads(): pl.pallas_call(pack_features, out_shape=[shaped((GROUP, ROWS, 256))] * 2,...]
    pallas_call x1, Pallas kernels: 0.07 us -> 32.9 us  [on_device_by_heads(): pl.pallas_call(pack_rows, out_shape=[shaped((ROWS, 2 * GROUP * HD))] * GR...]
    ppermute x34 -> x27, waiting for transfers between devices: 60.5 us -> 45.8 us  [swap(): return lax.ppermute(array, 'dp', [(i, i ^ mask) for i in range(16)])]
    unnamed x41 -> x18, local copies, waits for them, and re-layouts: 13.2 us -> 2.02 us
    ppermute x34 -> x27, starting transfers between devices: 35.3 us -> 29.4 us  [swap(): return lax.ppermute(array, 'dp', [(i, i ^ mask) for i in range(16)])]
    dynamic_slice x1 -> x0, local copies, waits for them, and re-layouts: 2.32 us -> none  [on_device_by_heads(): lax.dynamic_slice_in_dim(w_key, (1 - side) * 2048 + core * 1024, 1024, 0)]
    add x2 -> x1, other arithmetic: 1.97 us -> 0.06 us  [on_device_by_heads(): dv_sum = dv_keep + swap(after(dv_send, dk_sum), CORE)]
    pallas_call x4 -> x0, local copies, waits for them, and re-layouts: 1.76 us -> none  [on_device_by_heads(): pl.pallas_call(project_keys, out_shape=[shaped((ROWS, 2 * HD))] * GROUP +...]
  transfers between devices with their start and end apart: 37 -> 30, of which waited for: 13 -> 10; matrix products, arithmetic and copies ran while one was open for 7% -> 1% of each run, Pallas kernels for 14% -> 44%
where the time goes in v2:
time: 176 us; the launch traced here: 177 us
  Pallas kernels  95.3 us (54%)
  waiting for transfers between devices  45.8 us (26%)
  starting transfers between devices  32.1 us (18%)
  local copies, waits for them, and re-layouts  2.72 us (2%)
    ppermute x27, waiting for transfers between devices, swap(): return lax.ppermute(array, 'dp', [(i, i ^ mask) for i in range(16)])  45.8 us
    pallas_call x1, Pallas kernels, on_device_by_heads(): pl.pallas_call(pack_rows, out_shape=[shaped((ROWS, 2 * GROUP * HD))] * GR...  32.9 us
    ppermute x27, starting transfers between devices, swap(): return lax.ppermute(array, 'dp', [(i, i ^ mask) for i in range(16)])  29.4 us
    pallas_call x1, Pallas kernels, on_device_by_heads(): pl.pallas_call(pack_features, out_shape=[shaped((GROUP, ROWS, 256))] * 2,...  17.1 us
    pallas_call x1, Pallas kernels, on_device_by_heads(): pl.pallas_call(join_features, out_shape=[shaped((2, ROWS, 256))] * GROUP,...  17.1 us
    pallas_call x1, Pallas kernels, on_device_by_heads(): pl.pallas_call(attend, out_shape=[shaped((ROWS, GROUP * HD))] * GROUP + [...  15 us
    pallas_call x1, Pallas kernels, on_device_by_heads(): pl.pallas_call(project_keys, out_shape=[shaped((MARKED, 2 * HD))] * GROUP...  5.16 us
    pallas_call x1, Pallas kernels, on_device_by_heads(): pl.pallas_call(input_grad, out_shape=shaped((ROWS, features // 2)), in_sp...  5.07 us
  transfers between devices with their start and end apart: 30, of which 10 were waited for; matrix products, arithmetic and copies ran while one was open for 1% of the time, Pallas kernels for 44%

profile of v2, /device:TPU:0, one launch (start us, length us, event | category | flops | bytes accessed | tf_op | source)
XLA Modules:
  0.0 177.2 jit_solution(2896642668722680635)
XLA Ops:
  0.6 17.1 %pack_features.1 = (bf16[4,128,256]{2,1,0:T(8,128)(2,1)}, bf16[4,128,256]{2,1,0:T(8,128)(2,1)}) custom-call(bf16[128,4096]{1,0:T(8,128)(2,1)} %inputs_ref.2), custom_call_target="tpu_custom_call" | custom-call | tf_op jit(solution)/shard_map/pack_features/pallas_call | solution.py:534
  17.7 4.1 %collective-permute-start.4 = (bf16[4,128,256]{2,1,0:T(8,128)(2,1)}, bf16[4,128,256]{2,1,0:T(8,128)(2,1)S(1)}, u32[]{:S(2)}, u32[]{:S(2)}) collective-permute-start(bf16[4,128,256]{2,1,0:T(8,128)(2,1)} %get-tuple-element.59), channel_id=1, source_target_pairs={{0,16},{2,18},{4,20},{6,22},{8,24},{10,26},{12,28},{14,30},{16,0},... | collective-permute-start | bytes 786440 | tf_op jit(solution)/shard_map/ppermute | solution.py:220
  21.8 5.2 %project_keys.1 = (bf16[144,256]{1,0:T(8,128)(2,1)}, bf16[144,256]{1,0:T(8,128)(2,1)}, bf16[144,256]{1,0:T(8,128)(2,1)}, bf16[144,256]{1,0:T(8,128)(2,1)}, bf16[1024,512]{1,0:T(8,128)(2,1)}) custom-call(s32[2]{0:T(128)} %pos_ref.1, bf16[128,4096]{1,0:T(8,128)(2,1)} %inputs_ref.2, bf16[128,512]{1,0:T(8,128)(2,1)} %values_ref.1, bf16[4096,512]{1,0:T(8,128)(2,1)} %w_own.1), custom_call_target="tpu_custom_call" | custom-call | flops 536870912 | bytes 4194304 | tf_op jit(solution)/shard_map/project_keys/pallas_call | solution.py:544
  27.0 1.6 collective-permute-start.5
  28.5 1.6 collective-permute-start.6
  30.5 1.5 collective-permute-start.3
  32.0 32.9 %pack_rows.1 = (bf16[128,1024]{1,0:T(8,128)(2,1)}, bf16[128,1024]{1,0:T(8,128)(2,1)}, bf16[128,1024]{1,0:T(8,128)(2,1)}, bf16[128,1024]{1,0:T(8,128)(2,1)}) custom-call(bf16[128,2048]{1,0:T(8,128)(2,1)} %queries_ref, bf16[128,2048]{1,0:T(8,128)(2,1)} %grads_ref.1), custom_call_target="tpu_custom_call" | custom-call | tf_op jit(solution)/shard_map/pack_rows/pallas_call | solution.py:563
  68.0 1.6 collective-permute-start.1
  70.0 10.8 %collective-permute-done.8.far_pairs = bf16[576,256]{1,0:T(8,128)(2,1)S(1)} collective-permute-done((bf16[576,256]{1,0:T(8,128)(2,1)S(1)}, bf16[576,256]{1,0:T(8,128)(2,1)S(1)}, u32[]{:S(2)}, u32[]{:S(2)}) %collective-permute-start.8) | collective-permute-done | bytes 294944 | tf_op jit(solution)/shard_map/ppermute | solution.py:220
  80.8 1.8 %collective-permute-done.1.refs_2_ = bf16[128,1024]{1,0:T(8,128)(2,1)S(1)} collective-permute-done((bf16[128,1024]{1,0:T(8,128)(2,1)}, bf16[128,1024]{1,0:T(8,128)(2,1)S(1)}, u32[]{:S(2)}, u32[]{:S(2)}) %collective-permute-start.1) | collective-permute-done | bytes 262176 | tf_op jit(solution)/shard_map/ppermute | solution.py:220
  82.6 3.6 %collective-permute-done.2.refs_3_ = bf16[128,1024]{1,0:T(8,128)(2,1)S(1)} collective-permute-done((bf16[128,1024]{1,0:T(8,128)(2,1)}, bf16[128,1024]{1,0:T(8,128)(2,1)S(1)}, u32[]{:S(2)}, u32[]{:S(2)}) %collective-permute-start.2) | collective-permute-done | bytes 262176 | tf_op jit(solution)/shard_map/ppermute | solution.py:220
  86.2 17.1 %join_features.1 = (bf16[2,128,256]{2,1,0:T(8,128)(2,1)}, bf16[2,128,256]{2,1,0:T(8,128)(2,1)}, bf16[2,128,256]{2,1,0:T(8,128)(2,1)}, bf16[2,128,256]{2,1,0:T(8,128)(2,1)}) custom-call(bf16[4,128,256]{2,1,0:T(8,128)(2,1)} %get-tuple-element.69.near_ref, bf16[4,128,256]{2,1,0:T(8,128)(2,1)} %copy-done.6), custom_call_target="tpu_custom_call" | custom-call | tf_op jit(solution)/shard_map/join_features/pallas_call | solution.py:580
  104.2 2.6 %collective-permute-start.15 = (bf16[2,128,256]{2,1,0:T(8,128)(2,1)}, bf16[2,128,256]{2,1,0:T(8,128)(2,1)S(1)}, u32[]{:S(2)}, u32[]{:S(2)}) collective-permute-start(bf16[2,128,256]{2,1,0:T(8,128)(2,1)} %get-tuple-element.75), channel_id=1, source_target_pairs={{0,12},{2,14},{4,8},{6,10},{8,4},{10,6},{12,0},{14,2},{16,28},{18,... | collective-permute-start | bytes 393224 | tf_op jit(solution)/shard_map/ppermute | solution.py:220
  108.0 15.0 %attend.1 = (bf16[128,512]{1,0:T(8,128)(2,1)S(1)}, bf16[128,512]{1,0:T(8,128)(2,1)S(1)}, bf16[128,512]{1,0:T(8,128)(2,1)S(1)}, bf16[128,512]{1,0:T(8,128)(2,1)S(...) custom-call(s32[4]{0:T(128)S(1)} %copy-done.2, ...), custom_call_target="tpu_custom_call" | custom-call | flops 14000000000 | bytes 6291456 | tf_op jit(solution)/shard_map/attend/pallas_call | solution.py:604
  125.1 1.7 collective-permute-start.18
  128.3 1.9 %collective-permute-start.11 = (bf16[128,512]{1,0:T(8,128)(2,1)S(1)}, bf16[128,512]{1,0:T(8,128)(2,1)S(1)}, u32[]{:S(2)}, u32[]{:S(2)}) collective-permute-start(bf16[128,512]{1,0:T(8,128)(2,1)S(1)} %get-tuple-element.67), channel_id=1, source_target_pairs={{0,8},{2,10},{4,12},{6,14},{8,0},{10,2},{12,4},{14,6},{16,24},{18,... | collective-permute-start | bytes 393224 | tf_op jit(solution)/shard_map/ppermute | solution.py:220
  132.3 4.0 %collective-permute-done.11.refs_2_ = bf16[128,512]{1,0:T(8,128)(2,1)S(1)} collective-permute-done((bf16[128,512]{1,0:T(8,128)(2,1)S(1)}, bf16[128,512]{1,0:T(8,128)(2,1)S(1)}, u32[]{:S(2)}, u32[]{:S(2)}) %collective-permute-start.11) | collective-permute-done | bytes 131104 | tf_op jit(solution)/shard_map/ppermute | solution.py:220
  136.3 4.6 %collective-permute-done.12.refs_3_ = bf16[128,512]{1,0:T(8,128)(2,1)S(1)} collective-permute-done((bf16[128,512]{1,0:T(8,128)(2,1)S(1)}, bf16[128,512]{1,0:T(8,128)(2,1)S(1)}, u32[]{:S(2)}, u32[]{:S(2)}) %collective-permute-start.12) | collective-permute-done | bytes 131104 | tf_op jit(solution)/shard_map/ppermute | solution.py:220
  142.9 2.5 %collective-permute-start.20 = (bf16[1024,128]{1,0:T(8,128)(2,1)S(1)}, bf16[1024,128]{1,0:T(8,128)(2,1)S(1)}, u32[]{:S(2)}, u32[]{:S(2)}) collective-permute-start(bf16[1024,128]{1,0:T(8,128)(2,1)S(1)} %add_convert_fusion.refs_0_), channel_id=1, source_target_pairs={{0,8},{2,10},{4,12},{6,14},{8,0},{10,2},{12,4},{14,6},{16,24},{18,... | collective-permute-start | bytes 786440 | tf_op jit(solution)/shard_map/ppermute | solution.py:220
  146.0 6.1 %collective-permute-done.21.refs_3_ = bf16[1024,128]{1,0:T(8,128)(2,1)S(1)} collective-permute-done((bf16[1024,128]{1,0:T(8,128)(2,1)S(1)}, bf16[1024,128]{1,0:T(8,128)(2,1)S(1)}, u32[]{:S(2)}, u32[]{:S(2)}) %collective-permute-start.21) | collective-permute-done | bytes 262176 | tf_op jit(solution)/shard_map/ppermute | solution.py:220
  152.0 4.1 %collective-permute-done.20.refs_2_ = bf16[1024,128]{1,0:T(8,128)(2,1)S(1)} collective-permute-done((bf16[1024,128]{1,0:T(8,128)(2,1)S(1)}, bf16[1024,128]{1,0:T(8,128)(2,1)S(1)}, u32[]{:S(2)}, u32[]{:S(2)}) %collective-permute-start.20) | collective-permute-done | bytes 262176 | tf_op jit(solution)/shard_map/ppermute | solution.py:220
  159.2 7.7 %collective-permute-done.24 = bf16[512,128]{1,0:T(8,128)(2,1)S(1)} collective-permute-done((bf16[512,128]{1,0:T(8,128)(2,1)S(1)}, bf16[512,128]{1,0:T(8,128)(2,1)S(1)}, u32[]{:S(2)}, u32[]{:S(2)}) %collective-permute-start.24) | collective-permute-done | bytes 131104 | tf_op jit(solution)/shard_map/ppermute | solution.py:220
  167.6 2.5 %collective-permute-start.26 = (bf16[128,128]{1,0:T(8,128)(2,1)}, bf16[128,128]{1,0:T(8,128)(2,1)S(1)}, u32[]{:S(2)}, u32[]{:S(2)}) collective-permute-start(bf16[128,128]{1,0:T(8,128)(2,1)} %get-tuple-element.95), channel_id=1, source_target_pairs={{0,8},{2,10},{4,12},{6,14},{8,0},{10,2},{12,4},{14,6},{16,24},{18,... | collective-permute-start | bytes 98312 | tf_op jit(solution)/shard_map/ppermute | solution.py:220
  171.1 5.1 %input_grad.1 = bf16[128,2048]{1,0:T(8,128)(2,1)} custom-call(bf16[4,128,128]{2,1,0:T(8,128)(2,1)} %copy-done.5, bf16[4,128,128]{2,1,0:T(8,128)(2,1)} %collective-permute-done.28.other_ref, bf16[4096,512]{1,0:T(8,128)(2,1)} %w_own.1, bf16[1024,512]{1,0:T(8,128)(2,1)} %copy-done.3, bf16[1024,512]{1,0:T(8,128)(2,1)} %copy-done.4), custom_call_target="tpu_custom_call" | custom-call | flops 536870912 | bytes 5242880 | tf_op jit(solution)/shard_map/input_grad/pallas_call | solution.py:681
  (78 shorter events, 19.7 us)
Async XLA Ops:
  17.7 47.3 %collective-permute-start.4 = (bf16[4,128,256]{2,1,0:T(8,128)(2,1)}, bf16[4,128,256]{2,1,0:T(8,128)(2,1)S(1)}, u32[]{:S(2)}, u32[]{:S(2)}) collective-permute-start(bf16[4,128,256]{2,1,0:T(8,128)(2,1)} %get-tuple-element.59), channel_id=1, source_target_pairs={{0,16},{2,18},{4,20},{6,22},{8,24},{10,26},{12,28},{14,30},{16,0},... | collective-permute-start | bytes 786440 | tf_op jit(solution)/shard_map/ppermute | solution.py:220
  27.0 39.0 %collective-permute-start.5 = (bf16[144,256]{1,0:T(8,128)(2,1)}, bf16[144,256]{1,0:T(8,128)(2,1)S(1)}, u32[]{:S(2)}, u32[]{:S(2)}) collective-permute-start(bf16[144,256]{1,0:T(8,128)(2,1)} %get-tuple-element.61), channel_id=1, source_target_pairs={{0,4},{2,6},{4,0},{6,2},{8,12},{10,14},{12,8},{14,10},{16,20},{18,... | collective-permute-start | bytes 221192 | tf_op jit(solution)/shard_map/ppermute | solution.py:220
  28.5 37.5 %collective-permute-start.6 = (bf16[144,256]{1,0:T(8,128)(2,1)}, bf16[144,256]{1,0:T(8,128)(2,1)S(1)}, u32[]{:S(2)}, u32[]{:S(2)}) collective-permute-start(bf16[144,256]{1,0:T(8,128)(2,1)} %get-tuple-element.62), channel_id=1, source_target_pairs={{0,8},{2,10},{4,12},{6,14},{8,0},{10,2},{12,4},{14,6},{16,24},{18,... | collective-permute-start | bytes 221192 | tf_op jit(solution)/shard_map/ppermute | solution.py:220
  30.1 35.9 %collective-permute-start.7 = (bf16[144,256]{1,0:T(8,128)(2,1)}, bf16[144,256]{1,0:T(8,128)(2,1)S(1)}, u32[]{:S(2)}, u32[]{:S(2)}) collective-permute-start(bf16[144,256]{1,0:T(8,128)(2,1)} %get-tuple-element.63), channel_id=1, source_target_pairs={{0,12},{2,14},{4,8},{6,10},{8,4},{10,6},{12,0},{14,2},{16,28},{18,... | collective-permute-start | bytes 221192 | tf_op jit(solution)/shard_map/ppermute | solution.py:220
  30.5 77.4 %collective-permute-start.3 = (bf16[1024,512]{1,0:T(8,128)(2,1)}, bf16[1024,512]{1,0:T(8,128)(2,1)S(1)}, u32[]{:S(2)}, u32[]{:S(2)}) collective-permute-start(bf16[1024,512]{1,0:T(8,128)(2,1)} %get-tuple-element.56), channel_id=1, source_target_pairs={{0,1},{1,0},{2,3},{3,2},{4,5},{5,4},{6,7},{7,6},{8,9},{9,8},{10,11... | collective-permute-start | bytes 3145736 | tf_op jit(solution)/shard_map/ppermute | solution.py:224
  66.1 14.7 %collective-permute-start.8 = (bf16[576,256]{1,0:T(8,128)(2,1)S(1)}, bf16[576,256]{1,0:T(8,128)(2,1)S(1)}, u32[]{:S(2)}, u32[]{:S(2)}) collective-permute-start(bf16[576,256]{1,0:T(8,128)(2,1)S(1)} %get-tuple-element.99.own_pairs), channel_id=1, source_target_pairs={{0,16},{2,18},{4,20},{6,22},{8,24},{10,26},{12,28},{14,30},{16,0},... | collective-permute-start | bytes 884744 | tf_op jit(solution)/shard_map/ppermute | solution.py:220
  66.5 14.4 %collective-permute-start = (bf16[128,1024]{1,0:T(8,128)(2,1)}, bf16[128,1024]{1,0:T(8,128)(2,1)S(1)}, u32[]{:S(2)}, u32[]{:S(2)}) collective-permute-start(bf16[128,1024]{1,0:T(8,128)(2,1)} %get-tuple-element.52), channel_id=1, source_target_pairs={{0,4},{2,6},{4,0},{6,2},{8,12},{10,14},{12,8},{14,10},{16,20},{18,... | collective-permute-start | bytes 786440 | tf_op jit(solution)/shard_map/ppermute | solution.py:220
  68.0 14.7 %collective-permute-start.1 = (bf16[128,1024]{1,0:T(8,128)(2,1)}, bf16[128,1024]{1,0:T(8,128)(2,1)S(1)}, u32[]{:S(2)}, u32[]{:S(2)}) collective-permute-start(bf16[128,1024]{1,0:T(8,128)(2,1)} %get-tuple-element.53), channel_id=1, source_target_pairs={{0,8},{2,10},{4,12},{6,14},{8,0},{10,2},{12,4},{14,6},{16,24},{18,... | collective-permute-start | bytes 786440 | tf_op jit(solution)/shard_map/ppermute | solution.py:220
  69.5 16.7 %collective-permute-start.2 = (bf16[128,1024]{1,0:T(8,128)(2,1)}, bf16[128,1024]{1,0:T(8,128)(2,1)S(1)}, u32[]{:S(2)}, u32[]{:S(2)}) collective-permute-start(bf16[128,1024]{1,0:T(8,128)(2,1)} %get-tuple-element.54), channel_id=1, source_target_pairs={{0,12},{2,14},{4,8},{6,10},{8,4},{10,6},{12,0},{14,2},{16,28},{18,... | collective-permute-start | bytes 786440 | tf_op jit(solution)/shard_map/ppermute | solution.py:220
  86.2 21.8 %collective-permute-start.9 = (bf16[1152,256]{1,0:T(8,128)(2,1)S(1)}, bf16[1152,256]{1,0:T(8,128)(2,1)S(1)}, u32[]{:S(2)}, u32[]{:S(2)}) collective-permute-start(bf16[1152,256]{1,0:T(8,128)(2,1)S(1)} %constant_dynamic-update-slice_fusion.4), channel_id=1, source_target_pairs={{0,2},{2,0},{4,6},{6,4},{8,10},{10,8},{12,14},{14,12},{16,18},{18,... | collective-permute-start | bytes 1769480 | tf_op jit(solution)/shard_map/ppermute | solution.py:220
  103.3 19.7 %collective-permute-start.13 = (bf16[2,128,256]{2,1,0:T(8,128)(2,1)}, bf16[2,128,256]{2,1,0:T(8,128)(2,1)S(1)}, u32[]{:S(2)}, u32[]{:S(2)}) collective-permute-start(bf16[2,128,256]{2,1,0:T(8,128)(2,1)} %get-tuple-element.73), channel_id=1, source_target_pairs={{0,4},{2,6},{4,0},{6,2},{8,12},{10,14},{12,8},{14,10},{16,20},{18,... | collective-permute-start | bytes 393224 | tf_op jit(solution)/shard_map/ppermute | solution.py:220
  104.2 18.8 %collective-permute-start.14 = (bf16[2,128,256]{2,1,0:T(8,128)(2,1)}, bf16[2,128,256]{2,1,0:T(8,128)(2,1)S(1)}, u32[]{:S(2)}, u32[]{:S(2)}) collective-permute-start(bf16[2,128,256]{2,1,0:T(8,128)(2,1)} %get-tuple-element.74), channel_id=1, source_target_pairs={{0,8},{2,10},{4,12},{6,14},{8,0},{10,2},{12,4},{14,6},{16,24},{18,... | collective-permute-start | bytes 393224 | tf_op jit(solution)/shard_map/ppermute | solution.py:220
  104.2 18.8 %collective-permute-start.15 = (bf16[2,128,256]{2,1,0:T(8,128)(2,1)}, bf16[2,128,256]{2,1,0:T(8,128)(2,1)S(1)}, u32[]{:S(2)}, u32[]{:S(2)}) collective-permute-start(bf16[2,128,256]{2,1,0:T(8,128)(2,1)} %get-tuple-element.75), channel_id=1, source_target_pairs={{0,12},{2,14},{4,8},{6,10},{8,4},{10,6},{12,0},{14,2},{16,28},{18,... | collective-permute-start | bytes 393224 | tf_op jit(solution)/shard_map/ppermute | solution.py:220
  125.1 16.7 %collective-permute-start.18 = (bf16[1024,128]{1,0:T(8,128)(2,1)S(1)}, bf16[1024,128]{1,0:T(8,128)(2,1)S(1)}, u32[]{:S(2)}, u32[]{:S(2)}) collective-permute-start(bf16[1024,128]{1,0:T(8,128)(2,1)S(1)} %get-tuple-element.90), channel_id=1, source_target_pairs={{0,16},{2,18},{4,20},{6,22},{8,24},{10,26},{12,28},{14,30},{16,0},... | collective-permute-start | bytes 786440 | tf_op jit(solution)/shard_map/ppermute | solution.py:220
  130.1 10.8 %collective-permute-start.12 = (bf16[128,512]{1,0:T(8,128)(2,1)S(1)}, bf16[128,512]{1,0:T(8,128)(2,1)S(1)}, u32[]{:S(2)}, u32[]{:S(2)}) collective-permute-start(bf16[128,512]{1,0:T(8,128)(2,1)S(1)} %get-tuple-element.68), channel_id=1, source_target_pairs={{0,12},{2,14},{4,8},{6,10},{8,4},{10,6},{12,0},{14,2},{16,28},{18,... | collective-permute-start | bytes 393224 | tf_op jit(solution)/shard_map/ppermute | solution.py:220
  130.3 15.1 %collective-permute-start.16 = (bf16[256,1024]{1,0:T(8,128)(2,1)S(1)}, bf16[256,1024]{1,0:T(8,128)(2,1)S(1)}, u32[]{:S(2)}, u32[]{:S(2)}) collective-permute-start(bf16[256,1024]{1,0:T(8,128)(2,1)S(1)} %turn_features.1.own_ref), channel_id=1, source_target_pairs={{0,1},{1,0},{2,3},{3,2},{4,5},{5,4},{6,7},{7,6},{8,9},{9,8},{10,11... | collective-permute-start | bytes 1572872 | tf_op jit(solution)/shard_map/ppermute | solution.py:224
  141.8 10.2 %collective-permute-start.21 = (bf16[1024,128]{1,0:T(8,128)(2,1)S(1)}, bf16[1024,128]{1,0:T(8,128)(2,1)S(1)}, u32[]{:S(2)}, u32[]{:S(2)}) collective-permute-start(bf16[1024,128]{1,0:T(8,128)(2,1)S(1)} %add_convert_fusion.refs_0_), channel_id=1, source_target_pairs={{0,12},{2,14},{4,8},{6,10},{8,4},{10,6},{12,0},{14,2},{16,28},{18,... | collective-permute-start | bytes 786440 | tf_op jit(solution)/shard_map/ppermute | solution.py:220
  142.9 13.3 %collective-permute-start.20 = (bf16[1024,128]{1,0:T(8,128)(2,1)S(1)}, bf16[1024,128]{1,0:T(8,128)(2,1)S(1)}, u32[]{:S(2)}, u32[]{:S(2)}) collective-permute-start(bf16[1024,128]{1,0:T(8,128)(2,1)S(1)} %add_convert_fusion.refs_0_), channel_id=1, source_target_pairs={{0,8},{2,10},{4,12},{6,14},{8,0},{10,2},{12,4},{14,6},{16,24},{18,... | collective-permute-start | bytes 786440 | tf_op jit(solution)/shard_map/ppermute | solution.py:220
  145.4 10.8 %collective-permute-start.19 = (bf16[1024,128]{1,0:T(8,128)(2,1)S(1)}, bf16[1024,128]{1,0:T(8,128)(2,1)S(1)}, u32[]{:S(2)}, u32[]{:S(2)}) collective-permute-start(bf16[1024,128]{1,0:T(8,128)(2,1)S(1)} %add_convert_fusion.refs_0_), channel_id=1, source_target_pairs={{0,4},{2,6},{4,0},{6,2},{8,12},{10,14},{12,8},{14,10},{16,20},{18,... | collective-permute-start | bytes 786440 | tf_op jit(solution)/shard_map/ppermute | solution.py:220
  145.4 11.8 %collective-permute-start.23 = (f32[1024,128]{1,0:T(8,128)S(1)}, f32[1024,128]{1,0:T(8,128)S(1)}, u32[]{:S(2)}, u32[]{:S(2)}) collective-permute-start(f32[1024,128]{1,0:T(8,128)S(1)} %get-tuple-element.84), channel_id=1, source_target_pairs={{0,2},{2,0},{4,6},{6,4},{8,10},{10,8},{12,14},{14,12},{16,18},{18,... | collective-permute-start | bytes 1572872 | tf_op jit(solution)/shard_map/ppermute | solution.py:220
  145.4 24.7 %collective-permute-start.29 = (bf16[1024,512]{1,0:T(8,128)(2,1)S(1)}, bf16[1024,512]{1,0:T(8,128)(2,1)S(1)}, u32[]{:S(2)}, u32[]{:S(2)}) collective-permute-start(bf16[1024,512]{1,0:T(8,128)(2,1)S(1)} %collective-permute-done.3.w_near), channel_id=1, source_target_pairs={{0,2},{2,0},{4,6},{6,4},{8,10},{10,8},{12,14},{14,12},{16,18},{18,... | collective-permute-start | bytes 3145736 | tf_op jit(solution)/shard_map/ppermute | solution.py:220
  157.1 19.2 %collective-permute-start.22 = (f32[256,512]{1,0:T(8,128)S(1)}, f32[256,512]{1,0:T(8,128)S(1)}, u32[]{:S(2)}, u32[]{:S(2)}) collective-permute-start(f32[256,512]{1,0:T(8,128)S(1)} %get-tuple-element.81), channel_id=1, source_target_pairs={{0,2},{2,0},{4,6},{6,4},{8,10},{10,8},{12,14},{14,12},{16,18},{18,... | collective-permute-start | bytes 1572872 | tf_op jit(solution)/shard_map/ppermute | solution.py:220
  157.3 9.7 %collective-permute-start.24 = (bf16[512,128]{1,0:T(8,128)(2,1)S(1)}, bf16[512,128]{1,0:T(8,128)(2,1)S(1)}, u32[]{:S(2)}, u32[]{:S(2)}) collective-permute-start(bf16[512,128]{1,0:T(8,128)(2,1)S(1)} %slice.68), channel_id=1, source_target_pairs={{0,16},{2,18},{4,20},{6,22},{8,24},{10,26},{12,28},{14,30},{16,0},... | collective-permute-start | bytes 393224 | tf_op jit(solution)/shard_map/ppermute | solution.py:220
  158.5 12.6 %collective-permute-start.28 = (bf16[4,128,128]{2,1,0:T(8,128)(2,1)S(1)}, bf16[4,128,128]{2,1,0:T(8,128)(2,1)}, u32[]{:S(2)}, u32[]{:S(2)}) collective-permute-start(bf16[4,128,128]{2,1,0:T(8,128)(2,1)S(1)} %pad_maximum_fusion.own_ref), channel_id=1, source_target_pairs={{0,1},{1,0},{2,3},{3,2},{4,5},{5,4},{6,7},{7,6},{8,9},{9,8},{10,11... | collective-permute-start | bytes 393224 | tf_op jit(solution)/shard_map/ppermute | solution.py:224
  (13 other events, 213.5 us)

commit v3 on v0

--- a/solution.py
+++ b/solution.py
@@ -3,6 +3,8 @@
 import jax
 import jax.numpy as jnp
 from jax import lax
+from jax.experimental import pallas as pl
+from jax.experimental.pallas import tpu as pltpu
 from jax.sharding import PartitionSpec as P
 
 HD = 128
@@ -200,9 +202,553 @@
     return (d_query, d_value, d_input, d_wkey)
 
 
+CORE, Z_HI = 1, 8
+GROUP = 4
+ROWS = 128
+TILE = 256
+UNROLLED = 5
+ATTEND_COST = 1 << 20
+PART = 512
+MARKED = ROWS + 16
+Q_BLOCKS = GROUP * ROWS // BLK
+SMEM = pltpu.SMEM
+VMEM = pltpu.VMEM
+HBM = pltpu.HBM
+DMA = pltpu.SemaphoreType.DMA
+
+
+def swap(array, mask):
+    return lax.ppermute(array, "dp", [(i, i ^ mask) for i in range(16)])
+
+
+def swap_tensor(array):
+    return lax.ppermute(array, "tensor", [(0, 1), (1, 0)])
+
+
+def own_head():
+    return (lax.axis_index("dp") >> 1) & 3
+
+
+def columns(index, width):
+    return pl.ds(pl.multiple_of(index * width, width), width)
+
+
+def whole_spec(space=VMEM):
+    return pl.BlockSpec(memory_space=space)
+
+
+def after(array, *earlier):
+    return lax.optimization_barrier((array,) + earlier)[0]
+
+
+def copy_all(pairs, semaphores):
+    copies = [
+        pltpu.make_async_copy(source, target, semaphores.at[i])
+        for i, (source, target) in enumerate(pairs)
+    ]
+    for copy in copies:
+        copy.start()
+    return copies
+
+
+def project_keys(pos_ref, inputs_ref, values_ref, w_ref, *refs):
+    pair_refs = refs[:GROUP]
+    inputs, weights, total, semaphores = refs[GROUP:]
+    head = own_head()
+    spans = [pl.ds(k * PART, PART) for k in range(weights.shape[0] // PART)]
+    copies = copy_all(
+        [(inputs_ref, inputs)] + [(w_ref.at[span], weights.at[span]) for span in spans],
+        semaphores,
+    )
+    lanes = lax.broadcasted_iota(jnp.int32, (16, 2 * HD), 1)
+    marks = jnp.where(lanes == 0, pos_ref[0], jnp.where(lanes == 1, pos_ref[1], 0))
+    for m in range(GROUP):
+        pair_refs[m][:ROWS, HD:] = values_ref[:, columns(head ^ m, HD)]
+        pair_refs[m][ROWS:] = marks.astype(jnp.float32).astype(jnp.bfloat16)
+    copies[0].wait()
+    for k, span in enumerate(spans):
+        copies[1 + k].wait()
+        part = jnp.dot(inputs[:, span], weights[span], preferred_element_type=jnp.float32)
+        total[...] = part if k == 0 else total[...] + part
+    for m in range(GROUP):
+        pair_refs[m][:ROWS, :HD] = total[:, columns(head ^ m, HD)].astype(jnp.bfloat16)
+
+
+def pack_rows(queries_ref, grads_ref, *out_refs):
+    head = own_head()
+    for m, out_ref in enumerate(out_refs):
+        span = columns(head ^ m, GROUP * HD)
+        out_ref[:, : GROUP * HD] = queries_ref[:, span]
+        out_ref[:, GROUP * HD :] = grads_ref[:, span]
+
+
+def pack_weights(w_ref, leaving_ref, semaphore):
+    first = (1 - lax.axis_index("tensor")) * 2 + (lax.axis_index("dp") & 1)
+    copy = pltpu.make_async_copy(w_ref.at[columns(first, 2 * PART)], leaving_ref, semaphore)
+    copy.start()
+    copy.wait()
+
+
+def pack_features(inputs_ref, near_ref, far_ref):
+    chip = lax.axis_index("dp") >> 1
+    side = lax.axis_index("tensor")
+    for m in range(GROUP):
+        near_ref[m] = inputs_ref[:, columns(2 * (chip ^ m) + side, 256)]
+        far_ref[m] = inputs_ref[:, columns(2 * (chip ^ (m + GROUP)) + side, 256)]
+
+
+def join_features(near_ref, far_ref, *joined_refs):
+    for m, joined_ref in enumerate(joined_refs):
+        joined_ref[0] = near_ref[m]
+        joined_ref[1] = far_ref[m]
+
+
+def turn_features(*refs):
+    for j in range(2 * GROUP):
+        turned = refs[j % GROUP][j // GROUP].astype(jnp.float32).T
+        refs[-1][:, j * ROWS : (j + 1) * ROWS] = turned.astype(jnp.bfloat16)
+
+
+def dot_nt(left, right):
+    return lax.dot_general(
+        left, right, (((1,), (1,)), ((), ())), preferred_element_type=jnp.float32
+    )
+
+
+def folded(array, reduce):
+    return reduce(array.reshape(-1, 8, array.shape[-1]), axis=0)
+
+
+def first_row_of(positions):
+    def first_row(block):
+        return pl.multiple_of(positions[block // 2, block % 2] * BLK, BLK)
+
+    return first_row
+
+
+def attend_rows(
+    first_part, first_row, lens_ref, row_refs, dq_refs, keys, keys_t, values, dk, dv, scratch
+):
+    q_rows, g_rows, dq_all, scores, d_prob = scratch
+    score_scale = 1.0 / math.sqrt(HD)
+    base_two = score_scale * math.log2(math.e)
+    parts = len(row_refs)
+    for block in range(2 * parts):
+        here = pl.ds(block % 2 * BLK, BLK)
+        for h in range(GROUP):
+            there = pl.ds(h * BLK, BLK)
+            q_rows[block, there] = row_refs[block // 2][here, h * HD : (h + 1) * HD]
+            g_rows[block, there] = row_refs[block // 2][
+                here, (GROUP + h) * HD : (GROUP + h + 1) * HD
+            ]
+    starts = [lens_ref[0]]
+    for k in (1, 2):
+        starts.append(starts[-1] + lens_ref[k])
+
+    def document_start(position):
+        found = jnp.zeros_like(position)
+        for start in starts:
+            found = jnp.where(start <= position, start, found)
+        return found
+
+    @pl.loop(0, 2 * parts)
+    def _(block):
+        first = first_row(2 * first_part + block)
+        lanes = lax.broadcasted_iota(jnp.int32, (1, GROUP * BLK), 1)
+        position = first + (lanes & (BLK - 1))
+        start = document_start(position)
+        low = document_start(first) // TILE
+        count = (first + BLK - 1) // TILE + 1 - low
+
+        def run(over_tiles):
+            query = q_rows[block]
+            grad = g_rows[block]
+            zeros = jnp.zeros((8, GROUP * BLK), jnp.float32)
+
+            def visit_scores(k, row_max):
+                here = columns(low + k, TILE)
+                raw = dot_nt(keys[here], query)
+                row = (low + k) * TILE + lax.broadcasted_iota(jnp.int32, raw.shape, 0)
+                raw = jnp.where((row <= position) & (row >= start), raw, masked_fill)
+                scores[k] = raw
+                d_prob[k] = dot_nt(values[here], grad)
+                return jnp.maximum(row_max, folded(raw, jnp.max))
+
+            row_max = over_tiles(visit_scores, zeros + masked_fill)
+            row_max = jnp.max(row_max, axis=0, keepdims=True)
+
+            def visit_sums(k, running):
+                terms = jnp.exp2((scores[k] - row_max) * base_two)
+                scores[k] = terms
+                return (
+                    running[0] + folded(terms, jnp.sum),
+                    running[1] + folded(terms * d_prob[k], jnp.sum),
+                )
+
+            row_sum, weighted = over_tiles(visit_sums, (zeros, zeros))
+            inverse = 1.0 / jnp.sum(row_sum, axis=0, keepdims=True)
+            delta = jnp.sum(weighted, axis=0, keepdims=True) * inverse
+
+            def visit_grads(k, dq):
+                here = columns(low + k, TILE)
+                prob = scores[k] * inverse
+                score_bf = (prob * (d_prob[k] - delta)).astype(jnp.bfloat16)
+                dk[here] += jnp.dot(score_bf, query, preferred_element_type=jnp.float32)
+                dv[here] += jnp.dot(
+                    prob.astype(jnp.bfloat16), grad, preferred_element_type=jnp.float32
+                )
+                return dq + jnp.dot(
+                    keys_t[:, here], score_bf, preferred_element_type=jnp.float32
+                )
+
+            dq = over_tiles(visit_grads, jnp.zeros((HD, GROUP * BLK), jnp.float32))
+            dq = (dq * score_scale).T.astype(jnp.bfloat16)
+            for h in range(GROUP):
+                dq_all[block, :, h * HD : (h + 1) * HD] = dq[h * BLK : (h + 1) * BLK]
+
+        for fixed in range(1, UNROLLED + 1):
+
+            @pl.when(count == fixed)
+            def _(fixed=fixed):
+                def over_tiles(visit, running):
+                    for k in range(fixed):
+                        running = visit(k, running)
+                    return running
+
+                run(over_tiles)
+
+        @pl.when(count > UNROLLED)
+        def _():
+            run(lambda visit, running: lax.fori_loop(0, count, visit, running))
+
+    for block in range(2 * parts):
+        dq_refs[block // 2][pl.ds(block % 2 * BLK, BLK)] = dq_all[block]
+
+
+def attend_first(lens_ref, *refs):
+    row_refs, refs = refs[: GROUP - 1], refs[GROUP - 1 :]
+    own_a, own_b, far_a, far_b, core_pairs, refs = *refs[:5], refs[5:]
+    dq_refs, refs = refs[: GROUP - 1], refs[GROUP - 1 :]
+    keys, keys_t, values, dk, dv, marks, refs = *refs[:6], refs[6:]
+    scratch, (positions, semaphore) = refs[:5], refs[5:]
+    reach = 2 * MARKED
+    pair_refs = [own_a, own_b]
+    pair_refs += [core_pairs.at[pl.ds(k * reach, reach)] for k in range(2)]
+    pair_refs += [far_a, far_b]
+    pair_refs += [core_pairs.at[pl.ds(k * reach, reach)] for k in range(2, 4)]
+    for part in range(4 * GROUP):
+        here = pl.ds(part % 2 * MARKED + ROWS, 16)
+        row = pair_refs[part // 2][here, :HD].astype(jnp.float32).astype(jnp.int32)
+        marks[part : part + 1] = row[:1]
+    to_scalars = pltpu.make_async_copy(marks, positions, semaphore)
+    to_scalars.start()
+    dk[...] = jnp.zeros_like(dk)
+    dv[...] = jnp.zeros_like(dv)
+    to_scalars.wait()
+    first_row = first_row_of(positions)
+    for block in range(4 * Q_BLOCKS):
+        part = block // 2
+        here = pl.ds(part % 2 * MARKED + block % 2 * BLK, BLK)
+        there = pl.ds(first_row(block), BLK)
+        keys[there] = pair_refs[part // 2][here, :HD]
+        values[there] = pair_refs[part // 2][here, HD:]
+    for tile in range(keys.shape[0] // TILE):
+        here = pl.ds(tile * TILE, TILE)
+        keys_t[:, here] = keys[here].astype(jnp.float32).T.astype(jnp.bfloat16)
+    attend_rows(
+        0, first_row, lens_ref, row_refs, dq_refs, keys, keys_t, values, dk, dv, scratch
+    )
+
+
+def attend_last(lens_ref, row_ref, keys, keys_t, values, dk_first, dv_first, marks, *refs):
+    dq_ref, kept, sent, dk, dv, refs = *refs[:5], refs[5:]
+    scratch, (positions, semaphore) = refs[:5], refs[5:]
+    score_scale = 1.0 / math.sqrt(HD)
+    to_scalars = pltpu.make_async_copy(marks, positions, semaphore)
+    to_scalars.start()
+    dk[...] = dk_first[...]
+    dv[...] = dv_first[...]
+    to_scalars.wait()
+    first_row = first_row_of(positions)
+    attend_rows(
+        GROUP - 1, first_row, lens_ref, [row_ref], [dq_ref], keys, keys_t, values, dk, dv, scratch
+    )
+    for block in range(4 * Q_BLOCKS):
+        quarter = block // Q_BLOCKS
+        here = pl.ds(quarter // 2 * Q_BLOCKS * BLK + block % Q_BLOCKS * BLK, BLK)
+        there = pl.ds(first_row(block), BLK)
+        out_ref = sent if quarter % 2 else kept
+        out_ref[here, :HD] = dk[there] * score_scale
+        out_ref[here, HD:] = dv[there]
+
+
+def weight_grad(own_ref, other_ref, *refs):
+    grad_refs, (keep_ref, send_ref, grads) = refs[:GROUP], refs[GROUP:]
+    head = own_head()
+    for k, grad_ref in enumerate(grad_refs):
+        for far in range(2):
+            for m in range(GROUP):
+                here = pl.ds((far * GROUP + m) * ROWS, ROWS)
+                there = pl.ds((far * GROUP + (m ^ k)) * ROWS, ROWS)
+                grads[here, columns(head ^ k, HD)] = grad_ref[there]
+    own = jnp.dot(own_ref[...], grads[...], preferred_element_type=jnp.float32)
+    other = jnp.dot(other_ref[...], grads[...], preferred_element_type=jnp.float32)
+    crossed = (lax.axis_index("dp") & 1) ^ lax.axis_index("tensor")
+
+    @pl.when(crossed == 0)
+    def _():
+        keep_ref[...] = own
+        send_ref[...] = other
+
+    @pl.when(crossed == 1)
+    def _():
+        keep_ref[...] = other
+        send_ref[...] = own
+
+
+def input_grad(own_ref, other_ref, w_own, w_near, w_far, out_ref, own_all, other_all):
+    head = own_head()
+    core = lax.axis_index("dp") & 1
+    side = lax.axis_index("tensor")
+    for k in range(GROUP):
+        own_all[:, columns(head ^ k, HD)] = own_ref[k]
+        other_all[:, columns(head ^ k, HD)] = other_ref[k]
+    for k in range(4):
+        chunk = 2 * (core ^ (k // 2)) + k % 2
+        w_other = (w_near, w_far)[k // 2][pl.ds(k % 2 * PART, PART)]
+        part = dot_nt(own_all[...], w_own[columns(side * 4 + chunk, PART)])
+        part = part + dot_nt(other_all[...], w_other)
+        out_ref[:, columns(chunk, PART)] = part.astype(jnp.bfloat16)
+
+
+def pack_grads(value_ref, row_ref, *refs):
+    for m, out_ref in enumerate(refs):
+        out_ref[:, :HD] = value_ref[m * ROWS : (m + 1) * ROWS]
+    refs[-1][:, HD:] = row_ref[...]
+
+
+def finish(keep_ref, arrived_ref, *refs):
+    row_refs, grad_refs, refs = refs[: GROUP - 1], refs[GROUP - 1 : 2 * GROUP - 1], refs[2 * GROUP - 1 :]
+    weight_out, query_out, value_out = refs
+    head = own_head()
+    weight_out[...] = keep_ref[...] + arrived_ref[...]
+    for m in range(GROUP):
+        row = row_refs[m][...] if m < GROUP - 1 else grad_refs[m][:, HD:]
+        query_out[:, columns(head ^ m, GROUP * HD)] = row
+        value_out[:, columns(head ^ m, HD)] = grad_refs[m][:, :HD]
+
+
+def shaped(shape, dtype=jnp.bfloat16):
+    return jax.ShapeDtypeStruct(shape, dtype)
+
+
+def limits(mebibytes):
+    return pltpu.CompilerParams(vmem_limit_bytes=mebibytes << 20)
+
+
+def with_partners(arrays):
+    return [arrays[0]] + [swap(arrays[m], 2 * m) for m in range(1, len(arrays))]
+
+
+def on_device_by_heads(inputs, w_key, values, queries, d_out, doc_lens, block_pos):
+    features = inputs.shape[1]
+    kv_columns = values.shape[1]
+    total_rows = 16 * ROWS
+    half, quarter = total_rows // 2, total_rows // 4
+    vmem, smem, hbm = whole_spec(), whole_spec(SMEM), whole_spec(HBM)
+
+    pairs = pl.pallas_call(
+        project_keys,
+        out_shape=[shaped((MARKED, 2 * HD))] * GROUP,
+        in_specs=[smem, hbm, vmem, hbm],
+        out_specs=[vmem] * GROUP,
+        scratch_shapes=[
+            VMEM((ROWS, features), jnp.bfloat16),
+            VMEM((features, kv_columns), jnp.bfloat16),
+            VMEM((ROWS, kv_columns), jnp.float32),
+            DMA((1 + features // PART,)),
+        ],
+        compiler_params=limits(60),
+        cost_estimate=pl.CostEstimate(
+            flops=2 * ROWS * features * kv_columns,
+            bytes_accessed=features * kv_columns * 2,
+            transcendentals=0,
+        ),
+        name="project_keys",
+    )(block_pos, inputs, values, w_key)
+
+    packed_rows = pl.pallas_call(
+        pack_rows,
+        out_shape=[shaped((ROWS, 2 * GROUP * HD))] * GROUP,
+        in_specs=[vmem] * 2,
+        out_specs=[vmem] * GROUP,
+        compiler_params=limits(8),
+        name="pack_rows",
+    )(after(queries, pairs[0]), d_out)
+
+    leaving = pl.pallas_call(
+        pack_weights,
+        out_shape=shaped((2 * PART, kv_columns)),
+        in_specs=[hbm],
+        out_specs=vmem,
+        scratch_shapes=[DMA],
+        compiler_params=limits(56),
+        name="pack_weights",
+    )(after(w_key, packed_rows[0]))
+    pairs = [after(pairs[0], leaving)] + list(pairs[1:])
+    pairs = with_partners(pairs)
+    own_a = jnp.concatenate(pairs[:2], axis=0)
+    own_b = jnp.concatenate(pairs[2:], axis=0)
+    far_a = swap(own_a, Z_HI)
+    far_b = swap(own_b, Z_HI)
+    rows = with_partners(packed_rows)
+
+    near_features, far_features = pl.pallas_call(
+        pack_features,
+        out_shape=[shaped((GROUP, ROWS, 256))] * 2,
+        in_specs=[vmem],
+        out_specs=[vmem] * 2,
+        compiler_params=limits(8),
+        name="pack_features",
+    )(after(inputs, own_a))
+    w_near = swap_tensor(leaving)
+    near_pairs = jnp.concatenate([own_a, own_b, far_a, far_b], axis=0)
+    core_pairs = swap(after(near_pairs, near_features, leaving, rows[1], rows[2]), CORE)
+    far_features = swap(far_features, Z_HI)
+
+    row_grad = shaped((ROWS, GROUP * HD))
+    sorted_rows = shaped((total_rows, HD))
+    sums = shaped((total_rows, HD), jnp.float32)
+    half_sums = shaped((half, 2 * HD), jnp.float32)
+
+    def attend_scratch(blocks):
+        stacked = VMEM((blocks, GROUP * BLK, HD), jnp.bfloat16)
+        tiles = VMEM((total_rows // TILE, TILE, GROUP * BLK), jnp.float32)
+        return [
+            stacked,
+            stacked,
+            VMEM((blocks, BLK, GROUP * HD), jnp.bfloat16),
+            tiles,
+            tiles,
+            SMEM((4 * GROUP, HD), jnp.int32),
+            DMA,
+        ]
+
+    *row_grads, keys, keys_t, all_values, dk_first, dv_first, marks = pl.pallas_call(
+        attend_first,
+        out_shape=[row_grad] * (GROUP - 1)
+        + [sorted_rows, shaped((HD, total_rows)), sorted_rows, sums, sums]
+        + [shaped((4 * GROUP, HD), jnp.int32)],
+        in_specs=[smem] + [vmem] * (GROUP + 4),
+        out_specs=[vmem] * (GROUP + 5),
+        scratch_shapes=attend_scratch(Q_BLOCKS - 2),
+        compiler_params=limits(20),
+        cost_estimate=pl.CostEstimate(flops=ATTEND_COST, bytes_accessed=0, transcendentals=0),
+        name="attend_first",
+    )(doc_lens, *rows[:-1], own_a, own_b, far_a, far_b, core_pairs)
+    last_grad, kept, sent = pl.pallas_call(
+        attend_last,
+        out_shape=[row_grad, half_sums, half_sums],
+        in_specs=[smem] + [vmem] * 7,
+        out_specs=[vmem] * 3,
+        scratch_shapes=[VMEM((total_rows, HD), jnp.float32)] * 2 + attend_scratch(2),
+        compiler_params=limits(20),
+        cost_estimate=pl.CostEstimate(flops=ATTEND_COST, bytes_accessed=0, transcendentals=0),
+        name="attend_last",
+    )(doc_lens, rows[-1], keys, keys_t, all_values, dk_first, dv_first, marks)
+
+    sent = after(sent, far_features, w_near)
+    row_grads = with_partners(row_grads)
+    grads = after(kept, *row_grads) + swap(sent, CORE)
+    dk_sum, dv_sum = grads[:, :HD], grads[:, HD:]
+    dk_far = swap(dk_sum.astype(jnp.bfloat16), Z_HI)
+    w_far = swap(after(w_near, dk_sum), CORE)
+
+    feature_parts = pl.pallas_call(
+        join_features,
+        out_shape=[shaped((2, ROWS, 256))] * GROUP,
+        in_specs=[vmem] * 2,
+        out_specs=[vmem] * GROUP,
+        compiler_params=limits(16),
+        name="join_features",
+    )(after(near_features, sent), far_features)
+    own_features = pl.pallas_call(
+        turn_features,
+        out_shape=shaped((256, half)),
+        in_specs=[vmem] * GROUP,
+        out_specs=vmem,
+        compiler_params=limits(16),
+        name="turn_features",
+    )(*with_partners(feature_parts))
+    other_features = swap_tensor(own_features)
+
+    dk_far = jnp.concatenate([dk_far[quarter:], dk_far[:quarter]], axis=0)
+    key_grad = (dk_sum + dk_far.astype(jnp.float32)).astype(jnp.bfloat16)
+    key_grad = after(key_grad, own_features, w_far)
+    key_grads = with_partners([key_grad] * GROUP)
+    own_key_grad = jnp.stack([key_grads[m][m * ROWS : (m + 1) * ROWS] for m in range(GROUP)])
+    other_key_grad = swap_tensor(own_key_grad)
+
+    dv_far = swap(after(dv_sum[quarter:].astype(jnp.bfloat16), key_grad), Z_HI)
+    value_grad = (dv_sum[:quarter] + dv_far.astype(jnp.float32)).astype(jnp.bfloat16)
+    packed_grads = pl.pallas_call(
+        pack_grads,
+        out_shape=[shaped((ROWS, HD))] * (GROUP - 1) + [shaped((ROWS, (GROUP + 1) * HD))],
+        in_specs=[vmem] * 2,
+        out_specs=[vmem] * GROUP,
+        compiler_params=limits(16),
+        name="pack_grads",
+    )(value_grad, last_grad)
+    packed_grads = [after(packed_grads[0], own_key_grad)] + [
+        after(grad, own_key_grad) for grad in packed_grads[1:]
+    ]
+
+    keep, send = pl.pallas_call(
+        weight_grad,
+        out_shape=[shaped((256, kv_columns), jnp.float32)] * 2,
+        in_specs=[vmem] * (2 + GROUP),
+        out_specs=[vmem] * 2,
+        scratch_shapes=[VMEM((half, kv_columns), jnp.bfloat16)],
+        compiler_params=limits(24),
+        cost_estimate=pl.CostEstimate(
+            flops=4 * 256 * half * kv_columns, bytes_accessed=4 << 20, transcendentals=0
+        ),
+        name="weight_grad",
+    )(own_features, other_features, *key_grads)
+    arrived = swap(send, CORE)
+
+    d_input = pl.pallas_call(
+        input_grad,
+        out_shape=shaped((ROWS, features // 2)),
+        in_specs=[vmem] * 5,
+        out_specs=vmem,
+        scratch_shapes=[VMEM((ROWS, kv_columns), jnp.bfloat16)] * 2,
+        compiler_params=limits(16),
+        cost_estimate=pl.CostEstimate(
+            flops=4 * ROWS * 2048 * kv_columns, bytes_accessed=5 << 20, transcendentals=0
+        ),
+        name="input_grad",
+    )(after(own_key_grad, send), other_key_grad, w_key, w_near, w_far)
+
+    d_wkey, d_query, d_value = pl.pallas_call(
+        finish,
+        out_shape=[
+            shaped((256, kv_columns), jnp.float32),
+            shaped(queries.shape),
+            shaped(values.shape),
+        ],
+        in_specs=[vmem] * (1 + 2 * GROUP),
+        out_specs=[vmem] * 3,
+        compiler_params=limits(16),
+        name="finish",
+    )(keep, arrived, *row_grads, *with_partners(packed_grads))
+    return (d_query, d_value, d_input, d_wkey)
+
+
 def solution(mesh):
+    by_heads = mesh.shape["dp"] == 16 and mesh.shape["tensor"] == 2
     return jax.shard_map(
-        on_device,
+        on_device_by_heads if by_heads else on_device,
         mesh=mesh,
         in_specs=(
             P("dp", None),

time: 440 us -> 98.4 us (0.22)
  waiting for transfers between devices: 182 us -> 39.6 us
  blocking collectives: 123 us -> 0 us
  local copies, waits for them, and re-layouts: 46.9 us -> 0.19 us
  matrix products: 42.9 us -> 0 us
  starting transfers between devices: 0.16 us -> 34.7 us
  Pallas kernels: 0 us -> 22.8 us
  other arithmetic: 21.9 us -> 0.25 us
  between operations: 14.7 us -> 0.95 us
  loops' own time: 5.87 us -> 0 us
    reduce_scatter x2 -> x0, waiting for transfers between devices: 119 us -> none  [the longest x1 98.3 us: on_device(): lax.psum_scatter(lax.dot_general(inputs, key_grad, (((0,), (0,)), ((), ()...]
    all_to_all x1 -> x0, blocking collectives: 109 us -> none  [on_device(): lax.all_to_all(buffer_rows.astype(jnp.bfloat16), 'dp', split_axis=0, conc...]
    all_gather x2 -> x0, waiting for transfers between devices: 63.3 us -> none  [the longest x1 38.8 us: on_device(): lax.all_gather(values, 'dp', axis=0, tiled=True)]
    dot_general x24 -> x0, matrix products: 42.9 us -> none  [the longest x6 9.66 us: scored(): jnp.einsum('qcgd,kcd->cgqk', query_heads, key_split, preferred_element_ty...]
    ppermute x0 -> x29, waiting for transfers between devices: none -> 39.6 us  [the longest x26 32 us: swap(): return lax.ppermute(array, 'dp', [(i, i ^ mask) for i in range(16)])]
    ppermute x0 -> x29, starting transfers between devices: none -> 34.7 us  [the longest x26 29.3 us: swap(): return lax.ppermute(array, 'dp', [(i, i ^ mask) for i in range(16)])]
    pallas_call x0 -> x12, Pallas kernels: none -> 22.8 us  [the longest x1 7.49 us: on_device_by_heads(): pl.pallas_call(attend_first, out_shape=[row_grad] * (GROUP - 1) + [sorted...]
    unnamed x1 -> x0, blocking collectives: 13.7 us -> none
  transfers between devices with their start and end apart: 4 -> 29, of which waited for: 4 -> 14; matrix products, arithmetic and copies ran while one was open for 4% -> 0% of each run, Pallas kernels for 0% -> 17%
where the time goes in v3:
time: 98.4 us; the launch traced here: 98.5 us
  waiting for transfers between devices  39.6 us (40%)
  starting transfers between devices  34.7 us (35%)
  Pallas kernels  22.8 us (23%)
    ppermute x26, waiting for transfers between devices, swap(): return lax.ppermute(array, 'dp', [(i, i ^ mask) for i in range(16)])  32 us
    ppermute x26, starting transfers between devices, swap(): return lax.ppermute(array, 'dp', [(i, i ^ mask) for i in range(16)])  29.3 us
    ppermute x3, waiting for transfers between devices, swap_tensor(): return lax.ppermute(array, 'tensor', [(0, 1), (1, 0)])  7.57 us
    pallas_call x1, Pallas kernels, on_device_by_heads(): pl.pallas_call(attend_first, out_shape=[row_grad] * (GROUP - 1) + [sorted...  7.49 us
    ppermute x3, starting transfers between devices, swap_tensor(): return lax.ppermute(array, 'tensor', [(0, 1), (1, 0)])  5.34 us
    pallas_call x1, Pallas kernels, on_device_by_heads(): pl.pallas_call(project_keys, out_shape=[shaped((MARKED, 2 * HD))] * GROUP...  4.51 us
    pallas_call x1, Pallas kernels, on_device_by_heads(): pl.pallas_call(attend_last, out_shape=[row_grad, half_sums, half_sums], i...  3.85 us
    pallas_call x1, Pallas kernels, on_device_by_heads(): pl.pallas_call(input_grad, out_shape=shaped((ROWS, features // 2)), in_sp...  2.27 us
  transfers between devices with their start and end apart: 29, of which 14 were waited for; matrix products, arithmetic and copies ran while one was open for 0% of the time, Pallas kernels for 17%

profile of v3, /device:TPU:0, one launch (start us, length us, event | category | flops | bytes accessed | tf_op | source)
XLA Modules:
  0.0 98.5 jit_solution(17286802956499900978)
XLA Ops:
  0.7 4.5 %project_keys.1 = (bf16[144,256]{1,0:T(8,128)(2,1)}, bf16[144,256]{1,0:T(8,128)(2,1)}, bf16[144,256]{1,0:T(8,128)(2,1)}, bf16[144,256]{1,0:T(8,128)(2,1)}) custom-call(s32[2]{0:T(128)} %pos_ref.1, bf16[128,4096]{1,0:T(8,128)(2,1)} %inputs_ref.2, bf16[128,512]{1,0:T(8,128)(2,1)} %values_ref.1, bf16[4096,512]{1,0:T(8,128)(2,1)} %w_own.1), custom_call_target="tpu_custom_call" | custom-call | flops 536870912 | bytes 4194304 | tf_op jit(solution)/shard_map/project_keys/pallas_call | solution.py:560
  5.2 3.0 %collective-permute-start = (bf16[144,256]{1,0:T(8,128)(2,1)}, bf16[144,256]{1,0:T(8,128)(2,1)S(1)}, u32[]{:S(2)}, u32[]{:S(2)}) collective-permute-start(bf16[144,256]{1,0:T(8,128)(2,1)} %get-tuple-element.60), channel_id=1, source_target_pairs={{0,4},{2,6},{4,0},{6,2},{8,12},{10,14},{12,8},{14,10},{16,20},{18,... | collective-permute-start | bytes 221192 | tf_op jit(solution)/shard_map/ppermute | solution.py:221
  8.2 1.6 %collective-permute-start.4 = (bf16[144,256]{1,0:T(8,128)(2,1)}, bf16[144,256]{1,0:T(8,128)(2,1)S(1)}, u32[]{:S(2)}, u32[]{:S(2)}) collective-permute-start(bf16[144,256]{1,0:T(8,128)(2,1)} %get-tuple-element.66), channel_id=1, source_target_pairs={{0,8},{2,10},{4,12},{6,14},{8,0},{10,2},{12,4},{14,6},{16,24},{18,... | collective-permute-start | bytes 221192 | tf_op jit(solution)/shard_map/ppermute | solution.py:221
  9.9 2.2 %pack_weights.1 = bf16[1024,512]{1,0:T(8,128)(2,1)} custom-call(bf16[4096,512]{1,0:T(8,128)(2,1)} %w_own.1), custom_call_target="tpu_custom_call" | custom-call | tf_op jit(solution)/shard_map/pack_weights/pallas_call | solution.py:589
  12.2 2.0 %collective-permute-start.10 = (bf16[1024,512]{1,0:T(8,128)(2,1)}, bf16[1024,512]{1,0:T(8,128)(2,1)S(1)}, u32[]{:S(2)}, u32[]{:S(2)}) collective-permute-start(bf16[1024,512]{1,0:T(8,128)(2,1)} %pack_weights.1), channel_id=1, source_target_pairs={{0,1},{1,0},{2,3},{3,2},{4,5},{5,4},{6,7},{7,6},{8,9},{9,8},{10,11... | collective-permute-start | bytes 3145736 | tf_op jit(solution)/shard_map/ppermute | solution.py:225
  14.2 2.7 %collective-permute-start.6 = (bf16[288,256]{1,0:T(8,128)(2,1)S(1)}, bf16[288,256]{1,0:T(8,128)(2,1)S(1)}, u32[]{:S(2)}, u32[]{:S(2)}) collective-permute-start(bf16[288,256]{1,0:T(8,128)(2,1)S(1)} %get-tuple-element.113.refs_3_), channel_id=1, source_target_pairs={{0,16},{2,18},{4,20},{6,22},{8,24},{10,26},{12,28},{14,30},{16,0},... | collective-permute-start | bytes 442376 | tf_op jit(solution)/shard_map/ppermute | solution.py:221
  18.8 1.6 %collective-permute-start.3 = (bf16[128,1024]{1,0:T(8,128)(2,1)S(1)}, bf16[128,1024]{1,0:T(8,128)(2,1)S(1)}, u32[]{:S(2)}, u32[]{:S(2)}) collective-permute-start(bf16[128,1024]{1,0:T(8,128)(2,1)S(1)} %get-tuple-element.65), channel_id=1, source_target_pairs={{0,8},{2,10},{4,12},{6,14},{8,0},{10,2},{12,4},{14,6},{16,24},{18,... | collective-permute-start | bytes 786440 | tf_op jit(solution)/shard_map/ppermute | solution.py:221
  20.4 6.8 %collective-permute-done.6.refs_5_ = bf16[288,256]{1,0:T(8,128)(2,1)S(1)} collective-permute-done((bf16[288,256]{1,0:T(8,128)(2,1)S(1)}, bf16[288,256]{1,0:T(8,128)(2,1)S(1)}, u32[]{:S(2)}, u32[]{:S(2)}) %collective-permute-start.6) | collective-permute-done | bytes 147488 | tf_op jit(solution)/shard_map/ppermute | solution.py:221
  27.2 2.0 %collective-permute-done.7.refs_6_ = bf16[288,256]{1,0:T(8,128)(2,1)S(1)} collective-permute-done((bf16[288,256]{1,0:T(8,128)(2,1)S(1)}, bf16[288,256]{1,0:T(8,128)(2,1)S(1)}, u32[]{:S(2)}, u32[]{:S(2)}) %collective-permute-start.7) | collective-permute-done | bytes 147488 | tf_op jit(solution)/shard_map/ppermute | solution.py:221
  31.1 4.2 %collective-permute-start.9 = (bf16[4,128,256]{2,1,0:T(8,128)(2,1)S(1)}, bf16[4,128,256]{2,1,0:T(8,128)(2,1)S(1)}, u32[]{:S(2)}, u32[]{:S(2)}) collective-permute-start(bf16[4,128,256]{2,1,0:T(8,128)(2,1)S(1)} %get-tuple-element.76), channel_id=1, source_target_pairs={{0,16},{2,18},{4,20},{6,22},{8,24},{10,26},{12,28},{14,30},{16,0},... | collective-permute-start | bytes 786440 | tf_op jit(solution)/shard_map/ppermute | solution.py:221
  35.2 7.5 %attend_first.1 = (bf16[128,512]{1,0:T(8,128)(2,1)S(1)}, bf16[128,512]{1,0:T(8,128)(2,1)S(1)}, bf16[128,512]{1,0:T(8,128)(2,1)S(1)}, bf16[2048,128]{1,0:T(8,128)...) custom-call(s32[4]{0:T(128)S(1)} %copy-done.4, ...), custom_call_target="tpu_custom_call" | custom-call | flops 1048576 | tf_op jit(solution)/shard_map/attend_first/pallas_call | solution.py:637
  44.2 3.9 %attend_last.1 = (bf16[128,512]{1,0:T(8,128)(2,1)S(1)}, f32[1024,256]{1,0:T(8,128)S(1)}, f32[1024,256]{1,0:T(8,128)S(1)}) custom-call(s32[4]{0:T(128)S(1)} %copy-done.4, bf16[128,1024]{1,0:T(8,128)(2,1)S(1)} %collective-permute-done.1.row_ref, bf16[2048,128]{1,0:T(8,128)(2,1)S(1)} %get-tuple-element.69.keys, bf16[128,2048]{1,0:T(8,128)(2,1)S(1)} %get-tuple-element.70.keys_t, ...), custom_call_target="tpu_custom_call" | custom-call | flops 1048576 | tf_op jit(solution)/shard_map/attend_last/pallas_call | solution.py:649
  50.0 4.1 %collective-permute-done.15.refs_1_ = bf16[128,512]{1,0:T(8,128)(2,1)S(1)} collective-permute-done((bf16[128,512]{1,0:T(8,128)(2,1)S(1)}, bf16[128,512]{1,0:T(8,128)(2,1)S(1)}, u32[]{:S(2)}, u32[]{:S(2)}) %collective-permute-start.15) | collective-permute-done | bytes 131104 | tf_op jit(solution)/shard_map/ppermute | solution.py:221
  55.9 1.8 %collective-permute-start.11 = (bf16[2,128,256]{2,1,0:T(8,128)(2,1)S(1)}, bf16[2,128,256]{2,1,0:T(8,128)(2,1)S(1)}, u32[]{:S(2)}, u32[]{:S(2)}) collective-permute-start(bf16[2,128,256]{2,1,0:T(8,128)(2,1)S(1)} %get-tuple-element.80), channel_id=1, source_target_pairs={{0,4},{2,6},{4,0},{6,2},{8,12},{10,14},{12,8},{14,10},{16,20},{18,... | collective-permute-start | bytes 393224 | tf_op jit(solution)/shard_map/ppermute | solution.py:221
  57.7 1.7 %collective-permute-start.12 = (bf16[2,128,256]{2,1,0:T(8,128)(2,1)S(1)}, bf16[2,128,256]{2,1,0:T(8,128)(2,1)S(1)}, u32[]{:S(2)}, u32[]{:S(2)}) collective-permute-start(bf16[2,128,256]{2,1,0:T(8,128)(2,1)S(1)} %get-tuple-element.81), channel_id=1, source_target_pairs={{0,8},{2,10},{4,12},{6,14},{8,0},{10,2},{12,4},{14,6},{16,24},{18,... | collective-permute-start | bytes 393224 | tf_op jit(solution)/shard_map/ppermute | solution.py:221
  61.0 4.3 %collective-permute-done.12.refs_2_ = bf16[2,128,256]{2,1,0:T(8,128)(2,1)S(1)} collective-permute-done((bf16[2,128,256]{2,1,0:T(8,128)(2,1)S(1)}, bf16[2,128,256]{2,1,0:T(8,128)(2,1)S(1)}, u32[]{:S(2)}, u32[]{:S(2)}) %collective-permute-start.12) | collective-permute-done | bytes 131104 | tf_op jit(solution)/shard_map/ppermute | solution.py:221
  65.3 5.1 %collective-permute-done.13.refs_3_ = bf16[2,128,256]{2,1,0:T(8,128)(2,1)S(1)} collective-permute-done((bf16[2,128,256]{2,1,0:T(8,128)(2,1)S(1)}, bf16[2,128,256]{2,1,0:T(8,128)(2,1)S(1)}, u32[]{:S(2)}, u32[]{:S(2)}) %collective-permute-start.13) | collective-permute-done | bytes 131104 | tf_op jit(solution)/shard_map/ppermute | solution.py:221
  72.4 2.6 %collective-permute-start.21 = (bf16[1024,128]{1,0:T(8,128)(2,1)S(1)}, bf16[1024,128]{1,0:T(8,128)(2,1)S(1)}, u32[]{:S(2)}, u32[]{:S(2)}) collective-permute-start(bf16[1024,128]{1,0:T(8,128)(2,1)S(1)} %add_convert_fusion.refs_0_), channel_id=1, source_target_pairs={{0,8},{2,10},{4,12},{6,14},{8,0},{10,2},{12,4},{14,6},{16,24},{18,... | collective-permute-start | bytes 786440 | tf_op jit(solution)/shard_map/ppermute | solution.py:221
  76.3 7.1 %collective-permute-done.14.other_ref = bf16[256,1024]{1,0:T(8,128)(2,1)S(1)} collective-permute-done((bf16[256,1024]{1,0:T(8,128)(2,1)S(1)}, bf16[256,1024]{1,0:T(8,128)(2,1)S(1)}, u32[]{:S(2)}, u32[]{:S(2)}) %collective-permute-start.14) | collective-permute-done | bytes 524320 | tf_op jit(solution)/shard_map/ppermute | solution.py:225
  83.3 2.0 %collective-permute-done.22.refs_3_ = bf16[1024,128]{1,0:T(8,128)(2,1)S(1)} collective-permute-done((bf16[1024,128]{1,0:T(8,128)(2,1)S(1)}, bf16[1024,128]{1,0:T(8,128)(2,1)S(1)}, u32[]{:S(2)}, u32[]{:S(2)}) %collective-permute-start.22) | collective-permute-done | bytes 262176 | tf_op jit(solution)/shard_map/ppermute | solution.py:221
  86.9 1.8 %collective-permute-start.28 = (bf16[4,128,128]{2,1,0:T(8,128)(2,1)S(1)}, bf16[4,128,128]{2,1,0:T(8,128)(2,1)S(1)}, u32[]{:S(2)}, u32[]{:S(2)}) collective-permute-start(bf16[4,128,128]{2,1,0:T(8,128)(2,1)S(1)} %pad_maximum_fusion.own_ref), channel_id=1, source_target_pairs={{0,1},{1,0},{2,3},{3,2},{4,5},{5,4},{6,7},{7,6},{8,9},{9,8},{10,11... | collective-permute-start | bytes 393224 | tf_op jit(solution)/shard_map/ppermute | solution.py:225
  89.9 2.5 %collective-permute-start.26 = (bf16[128,128]{1,0:T(8,128)(2,1)S(1)}, bf16[128,128]{1,0:T(8,128)(2,1)S(1)}, u32[]{:S(2)}, u32[]{:S(2)}) collective-permute-start(bf16[128,128]{1,0:T(8,128)(2,1)S(1)} %get-tuple-element.99), channel_id=1, source_target_pairs={{0,8},{2,10},{4,12},{6,14},{8,0},{10,2},{12,4},{14,6},{16,24},{18,... | collective-permute-start | bytes 98312 | tf_op jit(solution)/shard_map/ppermute | solution.py:221
  92.9 2.3 %input_grad.1 = bf16[128,2048]{1,0:T(8,128)(2,1)} custom-call(bf16[4,128,128]{2,1,0:T(8,128)(2,1)S(1)} %pad_maximum_fusion.own_ref, bf16[4,128,128]{2,1,0:T(8,128)(2,1)S(1)} %collective-permute-done.28.other_ref, bf16[4096,512]{1,0:T(8,128)(2,1)S(1)} %copy-done, bf16[1024,512]{1,0:T(8,128)(2,1)S(1)} %collective-permute-done.10.w_near, ...), custom_call_target="tpu_custom_call" | custom-call | flops 536870912 | bytes 5242880 | tf_op jit(solution)/shard_map/input_grad/pallas_call | solution.py:720
  95.2 2.2 %collective-permute-done.26.refs_5_ = bf16[128,128]{1,0:T(8,128)(2,1)S(1)} collective-permute-done((bf16[128,128]{1,0:T(8,128)(2,1)S(1)}, bf16[128,128]{1,0:T(8,128)(2,1)S(1)}, u32[]{:S(2)}, u32[]{:S(2)}) %collective-permute-start.26) | collective-permute-done | bytes 32800 | tf_op jit(solution)/shard_map/ppermute | solution.py:221
  (75 shorter events, 18.2 us)
Async XLA Ops:
  5.2 9.0 %collective-permute-start = (bf16[144,256]{1,0:T(8,128)(2,1)}, bf16[144,256]{1,0:T(8,128)(2,1)S(1)}, u32[]{:S(2)}, u32[]{:S(2)}) collective-permute-start(bf16[144,256]{1,0:T(8,128)(2,1)} %get-tuple-element.60), channel_id=1, source_target_pairs={{0,4},{2,6},{4,0},{6,2},{8,12},{10,14},{12,8},{14,10},{16,20},{18,... | collective-permute-start | bytes 221192 | tf_op jit(solution)/shard_map/ppermute | solution.py:221
  8.2 8.6 %collective-permute-start.4 = (bf16[144,256]{1,0:T(8,128)(2,1)}, bf16[144,256]{1,0:T(8,128)(2,1)S(1)}, u32[]{:S(2)}, u32[]{:S(2)}) collective-permute-start(bf16[144,256]{1,0:T(8,128)(2,1)} %get-tuple-element.66), channel_id=1, source_target_pairs={{0,8},{2,10},{4,12},{6,14},{8,0},{10,2},{12,4},{14,6},{16,24},{18,... | collective-permute-start | bytes 221192 | tf_op jit(solution)/shard_map/ppermute | solution.py:221
  9.8 7.1 %collective-permute-start.5 = (bf16[144,256]{1,0:T(8,128)(2,1)}, bf16[144,256]{1,0:T(8,128)(2,1)S(1)}, u32[]{:S(2)}, u32[]{:S(2)}) collective-permute-start(bf16[144,256]{1,0:T(8,128)(2,1)} %get-tuple-element.67), channel_id=1, source_target_pairs={{0,12},{2,14},{4,8},{6,10},{8,4},{10,6},{12,0},{14,2},{16,28},{18,... | collective-permute-start | bytes 221192 | tf_op jit(solution)/shard_map/ppermute | solution.py:221
  12.2 36.0 %collective-permute-start.10 = (bf16[1024,512]{1,0:T(8,128)(2,1)}, bf16[1024,512]{1,0:T(8,128)(2,1)S(1)}, u32[]{:S(2)}, u32[]{:S(2)}) collective-permute-start(bf16[1024,512]{1,0:T(8,128)(2,1)} %pack_weights.1), channel_id=1, source_target_pairs={{0,1},{1,0},{2,3},{3,2},{4,5},{5,4},{6,7},{7,6},{8,9},{9,8},{10,11... | collective-permute-start | bytes 3145736 | tf_op jit(solution)/shard_map/ppermute | solution.py:225
  14.2 13.0 %collective-permute-start.6 = (bf16[288,256]{1,0:T(8,128)(2,1)S(1)}, bf16[288,256]{1,0:T(8,128)(2,1)S(1)}, u32[]{:S(2)}, u32[]{:S(2)}) collective-permute-start(bf16[288,256]{1,0:T(8,128)(2,1)S(1)} %get-tuple-element.113.refs_3_), channel_id=1, source_target_pairs={{0,16},{2,18},{4,20},{6,22},{8,24},{10,26},{12,28},{14,30},{16,0},... | collective-permute-start | bytes 442376 | tf_op jit(solution)/shard_map/ppermute | solution.py:221
  16.9 12.3 %collective-permute-start.7 = (bf16[288,256]{1,0:T(8,128)(2,1)S(1)}, bf16[288,256]{1,0:T(8,128)(2,1)S(1)}, u32[]{:S(2)}, u32[]{:S(2)}) collective-permute-start(bf16[288,256]{1,0:T(8,128)(2,1)S(1)} %get-tuple-element.109.refs_4_), channel_id=1, source_target_pairs={{0,16},{2,18},{4,20},{6,22},{8,24},{10,26},{12,28},{14,30},{16,0},... | collective-permute-start | bytes 442376 | tf_op jit(solution)/shard_map/ppermute | solution.py:221
  17.9 11.3 %collective-permute-start.2 = (bf16[128,1024]{1,0:T(8,128)(2,1)S(1)}, bf16[128,1024]{1,0:T(8,128)(2,1)S(1)}, u32[]{:S(2)}, u32[]{:S(2)}) collective-permute-start(bf16[128,1024]{1,0:T(8,128)(2,1)S(1)} %get-tuple-element.64), channel_id=1, source_target_pairs={{0,4},{2,6},{4,0},{6,2},{8,12},{10,14},{12,8},{14,10},{16,20},{18,... | collective-permute-start | bytes 786440 | tf_op jit(solution)/shard_map/ppermute | solution.py:221
  18.8 11.2 %collective-permute-start.3 = (bf16[128,1024]{1,0:T(8,128)(2,1)S(1)}, bf16[128,1024]{1,0:T(8,128)(2,1)S(1)}, u32[]{:S(2)}, u32[]{:S(2)}) collective-permute-start(bf16[128,1024]{1,0:T(8,128)(2,1)S(1)} %get-tuple-element.65), channel_id=1, source_target_pairs={{0,8},{2,10},{4,12},{6,14},{8,0},{10,2},{12,4},{14,6},{16,24},{18,... | collective-permute-start | bytes 786440 | tf_op jit(solution)/shard_map/ppermute | solution.py:221
  30.0 14.3 %collective-permute-start.1 = (bf16[128,1024]{1,0:T(8,128)(2,1)S(1)}, bf16[128,1024]{1,0:T(8,128)(2,1)S(1)}, u32[]{:S(2)}, u32[]{:S(2)}) collective-permute-start(bf16[128,1024]{1,0:T(8,128)(2,1)S(1)} %get-tuple-element.63), channel_id=1, source_target_pairs={{0,12},{2,14},{4,8},{6,10},{8,4},{10,6},{12,0},{14,2},{16,28},{18,... | collective-permute-start | bytes 786440 | tf_op jit(solution)/shard_map/ppermute | solution.py:221
  31.1 17.0 %collective-permute-start.9 = (bf16[4,128,256]{2,1,0:T(8,128)(2,1)S(1)}, bf16[4,128,256]{2,1,0:T(8,128)(2,1)S(1)}, u32[]{:S(2)}, u32[]{:S(2)}) collective-permute-start(bf16[4,128,256]{2,1,0:T(8,128)(2,1)S(1)} %get-tuple-element.76), channel_id=1, source_target_pairs={{0,16},{2,18},{4,20},{6,22},{8,24},{10,26},{12,28},{14,30},{16,0},... | collective-permute-start | bytes 786440 | tf_op jit(solution)/shard_map/ppermute | solution.py:221
  48.1 7.2 %collective-permute-start.17 = (f32[1024,256]{1,0:T(8,128)S(1)}, f32[1024,256]{1,0:T(8,128)S(1)}, u32[]{:S(2)}, u32[]{:S(2)}) collective-permute-start(f32[1024,256]{1,0:T(8,128)S(1)} %get-tuple-element.77), channel_id=1, source_target_pairs={{0,2},{2,0},{4,6},{6,4},{8,10},{10,8},{12,14},{14,12},{16,18},{18,... | collective-permute-start | bytes 3145736 | tf_op jit(solution)/shard_map/ppermute | solution.py:221
  48.2 24.1 %collective-permute-start.19 = (bf16[1024,512]{1,0:T(8,128)(2,1)S(1)}, bf16[1024,512]{1,0:T(8,128)(2,1)S(1)}, u32[]{:S(2)}, u32[]{:S(2)}) collective-permute-start(bf16[1024,512]{1,0:T(8,128)(2,1)S(1)} %collective-permute-done.10.w_near), channel_id=1, source_target_pairs={{0,2},{2,0},{4,6},{6,4},{8,10},{10,8},{12,14},{14,12},{16,18},{18,... | collective-permute-start | bytes 3145736 | tf_op jit(solution)/shard_map/ppermute | solution.py:221
  55.5 16.7 %collective-permute-start.18 = (bf16[1024,128]{1,0:T(8,128)(2,1)S(1)}, bf16[1024,128]{1,0:T(8,128)(2,1)S(1)}, u32[]{:S(2)}, u32[]{:S(2)}) collective-permute-start(bf16[1024,128]{1,0:T(8,128)(2,1)S(1)} %slice.59), channel_id=1, source_target_pairs={{0,16},{2,18},{4,20},{6,22},{8,24},{10,26},{12,28},{14,30},{16,0},... | collective-permute-start | bytes 786440 | tf_op jit(solution)/shard_map/ppermute | solution.py:221
  57.7 7.6 %collective-permute-start.12 = (bf16[2,128,256]{2,1,0:T(8,128)(2,1)S(1)}, bf16[2,128,256]{2,1,0:T(8,128)(2,1)S(1)}, u32[]{:S(2)}, u32[]{:S(2)}) collective-permute-start(bf16[2,128,256]{2,1,0:T(8,128)(2,1)S(1)} %get-tuple-element.81), channel_id=1, source_target_pairs={{0,8},{2,10},{4,12},{6,14},{8,0},{10,2},{12,4},{14,6},{16,24},{18,... | collective-permute-start | bytes 393224 | tf_op jit(solution)/shard_map/ppermute | solution.py:221
  59.5 11.0 %collective-permute-start.13 = (bf16[2,128,256]{2,1,0:T(8,128)(2,1)S(1)}, bf16[2,128,256]{2,1,0:T(8,128)(2,1)S(1)}, u32[]{:S(2)}, u32[]{:S(2)}) collective-permute-start(bf16[2,128,256]{2,1,0:T(8,128)(2,1)S(1)} %get-tuple-element.82), channel_id=1, source_target_pairs={{0,12},{2,14},{4,8},{6,10},{8,4},{10,6},{12,0},{14,2},{16,28},{18,... | collective-permute-start | bytes 393224 | tf_op jit(solution)/shard_map/ppermute | solution.py:221
  70.6 12.7 %collective-permute-start.14 = (bf16[256,1024]{1,0:T(8,128)(2,1)S(1)}, bf16[256,1024]{1,0:T(8,128)(2,1)S(1)}, u32[]{:S(2)}, u32[]{:S(2)}) collective-permute-start(bf16[256,1024]{1,0:T(8,128)(2,1)S(1)} %turn_features.1.own_ref), channel_id=1, source_target_pairs={{0,1},{1,0},{2,3},{3,2},{4,5},{5,4},{6,7},{7,6},{8,9},{9,8},{10,11... | collective-permute-start | bytes 1572872 | tf_op jit(solution)/shard_map/ppermute | solution.py:225
  72.3 13.0 %collective-permute-start.22 = (bf16[1024,128]{1,0:T(8,128)(2,1)S(1)}, bf16[1024,128]{1,0:T(8,128)(2,1)S(1)}, u32[]{:S(2)}, u32[]{:S(2)}) collective-permute-start(bf16[1024,128]{1,0:T(8,128)(2,1)S(1)} %add_convert_fusion.refs_0_), channel_id=1, source_target_pairs={{0,12},{2,14},{4,8},{6,10},{8,4},{10,6},{12,0},{14,2},{16,28},{18,... | collective-permute-start | bytes 786440 | tf_op jit(solution)/shard_map/ppermute | solution.py:221
  72.4 13.5 %collective-permute-start.21 = (bf16[1024,128]{1,0:T(8,128)(2,1)S(1)}, bf16[1024,128]{1,0:T(8,128)(2,1)S(1)}, u32[]{:S(2)}, u32[]{:S(2)}) collective-permute-start(bf16[1024,128]{1,0:T(8,128)(2,1)S(1)} %add_convert_fusion.refs_0_), channel_id=1, source_target_pairs={{0,8},{2,10},{4,12},{6,14},{8,0},{10,2},{12,4},{14,6},{16,24},{18,... | collective-permute-start | bytes 786440 | tf_op jit(solution)/shard_map/ppermute | solution.py:221
  74.9 10.9 %collective-permute-start.20 = (bf16[1024,128]{1,0:T(8,128)(2,1)S(1)}, bf16[1024,128]{1,0:T(8,128)(2,1)S(1)}, u32[]{:S(2)}, u32[]{:S(2)}) collective-permute-start(bf16[1024,128]{1,0:T(8,128)(2,1)S(1)} %add_convert_fusion.refs_0_), channel_id=1, source_target_pairs={{0,4},{2,6},{4,0},{6,2},{8,12},{10,14},{12,8},{14,10},{16,20},{18,... | collective-permute-start | bytes 786440 | tf_op jit(solution)/shard_map/ppermute | solution.py:221
  75.9 12.9 %collective-permute-start.24 = (bf16[512,128]{1,0:T(8,128)(2,1)S(1)}, bf16[512,128]{1,0:T(8,128)(2,1)S(1)}, u32[]{:S(2)}, u32[]{:S(2)}) collective-permute-start(bf16[512,128]{1,0:T(8,128)(2,1)S(1)} %slice.58), channel_id=1, source_target_pairs={{0,16},{2,18},{4,20},{6,22},{8,24},{10,26},{12,28},{14,30},{16,0},... | collective-permute-start | bytes 393224 | tf_op jit(solution)/shard_map/ppermute | solution.py:221
  86.8 10.6 %collective-permute-start.23 = (f32[256,512]{1,0:T(8,128)S(1)}, f32[256,512]{1,0:T(8,128)S(1)}, u32[]{:S(2)}, u32[]{:S(2)}) collective-permute-start(f32[256,512]{1,0:T(8,128)S(1)} %get-tuple-element.91), channel_id=1, source_target_pairs={{0,2},{2,0},{4,6},{6,4},{8,10},{10,8},{12,14},{14,12},{16,18},{18,... | collective-permute-start | bytes 1572872 | tf_op jit(solution)/shard_map/ppermute | solution.py:221
  86.9 6.0 %collective-permute-start.28 = (bf16[4,128,128]{2,1,0:T(8,128)(2,1)S(1)}, bf16[4,128,128]{2,1,0:T(8,128)(2,1)S(1)}, u32[]{:S(2)}, u32[]{:S(2)}) collective-permute-start(bf16[4,128,128]{2,1,0:T(8,128)(2,1)S(1)} %pad_maximum_fusion.own_ref), channel_id=1, source_target_pairs={{0,1},{1,0},{2,3},{3,2},{4,5},{5,4},{6,7},{7,6},{8,9},{9,8},{10,11... | collective-permute-start | bytes 393224 | tf_op jit(solution)/shard_map/ppermute | solution.py:225
  88.8 8.5 %collective-permute-start.27 = (bf16[128,640]{1,0:T(8,128)(2,1)S(1)}, bf16[128,640]{1,0:T(8,128)(2,1)S(1)}, u32[]{:S(2)}, u32[]{:S(2)}) collective-permute-start(bf16[128,640]{1,0:T(8,128)(2,1)S(1)} %get-tuple-element.101), channel_id=1, source_target_pairs={{0,12},{2,14},{4,8},{6,10},{8,4},{10,6},{12,0},{14,2},{16,28},{18,... | collective-permute-start | bytes 491528 | tf_op jit(solution)/shard_map/ppermute | solution.py:221
  89.9 7.5 %collective-permute-start.26 = (bf16[128,128]{1,0:T(8,128)(2,1)S(1)}, bf16[128,128]{1,0:T(8,128)(2,1)S(1)}, u32[]{:S(2)}, u32[]{:S(2)}) collective-permute-start(bf16[128,128]{1,0:T(8,128)(2,1)S(1)} %get-tuple-element.99), channel_id=1, source_target_pairs={{0,8},{2,10},{4,12},{6,14},{8,0},{10,2},{12,4},{14,6},{16,24},{18,... | collective-permute-start | bytes 98312 | tf_op jit(solution)/shard_map/ppermute | solution.py:221
  (11 other events, 131.5 us)

commit v4 on v3

--- a/solution.py
+++ b/solution.py
@@ -586,6 +586,22 @@
         name="pack_rows",
     )(after(queries, pairs[0]), d_out)
 
+    pairs = [after(pairs[0], packed_rows[0])] + list(pairs[1:])
+    pairs = with_partners(pairs)
+    own_a = jnp.concatenate(pairs[:2], axis=0)
+    own_b = jnp.concatenate(pairs[2:], axis=0)
+    far_a = swap(own_a, Z_HI)
+    far_b = swap(own_b, Z_HI)
+    rows = with_partners(packed_rows)
+
+    near_features, far_features = pl.pallas_call(
+        pack_features,
+        out_shape=[shaped((GROUP, ROWS, 256))] * 2,
+        in_specs=[vmem],
+        out_specs=[vmem] * 2,
+        compiler_params=limits(8),
+        name="pack_features",
+    )(after(inputs, own_a))
     leaving = pl.pallas_call(
         pack_weights,
         out_shape=shaped((2 * PART, kv_columns)),
@@ -594,23 +610,7 @@
         scratch_shapes=[DMA],
         compiler_params=limits(56),
         name="pack_weights",
-    )(after(w_key, packed_rows[0]))
-    pairs = [after(pairs[0], leaving)] + list(pairs[1:])
-    pairs = with_partners(pairs)
-    own_a = jnp.concatenate(pairs[:2], axis=0)
-    own_b = jnp.concatenate(pairs[2:], axis=0)
-    far_a = swap(own_a, Z_HI)
-    far_b = swap(own_b, Z_HI)
-    rows = with_partners(packed_rows)
-
-    near_features, far_features = pl.pallas_call(
-        pack_features,
-        out_shape=[shaped((GROUP, ROWS, 256))] * 2,
-        in_specs=[vmem],
-        out_specs=[vmem] * 2,
-        compiler_params=limits(8),
-        name="pack_features",
-    )(after(inputs, own_a))
+    )(after(w_key, own_b))
     w_near = swap_tensor(leaving)
     near_pairs = jnp.concatenate([own_a, own_b, far_a, far_b], axis=0)
     core_pairs = swap(after(near_pairs, near_features, leaving, rows[1], rows[2]), CORE)
@@ -655,11 +655,11 @@
         compiler_params=limits(20),
         cost_estimate=pl.CostEstimate(flops=ATTEND_COST, bytes_accessed=0, transcendentals=0),
         name="attend_last",
-    )(doc_lens, rows[-1], keys, keys_t, all_values, dk_first, dv_first, marks)
-
-    sent = after(sent, far_features, w_near)
+    )(doc_lens, after(rows[-1], w_near), keys, keys_t, all_values, dk_first, dv_first, marks)
+
     row_grads = with_partners(row_grads)
-    grads = after(kept, *row_grads) + swap(sent, CORE)
+    sent = after(sent, far_features, *row_grads)
+    grads = kept + swap(sent, CORE)
     dk_sum, dv_sum = grads[:, :HD], grads[:, HD:]
     dk_far = swap(dk_sum.astype(jnp.bfloat16), Z_HI)
     w_far = swap(after(w_near, dk_sum), CORE)
@@ -678,6 +678,7 @@
         in_specs=[vmem] * GROUP,
         out_specs=vmem,
         compiler_params=limits(16),
+        cost_estimate=pl.CostEstimate(flops=4_000_000_000, bytes_accessed=0, transcendentals=0),
         name="turn_features",
     )(*with_partners(feature_parts))
     other_features = swap_tensor(own_features)

time: 98.4 us -> 95.6 us (0.972)
  waiting for transfers between devices: 39.6 us -> 37.2 us
  starting transfers between devices: 34.7 us -> 33 us
    ppermute x3, waiting for transfers between devices: 7.57 us -> 3.53 us  [swap_tensor(): return lax.ppermute(array, 'tensor', [(0, 1), (1, 0)])]
    ppermute x26, waiting for transfers between devices: 32 us -> 33.7 us  [swap(): return lax.ppermute(array, 'dp', [(i, i ^ mask) for i in range(16)])]
    ppermute x26, starting transfers between devices: 29.3 us -> 28.3 us  [swap(): return lax.ppermute(array, 'dp', [(i, i ^ mask) for i in range(16)])]
  transfers between devices with their start and end apart: 29 -> 29, of which waited for: 14 -> 15; matrix products, arithmetic and copies ran while one was open for 0% -> 1% of each run, Pallas kernels for 17% -> 19%
where the time goes in v4:
time: 95.6 us; the launch traced here: 96 us
  waiting for transfers between devices  37.2 us (39%)
  starting transfers between devices  33 us (35%)
  Pallas kernels  23.5 us (25%)
  local copies, waits for them, and re-layouts  1.07 us (1%)
    ppermute x26, waiting for transfers between devices, swap(): return lax.ppermute(array, 'dp', [(i, i ^ mask) for i in range(16)])  33.7 us
    ppermute x26, starting transfers between devices, swap(): return lax.ppermute(array, 'dp', [(i, i ^ mask) for i in range(16)])  28.3 us
    pallas_call x1, Pallas kernels, on_device_by_heads(): pl.pallas_call(attend_first, out_shape=[row_grad] * (GROUP - 1) + [sorted...  8.36 us
    ppermute x3, starting transfers between devices, swap_tensor(): return lax.ppermute(array, 'tensor', [(0, 1), (1, 0)])  4.73 us
    pallas_call x1, Pallas kernels, on_device_by_heads(): pl.pallas_call(project_keys, out_shape=[shaped((MARKED, 2 * HD))] * GROUP...  4.51 us
    pallas_call x1, Pallas kernels, on_device_by_heads(): pl.pallas_call(attend_last, out_shape=[row_grad, half_sums, half_sums], i...  3.67 us
    ppermute x3, waiting for transfers between devices, swap_tensor(): return lax.ppermute(array, 'tensor', [(0, 1), (1, 0)])  3.53 us
    pallas_call x1, Pallas kernels, on_device_by_heads(): pl.pallas_call(input_grad, out_shape=shaped((ROWS, features // 2)), in_sp...  2.27 us
  transfers between devices with their start and end apart: 29, of which 15 were waited for; matrix products, arithmetic and copies ran while one was open for 1% of the time, Pallas kernels for 19%

profile of v4, /device:TPU:0, one launch (start us, length us, event | category | flops | bytes accessed | tf_op | source)
XLA Modules:
  0.0 96.0 jit_solution(4409610820037409337)
XLA Ops:
  0.7 4.5 %project_keys.1 = (bf16[144,256]{1,0:T(8,128)(2,1)}, bf16[144,256]{1,0:T(8,128)(2,1)}, bf16[144,256]{1,0:T(8,128)(2,1)}, bf16[144,256]{1,0:T(8,128)(2,1)}) custom-call(s32[2]{0:T(128)} %pos_ref.1, bf16[128,4096]{1,0:T(8,128)(2,1)} %inputs_ref.2, bf16[128,512]{1,0:T(8,128)(2,1)} %values_ref.1, bf16[4096,512]{1,0:T(8,128)(2,1)} %w_own.1), custom_call_target="tpu_custom_call" | custom-call | flops 536870912 | bytes 4194304 | tf_op jit(solution)/shard_map/project_keys/pallas_call | solution.py:560
  5.2 3.0 %collective-permute-start = (bf16[144,256]{1,0:T(8,128)(2,1)}, bf16[144,256]{1,0:T(8,128)(2,1)S(1)}, u32[]{:S(2)}, u32[]{:S(2)}) collective-permute-start(bf16[144,256]{1,0:T(8,128)(2,1)} %get-tuple-element.59), channel_id=1, source_target_pairs={{0,4},{2,6},{4,0},{6,2},{8,12},{10,14},{12,8},{14,10},{16,20},{18,... | collective-permute-start | bytes 221192 | tf_op jit(solution)/shard_map/ppermute | solution.py:221
  10.8 3.1 %collective-permute-start.7 = (bf16[288,256]{1,0:T(8,128)(2,1)S(1)}, bf16[288,256]{1,0:T(8,128)(2,1)S(1)}, u32[]{:S(2)}, u32[]{:S(2)}) collective-permute-start(bf16[288,256]{1,0:T(8,128)(2,1)S(1)} %get-tuple-element.113.refs_3_), channel_id=1, source_target_pairs={{0,16},{2,18},{4,20},{6,22},{8,24},{10,26},{12,28},{14,30},{16,0},... | collective-permute-start | bytes 442376 | tf_op jit(solution)/shard_map/ppermute | solution.py:221
  13.9 2.4 %collective-permute-done.3 = bf16[144,256]{1,0:T(8,128)(2,1)S(1)} collective-permute-done((bf16[144,256]{1,0:T(8,128)(2,1)}, bf16[144,256]{1,0:T(8,128)(2,1)S(1)}, u32[]{:S(2)}, u32[]{:S(2)}) %collective-permute-start.3) | collective-permute-done | bytes 73760 | tf_op jit(solution)/shard_map/ppermute | solution.py:221
  16.3 2.3 %pack_weights.1 = bf16[1024,512]{1,0:T(8,128)(2,1)} custom-call(bf16[4096,512]{1,0:T(8,128)(2,1)} %w_own.1), custom_call_target="tpu_custom_call" | custom-call | tf_op jit(solution)/shard_map/pack_weights/pallas_call | solution.py:605
  18.6 1.6 %collective-permute-start.4 = (bf16[1024,512]{1,0:T(8,128)(2,1)}, bf16[1024,512]{1,0:T(8,128)(2,1)S(1)}, u32[]{:S(2)}, u32[]{:S(2)}) collective-permute-start(bf16[1024,512]{1,0:T(8,128)(2,1)} %pack_weights.1), channel_id=1, source_target_pairs={{0,1},{1,0},{2,3},{3,2},{4,5},{5,4},{6,7},{7,6},{8,9},{9,8},{10,11... | collective-permute-start | bytes 3145736 | tf_op jit(solution)/shard_map/ppermute | solution.py:225
  20.2 2.3 %collective-permute-start.8 = (bf16[288,256]{1,0:T(8,128)(2,1)S(1)}, bf16[288,256]{1,0:T(8,128)(2,1)S(1)}, u32[]{:S(2)}, u32[]{:S(2)}) collective-permute-start(bf16[288,256]{1,0:T(8,128)(2,1)S(1)} %get-tuple-element.109.refs_4_), channel_id=1, source_target_pairs={{0,16},{2,18},{4,20},{6,22},{8,24},{10,26},{12,28},{14,30},{16,0},... | collective-permute-start | bytes 442376 | tf_op jit(solution)/shard_map/ppermute | solution.py:221
  23.3 4.0 %collective-permute-done.8.refs_6_ = bf16[288,256]{1,0:T(8,128)(2,1)S(1)} collective-permute-done((bf16[288,256]{1,0:T(8,128)(2,1)S(1)}, bf16[288,256]{1,0:T(8,128)(2,1)S(1)}, u32[]{:S(2)}, u32[]{:S(2)}) %collective-permute-start.8) | collective-permute-done | bytes 147488 | tf_op jit(solution)/shard_map/ppermute | solution.py:221
  28.8 2.0 %collective-permute-done.6.refs_2_ = bf16[128,1024]{1,0:T(8,128)(2,1)S(1)} collective-permute-done((bf16[128,1024]{1,0:T(8,128)(2,1)S(1)}, bf16[128,1024]{1,0:T(8,128)(2,1)S(1)}, u32[]{:S(2)}, u32[]{:S(2)}) %collective-permute-start.6) | collective-permute-done | bytes 262176 | tf_op jit(solution)/shard_map/ppermute | solution.py:221
  31.5 2.3 %collective-permute-start.10 = (bf16[4,128,256]{2,1,0:T(8,128)(2,1)S(1)}, bf16[4,128,256]{2,1,0:T(8,128)(2,1)S(1)}, u32[]{:S(2)}, u32[]{:S(2)}) collective-permute-start(bf16[4,128,256]{2,1,0:T(8,128)(2,1)S(1)} %get-tuple-element.77), channel_id=1, source_target_pairs={{0,16},{2,18},{4,20},{6,22},{8,24},{10,26},{12,28},{14,30},{16,0},... | collective-permute-start | bytes 786440 | tf_op jit(solution)/shard_map/ppermute | solution.py:221
  33.9 8.4 %attend_first.1 = (bf16[128,512]{1,0:T(8,128)(2,1)S(1)}, bf16[128,512]{1,0:T(8,128)(2,1)S(1)}, bf16[128,512]{1,0:T(8,128)(2,1)S(1)}, bf16[2048,128]{1,0:T(8,128)...) custom-call(s32[4]{0:T(128)S(1)} %copy-done.4, ...), custom_call_target="tpu_custom_call" | custom-call | flops 1048576 | tf_op jit(solution)/shard_map/attend_first/pallas_call | solution.py:637
  43.3 2.2 %collective-permute-done.1.row_ref = bf16[128,1024]{1,0:T(8,128)(2,1)S(1)} collective-permute-done((bf16[128,1024]{1,0:T(8,128)(2,1)S(1)}, bf16[128,1024]{1,0:T(8,128)(2,1)S(1)}, u32[]{:S(2)}, u32[]{:S(2)}) %collective-permute-start.1) | collective-permute-done | bytes 262176 | tf_op jit(solution)/shard_map/ppermute | solution.py:221
  45.5 3.7 %attend_last.1 = (bf16[128,512]{1,0:T(8,128)(2,1)S(1)}, f32[1024,256]{1,0:T(8,128)S(1)}, f32[1024,256]{1,0:T(8,128)S(1)}) custom-call(s32[4]{0:T(128)S(1)} %copy-done.4, bf16[128,1024]{1,0:T(8,128)(2,1)S(1)} %collective-permute-done.1.row_ref, bf16[2048,128]{1,0:T(8,128)(2,1)S(1)} %get-tuple-element.70.keys, bf16[128,2048]{1,0:T(8,128)(2,1)S(1)} %get-tuple-element.71.keys_t, ...), custom_call_target="tpu_custom_call" | custom-call | flops 1048576 | tf_op jit(solution)/shard_map/attend_last/pallas_call | solution.py:649
  51.0 2.4 %collective-permute-start.15 = (bf16[2,128,256]{2,1,0:T(8,128)(2,1)S(1)}, bf16[2,128,256]{2,1,0:T(8,128)(2,1)S(1)}, u32[]{:S(2)}, u32[]{:S(2)}) collective-permute-start(bf16[2,128,256]{2,1,0:T(8,128)(2,1)S(1)} %get-tuple-element.86), channel_id=1, source_target_pairs={{0,12},{2,14},{4,8},{6,10},{8,4},{10,6},{12,0},{14,2},{16,28},{18,... | collective-permute-start | bytes 393224 | tf_op jit(solution)/shard_map/ppermute | solution.py:221
  55.4 5.9 %collective-permute-done.14.refs_2_ = bf16[2,128,256]{2,1,0:T(8,128)(2,1)S(1)} collective-permute-done((bf16[2,128,256]{2,1,0:T(8,128)(2,1)S(1)}, bf16[2,128,256]{2,1,0:T(8,128)(2,1)S(1)}, u32[]{:S(2)}, u32[]{:S(2)}) %collective-permute-start.14) | collective-permute-done | bytes 131104 | tf_op jit(solution)/shard_map/ppermute | solution.py:221
  63.6 4.1 %collective-permute-done.18 = bf16[1024,128]{1,0:T(8,128)(2,1)S(1)} collective-permute-done((bf16[1024,128]{1,0:T(8,128)(2,1)S(1)}, bf16[1024,128]{1,0:T(8,128)(2,1)S(1)}, u32[]{:S(2)}, u32[]{:S(2)}) %collective-permute-start.18) | collective-permute-done | bytes 262176 | tf_op jit(solution)/shard_map/ppermute | solution.py:221
  68.5 1.9 %collective-permute-start.21 = (bf16[1024,128]{1,0:T(8,128)(2,1)S(1)}, bf16[1024,128]{1,0:T(8,128)(2,1)S(1)}, u32[]{:S(2)}, u32[]{:S(2)}) collective-permute-start(bf16[1024,128]{1,0:T(8,128)(2,1)S(1)} %add_convert_fusion.refs_0_), channel_id=1, source_target_pairs={{0,8},{2,10},{4,12},{6,14},{8,0},{10,2},{12,4},{14,6},{16,24},{18,... | collective-permute-start | bytes 786440 | tf_op jit(solution)/shard_map/ppermute | solution.py:221
  72.6 3.0 %collective-permute-done.16.other_ref = bf16[256,1024]{1,0:T(8,128)(2,1)S(1)} collective-permute-done((bf16[256,1024]{1,0:T(8,128)(2,1)S(1)}, bf16[256,1024]{1,0:T(8,128)(2,1)S(1)}, u32[]{:S(2)}, u32[]{:S(2)}) %collective-permute-start.16) | collective-permute-done | bytes 524320 | tf_op jit(solution)/shard_map/ppermute | solution.py:225
  75.6 4.0 %collective-permute-done.22.refs_3_ = bf16[1024,128]{1,0:T(8,128)(2,1)S(1)} collective-permute-done((bf16[1024,128]{1,0:T(8,128)(2,1)S(1)}, bf16[1024,128]{1,0:T(8,128)(2,1)S(1)}, u32[]{:S(2)}, u32[]{:S(2)}) %collective-permute-start.22) | collective-permute-done | bytes 262176 | tf_op jit(solution)/shard_map/ppermute | solution.py:221
  79.6 3.8 %collective-permute-done.21.refs_2_ = bf16[1024,128]{1,0:T(8,128)(2,1)S(1)} collective-permute-done((bf16[1024,128]{1,0:T(8,128)(2,1)S(1)}, bf16[1024,128]{1,0:T(8,128)(2,1)S(1)}, u32[]{:S(2)}, u32[]{:S(2)}) %collective-permute-start.21) | collective-permute-done | bytes 262176 | tf_op jit(solution)/shard_map/ppermute | solution.py:221
  84.5 2.4 %collective-permute-start.28 = (bf16[4,128,128]{2,1,0:T(8,128)(2,1)S(1)}, bf16[4,128,128]{2,1,0:T(8,128)(2,1)S(1)}, u32[]{:S(2)}, u32[]{:S(2)}) collective-permute-start(bf16[4,128,128]{2,1,0:T(8,128)(2,1)S(1)} %pad_maximum_fusion.own_ref), channel_id=1, source_target_pairs={{0,1},{1,0},{2,3},{3,2},{4,5},{5,4},{6,7},{7,6},{8,9},{9,8},{10,11... | collective-permute-start | bytes 393224 | tf_op jit(solution)/shard_map/ppermute | solution.py:225
  87.0 1.9 %collective-permute-start.26 = (bf16[128,128]{1,0:T(8,128)(2,1)S(1)}, bf16[128,128]{1,0:T(8,128)(2,1)S(1)}, u32[]{:S(2)}, u32[]{:S(2)}) collective-permute-start(bf16[128,128]{1,0:T(8,128)(2,1)S(1)} %get-tuple-element.99), channel_id=1, source_target_pairs={{0,8},{2,10},{4,12},{6,14},{8,0},{10,2},{12,4},{14,6},{16,24},{18,... | collective-permute-start | bytes 98312 | tf_op jit(solution)/shard_map/ppermute | solution.py:221
  88.9 1.6 %collective-permute-start.25 = (bf16[128,128]{1,0:T(8,128)(2,1)S(1)}, bf16[128,128]{1,0:T(8,128)(2,1)S(1)}, u32[]{:S(2)}, u32[]{:S(2)}) collective-permute-start(bf16[128,128]{1,0:T(8,128)(2,1)S(1)} %get-tuple-element.97), channel_id=1, source_target_pairs={{0,4},{2,6},{4,0},{6,2},{8,12},{10,14},{12,8},{14,10},{16,20},{18,... | collective-permute-start | bytes 98312 | tf_op jit(solution)/shard_map/ppermute | solution.py:221
  91.0 2.3 %input_grad.1 = bf16[128,2048]{1,0:T(8,128)(2,1)} custom-call(bf16[4,128,128]{2,1,0:T(8,128)(2,1)S(1)} %pad_maximum_fusion.own_ref, bf16[4,128,128]{2,1,0:T(8,128)(2,1)S(1)} %collective-permute-done.28.other_ref, bf16[4096,512]{1,0:T(8,128)(2,1)S(1)} %copy-done, bf16[1024,512]{1,0:T(8,128)(2,1)S(1)} %collective-permute-done.4.w_near, ...), custom_call_target="tpu_custom_call" | custom-call | flops 536870912 | bytes 5242880 | tf_op jit(solution)/shard_map/input_grad/pallas_call | solution.py:721
  (73 shorter events, 20.2 us)
Async XLA Ops:
  9.8 6.5 %collective-permute-start.3 = (bf16[144,256]{1,0:T(8,128)(2,1)}, bf16[144,256]{1,0:T(8,128)(2,1)S(1)}, u32[]{:S(2)}, u32[]{:S(2)}) collective-permute-start(bf16[144,256]{1,0:T(8,128)(2,1)} %get-tuple-element.64), channel_id=1, source_target_pairs={{0,12},{2,14},{4,8},{6,10},{8,4},{10,6},{12,0},{14,2},{16,28},{18,... | collective-permute-start | bytes 221192 | tf_op jit(solution)/shard_map/ppermute | solution.py:221
  10.8 12.5 %collective-permute-start.7 = (bf16[288,256]{1,0:T(8,128)(2,1)S(1)}, bf16[288,256]{1,0:T(8,128)(2,1)S(1)}, u32[]{:S(2)}, u32[]{:S(2)}) collective-permute-start(bf16[288,256]{1,0:T(8,128)(2,1)S(1)} %get-tuple-element.113.refs_3_), channel_id=1, source_target_pairs={{0,16},{2,18},{4,20},{6,22},{8,24},{10,26},{12,28},{14,30},{16,0},... | collective-permute-start | bytes 442376 | tf_op jit(solution)/shard_map/ppermute | solution.py:221
  18.6 27.0 %collective-permute-start.4 = (bf16[1024,512]{1,0:T(8,128)(2,1)}, bf16[1024,512]{1,0:T(8,128)(2,1)S(1)}, u32[]{:S(2)}, u32[]{:S(2)}) collective-permute-start(bf16[1024,512]{1,0:T(8,128)(2,1)} %pack_weights.1), channel_id=1, source_target_pairs={{0,1},{1,0},{2,3},{3,2},{4,5},{5,4},{6,7},{7,6},{8,9},{9,8},{10,11... | collective-permute-start | bytes 3145736 | tf_op jit(solution)/shard_map/ppermute | solution.py:225
  20.2 7.1 %collective-permute-start.8 = (bf16[288,256]{1,0:T(8,128)(2,1)S(1)}, bf16[288,256]{1,0:T(8,128)(2,1)S(1)}, u32[]{:S(2)}, u32[]{:S(2)}) collective-permute-start(bf16[288,256]{1,0:T(8,128)(2,1)S(1)} %get-tuple-element.109.refs_4_), channel_id=1, source_target_pairs={{0,16},{2,18},{4,20},{6,22},{8,24},{10,26},{12,28},{14,30},{16,0},... | collective-permute-start | bytes 442376 | tf_op jit(solution)/shard_map/ppermute | solution.py:221
  22.4 6.4 %collective-permute-start.5 = (bf16[128,1024]{1,0:T(8,128)(2,1)S(1)}, bf16[128,1024]{1,0:T(8,128)(2,1)S(1)}, u32[]{:S(2)}, u32[]{:S(2)}) collective-permute-start(bf16[128,1024]{1,0:T(8,128)(2,1)S(1)} %get-tuple-element.67), channel_id=1, source_target_pairs={{0,4},{2,6},{4,0},{6,2},{8,12},{10,14},{12,8},{14,10},{16,20},{18,... | collective-permute-start | bytes 786440 | tf_op jit(solution)/shard_map/ppermute | solution.py:221
  23.0 7.7 %collective-permute-start.6 = (bf16[128,1024]{1,0:T(8,128)(2,1)S(1)}, bf16[128,1024]{1,0:T(8,128)(2,1)S(1)}, u32[]{:S(2)}, u32[]{:S(2)}) collective-permute-start(bf16[128,1024]{1,0:T(8,128)(2,1)S(1)} %get-tuple-element.68), channel_id=1, source_target_pairs={{0,8},{2,10},{4,12},{6,14},{8,0},{10,2},{12,4},{14,6},{16,24},{18,... | collective-permute-start | bytes 786440 | tf_op jit(solution)/shard_map/ppermute | solution.py:221
  30.8 14.8 %collective-permute-start.1 = (bf16[128,1024]{1,0:T(8,128)(2,1)S(1)}, bf16[128,1024]{1,0:T(8,128)(2,1)S(1)}, u32[]{:S(2)}, u32[]{:S(2)}) collective-permute-start(bf16[128,1024]{1,0:T(8,128)(2,1)S(1)} %get-tuple-element.62), channel_id=1, source_target_pairs={{0,12},{2,14},{4,8},{6,10},{8,4},{10,6},{12,0},{14,2},{16,28},{18,... | collective-permute-start | bytes 786440 | tf_op jit(solution)/shard_map/ppermute | solution.py:221
  31.5 17.7 %collective-permute-start.10 = (bf16[4,128,256]{2,1,0:T(8,128)(2,1)S(1)}, bf16[4,128,256]{2,1,0:T(8,128)(2,1)S(1)}, u32[]{:S(2)}, u32[]{:S(2)}) collective-permute-start(bf16[4,128,256]{2,1,0:T(8,128)(2,1)S(1)} %get-tuple-element.77), channel_id=1, source_target_pairs={{0,16},{2,18},{4,20},{6,22},{8,24},{10,26},{12,28},{14,30},{16,0},... | collective-permute-start | bytes 786440 | tf_op jit(solution)/shard_map/ppermute | solution.py:221
  42.2 7.0 %collective-permute-start.11 = (bf16[128,512]{1,0:T(8,128)(2,1)S(1)}, bf16[128,512]{1,0:T(8,128)(2,1)S(1)}, u32[]{:S(2)}, u32[]{:S(2)}) collective-permute-start(bf16[128,512]{1,0:T(8,128)(2,1)S(1)} %get-tuple-element.79), channel_id=1, source_target_pairs={{0,4},{2,6},{4,0},{6,2},{8,12},{10,14},{12,8},{14,10},{16,20},{18,... | collective-permute-start | bytes 393224 | tf_op jit(solution)/shard_map/ppermute | solution.py:221
  42.3 6.9 %collective-permute-start.12 = (bf16[128,512]{1,0:T(8,128)(2,1)S(1)}, bf16[128,512]{1,0:T(8,128)(2,1)S(1)}, u32[]{:S(2)}, u32[]{:S(2)}) collective-permute-start(bf16[128,512]{1,0:T(8,128)(2,1)S(1)} %get-tuple-element.80), channel_id=1, source_target_pairs={{0,8},{2,10},{4,12},{6,14},{8,0},{10,2},{12,4},{14,6},{16,24},{18,... | collective-permute-start | bytes 393224 | tf_op jit(solution)/shard_map/ppermute | solution.py:221
  49.3 18.4 %collective-permute-start.19 = (bf16[1024,512]{1,0:T(8,128)(2,1)S(1)}, bf16[1024,512]{1,0:T(8,128)(2,1)S(1)}, u32[]{:S(2)}, u32[]{:S(2)}) collective-permute-start(bf16[1024,512]{1,0:T(8,128)(2,1)S(1)} %collective-permute-done.4.w_near), channel_id=1, source_target_pairs={{0,2},{2,0},{4,6},{6,4},{8,10},{10,8},{12,14},{14,12},{16,18},{18,... | collective-permute-start | bytes 3145736 | tf_op jit(solution)/shard_map/ppermute | solution.py:221
  51.0 10.3 %collective-permute-start.14 = (bf16[2,128,256]{2,1,0:T(8,128)(2,1)S(1)}, bf16[2,128,256]{2,1,0:T(8,128)(2,1)S(1)}, u32[]{:S(2)}, u32[]{:S(2)}) collective-permute-start(bf16[2,128,256]{2,1,0:T(8,128)(2,1)S(1)} %get-tuple-element.85), channel_id=1, source_target_pairs={{0,8},{2,10},{4,12},{6,14},{8,0},{10,2},{12,4},{14,6},{16,24},{18,... | collective-permute-start | bytes 393224 | tf_op jit(solution)/shard_map/ppermute | solution.py:221
  51.0 11.6 %collective-permute-start.15 = (bf16[2,128,256]{2,1,0:T(8,128)(2,1)S(1)}, bf16[2,128,256]{2,1,0:T(8,128)(2,1)S(1)}, u32[]{:S(2)}, u32[]{:S(2)}) collective-permute-start(bf16[2,128,256]{2,1,0:T(8,128)(2,1)S(1)} %get-tuple-element.86), channel_id=1, source_target_pairs={{0,12},{2,14},{4,8},{6,10},{8,4},{10,6},{12,0},{14,2},{16,28},{18,... | collective-permute-start | bytes 393224 | tf_op jit(solution)/shard_map/ppermute | solution.py:221
  53.6 14.1 %collective-permute-start.18 = (bf16[1024,128]{1,0:T(8,128)(2,1)S(1)}, bf16[1024,128]{1,0:T(8,128)(2,1)S(1)}, u32[]{:S(2)}, u32[]{:S(2)}) collective-permute-start(bf16[1024,128]{1,0:T(8,128)(2,1)S(1)} %slice.59), channel_id=1, source_target_pairs={{0,16},{2,18},{4,20},{6,22},{8,24},{10,26},{12,28},{14,30},{16,0},... | collective-permute-start | bytes 786440 | tf_op jit(solution)/shard_map/ppermute | solution.py:221
  62.8 12.8 %collective-permute-start.16 = (bf16[256,1024]{1,0:T(8,128)(2,1)S(1)}, bf16[256,1024]{1,0:T(8,128)(2,1)S(1)}, u32[]{:S(2)}, u32[]{:S(2)}) collective-permute-start(bf16[256,1024]{1,0:T(8,128)(2,1)S(1)} %turn_features.1.own_ref), channel_id=1, source_target_pairs={{0,1},{1,0},{2,3},{3,2},{4,5},{5,4},{6,7},{7,6},{8,9},{9,8},{10,11... | collective-permute-start | bytes 1572872 | tf_op jit(solution)/shard_map/ppermute | solution.py:225
  67.8 11.8 %collective-permute-start.22 = (bf16[1024,128]{1,0:T(8,128)(2,1)S(1)}, bf16[1024,128]{1,0:T(8,128)(2,1)S(1)}, u32[]{:S(2)}, u32[]{:S(2)}) collective-permute-start(bf16[1024,128]{1,0:T(8,128)(2,1)S(1)} %add_convert_fusion.refs_0_), channel_id=1, source_target_pairs={{0,12},{2,14},{4,8},{6,10},{8,4},{10,6},{12,0},{14,2},{16,28},{18,... | collective-permute-start | bytes 786440 | tf_op jit(solution)/shard_map/ppermute | solution.py:221
  68.5 14.9 %collective-permute-start.21 = (bf16[1024,128]{1,0:T(8,128)(2,1)S(1)}, bf16[1024,128]{1,0:T(8,128)(2,1)S(1)}, u32[]{:S(2)}, u32[]{:S(2)}) collective-permute-start(bf16[1024,128]{1,0:T(8,128)(2,1)S(1)} %add_convert_fusion.refs_0_), channel_id=1, source_target_pairs={{0,8},{2,10},{4,12},{6,14},{8,0},{10,2},{12,4},{14,6},{16,24},{18,... | collective-permute-start | bytes 786440 | tf_op jit(solution)/shard_map/ppermute | solution.py:221
  70.4 13.0 %collective-permute-start.20 = (bf16[1024,128]{1,0:T(8,128)(2,1)S(1)}, bf16[1024,128]{1,0:T(8,128)(2,1)S(1)}, u32[]{:S(2)}, u32[]{:S(2)}) collective-permute-start(bf16[1024,128]{1,0:T(8,128)(2,1)S(1)} %add_convert_fusion.refs_0_), channel_id=1, source_target_pairs={{0,4},{2,6},{4,0},{6,2},{8,12},{10,14},{12,8},{14,10},{16,20},{18,... | collective-permute-start | bytes 786440 | tf_op jit(solution)/shard_map/ppermute | solution.py:221
  71.4 15.5 %collective-permute-start.24 = (bf16[512,128]{1,0:T(8,128)(2,1)S(1)}, bf16[512,128]{1,0:T(8,128)(2,1)S(1)}, u32[]{:S(2)}, u32[]{:S(2)}) collective-permute-start(bf16[512,128]{1,0:T(8,128)(2,1)S(1)} %slice.58), channel_id=1, source_target_pairs={{0,16},{2,18},{4,20},{6,22},{8,24},{10,26},{12,28},{14,30},{16,0},... | collective-permute-start | bytes 393224 | tf_op jit(solution)/shard_map/ppermute | solution.py:221
  84.3 10.6 %collective-permute-start.23 = (f32[256,512]{1,0:T(8,128)S(1)}, f32[256,512]{1,0:T(8,128)S(1)}, u32[]{:S(2)}, u32[]{:S(2)}) collective-permute-start(f32[256,512]{1,0:T(8,128)S(1)} %get-tuple-element.91), channel_id=1, source_target_pairs={{0,2},{2,0},{4,6},{6,4},{8,10},{10,8},{12,14},{14,12},{16,18},{18,... | collective-permute-start | bytes 1572872 | tf_op jit(solution)/shard_map/ppermute | solution.py:221
  84.5 6.5 %collective-permute-start.28 = (bf16[4,128,128]{2,1,0:T(8,128)(2,1)S(1)}, bf16[4,128,128]{2,1,0:T(8,128)(2,1)S(1)}, u32[]{:S(2)}, u32[]{:S(2)}) collective-permute-start(bf16[4,128,128]{2,1,0:T(8,128)(2,1)S(1)} %pad_maximum_fusion.own_ref), channel_id=1, source_target_pairs={{0,1},{1,0},{2,3},{3,2},{4,5},{5,4},{6,7},{7,6},{8,9},{9,8},{10,11... | collective-permute-start | bytes 393224 | tf_op jit(solution)/shard_map/ppermute | solution.py:225
  86.9 8.0 %collective-permute-start.27 = (bf16[128,640]{1,0:T(8,128)(2,1)S(1)}, bf16[128,640]{1,0:T(8,128)(2,1)S(1)}, u32[]{:S(2)}, u32[]{:S(2)}) collective-permute-start(bf16[128,640]{1,0:T(8,128)(2,1)S(1)} %get-tuple-element.101), channel_id=1, source_target_pairs={{0,12},{2,14},{4,8},{6,10},{8,4},{10,6},{12,0},{14,2},{16,28},{18,... | collective-permute-start | bytes 491528 | tf_op jit(solution)/shard_map/ppermute | solution.py:221
  87.0 6.8 %collective-permute-start.26 = (bf16[128,128]{1,0:T(8,128)(2,1)S(1)}, bf16[128,128]{1,0:T(8,128)(2,1)S(1)}, u32[]{:S(2)}, u32[]{:S(2)}) collective-permute-start(bf16[128,128]{1,0:T(8,128)(2,1)S(1)} %get-tuple-element.99), channel_id=1, source_target_pairs={{0,8},{2,10},{4,12},{6,14},{8,0},{10,2},{12,4},{14,6},{16,24},{18,... | collective-permute-start | bytes 98312 | tf_op jit(solution)/shard_map/ppermute | solution.py:221
  88.9 6.0 %collective-permute-start.25 = (bf16[128,128]{1,0:T(8,128)(2,1)S(1)}, bf16[128,128]{1,0:T(8,128)(2,1)S(1)}, u32[]{:S(2)}, u32[]{:S(2)}) collective-permute-start(bf16[128,128]{1,0:T(8,128)(2,1)S(1)} %get-tuple-element.97), channel_id=1, source_target_pairs={{0,4},{2,6},{4,0},{6,2},{8,12},{10,14},{12,8},{14,10},{16,20},{18,... | collective-permute-start | bytes 98312 | tf_op jit(solution)/shard_map/ppermute | solution.py:221
  (10 other events, 112.7 us)

commit v5 on v4

--- a/solution.py
+++ b/solution.py
@@ -207,7 +207,7 @@
 ROWS = 128
 TILE = 256
 UNROLLED = 5
-ATTEND_COST = 1 << 20
+ATTEND_COST = 4_000_000_000
 PART = 512
 MARKED = ROWS + 16
 Q_BLOCKS = GROUP * ROWS // BLK
@@ -483,14 +483,14 @@
 
 
 def weight_grad(own_ref, other_ref, *refs):
-    grad_refs, (keep_ref, send_ref, grads) = refs[:GROUP], refs[GROUP:]
+    near_refs, far_refs = refs[:GROUP], refs[GROUP : 2 * GROUP]
+    keep_ref, send_ref, grads = refs[2 * GROUP :]
     head = own_head()
-    for k, grad_ref in enumerate(grad_refs):
-        for far in range(2):
+    for k in range(GROUP):
+        for far, grad_ref in enumerate((near_refs[k], far_refs[k])):
             for m in range(GROUP):
                 here = pl.ds((far * GROUP + m) * ROWS, ROWS)
-                there = pl.ds((far * GROUP + (m ^ k)) * ROWS, ROWS)
-                grads[here, columns(head ^ k, HD)] = grad_ref[there]
+                grads[here, columns(head ^ k, HD)] = grad_ref[pl.ds((m ^ k) * ROWS, ROWS)]
     own = jnp.dot(own_ref[...], grads[...], preferred_element_type=jnp.float32)
     other = jnp.dot(other_ref[...], grads[...], preferred_element_type=jnp.float32)
     crossed = (lax.axis_index("dp") & 1) ^ lax.axis_index("tensor")
@@ -521,21 +521,16 @@
         out_ref[:, columns(chunk, PART)] = part.astype(jnp.bfloat16)
 
 
-def pack_grads(value_ref, row_ref, *refs):
-    for m, out_ref in enumerate(refs):
-        out_ref[:, :HD] = value_ref[m * ROWS : (m + 1) * ROWS]
-    refs[-1][:, HD:] = row_ref[...]
+def place_rows(*refs):
+    for m, ref in enumerate(refs[:GROUP]):
+        refs[GROUP][:, columns(own_head() ^ m, GROUP * HD)] = ref[...]
 
 
 def finish(keep_ref, arrived_ref, *refs):
-    row_refs, grad_refs, refs = refs[: GROUP - 1], refs[GROUP - 1 : 2 * GROUP - 1], refs[2 * GROUP - 1 :]
-    weight_out, query_out, value_out = refs
-    head = own_head()
+    value_refs, (weight_out, value_out) = refs[:GROUP], refs[GROUP:]
     weight_out[...] = keep_ref[...] + arrived_ref[...]
     for m in range(GROUP):
-        row = row_refs[m][...] if m < GROUP - 1 else grad_refs[m][:, HD:]
-        query_out[:, columns(head ^ m, GROUP * HD)] = row
-        value_out[:, columns(head ^ m, HD)] = grad_refs[m][:, :HD]
+        value_out[:, columns(own_head() ^ m, HD)] = value_refs[m][...]
 
 
 def shaped(shape, dtype=jnp.bfloat16):
@@ -662,7 +657,6 @@
     grads = kept + swap(sent, CORE)
     dk_sum, dv_sum = grads[:, :HD], grads[:, HD:]
     dk_far = swap(dk_sum.astype(jnp.bfloat16), Z_HI)
-    w_far = swap(after(w_near, dk_sum), CORE)
 
     feature_parts = pl.pallas_call(
         join_features,
@@ -672,42 +666,50 @@
         compiler_params=limits(16),
         name="join_features",
     )(after(near_features, sent), far_features)
+    feature_parts = with_partners(feature_parts)
     own_features = pl.pallas_call(
         turn_features,
         out_shape=shaped((256, half)),
         in_specs=[vmem] * GROUP,
         out_specs=vmem,
         compiler_params=limits(16),
-        cost_estimate=pl.CostEstimate(flops=4_000_000_000, bytes_accessed=0, transcendentals=0),
+        cost_estimate=pl.CostEstimate(flops=1_000_000, bytes_accessed=0, transcendentals=0),
         name="turn_features",
-    )(*with_partners(feature_parts))
+    )(after(feature_parts[0], dk_sum), *feature_parts[1:])
     other_features = swap_tensor(own_features)
+    w_far = swap(after(w_near, dk_sum), CORE)
 
     dk_far = jnp.concatenate([dk_far[quarter:], dk_far[:quarter]], axis=0)
     key_grad = (dk_sum + dk_far.astype(jnp.float32)).astype(jnp.bfloat16)
-    key_grad = after(key_grad, own_features, w_far)
-    key_grads = with_partners([key_grad] * GROUP)
-    own_key_grad = jnp.stack([key_grads[m][m * ROWS : (m + 1) * ROWS] for m in range(GROUP)])
-    other_key_grad = swap_tensor(own_key_grad)
-
+    last_back = swap(after(last_grad, dk_sum), 6)
+    key_grad = after(key_grad, own_features, w_far, last_back)
+    from_x, from_z = swap(key_grad, 2), swap(key_grad, 4)
     dv_far = swap(after(dv_sum[quarter:].astype(jnp.bfloat16), key_grad), Z_HI)
     value_grad = (dv_sum[:quarter] + dv_far.astype(jnp.float32)).astype(jnp.bfloat16)
-    packed_grads = pl.pallas_call(
-        pack_grads,
-        out_shape=[shaped((ROWS, HD))] * (GROUP - 1) + [shaped((ROWS, (GROUP + 1) * HD))],
-        in_specs=[vmem] * 2,
-        out_specs=[vmem] * GROUP,
-        compiler_params=limits(16),
-        name="pack_grads",
-    )(value_grad, last_grad)
-    packed_grads = [after(packed_grads[0], own_key_grad)] + [
-        after(grad, own_key_grad) for grad in packed_grads[1:]
-    ]
-
+    from_x = after(from_x, value_grad)
+    from_z = after(from_z, value_grad)
+    near_grads = [part[:quarter] for part in (key_grad, from_x, from_z)]
+    far_grads = [part[quarter:] for part in (key_grad, from_x, from_z)]
+    value_grads = with_partners([
+        after(value_grad[m * ROWS : (m + 1) * ROWS], from_x, from_z) for m in range(GROUP)
+    ])
+    near_grads.append(swap(near_grads[2], 2))
+    far_grads.append(swap(far_grads[1], 4))
+    own_key_grad = jnp.stack([near_grads[m][m * ROWS : (m + 1) * ROWS] for m in range(GROUP)])
+    other_key_grad = swap_tensor(own_key_grad)
+
+    d_query = pl.pallas_call(
+        place_rows,
+        out_shape=shaped(queries.shape),
+        in_specs=[vmem] * GROUP,
+        out_specs=vmem,
+        compiler_params=limits(8),
+        name="place_rows",
+    )(*row_grads, last_back)
     keep, send = pl.pallas_call(
         weight_grad,
         out_shape=[shaped((256, kv_columns), jnp.float32)] * 2,
-        in_specs=[vmem] * (2 + GROUP),
+        in_specs=[vmem] * (2 + 2 * GROUP),
         out_specs=[vmem] * 2,
         scratch_shapes=[VMEM((half, kv_columns), jnp.bfloat16)],
         compiler_params=limits(24),
@@ -715,7 +717,7 @@
             flops=4 * 256 * half * kv_columns, bytes_accessed=4 << 20, transcendentals=0
         ),
         name="weight_grad",
-    )(own_features, other_features, *key_grads)
+    )(after(own_features, d_query, *value_grads), other_features, *near_grads, *far_grads)
     arrived = swap(send, CORE)
 
     d_input = pl.pallas_call(
@@ -731,18 +733,14 @@
         name="input_grad",
     )(after(own_key_grad, send), other_key_grad, w_key, w_near, w_far)
 
-    d_wkey, d_query, d_value = pl.pallas_call(
+    d_wkey, d_value = pl.pallas_call(
         finish,
-        out_shape=[
-            shaped((256, kv_columns), jnp.float32),
-            shaped(queries.shape),
-            shaped(values.shape),
-        ],
-        in_specs=[vmem] * (1 + 2 * GROUP),
-        out_specs=[vmem] * 3,
+        out_shape=[shaped((256, kv_columns), jnp.float32), shaped(values.shape)],
+        in_specs=[vmem] * (2 + GROUP),
+        out_specs=[vmem] * 2,
         compiler_params=limits(16),
         name="finish",
-    )(keep, arrived, *row_grads, *with_partners(packed_grads))
+    )(keep, arrived, *value_grads)
     return (d_query, d_value, d_input, d_wkey)
 
 

time: 95.6 us -> 102 us (1.067)
  starting transfers between devices: 33 us -> 38.4 us
    ppermute x26 -> x28, starting transfers between devices: 28.3 us -> 33.6 us  [swap(): return lax.ppermute(array, 'dp', [(i, i ^ mask) for i in range(16)])]
    ppermute x3, waiting for transfers between devices: 3.53 us -> 5.41 us  [swap_tensor(): return lax.ppermute(array, 'tensor', [(0, 1), (1, 0)])]
    ppermute x26 -> x28, waiting for transfers between devices: 33.7 us -> 32.1 us  [swap(): return lax.ppermute(array, 'dp', [(i, i ^ mask) for i in range(16)])]
  transfers between devices with their start and end apart: 29 -> 31, of which waited for: 15 -> 17; matrix products, arithmetic and copies ran while one was open for 1% -> 1% of each run, Pallas kernels for 19% -> 17%
where the time goes in v5:
time: 102 us
  starting transfers between devices  38.4 us (38%)
  waiting for transfers between devices  37.5 us (37%)
  Pallas kernels  24 us (24%)
  local copies, waits for them, and re-layouts  1.13 us (1%)
    ppermute x28, starting transfers between devices, swap(): return lax.ppermute(array, 'dp', [(i, i ^ mask) for i in range(16)])  33.6 us
    ppermute x28, waiting for transfers between devices, swap(): return lax.ppermute(array, 'dp', [(i, i ^ mask) for i in range(16)])  32.1 us
    pallas_call x1, Pallas kernels, on_device_by_heads(): pl.pallas_call(attend_first, out_shape=[row_grad] * (GROUP - 1) + [sorted...  8.43 us
    ppermute x3, waiting for transfers between devices, swap_tensor(): return lax.ppermute(array, 'tensor', [(0, 1), (1, 0)])  5.41 us
    ppermute x3, starting transfers between devices, swap_tensor(): return lax.ppermute(array, 'tensor', [(0, 1), (1, 0)])  4.79 us
    pallas_call x1, Pallas kernels, on_device_by_heads(): pl.pallas_call(project_keys, out_shape=[shaped((MARKED, 2 * HD))] * GROUP...  4.57 us
    pallas_call x1, Pallas kernels, on_device_by_heads(): pl.pallas_call(attend_last, out_shape=[row_grad, half_sums, half_sums], i...  3.46 us
    pallas_call x1, Pallas kernels, on_device_by_heads(): pl.pallas_call(input_grad, out_shape=shaped((ROWS, features // 2)), in_sp...  2.27 us
  transfers between devices with their start and end apart: 31, of which 17 were waited for; matrix products, arithmetic and copies ran while one was open for 1% of the time, Pallas kernels for 17%

profile of v5, /device:TPU:0, one launch (start us, length us, event | category | flops | bytes accessed | tf_op | source)
XLA Modules:
  0.0 102.2 jit_solution(17493264462082071661)
XLA Ops:
  0.7 4.6 %project_keys.1 = (bf16[144,256]{1,0:T(8,128)(2,1)}, bf16[144,256]{1,0:T(8,128)(2,1)}, bf16[144,256]{1,0:T(8,128)(2,1)}, bf16[144,256]{1,0:T(8,128)(2,1)}) custom-call(s32[2]{0:T(128)} %pos_ref.1, bf16[128,4096]{1,0:T(8,128)(2,1)} %inputs_ref.2, bf16[128,512]{1,0:T(8,128)(2,1)} %values_ref.1, bf16[4096,512]{1,0:T(8,128)(2,1)} %w_own.1), custom_call_target="tpu_custom_call" | custom-call | flops 536870912 | bytes 4194304 | tf_op jit(solution)/shard_map/project_keys/pallas_call | solution.py:555
  5.2 3.0 %collective-permute-start.2 = (bf16[144,256]{1,0:T(8,128)(2,1)}, bf16[144,256]{1,0:T(8,128)(2,1)S(1)}, u32[]{:S(2)}, u32[]{:S(2)}) collective-permute-start(bf16[144,256]{1,0:T(8,128)(2,1)} %get-tuple-element.61), channel_id=1, source_target_pairs={{0,4},{2,6},{4,0},{6,2},{8,12},{10,14},{12,8},{14,10},{16,20},{18,... | collective-permute-start | bytes 221192 | tf_op jit(solution)/shard_map/ppermute | solution.py:221
  10.9 3.1 %collective-permute-start.5 = (bf16[288,256]{1,0:T(8,128)(2,1)S(1)}, bf16[288,256]{1,0:T(8,128)(2,1)S(1)}, u32[]{:S(2)}, u32[]{:S(2)}) collective-permute-start(bf16[288,256]{1,0:T(8,128)(2,1)S(1)} %get-tuple-element.125.refs_3_), channel_id=1, source_target_pairs={{0,16},{2,18},{4,20},{6,22},{8,24},{10,26},{12,28},{14,30},{16,0},... | collective-permute-start | bytes 442376 | tf_op jit(solution)/shard_map/ppermute | solution.py:221
  14.0 2.4 %collective-permute-done.4 = bf16[144,256]{1,0:T(8,128)(2,1)S(1)} collective-permute-done((bf16[144,256]{1,0:T(8,128)(2,1)}, bf16[144,256]{1,0:T(8,128)(2,1)S(1)}, u32[]{:S(2)}, u32[]{:S(2)}) %collective-permute-start.4) | collective-permute-done | bytes 73760 | tf_op jit(solution)/shard_map/ppermute | solution.py:221
  16.4 2.3 %collective-permute-start.6 = (bf16[288,256]{1,0:T(8,128)(2,1)S(1)}, bf16[288,256]{1,0:T(8,128)(2,1)S(1)}, u32[]{:S(2)}, u32[]{:S(2)}) collective-permute-start(bf16[288,256]{1,0:T(8,128)(2,1)S(1)} %get-tuple-element.121.refs_4_), channel_id=1, source_target_pairs={{0,16},{2,18},{4,20},{6,22},{8,24},{10,26},{12,28},{14,30},{16,0},... | collective-permute-start | bytes 442376 | tf_op jit(solution)/shard_map/ppermute | solution.py:221
  19.6 2.2 %pack_weights.1 = bf16[1024,512]{1,0:T(8,128)(2,1)} custom-call(bf16[4096,512]{1,0:T(8,128)(2,1)} %w_own.1), custom_call_target="tpu_custom_call" | custom-call | tf_op jit(solution)/shard_map/pack_weights/pallas_call | solution.py:600
  24.2 2.4 %collective-permute-done.6.refs_6_ = bf16[288,256]{1,0:T(8,128)(2,1)S(1)} collective-permute-done((bf16[288,256]{1,0:T(8,128)(2,1)S(1)}, bf16[288,256]{1,0:T(8,128)(2,1)S(1)}, u32[]{:S(2)}, u32[]{:S(2)}) %collective-permute-start.6) | collective-permute-done | bytes 147488 | tf_op jit(solution)/shard_map/ppermute | solution.py:221
  26.6 2.3 %collective-permute-done.1.refs_2_ = bf16[128,1024]{1,0:T(8,128)(2,1)S(1)} collective-permute-done((bf16[128,1024]{1,0:T(8,128)(2,1)S(1)}, bf16[128,1024]{1,0:T(8,128)(2,1)S(1)}, u32[]{:S(2)}, u32[]{:S(2)}) %collective-permute-start.1) | collective-permute-done | bytes 262176 | tf_op jit(solution)/shard_map/ppermute | solution.py:221
  29.5 3.2 %collective-permute-start.12 = (bf16[4,128,256]{2,1,0:T(8,128)(2,1)S(1)}, bf16[4,128,256]{2,1,0:T(8,128)(2,1)S(1)}, u32[]{:S(2)}, u32[]{:S(2)}) collective-permute-start(bf16[4,128,256]{2,1,0:T(8,128)(2,1)S(1)} %get-tuple-element.82), channel_id=1, source_target_pairs={{0,16},{2,18},{4,20},{6,22},{8,24},{10,26},{12,28},{14,30},{16,0},... | collective-permute-start | bytes 786440 | tf_op jit(solution)/shard_map/ppermute | solution.py:221
  32.7 8.4 %attend_first.1 = (bf16[128,512]{1,0:T(8,128)(2,1)S(1)}, bf16[128,512]{1,0:T(8,128)(2,1)S(1)}, bf16[128,512]{1,0:T(8,128)(2,1)S(1)}, bf16[2048,128]{1,0:T(8,128)...) custom-call(s32[4]{0:T(128)S(1)} %copy-done.4, ...), custom_call_target="tpu_custom_call" | custom-call | flops 4000000000 | tf_op jit(solution)/shard_map/attend_first/pallas_call | solution.py:632
  44.7 3.5 %attend_last.1 = (bf16[128,512]{1,0:T(8,128)(2,1)S(1)}, f32[1024,256]{1,0:T(8,128)S(1)}, f32[1024,256]{1,0:T(8,128)S(1)}) custom-call(s32[4]{0:T(128)S(1)} %copy-done.4, bf16[128,1024]{1,0:T(8,128)(2,1)S(1)} %collective-permute-done.10.row_ref, bf16[2048,128]{1,0:T(8,128)(2,1)S(1)} %get-tuple-element.73.keys, ...), custom_call_target="tpu_custom_call" | custom-call | flops 4000000000 | tf_op jit(solution)/shard_map/attend_last/pallas_call | solution.py:644
  48.2 2.6 %collective-permute-done.13 = f32[1024,256]{1,0:T(8,128)S(1)} collective-permute-done((f32[1024,256]{1,0:T(8,128)S(1)}, f32[1024,256]{1,0:T(8,128)S(1)}, u32[]{:S(2)}, u32[]{:S(2)}) %collective-permute-start.13) | collective-permute-done | bytes 1048608 | tf_op jit(solution)/shard_map/ppermute | solution.py:221
  57.1 2.3 %collective-permute-start.14 = (bf16[128,512]{1,0:T(8,128)(2,1)S(1)}, bf16[128,512]{1,0:T(8,128)(2,1)S(1)}, u32[]{:S(2)}, u32[]{:S(2)}) collective-permute-start(bf16[128,512]{1,0:T(8,128)(2,1)S(1)} %get-tuple-element.84), channel_id=1, source_target_pairs={{0,12},{2,14},{4,8},{6,10},{8,4},{10,6},{12,0},{14,2},{16,28},{18,... | collective-permute-start | bytes 393224 | tf_op jit(solution)/shard_map/ppermute | solution.py:221
  59.4 3.7 %collective-permute-done.16.refs_2_ = bf16[2,128,256]{2,1,0:T(8,128)(2,1)S(1)} collective-permute-done((bf16[2,128,256]{2,1,0:T(8,128)(2,1)S(1)}, bf16[2,128,256]{2,1,0:T(8,128)(2,1)S(1)}, u32[]{:S(2)}, u32[]{:S(2)}) %collective-permute-start.16) | collective-permute-done | bytes 131104 | tf_op jit(solution)/shard_map/ppermute | solution.py:221
  63.1 2.8 %collective-permute-done.17.refs_3_ = bf16[2,128,256]{2,1,0:T(8,128)(2,1)S(1)} collective-permute-done((bf16[2,128,256]{2,1,0:T(8,128)(2,1)S(1)}, bf16[2,128,256]{2,1,0:T(8,128)(2,1)S(1)}, u32[]{:S(2)}, u32[]{:S(2)}) %collective-permute-start.17) | collective-permute-done | bytes 131104 | tf_op jit(solution)/shard_map/ppermute | solution.py:221
  67.7 2.8 %collective-permute-done.14.refs_3_ = bf16[128,512]{1,0:T(8,128)(2,1)S(1)} collective-permute-done((bf16[128,512]{1,0:T(8,128)(2,1)S(1)}, bf16[128,512]{1,0:T(8,128)(2,1)S(1)}, u32[]{:S(2)}, u32[]{:S(2)}) %collective-permute-start.14) | collective-permute-done | bytes 131104 | tf_op jit(solution)/shard_map/ppermute | solution.py:221
  72.7 3.3 %collective-permute-start.20 = (bf16[512,128]{1,0:T(8,128)(2,1)S(1)}, bf16[512,128]{1,0:T(8,128)(2,1)S(1)}, u32[]{:S(2)}, u32[]{:S(2)}) collective-permute-start(bf16[512,128]{1,0:T(8,128)(2,1)S(1)} %slice.103), channel_id=1, source_target_pairs={{0,16},{2,18},{4,20},{6,22},{8,24},{10,26},{12,28},{14,30},{16,0},... | collective-permute-start | bytes 393224 | tf_op jit(solution)/shard_map/ppermute | solution.py:221
  76.0 4.3 %collective-permute-done.20 = bf16[512,128]{1,0:T(8,128)(2,1)S(1)} collective-permute-done((bf16[512,128]{1,0:T(8,128)(2,1)S(1)}, bf16[512,128]{1,0:T(8,128)(2,1)S(1)}, u32[]{:S(2)}, u32[]{:S(2)}) %collective-permute-start.20) | collective-permute-done | bytes 131104 | tf_op jit(solution)/shard_map/ppermute | solution.py:221
  80.4 2.1 %collective-permute-done.22 = bf16[1024,128]{1,0:T(8,128)(2,1)S(1)} collective-permute-done((bf16[1024,128]{1,0:T(8,128)(2,1)S(1)}, bf16[1024,128]{1,0:T(8,128)(2,1)S(1)}, u32[]{:S(2)}, u32[]{:S(2)}) %collective-permute-start.22) | collective-permute-done | bytes 262176 | tf_op jit(solution)/shard_map/ppermute | solution.py:221
  84.7 1.9 %collective-permute-start.24 = (bf16[128,128]{1,0:T(8,128)(2,1)S(1)}, bf16[128,128]{1,0:T(8,128)(2,1)S(1)}, u32[]{:S(2)}, u32[]{:S(2)}) collective-permute-start(bf16[128,128]{1,0:T(8,128)(2,1)S(1)} %get-tuple-element.98), channel_id=1, source_target_pairs={{0,8},{2,10},{4,12},{6,14},{8,0},{10,2},{12,4},{14,6},{16,24},{18,... | collective-permute-start | bytes 98312 | tf_op jit(solution)/shard_map/ppermute | solution.py:221
  86.7 2.0 %collective-permute-start.28 = (bf16[512,128]{1,0:T(8,128)(2,1)S(1)}, bf16[512,128]{1,0:T(8,128)(2,1)S(1)}, u32[]{:S(2)}, u32[]{:S(2)}) collective-permute-start(bf16[512,128]{1,0:T(8,128)(2,1)S(1)} %get-tuple-element.110.refs_5_), channel_id=1, source_target_pairs={{0,8},{2,10},{4,12},{6,14},{8,0},{10,2},{12,4},{14,6},{16,24},{18,... | collective-permute-start | bytes 393224 | tf_op jit(solution)/shard_map/ppermute | solution.py:221
  89.0 2.4 %collective-permute-done.25.refs_3_ = bf16[128,128]{1,0:T(8,128)(2,1)S(1)} collective-permute-done((bf16[128,128]{1,0:T(8,128)(2,1)S(1)}, bf16[128,128]{1,0:T(8,128)(2,1)S(1)}, u32[]{:S(2)}, u32[]{:S(2)}) %collective-permute-start.25) | collective-permute-done | bytes 32800 | tf_op jit(solution)/shard_map/ppermute | solution.py:221
  94.7 4.3 %collective-permute-done.30.other_ref = bf16[4,128,128]{2,1,0:T(8,128)(2,1)S(1)} collective-permute-done((bf16[4,128,128]{2,1,0:T(8,128)(2,1)S(1)}, bf16[4,128,128]{2,1,0:T(8,128)(2,1)S(1)}, u32[]{:S(2)}, u32[]{:S(2)}) %collective-permute-start.30) | collective-permute-done | bytes 131104 | tf_op jit(solution)/shard_map/ppermute | solution.py:225
  99.0 2.3 %input_grad.1 = bf16[128,2048]{1,0:T(8,128)(2,1)} custom-call(bf16[4,128,128]{2,1,0:T(8,128)(2,1)S(1)} %pad_maximum_fusion.own_ref, bf16[4,128,128]{2,1,0:T(8,128)(2,1)S(1)} %collective-permute-done.30.other_ref, bf16[4096,512]{1,0:T(8,128)(2,1)S(1)} %copy-done, bf16[1024,512]{1,0:T(8,128)(2,1)S(1)} %collective-permute-done.11.w_near, ...), custom_call_target="tpu_custom_call" | custom-call | flops 536870912 | bytes 5242880 | tf_op jit(solution)/shard_map/input_grad/pallas_call | solution.py:723
  (80 shorter events, 27.0 us)
Async XLA Ops:
  8.2 5.7 %collective-permute-start.3 = (bf16[144,256]{1,0:T(8,128)(2,1)}, bf16[144,256]{1,0:T(8,128)(2,1)S(1)}, u32[]{:S(2)}, u32[]{:S(2)}) collective-permute-start(bf16[144,256]{1,0:T(8,128)(2,1)} %get-tuple-element.62), channel_id=1, source_target_pairs={{0,8},{2,10},{4,12},{6,14},{8,0},{10,2},{12,4},{14,6},{16,24},{18,... | collective-permute-start | bytes 221192 | tf_op jit(solution)/shard_map/ppermute | solution.py:221
  9.8 6.5 %collective-permute-start.4 = (bf16[144,256]{1,0:T(8,128)(2,1)}, bf16[144,256]{1,0:T(8,128)(2,1)S(1)}, u32[]{:S(2)}, u32[]{:S(2)}) collective-permute-start(bf16[144,256]{1,0:T(8,128)(2,1)} %get-tuple-element.63), channel_id=1, source_target_pairs={{0,12},{2,14},{4,8},{6,10},{8,4},{10,6},{12,0},{14,2},{16,28},{18,... | collective-permute-start | bytes 221192 | tf_op jit(solution)/shard_map/ppermute | solution.py:221
  10.9 13.3 %collective-permute-start.5 = (bf16[288,256]{1,0:T(8,128)(2,1)S(1)}, bf16[288,256]{1,0:T(8,128)(2,1)S(1)}, u32[]{:S(2)}, u32[]{:S(2)}) collective-permute-start(bf16[288,256]{1,0:T(8,128)(2,1)S(1)} %get-tuple-element.125.refs_3_), channel_id=1, source_target_pairs={{0,16},{2,18},{4,20},{6,22},{8,24},{10,26},{12,28},{14,30},{16,0},... | collective-permute-start | bytes 442376 | tf_op jit(solution)/shard_map/ppermute | solution.py:221
  16.4 10.2 %collective-permute-start.6 = (bf16[288,256]{1,0:T(8,128)(2,1)S(1)}, bf16[288,256]{1,0:T(8,128)(2,1)S(1)}, u32[]{:S(2)}, u32[]{:S(2)}) collective-permute-start(bf16[288,256]{1,0:T(8,128)(2,1)S(1)} %get-tuple-element.121.refs_4_), channel_id=1, source_target_pairs={{0,16},{2,18},{4,20},{6,22},{8,24},{10,26},{12,28},{14,30},{16,0},... | collective-permute-start | bytes 442376 | tf_op jit(solution)/shard_map/ppermute | solution.py:221
  18.7 7.9 %collective-permute-start = (bf16[128,1024]{1,0:T(8,128)(2,1)S(1)}, bf16[128,1024]{1,0:T(8,128)(2,1)S(1)}, u32[]{:S(2)}, u32[]{:S(2)}) collective-permute-start(bf16[128,1024]{1,0:T(8,128)(2,1)S(1)} %get-tuple-element.58), channel_id=1, source_target_pairs={{0,4},{2,6},{4,0},{6,2},{8,12},{10,14},{12,8},{14,10},{16,20},{18,... | collective-permute-start | bytes 786440 | tf_op jit(solution)/shard_map/ppermute | solution.py:221
  19.3 9.6 %collective-permute-start.1 = (bf16[128,1024]{1,0:T(8,128)(2,1)S(1)}, bf16[128,1024]{1,0:T(8,128)(2,1)S(1)}, u32[]{:S(2)}, u32[]{:S(2)}) collective-permute-start(bf16[128,1024]{1,0:T(8,128)(2,1)S(1)} %get-tuple-element.59), channel_id=1, source_target_pairs={{0,8},{2,10},{4,12},{6,14},{8,0},{10,2},{12,4},{14,6},{16,24},{18,... | collective-permute-start | bytes 786440 | tf_op jit(solution)/shard_map/ppermute | solution.py:221
  21.8 22.9 %collective-permute-start.11 = (bf16[1024,512]{1,0:T(8,128)(2,1)}, bf16[1024,512]{1,0:T(8,128)(2,1)S(1)}, u32[]{:S(2)}, u32[]{:S(2)}) collective-permute-start(bf16[1024,512]{1,0:T(8,128)(2,1)} %pack_weights.1), channel_id=1, source_target_pairs={{0,1},{1,0},{2,3},{3,2},{4,5},{5,4},{6,7},{7,6},{8,9},{9,8},{10,11... | collective-permute-start | bytes 3145736 | tf_op jit(solution)/shard_map/ppermute | solution.py:225
  28.9 14.6 %collective-permute-start.10 = (bf16[128,1024]{1,0:T(8,128)(2,1)S(1)}, bf16[128,1024]{1,0:T(8,128)(2,1)S(1)}, u32[]{:S(2)}, u32[]{:S(2)}) collective-permute-start(bf16[128,1024]{1,0:T(8,128)(2,1)S(1)} %get-tuple-element.71), channel_id=1, source_target_pairs={{0,12},{2,14},{4,8},{6,10},{8,4},{10,6},{12,0},{14,2},{16,28},{18,... | collective-permute-start | bytes 786440 | tf_op jit(solution)/shard_map/ppermute | solution.py:221
  29.5 18.7 %collective-permute-start.12 = (bf16[4,128,256]{2,1,0:T(8,128)(2,1)S(1)}, bf16[4,128,256]{2,1,0:T(8,128)(2,1)S(1)}, u32[]{:S(2)}, u32[]{:S(2)}) collective-permute-start(bf16[4,128,256]{2,1,0:T(8,128)(2,1)S(1)} %get-tuple-element.82), channel_id=1, source_target_pairs={{0,16},{2,18},{4,20},{6,22},{8,24},{10,26},{12,28},{14,30},{16,0},... | collective-permute-start | bytes 786440 | tf_op jit(solution)/shard_map/ppermute | solution.py:221
  41.1 7.0 %collective-permute-start.8 = (bf16[128,512]{1,0:T(8,128)(2,1)S(1)}, bf16[128,512]{1,0:T(8,128)(2,1)S(1)}, u32[]{:S(2)}, u32[]{:S(2)}) collective-permute-start(bf16[128,512]{1,0:T(8,128)(2,1)S(1)} %get-tuple-element.69), channel_id=1, source_target_pairs={{0,4},{2,6},{4,0},{6,2},{8,12},{10,14},{12,8},{14,10},{16,20},{18,... | collective-permute-start | bytes 393224 | tf_op jit(solution)/shard_map/ppermute | solution.py:221
  42.2 5.9 %collective-permute-start.9 = (bf16[128,512]{1,0:T(8,128)(2,1)S(1)}, bf16[128,512]{1,0:T(8,128)(2,1)S(1)}, u32[]{:S(2)}, u32[]{:S(2)}) collective-permute-start(bf16[128,512]{1,0:T(8,128)(2,1)S(1)} %get-tuple-element.70), channel_id=1, source_target_pairs={{0,8},{2,10},{4,12},{6,14},{8,0},{10,2},{12,4},{14,6},{16,24},{18,... | collective-permute-start | bytes 393224 | tf_op jit(solution)/shard_map/ppermute | solution.py:221
  51.1 20.3 %collective-permute-start.19 = (bf16[1024,512]{1,0:T(8,128)(2,1)S(1)}, bf16[1024,512]{1,0:T(8,128)(2,1)S(1)}, u32[]{:S(2)}, u32[]{:S(2)}) collective-permute-start(bf16[1024,512]{1,0:T(8,128)(2,1)S(1)} %collective-permute-done.11.w_near), channel_id=1, source_target_pairs={{0,2},{2,0},{4,6},{6,4},{8,10},{10,8},{12,14},{14,12},{16,18},{18,... | collective-permute-start | bytes 3145736 | tf_op jit(solution)/shard_map/ppermute | solution.py:221
  51.3 5.8 %collective-permute-start.15 = (bf16[2,128,256]{2,1,0:T(8,128)(2,1)S(1)}, bf16[2,128,256]{2,1,0:T(8,128)(2,1)S(1)}, u32[]{:S(2)}, u32[]{:S(2)}) collective-permute-start(bf16[2,128,256]{2,1,0:T(8,128)(2,1)S(1)} %get-tuple-element.88), channel_id=1, source_target_pairs={{0,4},{2,6},{4,0},{6,2},{8,12},{10,14},{12,8},{14,10},{16,20},{18,... | collective-permute-start | bytes 393224 | tf_op jit(solution)/shard_map/ppermute | solution.py:221
  52.6 18.7 %collective-permute-start.18 = (bf16[1024,128]{1,0:T(8,128)(2,1)S(1)}, bf16[1024,128]{1,0:T(8,128)(2,1)S(1)}, u32[]{:S(2)}, u32[]{:S(2)}) collective-permute-start(bf16[1024,128]{1,0:T(8,128)(2,1)S(1)} %slice.119), channel_id=1, source_target_pairs={{0,16},{2,18},{4,20},{6,22},{8,24},{10,26},{12,28},{14,30},{16,0},... | collective-permute-start | bytes 786440 | tf_op jit(solution)/shard_map/ppermute | solution.py:221
  53.6 9.5 %collective-permute-start.16 = (bf16[2,128,256]{2,1,0:T(8,128)(2,1)S(1)}, bf16[2,128,256]{2,1,0:T(8,128)(2,1)S(1)}, u32[]{:S(2)}, u32[]{:S(2)}) collective-permute-start(bf16[2,128,256]{2,1,0:T(8,128)(2,1)S(1)} %get-tuple-element.89), channel_id=1, source_target_pairs={{0,8},{2,10},{4,12},{6,14},{8,0},{10,2},{12,4},{14,6},{16,24},{18,... | collective-permute-start | bytes 393224 | tf_op jit(solution)/shard_map/ppermute | solution.py:221
  54.6 11.3 %collective-permute-start.17 = (bf16[2,128,256]{2,1,0:T(8,128)(2,1)S(1)}, bf16[2,128,256]{2,1,0:T(8,128)(2,1)S(1)}, u32[]{:S(2)}, u32[]{:S(2)}) collective-permute-start(bf16[2,128,256]{2,1,0:T(8,128)(2,1)S(1)} %get-tuple-element.90), channel_id=1, source_target_pairs={{0,12},{2,14},{4,8},{6,10},{8,4},{10,6},{12,0},{14,2},{16,28},{18,... | collective-permute-start | bytes 393224 | tf_op jit(solution)/shard_map/ppermute | solution.py:221
  57.1 13.3 %collective-permute-start.14 = (bf16[128,512]{1,0:T(8,128)(2,1)S(1)}, bf16[128,512]{1,0:T(8,128)(2,1)S(1)}, u32[]{:S(2)}, u32[]{:S(2)}) collective-permute-start(bf16[128,512]{1,0:T(8,128)(2,1)S(1)} %get-tuple-element.84), channel_id=1, source_target_pairs={{0,12},{2,14},{4,8},{6,10},{8,4},{10,6},{12,0},{14,2},{16,28},{18,... | collective-permute-start | bytes 393224 | tf_op jit(solution)/shard_map/ppermute | solution.py:221
  66.1 25.3 %collective-permute-start.26 = (bf16[256,1024]{1,0:T(8,128)(2,1)S(1)}, bf16[256,1024]{1,0:T(8,128)(2,1)S(1)}, u32[]{:S(2)}, u32[]{:S(2)}) collective-permute-start(bf16[256,1024]{1,0:T(8,128)(2,1)S(1)} %turn_features.1.own_ref), channel_id=1, source_target_pairs={{0,1},{1,0},{2,3},{3,2},{4,5},{5,4},{6,7},{7,6},{8,9},{9,8},{10,11... | collective-permute-start | bytes 1572872 | tf_op jit(solution)/shard_map/ppermute | solution.py:225
  71.4 11.1 %collective-permute-start.22 = (bf16[1024,128]{1,0:T(8,128)(2,1)S(1)}, bf16[1024,128]{1,0:T(8,128)(2,1)S(1)}, u32[]{:S(2)}, u32[]{:S(2)}) collective-permute-start(bf16[1024,128]{1,0:T(8,128)(2,1)S(1)} %add_convert_fusion), channel_id=1, source_target_pairs={{0,8},{2,10},{4,12},{6,14},{8,0},{10,2},{12,4},{14,6},{16,24},{18,... | collective-permute-start | bytes 786440 | tf_op jit(solution)/shard_map/ppermute | solution.py:221
  71.5 11.1 %collective-permute-start.21 = (bf16[1024,128]{1,0:T(8,128)(2,1)S(1)}, bf16[1024,128]{1,0:T(8,128)(2,1)S(1)}, u32[]{:S(2)}, u32[]{:S(2)}) collective-permute-start(bf16[1024,128]{1,0:T(8,128)(2,1)S(1)} %add_convert_fusion), channel_id=1, source_target_pairs={{0,4},{2,6},{4,0},{6,2},{8,12},{10,14},{12,8},{14,10},{16,20},{18,... | collective-permute-start | bytes 786440 | tf_op jit(solution)/shard_map/ppermute | solution.py:221
  72.7 7.7 %collective-permute-start.20 = (bf16[512,128]{1,0:T(8,128)(2,1)S(1)}, bf16[512,128]{1,0:T(8,128)(2,1)S(1)}, u32[]{:S(2)}, u32[]{:S(2)}) collective-permute-start(bf16[512,128]{1,0:T(8,128)(2,1)S(1)} %slice.103), channel_id=1, source_target_pairs={{0,16},{2,18},{4,20},{6,22},{8,24},{10,26},{12,28},{14,30},{16,0},... | collective-permute-start | bytes 393224 | tf_op jit(solution)/shard_map/ppermute | solution.py:221
  82.9 8.5 %collective-permute-start.27 = (bf16[512,128]{1,0:T(8,128)(2,1)S(1)}, bf16[512,128]{1,0:T(8,128)(2,1)S(1)}, u32[]{:S(2)}, u32[]{:S(2)}) collective-permute-start(bf16[512,128]{1,0:T(8,128)(2,1)S(1)} %get-tuple-element.109.refs_2_), channel_id=1, source_target_pairs={{0,4},{2,6},{4,0},{6,2},{8,12},{10,14},{12,8},{14,10},{16,20},{18,... | collective-permute-start | bytes 393224 | tf_op jit(solution)/shard_map/ppermute | solution.py:221
  92.9 8.4 %collective-permute-start.29 = (f32[256,512]{1,0:T(8,128)S(1)}, f32[256,512]{1,0:T(8,128)S(1)}, u32[]{:S(2)}, u32[]{:S(2)}) collective-permute-start(f32[256,512]{1,0:T(8,128)S(1)} %get-tuple-element.102), channel_id=1, source_target_pairs={{0,2},{2,0},{4,6},{6,4},{8,10},{10,8},{12,14},{14,12},{16,18},{18,... | collective-permute-start | bytes 1572872 | tf_op jit(solution)/shard_map/ppermute | solution.py:221
  93.1 5.9 %collective-permute-start.30 = (bf16[4,128,128]{2,1,0:T(8,128)(2,1)S(1)}, bf16[4,128,128]{2,1,0:T(8,128)(2,1)S(1)}, u32[]{:S(2)}, u32[]{:S(2)}) collective-permute-start(bf16[4,128,128]{2,1,0:T(8,128)(2,1)S(1)} %pad_maximum_fusion.own_ref), channel_id=1, source_target_pairs={{0,1},{1,0},{2,3},{3,2},{4,5},{5,4},{6,7},{7,6},{8,9},{9,8},{10,11... | collective-permute-start | bytes 393224 | tf_op jit(solution)/shard_map/ppermute | solution.py:225
  (12 other events, 130.3 us)

commit v6 on v4

--- a/solution.py
+++ b/solution.py
@@ -207,7 +207,7 @@
 ROWS = 128
 TILE = 256
 UNROLLED = 5
-ATTEND_COST = 1 << 20
+ATTEND_COST = 4_000_000_000
 PART = 512
 MARKED = ROWS + 16
 Q_BLOCKS = GROUP * ROWS // BLK
@@ -521,21 +521,33 @@
         out_ref[:, columns(chunk, PART)] = part.astype(jnp.bfloat16)
 
 
-def pack_grads(value_ref, row_ref, *refs):
-    for m, out_ref in enumerate(refs):
-        out_ref[:, :HD] = value_ref[m * ROWS : (m + 1) * ROWS]
-    refs[-1][:, HD:] = row_ref[...]
-
-
-def finish(keep_ref, arrived_ref, *refs):
-    row_refs, grad_refs, refs = refs[: GROUP - 1], refs[GROUP - 1 : 2 * GROUP - 1], refs[2 * GROUP - 1 :]
+def sum_cores(kept_ref, arrived_ref, dk_ref, dk_bf_ref, *dv_refs):
+    dk = kept_ref[:, :HD] + arrived_ref[:, :HD]
+    dk_ref[...] = dk
+    dk_bf_ref[...] = dk.astype(jnp.bfloat16)
+    for m, dv_ref in enumerate(dv_refs):
+        for far in range(2):
+            here = pl.ds((far * GROUP + m) * ROWS, ROWS)
+            dv_ref[far] = (kept_ref[here, HD:] + arrived_ref[here, HD:]).astype(jnp.bfloat16)
+
+
+def sum_halves(near_ref, far_ref, out_ref):
+    quarter = GROUP * ROWS
+    for k in range(2):
+        here, there = pl.ds(k * quarter, quarter), pl.ds((1 - k) * quarter, quarter)
+        total = near_ref[here] + far_ref[there].astype(jnp.float32)
+        out_ref[here] = total.astype(jnp.bfloat16)
+
+
+def finish(keep_ref, arrived_ref, far_ref, *refs):
+    row_refs, value_refs, refs = refs[:GROUP], refs[GROUP : 2 * GROUP], refs[2 * GROUP :]
     weight_out, query_out, value_out = refs
     head = own_head()
     weight_out[...] = keep_ref[...] + arrived_ref[...]
     for m in range(GROUP):
-        row = row_refs[m][...] if m < GROUP - 1 else grad_refs[m][:, HD:]
-        query_out[:, columns(head ^ m, GROUP * HD)] = row
-        value_out[:, columns(head ^ m, HD)] = grad_refs[m][:, :HD]
+        query_out[:, columns(head ^ m, GROUP * HD)] = row_refs[m][...]
+        value = value_refs[m][0].astype(jnp.float32) + far_ref[m].astype(jnp.float32)
+        value_out[:, columns(head ^ m, HD)] = value.astype(jnp.bfloat16)
 
 
 def shaped(shape, dtype=jnp.bfloat16):
@@ -554,7 +566,7 @@
     features = inputs.shape[1]
     kv_columns = values.shape[1]
     total_rows = 16 * ROWS
-    half, quarter = total_rows // 2, total_rows // 4
+    half = total_rows // 2
     vmem, smem, hbm = whole_spec(), whole_spec(SMEM), whole_spec(HBM)
 
     pairs = pl.pallas_call(
@@ -659,10 +671,18 @@
 
     row_grads = with_partners(row_grads)
     sent = after(sent, far_features, *row_grads)
-    grads = kept + swap(sent, CORE)
-    dk_sum, dv_sum = grads[:, :HD], grads[:, HD:]
-    dk_far = swap(dk_sum.astype(jnp.bfloat16), Z_HI)
-    w_far = swap(after(w_near, dk_sum), CORE)
+    dk_sum, dk_near, *value_grads = pl.pallas_call(
+        sum_cores,
+        out_shape=[shaped((half, HD), jnp.float32), shaped((half, HD))]
+        + [shaped((2, ROWS, HD))] * GROUP,
+        in_specs=[vmem] * 2,
+        out_specs=[vmem] * (2 + GROUP),
+        compiler_params=limits(16),
+        name="sum_cores",
+    )(kept, swap(sent, CORE))
+    dk_far = swap(dk_near, Z_HI)
+    value_grads = with_partners(value_grads)
+    value_far = jnp.stack([grad[1] for grad in value_grads])
 
     feature_parts = pl.pallas_call(
         join_features,
@@ -678,31 +698,28 @@
         in_specs=[vmem] * GROUP,
         out_specs=vmem,
         compiler_params=limits(16),
-        cost_estimate=pl.CostEstimate(flops=4_000_000_000, bytes_accessed=0, transcendentals=0),
+        cost_estimate=pl.CostEstimate(flops=1_000_000_000, bytes_accessed=0, transcendentals=0),
         name="turn_features",
     )(*with_partners(feature_parts))
     other_features = swap_tensor(own_features)
 
-    dk_far = jnp.concatenate([dk_far[quarter:], dk_far[:quarter]], axis=0)
-    key_grad = (dk_sum + dk_far.astype(jnp.float32)).astype(jnp.bfloat16)
-    key_grad = after(key_grad, own_features, w_far)
+    key_grad = pl.pallas_call(
+        sum_halves,
+        out_shape=shaped((half, HD)),
+        in_specs=[vmem] * 2,
+        out_specs=vmem,
+        compiler_params=limits(8),
+        cost_estimate=pl.CostEstimate(flops=1_000_000, bytes_accessed=0, transcendentals=0),
+        name="sum_halves",
+    )(dk_sum, dk_far)
+    key_grad = after(key_grad, own_features, value_far)
     key_grads = with_partners([key_grad] * GROUP)
+    w_far = swap(after(w_near, key_grad), CORE)
     own_key_grad = jnp.stack([key_grads[m][m * ROWS : (m + 1) * ROWS] for m in range(GROUP)])
     other_key_grad = swap_tensor(own_key_grad)
 
-    dv_far = swap(after(dv_sum[quarter:].astype(jnp.bfloat16), key_grad), Z_HI)
-    value_grad = (dv_sum[:quarter] + dv_far.astype(jnp.float32)).astype(jnp.bfloat16)
-    packed_grads = pl.pallas_call(
-        pack_grads,
-        out_shape=[shaped((ROWS, HD))] * (GROUP - 1) + [shaped((ROWS, (GROUP + 1) * HD))],
-        in_specs=[vmem] * 2,
-        out_specs=[vmem] * GROUP,
-        compiler_params=limits(16),
-        name="pack_grads",
-    )(value_grad, last_grad)
-    packed_grads = [after(packed_grads[0], own_key_grad)] + [
-        after(grad, own_key_grad) for grad in packed_grads[1:]
-    ]
+    value_far = swap(after(value_far, key_grad), Z_HI)
+    last_grad = swap(after(last_grad, own_key_grad), 6)
 
     keep, send = pl.pallas_call(
         weight_grad,
@@ -715,7 +732,7 @@
             flops=4 * 256 * half * kv_columns, bytes_accessed=4 << 20, transcendentals=0
         ),
         name="weight_grad",
-    )(own_features, other_features, *key_grads)
+    )(after(own_features, value_far), other_features, *key_grads)
     arrived = swap(send, CORE)
 
     d_input = pl.pallas_call(
@@ -738,11 +755,11 @@
             shaped(queries.shape),
             shaped(values.shape),
         ],
-        in_specs=[vmem] * (1 + 2 * GROUP),
+        in_specs=[vmem] * (3 + 2 * GROUP),
         out_specs=[vmem] * 3,
         compiler_params=limits(16),
         name="finish",
-    )(keep, arrived, *row_grads, *with_partners(packed_grads))
+    )(after(keep, d_input), arrived, value_far, *row_grads, last_grad, *value_grads)
     return (d_query, d_value, d_input, d_wkey)
 
 

time: 95.6 us -> 93.9 us (0.982)
  Pallas kernels: 23.5 us -> 22.2 us
    ppermute x26 -> x27, waiting for transfers between devices: 33.7 us -> 31.5 us  [swap(): return lax.ppermute(array, 'dp', [(i, i ^ mask) for i in range(16)])]
    ppermute x3, waiting for transfers between devices: 3.53 us -> 5.07 us  [swap_tensor(): return lax.ppermute(array, 'tensor', [(0, 1), (1, 0)])]
    pallas_call x1, Pallas kernels: 8.36 us -> 6.99 us  [on_device_by_heads(): pl.pallas_call(attend_first, out_shape=[row_grad] * (GROUP - 1) + [sorted...]
    ppermute x26 -> x27, starting transfers between devices: 28.3 us -> 28 us  [swap(): return lax.ppermute(array, 'dp', [(i, i ^ mask) for i in range(16)])]
  transfers between devices with their start and end apart: 29 -> 30, of which waited for: 15 -> 17; matrix products, arithmetic and copies ran while one was open for 1% -> 1% of each run, Pallas kernels for 19% -> 18%
where the time goes in v6:
time: 93.9 us; the launch traced here: 93.5 us
  waiting for transfers between devices  36.5 us (39%)
  starting transfers between devices  32.8 us (35%)
  Pallas kernels  22.2 us (24%)
  local copies, waits for them, and re-layouts  1.01 us (1%)
    ppermute x27, waiting for transfers between devices, swap(): return lax.ppermute(array, 'dp', [(i, i ^ mask) for i in range(16)])  31.5 us
    ppermute x27, starting transfers between devices, swap(): return lax.ppermute(array, 'dp', [(i, i ^ mask) for i in range(16)])  28 us
    pallas_call x1, Pallas kernels, on_device_by_heads(): pl.pallas_call(attend_first, out_shape=[row_grad] * (GROUP - 1) + [sorted...  6.99 us
    ppermute x3, waiting for transfers between devices, swap_tensor(): return lax.ppermute(array, 'tensor', [(0, 1), (1, 0)])  5.07 us
    ppermute x3, starting transfers between devices, swap_tensor(): return lax.ppermute(array, 'tensor', [(0, 1), (1, 0)])  4.79 us
    pallas_call x1, Pallas kernels, on_device_by_heads(): pl.pallas_call(project_keys, out_shape=[shaped((MARKED, 2 * HD))] * GROUP...  4.57 us
    pallas_call x1, Pallas kernels, on_device_by_heads(): pl.pallas_call(attend_last, out_shape=[row_grad, half_sums, half_sums], i...  3.46 us
    pallas_call x1, Pallas kernels, on_device_by_heads(): pl.pallas_call(input_grad, out_shape=shaped((ROWS, features // 2)), in_sp...  2.27 us
  transfers between devices with their start and end apart: 30, of which 17 were waited for; matrix products, arithmetic and copies ran while one was open for 1% of the time, Pallas kernels for 18%

profile of v6, /device:TPU:0, one launch (start us, length us, event | category | flops | bytes accessed | tf_op | source)
XLA Modules:
  0.0 93.5 jit_solution(8193435516347238397)
XLA Ops:
  0.7 4.6 %project_keys.1 = (bf16[144,256]{1,0:T(8,128)(2,1)}, bf16[144,256]{1,0:T(8,128)(2,1)}, bf16[144,256]{1,0:T(8,128)(2,1)}, bf16[144,256]{1,0:T(8,128)(2,1)}) custom-call(s32[2]{0:T(128)} %pos_ref.1, bf16[128,4096]{1,0:T(8,128)(2,1)} %inputs_ref.2, bf16[128,512]{1,0:T(8,128)(2,1)} %values_ref.1, bf16[4096,512]{1,0:T(8,128)(2,1)} %w_own.1), custom_call_target="tpu_custom_call" | custom-call | flops 536870912 | bytes 4194304 | tf_op jit(solution)/shard_map/project_keys/pallas_call | solution.py:572
  5.2 3.0 %collective-permute-start = (bf16[144,256]{1,0:T(8,128)(2,1)}, bf16[144,256]{1,0:T(8,128)(2,1)S(1)}, u32[]{:S(2)}, u32[]{:S(2)}) collective-permute-start(bf16[144,256]{1,0:T(8,128)(2,1)} %get-tuple-element.60), channel_id=1, source_target_pairs={{0,4},{2,6},{4,0},{6,2},{8,12},{10,14},{12,8},{14,10},{16,20},{18,... | collective-permute-start | bytes 221192 | tf_op jit(solution)/shard_map/ppermute | solution.py:221
  10.9 3.1 %collective-permute-start.7 = (bf16[288,256]{1,0:T(8,128)(2,1)S(1)}, bf16[288,256]{1,0:T(8,128)(2,1)S(1)}, u32[]{:S(2)}, u32[]{:S(2)}) collective-permute-start(bf16[288,256]{1,0:T(8,128)(2,1)S(1)} %get-tuple-element.113.refs_3_), channel_id=1, source_target_pairs={{0,16},{2,18},{4,20},{6,22},{8,24},{10,26},{12,28},{14,30},{16,0},... | collective-permute-start | bytes 442376 | tf_op jit(solution)/shard_map/ppermute | solution.py:221
  14.0 2.4 %collective-permute-done.3 = bf16[144,256]{1,0:T(8,128)(2,1)S(1)} collective-permute-done((bf16[144,256]{1,0:T(8,128)(2,1)}, bf16[144,256]{1,0:T(8,128)(2,1)S(1)}, u32[]{:S(2)}, u32[]{:S(2)}) %collective-permute-start.3) | collective-permute-done | bytes 73760 | tf_op jit(solution)/shard_map/ppermute | solution.py:221
  16.4 2.3 %collective-permute-start.8 = (bf16[288,256]{1,0:T(8,128)(2,1)S(1)}, bf16[288,256]{1,0:T(8,128)(2,1)S(1)}, u32[]{:S(2)}, u32[]{:S(2)}) collective-permute-start(bf16[288,256]{1,0:T(8,128)(2,1)S(1)} %get-tuple-element.109.refs_4_), channel_id=1, source_target_pairs={{0,16},{2,18},{4,20},{6,22},{8,24},{10,26},{12,28},{14,30},{16,0},... | collective-permute-start | bytes 442376 | tf_op jit(solution)/shard_map/ppermute | solution.py:221
  19.6 2.3 %pack_weights.1 = bf16[1024,512]{1,0:T(8,128)(2,1)} custom-call(bf16[4096,512]{1,0:T(8,128)(2,1)} %w_own.1), custom_call_target="tpu_custom_call" | custom-call | tf_op jit(solution)/shard_map/pack_weights/pallas_call | solution.py:617
  24.2 2.4 %collective-permute-done.8.refs_6_ = bf16[288,256]{1,0:T(8,128)(2,1)S(1)} collective-permute-done((bf16[288,256]{1,0:T(8,128)(2,1)S(1)}, bf16[288,256]{1,0:T(8,128)(2,1)S(1)}, u32[]{:S(2)}, u32[]{:S(2)}) %collective-permute-start.8) | collective-permute-done | bytes 147488 | tf_op jit(solution)/shard_map/ppermute | solution.py:221
  26.6 2.3 %collective-permute-done.6.refs_2_ = bf16[128,1024]{1,0:T(8,128)(2,1)S(1)} collective-permute-done((bf16[128,1024]{1,0:T(8,128)(2,1)S(1)}, bf16[128,1024]{1,0:T(8,128)(2,1)S(1)}, u32[]{:S(2)}, u32[]{:S(2)}) %collective-permute-start.6) | collective-permute-done | bytes 262176 | tf_op jit(solution)/shard_map/ppermute | solution.py:221
  29.5 3.2 %collective-permute-start.10 = (bf16[4,128,256]{2,1,0:T(8,128)(2,1)S(1)}, bf16[4,128,256]{2,1,0:T(8,128)(2,1)S(1)}, u32[]{:S(2)}, u32[]{:S(2)}) collective-permute-start(bf16[4,128,256]{2,1,0:T(8,128)(2,1)S(1)} %get-tuple-element.78), channel_id=1, source_target_pairs={{0,16},{2,18},{4,20},{6,22},{8,24},{10,26},{12,28},{14,30},{16,0},... | collective-permute-start | bytes 786440 | tf_op jit(solution)/shard_map/ppermute | solution.py:221
  32.7 7.0 %attend_first.1 = (bf16[128,512]{1,0:T(8,128)(2,1)S(1)}, bf16[128,512]{1,0:T(8,128)(2,1)S(1)}, bf16[128,512]{1,0:T(8,128)(2,1)S(1)}, bf16[2048,128]{1,0:T(8,128)...) custom-call(s32[4]{0:T(128)S(1)} %copy-done.4, ...), custom_call_target="tpu_custom_call" | custom-call | flops 4000000000 | tf_op jit(solution)/shard_map/attend_first/pallas_call | solution.py:649
  40.8 2.8 %collective-permute-done.1.row_ref = bf16[128,1024]{1,0:T(8,128)(2,1)S(1)} collective-permute-done((bf16[128,1024]{1,0:T(8,128)(2,1)S(1)}, bf16[128,1024]{1,0:T(8,128)(2,1)S(1)}, u32[]{:S(2)}, u32[]{:S(2)}) %collective-permute-start.1) | collective-permute-done | bytes 262176 | tf_op jit(solution)/shard_map/ppermute | solution.py:221
  44.7 3.5 %attend_last.1 = (bf16[128,512]{1,0:T(8,128)(2,1)S(1)}, f32[1024,256]{1,0:T(8,128)S(1)}, f32[1024,256]{1,0:T(8,128)S(1)}) custom-call(s32[4]{0:T(128)S(1)} %copy-done.4, bf16[128,1024]{1,0:T(8,128)(2,1)S(1)} %collective-permute-done.1.row_ref, bf16[2048,128]{1,0:T(8,128)(2,1)S(1)} %get-tuple-element.71.keys, bf16[128,2048]{1,0:T(8,128)(2,1)S(1)} %get-tuple-element.72.keys_t, ...), custom_call_target="tpu_custom_call" | custom-call | flops 4000000000 | tf_op jit(solution)/shard_map/attend_last/pallas_call | solution.py:661
  50.2 1.7 %collective-permute-start.15 = (bf16[2,128,256]{2,1,0:T(8,128)(2,1)S(1)}, bf16[2,128,256]{2,1,0:T(8,128)(2,1)S(1)}, u32[]{:S(2)}, u32[]{:S(2)}) collective-permute-start(bf16[2,128,256]{2,1,0:T(8,128)(2,1)S(1)} %get-tuple-element.87), channel_id=1, source_target_pairs={{0,12},{2,14},{4,8},{6,10},{8,4},{10,6},{12,0},{14,2},{16,28},{18,... | collective-permute-start | bytes 393224 | tf_op jit(solution)/shard_map/ppermute | solution.py:221
  55.6 3.0 %collective-permute-done.14.refs_2_ = bf16[2,128,256]{2,1,0:T(8,128)(2,1)S(1)} collective-permute-done((bf16[2,128,256]{2,1,0:T(8,128)(2,1)S(1)}, bf16[2,128,256]{2,1,0:T(8,128)(2,1)S(1)}, u32[]{:S(2)}, u32[]{:S(2)}) %collective-permute-start.14) | collective-permute-done | bytes 131104 | tf_op jit(solution)/shard_map/ppermute | solution.py:221
  58.6 3.2 %collective-permute-done.15.refs_3_ = bf16[2,128,256]{2,1,0:T(8,128)(2,1)S(1)} collective-permute-done((bf16[2,128,256]{2,1,0:T(8,128)(2,1)S(1)}, bf16[2,128,256]{2,1,0:T(8,128)(2,1)S(1)}, u32[]{:S(2)}, u32[]{:S(2)}) %collective-permute-start.15) | collective-permute-done | bytes 131104 | tf_op jit(solution)/shard_map/ppermute | solution.py:221
  62.0 1.6 %collective-permute-start.22 = (bf16[256,1024]{1,0:T(8,128)(2,1)S(1)}, bf16[256,1024]{1,0:T(8,128)(2,1)S(1)}, u32[]{:S(2)}, u32[]{:S(2)}) collective-permute-start(bf16[256,1024]{1,0:T(8,128)(2,1)S(1)} %turn_features.1.own_ref), channel_id=1, source_target_pairs={{0,1},{1,0},{2,3},{3,2},{4,5},{5,4},{6,7},{7,6},{8,9},{9,8},{10,11... | collective-permute-start | bytes 1572872 | tf_op jit(solution)/shard_map/ppermute | solution.py:225
  64.7 1.9 %collective-permute-done.20.far_ref = bf16[1024,128]{1,0:T(8,128)(2,1)S(1)} collective-permute-done((bf16[1024,128]{1,0:T(8,128)(2,1)S(1)}, bf16[1024,128]{1,0:T(8,128)(2,1)S(1)}, u32[]{:S(2)}, u32[]{:S(2)}) %collective-permute-start.20) | collective-permute-done | bytes 262176 | tf_op jit(solution)/shard_map/ppermute | solution.py:221
  68.0 2.1 %collective-permute-start.25 = (bf16[1024,128]{1,0:T(8,128)(2,1)S(1)}, bf16[1024,128]{1,0:T(8,128)(2,1)S(1)}, u32[]{:S(2)}, u32[]{:S(2)}) collective-permute-start(bf16[1024,128]{1,0:T(8,128)(2,1)S(1)} %sum_halves.1.refs_0_), channel_id=1, source_target_pairs={{0,12},{2,14},{4,8},{6,10},{8,4},{10,6},{12,0},{14,2},{16,28},{18,... | collective-permute-start | bytes 786440 | tf_op jit(solution)/shard_map/ppermute | solution.py:221
  71.5 2.6 %collective-permute-done.21.far_ref = bf16[4,128,128]{2,1,0:T(8,128)(2,1)S(1)} collective-permute-done((bf16[4,128,128]{2,1,0:T(8,128)(2,1)S(1)}, bf16[4,128,128]{2,1,0:T(8,128)(2,1)S(1)}, u32[]{:S(2)}, u32[]{:S(2)}) %collective-permute-start.21) | collective-permute-done | bytes 131104 | tf_op jit(solution)/shard_map/ppermute | solution.py:221
  74.6 5.2 %collective-permute-done.25.refs_3_ = bf16[1024,128]{1,0:T(8,128)(2,1)S(1)} collective-permute-done((bf16[1024,128]{1,0:T(8,128)(2,1)S(1)}, bf16[1024,128]{1,0:T(8,128)(2,1)S(1)}, u32[]{:S(2)}, u32[]{:S(2)}) %collective-permute-start.25) | collective-permute-done | bytes 262176 | tf_op jit(solution)/shard_map/ppermute | solution.py:221
  79.8 3.2 %collective-permute-done.24.refs_2_ = bf16[1024,128]{1,0:T(8,128)(2,1)S(1)} collective-permute-done((bf16[1024,128]{1,0:T(8,128)(2,1)S(1)}, bf16[1024,128]{1,0:T(8,128)(2,1)S(1)}, u32[]{:S(2)}, u32[]{:S(2)}) %collective-permute-start.24) | collective-permute-done | bytes 262176 | tf_op jit(solution)/shard_map/ppermute | solution.py:221
  84.1 1.6 %collective-permute-start.26 = (bf16[4,128,128]{2,1,0:T(8,128)(2,1)S(1)}, bf16[4,128,128]{2,1,0:T(8,128)(2,1)S(1)}, u32[]{:S(2)}, u32[]{:S(2)}) collective-permute-start(bf16[4,128,128]{2,1,0:T(8,128)(2,1)S(1)} %pad_maximum_fusion.1.own_ref), channel_id=1, source_target_pairs={{0,1},{1,0},{2,3},{3,2},{4,5},{5,4},{6,7},{7,6},{8,9},{9,8},{10,11... | collective-permute-start | bytes 393224 | tf_op jit(solution)/shard_map/ppermute | solution.py:225
  86.6 3.5 %collective-permute-done.26.other_ref = bf16[4,128,128]{2,1,0:T(8,128)(2,1)S(1)} collective-permute-done((bf16[4,128,128]{2,1,0:T(8,128)(2,1)S(1)}, bf16[4,128,128]{2,1,0:T(8,128)(2,1)S(1)}, u32[]{:S(2)}, u32[]{:S(2)}) %collective-permute-start.26) | collective-permute-done | bytes 131104 | tf_op jit(solution)/shard_map/ppermute | solution.py:225
  90.1 2.3 %input_grad.1 = bf16[128,2048]{1,0:T(8,128)(2,1)} custom-call(bf16[4,128,128]{2,1,0:T(8,128)(2,1)S(1)} %pad_maximum_fusion.1.own_ref, bf16[4,128,128]{2,1,0:T(8,128)(2,1)S(1)} %collective-permute-done.26.other_ref, bf16[4096,512]{1,0:T(8,128)(2,1)S(1)} %copy-done, bf16[1024,512]{1,0:T(8,128)(2,1)S(1)} %collective-permute-done.4.w_near, ...), custom_call_target="tpu_custom_call" | custom-call | flops 536870912 | bytes 5242880 | tf_op jit(solution)/shard_map/input_grad/pallas_call | solution.py:738
  (75 shorter events, 22.0 us)
Async XLA Ops:
  9.8 6.5 %collective-permute-start.3 = (bf16[144,256]{1,0:T(8,128)(2,1)}, bf16[144,256]{1,0:T(8,128)(2,1)S(1)}, u32[]{:S(2)}, u32[]{:S(2)}) collective-permute-start(bf16[144,256]{1,0:T(8,128)(2,1)} %get-tuple-element.65), channel_id=1, source_target_pairs={{0,12},{2,14},{4,8},{6,10},{8,4},{10,6},{12,0},{14,2},{16,28},{18,... | collective-permute-start | bytes 221192 | tf_op jit(solution)/shard_map/ppermute | solution.py:221
  10.9 13.3 %collective-permute-start.7 = (bf16[288,256]{1,0:T(8,128)(2,1)S(1)}, bf16[288,256]{1,0:T(8,128)(2,1)S(1)}, u32[]{:S(2)}, u32[]{:S(2)}) collective-permute-start(bf16[288,256]{1,0:T(8,128)(2,1)S(1)} %get-tuple-element.113.refs_3_), channel_id=1, source_target_pairs={{0,16},{2,18},{4,20},{6,22},{8,24},{10,26},{12,28},{14,30},{16,0},... | collective-permute-start | bytes 442376 | tf_op jit(solution)/shard_map/ppermute | solution.py:221
  16.4 10.2 %collective-permute-start.8 = (bf16[288,256]{1,0:T(8,128)(2,1)S(1)}, bf16[288,256]{1,0:T(8,128)(2,1)S(1)}, u32[]{:S(2)}, u32[]{:S(2)}) collective-permute-start(bf16[288,256]{1,0:T(8,128)(2,1)S(1)} %get-tuple-element.109.refs_4_), channel_id=1, source_target_pairs={{0,16},{2,18},{4,20},{6,22},{8,24},{10,26},{12,28},{14,30},{16,0},... | collective-permute-start | bytes 442376 | tf_op jit(solution)/shard_map/ppermute | solution.py:221
  18.7 7.9 %collective-permute-start.5 = (bf16[128,1024]{1,0:T(8,128)(2,1)S(1)}, bf16[128,1024]{1,0:T(8,128)(2,1)S(1)}, u32[]{:S(2)}, u32[]{:S(2)}) collective-permute-start(bf16[128,1024]{1,0:T(8,128)(2,1)S(1)} %get-tuple-element.68), channel_id=1, source_target_pairs={{0,4},{2,6},{4,0},{6,2},{8,12},{10,14},{12,8},{14,10},{16,20},{18,... | collective-permute-start | bytes 786440 | tf_op jit(solution)/shard_map/ppermute | solution.py:221
  19.3 9.6 %collective-permute-start.6 = (bf16[128,1024]{1,0:T(8,128)(2,1)S(1)}, bf16[128,1024]{1,0:T(8,128)(2,1)S(1)}, u32[]{:S(2)}, u32[]{:S(2)}) collective-permute-start(bf16[128,1024]{1,0:T(8,128)(2,1)S(1)} %get-tuple-element.69), channel_id=1, source_target_pairs={{0,8},{2,10},{4,12},{6,14},{8,0},{10,2},{12,4},{14,6},{16,24},{18,... | collective-permute-start | bytes 786440 | tf_op jit(solution)/shard_map/ppermute | solution.py:221
  21.8 22.9 %collective-permute-start.4 = (bf16[1024,512]{1,0:T(8,128)(2,1)}, bf16[1024,512]{1,0:T(8,128)(2,1)S(1)}, u32[]{:S(2)}, u32[]{:S(2)}) collective-permute-start(bf16[1024,512]{1,0:T(8,128)(2,1)} %pack_weights.1), channel_id=1, source_target_pairs={{0,1},{1,0},{2,3},{3,2},{4,5},{5,4},{6,7},{7,6},{8,9},{9,8},{10,11... | collective-permute-start | bytes 3145736 | tf_op jit(solution)/shard_map/ppermute | solution.py:225
  28.9 14.6 %collective-permute-start.1 = (bf16[128,1024]{1,0:T(8,128)(2,1)S(1)}, bf16[128,1024]{1,0:T(8,128)(2,1)S(1)}, u32[]{:S(2)}, u32[]{:S(2)}) collective-permute-start(bf16[128,1024]{1,0:T(8,128)(2,1)S(1)} %get-tuple-element.63), channel_id=1, source_target_pairs={{0,12},{2,14},{4,8},{6,10},{8,4},{10,6},{12,0},{14,2},{16,28},{18,... | collective-permute-start | bytes 786440 | tf_op jit(solution)/shard_map/ppermute | solution.py:221
  29.5 18.6 %collective-permute-start.10 = (bf16[4,128,256]{2,1,0:T(8,128)(2,1)S(1)}, bf16[4,128,256]{2,1,0:T(8,128)(2,1)S(1)}, u32[]{:S(2)}, u32[]{:S(2)}) collective-permute-start(bf16[4,128,256]{2,1,0:T(8,128)(2,1)S(1)} %get-tuple-element.78), channel_id=1, source_target_pairs={{0,16},{2,18},{4,20},{6,22},{8,24},{10,26},{12,28},{14,30},{16,0},... | collective-permute-start | bytes 786440 | tf_op jit(solution)/shard_map/ppermute | solution.py:221
  39.7 8.5 %collective-permute-start.11 = (bf16[128,512]{1,0:T(8,128)(2,1)S(1)}, bf16[128,512]{1,0:T(8,128)(2,1)S(1)}, u32[]{:S(2)}, u32[]{:S(2)}) collective-permute-start(bf16[128,512]{1,0:T(8,128)(2,1)S(1)} %get-tuple-element.80), channel_id=1, source_target_pairs={{0,4},{2,6},{4,0},{6,2},{8,12},{10,14},{12,8},{14,10},{16,20},{18,... | collective-permute-start | bytes 393224 | tf_op jit(solution)/shard_map/ppermute | solution.py:221
  40.6 7.6 %collective-permute-start.12 = (bf16[128,512]{1,0:T(8,128)(2,1)S(1)}, bf16[128,512]{1,0:T(8,128)(2,1)S(1)}, u32[]{:S(2)}, u32[]{:S(2)}) collective-permute-start(bf16[128,512]{1,0:T(8,128)(2,1)S(1)} %get-tuple-element.81), channel_id=1, source_target_pairs={{0,8},{2,10},{4,12},{6,14},{8,0},{10,2},{12,4},{14,6},{16,24},{18,... | collective-permute-start | bytes 393224 | tf_op jit(solution)/shard_map/ppermute | solution.py:221
  49.8 8.9 %collective-permute-start.14 = (bf16[2,128,256]{2,1,0:T(8,128)(2,1)S(1)}, bf16[2,128,256]{2,1,0:T(8,128)(2,1)S(1)}, u32[]{:S(2)}, u32[]{:S(2)}) collective-permute-start(bf16[2,128,256]{2,1,0:T(8,128)(2,1)S(1)} %get-tuple-element.86), channel_id=1, source_target_pairs={{0,8},{2,10},{4,12},{6,14},{8,0},{10,2},{12,4},{14,6},{16,24},{18,... | collective-permute-start | bytes 393224 | tf_op jit(solution)/shard_map/ppermute | solution.py:221
  50.2 11.6 %collective-permute-start.15 = (bf16[2,128,256]{2,1,0:T(8,128)(2,1)S(1)}, bf16[2,128,256]{2,1,0:T(8,128)(2,1)S(1)}, u32[]{:S(2)}, u32[]{:S(2)}) collective-permute-start(bf16[2,128,256]{2,1,0:T(8,128)(2,1)S(1)} %get-tuple-element.87), channel_id=1, source_target_pairs={{0,12},{2,14},{4,8},{6,10},{8,4},{10,6},{12,0},{14,2},{16,28},{18,... | collective-permute-start | bytes 393224 | tf_op jit(solution)/shard_map/ppermute | solution.py:221
  52.0 14.6 %collective-permute-start.20 = (bf16[1024,128]{1,0:T(8,128)(2,1)S(1)}, bf16[1024,128]{1,0:T(8,128)(2,1)S(1)}, u32[]{:S(2)}, u32[]{:S(2)}) collective-permute-start(bf16[1024,128]{1,0:T(8,128)(2,1)S(1)} %get-tuple-element.94), channel_id=1, source_target_pairs={{0,16},{2,18},{4,20},{6,22},{8,24},{10,26},{12,28},{14,30},{16,0},... | collective-permute-start | bytes 786440 | tf_op jit(solution)/shard_map/ppermute | solution.py:221
  53.2 10.4 %collective-permute-start.17 = (bf16[2,128,128]{2,1,0:T(8,128)(2,1)S(1)}, bf16[2,128,128]{2,1,0:T(8,128)(2,1)S(1)}, u32[]{:S(2)}, u32[]{:S(2)}) collective-permute-start(bf16[2,128,128]{2,1,0:T(8,128)(2,1)S(1)} %get-tuple-element.90), channel_id=1, source_target_pairs={{0,4},{2,6},{4,0},{6,2},{8,12},{10,14},{12,8},{14,10},{16,20},{18,... | collective-permute-start | bytes 196616 | tf_op jit(solution)/shard_map/ppermute | solution.py:221
  54.3 9.7 %collective-permute-start.18 = (bf16[2,128,128]{2,1,0:T(8,128)(2,1)S(1)}, bf16[2,128,128]{2,1,0:T(8,128)(2,1)S(1)}, u32[]{:S(2)}, u32[]{:S(2)}) collective-permute-start(bf16[2,128,128]{2,1,0:T(8,128)(2,1)S(1)} %get-tuple-element.91), channel_id=1, source_target_pairs={{0,8},{2,10},{4,12},{6,14},{8,0},{10,2},{12,4},{14,6},{16,24},{18,... | collective-permute-start | bytes 196616 | tf_op jit(solution)/shard_map/ppermute | solution.py:221
  58.6 6.0 %collective-permute-start.19 = (bf16[2,128,128]{2,1,0:T(8,128)(2,1)S(1)}, bf16[2,128,128]{2,1,0:T(8,128)(2,1)S(1)}, u32[]{:S(2)}, u32[]{:S(2)}) collective-permute-start(bf16[2,128,128]{2,1,0:T(8,128)(2,1)S(1)} %get-tuple-element.92), channel_id=1, source_target_pairs={{0,12},{2,14},{4,8},{6,10},{8,4},{10,6},{12,0},{14,2},{16,28},{18,... | collective-permute-start | bytes 196616 | tf_op jit(solution)/shard_map/ppermute | solution.py:221
  62.0 12.6 %collective-permute-start.22 = (bf16[256,1024]{1,0:T(8,128)(2,1)S(1)}, bf16[256,1024]{1,0:T(8,128)(2,1)S(1)}, u32[]{:S(2)}, u32[]{:S(2)}) collective-permute-start(bf16[256,1024]{1,0:T(8,128)(2,1)S(1)} %turn_features.1.own_ref), channel_id=1, source_target_pairs={{0,1},{1,0},{2,3},{3,2},{4,5},{5,4},{6,7},{7,6},{8,9},{9,8},{10,11... | collective-permute-start | bytes 1572872 | tf_op jit(solution)/shard_map/ppermute | solution.py:225
  66.6 7.4 %collective-permute-start.21 = (bf16[4,128,128]{2,1,0:T(8,128)(2,1)S(1)}, bf16[4,128,128]{2,1,0:T(8,128)(2,1)S(1)}, u32[]{:S(2)}, u32[]{:S(2)}) collective-permute-start(bf16[4,128,128]{2,1,0:T(8,128)(2,1)S(1)} %pad_maximum_fusion), channel_id=1, source_target_pairs={{0,16},{2,18},{4,20},{6,22},{8,24},{10,26},{12,28},{14,30},{16,0},... | collective-permute-start | bytes 393224 | tf_op jit(solution)/shard_map/ppermute | solution.py:221
  68.0 11.8 %collective-permute-start.25 = (bf16[1024,128]{1,0:T(8,128)(2,1)S(1)}, bf16[1024,128]{1,0:T(8,128)(2,1)S(1)}, u32[]{:S(2)}, u32[]{:S(2)}) collective-permute-start(bf16[1024,128]{1,0:T(8,128)(2,1)S(1)} %sum_halves.1.refs_0_), channel_id=1, source_target_pairs={{0,12},{2,14},{4,8},{6,10},{8,4},{10,6},{12,0},{14,2},{16,28},{18,... | collective-permute-start | bytes 786440 | tf_op jit(solution)/shard_map/ppermute | solution.py:221
  70.1 12.9 %collective-permute-start.24 = (bf16[1024,128]{1,0:T(8,128)(2,1)S(1)}, bf16[1024,128]{1,0:T(8,128)(2,1)S(1)}, u32[]{:S(2)}, u32[]{:S(2)}) collective-permute-start(bf16[1024,128]{1,0:T(8,128)(2,1)S(1)} %sum_halves.1.refs_0_), channel_id=1, source_target_pairs={{0,8},{2,10},{4,12},{6,14},{8,0},{10,2},{12,4},{14,6},{16,24},{18,... | collective-permute-start | bytes 786440 | tf_op jit(solution)/shard_map/ppermute | solution.py:221
  70.1 12.9 %collective-permute-start.23 = (bf16[1024,128]{1,0:T(8,128)(2,1)S(1)}, bf16[1024,128]{1,0:T(8,128)(2,1)S(1)}, u32[]{:S(2)}, u32[]{:S(2)}) collective-permute-start(bf16[1024,128]{1,0:T(8,128)(2,1)S(1)} %sum_halves.1.refs_0_), channel_id=1, source_target_pairs={{0,4},{2,6},{4,0},{6,2},{8,12},{10,14},{12,8},{14,10},{16,20},{18,... | collective-permute-start | bytes 786440 | tf_op jit(solution)/shard_map/ppermute | solution.py:221
  74.1 16.0 %collective-permute-start.27 = (bf16[1024,512]{1,0:T(8,128)(2,1)S(1)}, bf16[1024,512]{1,0:T(8,128)(2,1)S(1)}, u32[]{:S(2)}, u32[]{:S(2)}) collective-permute-start(bf16[1024,512]{1,0:T(8,128)(2,1)S(1)} %collective-permute-done.4.w_near), channel_id=1, source_target_pairs={{0,2},{2,0},{4,6},{6,4},{8,10},{10,8},{12,14},{14,12},{16,18},{18,... | collective-permute-start | bytes 3145736 | tf_op jit(solution)/shard_map/ppermute | solution.py:221
  84.0 8.4 %collective-permute-start.28 = (f32[256,512]{1,0:T(8,128)S(1)}, f32[256,512]{1,0:T(8,128)S(1)}, u32[]{:S(2)}, u32[]{:S(2)}) collective-permute-start(f32[256,512]{1,0:T(8,128)S(1)} %get-tuple-element.99), channel_id=1, source_target_pairs={{0,2},{2,0},{4,6},{6,4},{8,10},{10,8},{12,14},{14,12},{16,18},{18,... | collective-permute-start | bytes 1572872 | tf_op jit(solution)/shard_map/ppermute | solution.py:221
  85.7 6.6 %collective-permute-start.29 = (bf16[128,512]{1,0:T(8,128)(2,1)S(1)}, bf16[128,512]{1,0:T(8,128)(2,1)S(1)}, u32[]{:S(2)}, u32[]{:S(2)}) collective-permute-start(bf16[128,512]{1,0:T(8,128)(2,1)S(1)} %get-tuple-element.104), channel_id=1, source_target_pairs={{0,12},{2,14},{4,8},{6,10},{8,4},{10,6},{12,0},{14,2},{16,28},{18,... | collective-permute-start | bytes 393224 | tf_op jit(solution)/shard_map/ppermute | solution.py:221
  (11 other events, 128.8 us)

commit v7 on v6

--- a/solution.py
+++ b/solution.py
@@ -357,8 +357,11 @@
         lanes = lax.broadcasted_iota(jnp.int32, (1, GROUP * BLK), 1)
         position = first + (lanes & (BLK - 1))
         start = document_start(position)
-        low = document_start(first) // TILE
-        count = (first + BLK - 1) // TILE + 1 - low
+        low = document_start(first) // HD * HD
+        count = (first + BLK - low + TILE - 1) // TILE
+
+        def rows_of(k):
+            return pl.ds(pl.multiple_of(low + k * TILE, HD), TILE)
 
         def run(over_tiles):
             query = q_rows[block]
@@ -366,9 +369,9 @@
             zeros = jnp.zeros((8, GROUP * BLK), jnp.float32)
 
             def visit_scores(k, row_max):
-                here = columns(low + k, TILE)
+                here = rows_of(k)
                 raw = dot_nt(keys[here], query)
-                row = (low + k) * TILE + lax.broadcasted_iota(jnp.int32, raw.shape, 0)
+                row = low + k * TILE + lax.broadcasted_iota(jnp.int32, raw.shape, 0)
                 raw = jnp.where((row <= position) & (row >= start), raw, masked_fill)
                 scores[k] = raw
                 d_prob[k] = dot_nt(values[here], grad)
@@ -390,7 +393,7 @@
             delta = jnp.sum(weighted, axis=0, keepdims=True) * inverse
 
             def visit_grads(k, dq):
-                here = columns(low + k, TILE)
+                here = rows_of(k)
                 prob = scores[k] * inverse
                 score_bf = (prob * (d_prob[k] - delta)).astype(jnp.bfloat16)
                 dk[here] += jnp.dot(score_bf, query, preferred_element_type=jnp.float32)
@@ -452,6 +455,10 @@
         there = pl.ds(first_row(block), BLK)
         keys[there] = pair_refs[part // 2][here, :HD]
         values[there] = pair_refs[part // 2][here, HD:]
+    beyond = pl.ds(4 * GROUP * ROWS, HD)
+    keys[beyond] = jnp.zeros((HD, HD), jnp.bfloat16)
+    keys_t[:, beyond] = jnp.zeros((HD, HD), jnp.bfloat16)
+    values[beyond] = jnp.zeros((HD, HD), jnp.bfloat16)
     for tile in range(keys.shape[0] // TILE):
         here = pl.ds(tile * TILE, TILE)
         keys_t[:, here] = keys[here].astype(jnp.float32).T.astype(jnp.bfloat16)
@@ -629,8 +636,9 @@
     far_features = swap(far_features, Z_HI)
 
     row_grad = shaped((ROWS, GROUP * HD))
-    sorted_rows = shaped((total_rows, HD))
-    sums = shaped((total_rows, HD), jnp.float32)
+    padded_rows = total_rows + HD
+    sorted_rows = shaped((padded_rows, HD))
+    sums = shaped((padded_rows, HD), jnp.float32)
     half_sums = shaped((half, 2 * HD), jnp.float32)
 
     def attend_scratch(blocks):
@@ -649,7 +657,7 @@
     *row_grads, keys, keys_t, all_values, dk_first, dv_first, marks = pl.pallas_call(
         attend_first,
         out_shape=[row_grad] * (GROUP - 1)
-        + [sorted_rows, shaped((HD, total_rows)), sorted_rows, sums, sums]
+        + [sorted_rows, shaped((HD, padded_rows)), sorted_rows, sums, sums]
         + [shaped((4 * GROUP, HD), jnp.int32)],
         in_specs=[smem] + [vmem] * (GROUP + 4),
         out_specs=[vmem] * (GROUP + 5),
@@ -663,7 +671,7 @@
         out_shape=[row_grad, half_sums, half_sums],
         in_specs=[smem] + [vmem] * 7,
         out_specs=[vmem] * 3,
-        scratch_shapes=[VMEM((total_rows, HD), jnp.float32)] * 2 + attend_scratch(2),
+        scratch_shapes=[VMEM((padded_rows, HD), jnp.float32)] * 2 + attend_scratch(2),
         compiler_params=limits(20),
         cost_estimate=pl.CostEstimate(flops=ATTEND_COST, bytes_accessed=0, transcendentals=0),
         name="attend_last",
@@ -681,6 +689,7 @@
         name="sum_cores",
     )(kept, swap(sent, CORE))
     dk_far = swap(dk_near, Z_HI)
+    w_far = swap(after(w_near, sent), CORE)
     value_grads = with_partners(value_grads)
     value_far = jnp.stack([grad[1] for grad in value_grads])
 
@@ -712,9 +721,8 @@
         cost_estimate=pl.CostEstimate(flops=1_000_000, bytes_accessed=0, transcendentals=0),
         name="sum_halves",
     )(dk_sum, dk_far)
-    key_grad = after(key_grad, own_features, value_far)
+    key_grad = after(key_grad, own_features, value_far, w_far)
     key_grads = with_partners([key_grad] * GROUP)
-    w_far = swap(after(w_near, key_grad), CORE)
     own_key_grad = jnp.stack([key_grads[m][m * ROWS : (m + 1) * ROWS] for m in range(GROUP)])
     other_key_grad = swap_tensor(own_key_grad)
 
@@ -743,7 +751,7 @@
         scratch_shapes=[VMEM((ROWS, kv_columns), jnp.bfloat16)] * 2,
         compiler_params=limits(16),
         cost_estimate=pl.CostEstimate(
-            flops=4 * ROWS * 2048 * kv_columns, bytes_accessed=5 << 20, transcendentals=0
+            flops=8_000_000_000, bytes_accessed=5 << 20, transcendentals=0
         ),
         name="input_grad",
     )(after(own_key_grad, send), other_key_grad, w_key, w_near, w_far)

time: 93.9 us -> 95.9 us (1.021)
  waiting for transfers between devices: 36.5 us -> 40.4 us
  starting transfers between devices: 32.8 us -> 31.5 us
    ppermute x27, waiting for transfers between devices: 31.5 us -> 37 us  [swap(): return lax.ppermute(array, 'dp', [(i, i ^ mask) for i in range(16)])]
    ppermute x3, waiting for transfers between devices: 5.07 us -> 3.41 us  [swap_tensor(): return lax.ppermute(array, 'tensor', [(0, 1), (1, 0)])]
    ppermute x27, starting transfers between devices: 28 us -> 26.8 us  [swap(): return lax.ppermute(array, 'dp', [(i, i ^ mask) for i in range(16)])]
  transfers between devices with their start and end apart: 30 -> 30, of which waited for: 17 -> 15; matrix products, arithmetic and copies ran while one was open for 1% -> 1% of each run, Pallas kernels for 18% -> 17%
where the time goes in v7:
time: 95.9 us; the launch traced here: 95.5 us
  waiting for transfers between devices  40.4 us (42%)
  starting transfers between devices  31.5 us (33%)
  Pallas kernels  21.7 us (23%)
  local copies, waits for them, and re-layouts  1.01 us (1%)
    ppermute x27, waiting for transfers between devices, swap(): return lax.ppermute(array, 'dp', [(i, i ^ mask) for i in range(16)])  37 us
    ppermute x27, starting transfers between devices, swap(): return lax.ppermute(array, 'dp', [(i, i ^ mask) for i in range(16)])  26.8 us
    pallas_call x1, Pallas kernels, on_device_by_heads(): pl.pallas_call(attend_first, out_shape=[row_grad] * (GROUP - 1) + [sorted...  6.83 us
    ppermute x3, starting transfers between devices, swap_tensor(): return lax.ppermute(array, 'tensor', [(0, 1), (1, 0)])  4.75 us
    pallas_call x1, Pallas kernels, on_device_by_heads(): pl.pallas_call(project_keys, out_shape=[shaped((MARKED, 2 * HD))] * GROUP...  4.51 us
    ppermute x3, waiting for transfers between devices, swap_tensor(): return lax.ppermute(array, 'tensor', [(0, 1), (1, 0)])  3.41 us
    pallas_call x1, Pallas kernels, on_device_by_heads(): pl.pallas_call(attend_last, out_shape=[row_grad, half_sums, half_sums], i...  3.19 us
    pallas_call x1, Pallas kernels, on_device_by_heads(): pl.pallas_call(input_grad, out_shape=shaped((ROWS, features // 2)), in_sp...  2.28 us
  transfers between devices with their start and end apart: 30, of which 15 were waited for; matrix products, arithmetic and copies ran while one was open for 1% of the time, Pallas kernels for 17%

profile of v7, /device:TPU:0, one launch (start us, length us, event | category | flops | bytes accessed | tf_op | source)
XLA Modules:
  0.0 95.5 jit_solution(4109465884314724042)
XLA Ops:
  0.7 4.5 %project_keys.1 = (bf16[144,256]{1,0:T(8,128)(2,1)}, bf16[144,256]{1,0:T(8,128)(2,1)}, bf16[144,256]{1,0:T(8,128)(2,1)}, bf16[144,256]{1,0:T(8,128)(2,1)}) custom-call(s32[2]{0:T(128)} %pos_ref.1, bf16[128,4096]{1,0:T(8,128)(2,1)} %inputs_ref.2, bf16[128,512]{1,0:T(8,128)(2,1)} %values_ref.1, bf16[4096,512]{1,0:T(8,128)(2,1)} %w_own.1), custom_call_target="tpu_custom_call" | custom-call | flops 536870912 | bytes 4194304 | tf_op jit(solution)/shard_map/project_keys/pallas_call | solution.py:579
  5.2 3.0 %collective-permute-start = (bf16[144,256]{1,0:T(8,128)(2,1)}, bf16[144,256]{1,0:T(8,128)(2,1)S(1)}, u32[]{:S(2)}, u32[]{:S(2)}) collective-permute-start(bf16[144,256]{1,0:T(8,128)(2,1)} %get-tuple-element.60), channel_id=1, source_target_pairs={{0,4},{2,6},{4,0},{6,2},{8,12},{10,14},{12,8},{14,10},{16,20},{18,... | collective-permute-start | bytes 221192 | tf_op jit(solution)/shard_map/ppermute | solution.py:221
  8.2 1.6 %collective-permute-start.2 = (bf16[144,256]{1,0:T(8,128)(2,1)}, bf16[144,256]{1,0:T(8,128)(2,1)S(1)}, u32[]{:S(2)}, u32[]{:S(2)}) collective-permute-start(bf16[144,256]{1,0:T(8,128)(2,1)} %get-tuple-element.64), channel_id=1, source_target_pairs={{0,8},{2,10},{4,12},{6,14},{8,0},{10,2},{12,4},{14,6},{16,24},{18,... | collective-permute-start | bytes 221192 | tf_op jit(solution)/shard_map/ppermute | solution.py:221
  10.8 3.1 %collective-permute-start.7 = (bf16[288,256]{1,0:T(8,128)(2,1)S(1)}, bf16[288,256]{1,0:T(8,128)(2,1)S(1)}, u32[]{:S(2)}, u32[]{:S(2)}) collective-permute-start(bf16[288,256]{1,0:T(8,128)(2,1)S(1)} %get-tuple-element.113.refs_3_), channel_id=1, source_target_pairs={{0,16},{2,18},{4,20},{6,22},{8,24},{10,26},{12,28},{14,30},{16,0},... | collective-permute-start | bytes 442376 | tf_op jit(solution)/shard_map/ppermute | solution.py:221
  13.9 2.4 %collective-permute-done.3 = bf16[144,256]{1,0:T(8,128)(2,1)S(1)} collective-permute-done((bf16[144,256]{1,0:T(8,128)(2,1)}, bf16[144,256]{1,0:T(8,128)(2,1)S(1)}, u32[]{:S(2)}, u32[]{:S(2)}) %collective-permute-start.3) | collective-permute-done | bytes 73760 | tf_op jit(solution)/shard_map/ppermute | solution.py:221
  16.3 2.3 %collective-permute-start.8 = (bf16[288,256]{1,0:T(8,128)(2,1)S(1)}, bf16[288,256]{1,0:T(8,128)(2,1)S(1)}, u32[]{:S(2)}, u32[]{:S(2)}) collective-permute-start(bf16[288,256]{1,0:T(8,128)(2,1)S(1)} %get-tuple-element.109.refs_4_), channel_id=1, source_target_pairs={{0,16},{2,18},{4,20},{6,22},{8,24},{10,26},{12,28},{14,30},{16,0},... | collective-permute-start | bytes 442376 | tf_op jit(solution)/shard_map/ppermute | solution.py:221
  19.5 2.3 %pack_weights.1 = bf16[1024,512]{1,0:T(8,128)(2,1)} custom-call(bf16[4096,512]{1,0:T(8,128)(2,1)} %w_own.1), custom_call_target="tpu_custom_call" | custom-call | tf_op jit(solution)/shard_map/pack_weights/pallas_call | solution.py:624
  21.8 1.6 %collective-permute-start.4 = (bf16[1024,512]{1,0:T(8,128)(2,1)}, bf16[1024,512]{1,0:T(8,128)(2,1)S(1)}, u32[]{:S(2)}, u32[]{:S(2)}) collective-permute-start(bf16[1024,512]{1,0:T(8,128)(2,1)} %pack_weights.1), channel_id=1, source_target_pairs={{0,1},{1,0},{2,3},{3,2},{4,5},{5,4},{6,7},{7,6},{8,9},{9,8},{10,11... | collective-permute-start | bytes 3145736 | tf_op jit(solution)/shard_map/ppermute | solution.py:225
  24.2 2.4 %collective-permute-done.8.refs_6_ = bf16[288,256]{1,0:T(8,128)(2,1)S(1)} collective-permute-done((bf16[288,256]{1,0:T(8,128)(2,1)S(1)}, bf16[288,256]{1,0:T(8,128)(2,1)S(1)}, u32[]{:S(2)}, u32[]{:S(2)}) %collective-permute-start.8) | collective-permute-done | bytes 147488 | tf_op jit(solution)/shard_map/ppermute | solution.py:221
  26.6 2.3 %collective-permute-done.6.refs_2_ = bf16[128,1024]{1,0:T(8,128)(2,1)S(1)} collective-permute-done((bf16[128,1024]{1,0:T(8,128)(2,1)S(1)}, bf16[128,1024]{1,0:T(8,128)(2,1)S(1)}, u32[]{:S(2)}, u32[]{:S(2)}) %collective-permute-start.6) | collective-permute-done | bytes 262176 | tf_op jit(solution)/shard_map/ppermute | solution.py:221
  29.4 3.2 %collective-permute-start.10 = (bf16[4,128,256]{2,1,0:T(8,128)(2,1)S(1)}, bf16[4,128,256]{2,1,0:T(8,128)(2,1)S(1)}, u32[]{:S(2)}, u32[]{:S(2)}) collective-permute-start(bf16[4,128,256]{2,1,0:T(8,128)(2,1)S(1)} %get-tuple-element.78), channel_id=1, source_target_pairs={{0,16},{2,18},{4,20},{6,22},{8,24},{10,26},{12,28},{14,30},{16,0},... | collective-permute-start | bytes 786440 | tf_op jit(solution)/shard_map/ppermute | solution.py:221
  32.6 6.8 %attend_first.1 = (bf16[128,512]{1,0:T(8,128)(2,1)S(1)}, bf16[128,512]{1,0:T(8,128)(2,1)S(1)}, bf16[128,512]{1,0:T(8,128)(2,1)S(1)}, bf16[2176,128]{1,0:T(8,128)...) custom-call(s32[4]{0:T(128)S(1)} %copy-done.4, ...), custom_call_target="tpu_custom_call" | custom-call | flops 4000000000 | tf_op jit(solution)/shard_map/attend_first/pallas_call | solution.py:657
  40.3 3.2 %collective-permute-done.1.row_ref = bf16[128,1024]{1,0:T(8,128)(2,1)S(1)} collective-permute-done((bf16[128,1024]{1,0:T(8,128)(2,1)S(1)}, bf16[128,1024]{1,0:T(8,128)(2,1)S(1)}, u32[]{:S(2)}, u32[]{:S(2)}) %collective-permute-start.1) | collective-permute-done | bytes 262176 | tf_op jit(solution)/shard_map/ppermute | solution.py:221
  44.6 3.2 %attend_last.1 = (bf16[128,512]{1,0:T(8,128)(2,1)S(1)}, f32[1024,256]{1,0:T(8,128)S(1)}, f32[1024,256]{1,0:T(8,128)S(1)}) custom-call(s32[4]{0:T(128)S(1)} %copy-done.4, bf16[128,1024]{1,0:T(8,128)(2,1)S(1)} %collective-permute-done.1.row_ref, bf16[2176,128]{1,0:T(8,128)(2,1)S(1)} %get-tuple-element.71.keys, bf16[128,2176]{1,0:T(8,128)(2,1)S(1)} %get-tuple-element.72.keys_t, ...), custom_call_target="tpu_custom_call" | custom-call | flops 4000000000 | tf_op jit(solution)/shard_map/attend_last/pallas_call | solution.py:669
  55.5 4.0 %collective-permute-done.14.refs_2_ = bf16[2,128,256]{2,1,0:T(8,128)(2,1)S(1)} collective-permute-done((bf16[2,128,256]{2,1,0:T(8,128)(2,1)S(1)}, bf16[2,128,256]{2,1,0:T(8,128)(2,1)S(1)}, u32[]{:S(2)}, u32[]{:S(2)}) %collective-permute-start.14) | collective-permute-done | bytes 131104 | tf_op jit(solution)/shard_map/ppermute | solution.py:221
  59.6 1.6 %collective-permute-done.15.refs_3_ = bf16[2,128,256]{2,1,0:T(8,128)(2,1)S(1)} collective-permute-done((bf16[2,128,256]{2,1,0:T(8,128)(2,1)S(1)}, bf16[2,128,256]{2,1,0:T(8,128)(2,1)S(1)}, u32[]{:S(2)}, u32[]{:S(2)}) %collective-permute-start.15) | collective-permute-done | bytes 131104 | tf_op jit(solution)/shard_map/ppermute | solution.py:221
  61.5 5.1 %collective-permute-done.18.refs_6_ = bf16[2,128,128]{2,1,0:T(8,128)(2,1)S(1)} collective-permute-done((bf16[2,128,128]{2,1,0:T(8,128)(2,1)S(1)}, bf16[2,128,128]{2,1,0:T(8,128)(2,1)S(1)}, u32[]{:S(2)}, u32[]{:S(2)}) %collective-permute-start.18) | collective-permute-done | bytes 65568 | tf_op jit(solution)/shard_map/ppermute | solution.py:221
  69.9 2.2 %collective-permute-start.25 = (bf16[1024,128]{1,0:T(8,128)(2,1)S(1)}, bf16[1024,128]{1,0:T(8,128)(2,1)S(1)}, u32[]{:S(2)}, u32[]{:S(2)}) collective-permute-start(bf16[1024,128]{1,0:T(8,128)(2,1)S(1)} %sum_halves.1.refs_0_), channel_id=1, source_target_pairs={{0,8},{2,10},{4,12},{6,14},{8,0},{10,2},{12,4},{14,6},{16,24},{18,... | collective-permute-start | bytes 786440 | tf_op jit(solution)/shard_map/ppermute | solution.py:221
  74.1 6.5 %collective-permute-done.26.refs_3_ = bf16[1024,128]{1,0:T(8,128)(2,1)S(1)} collective-permute-done((bf16[1024,128]{1,0:T(8,128)(2,1)S(1)}, bf16[1024,128]{1,0:T(8,128)(2,1)S(1)}, u32[]{:S(2)}, u32[]{:S(2)}) %collective-permute-start.26) | collective-permute-done | bytes 262176 | tf_op jit(solution)/shard_map/ppermute | solution.py:221
  80.7 4.2 %collective-permute-done.25.refs_2_ = bf16[1024,128]{1,0:T(8,128)(2,1)S(1)} collective-permute-done((bf16[1024,128]{1,0:T(8,128)(2,1)S(1)}, bf16[1024,128]{1,0:T(8,128)(2,1)S(1)}, u32[]{:S(2)}, u32[]{:S(2)}) %collective-permute-start.25) | collective-permute-done | bytes 262176 | tf_op jit(solution)/shard_map/ppermute | solution.py:221
  84.9 1.6 %collective-permute-start.27 = (bf16[4,128,128]{2,1,0:T(8,128)(2,1)S(1)}, bf16[4,128,128]{2,1,0:T(8,128)(2,1)S(1)}, u32[]{:S(2)}, u32[]{:S(2)}) collective-permute-start(bf16[4,128,128]{2,1,0:T(8,128)(2,1)S(1)} %pad_maximum_fusion.1.own_ref), channel_id=1, source_target_pairs={{0,1},{1,0},{2,3},{3,2},{4,5},{5,4},{6,7},{7,6},{8,9},{9,8},{10,11... | collective-permute-start | bytes 393224 | tf_op jit(solution)/shard_map/ppermute | solution.py:225
  87.7 2.3 %collective-permute-done.27.other_ref = bf16[4,128,128]{2,1,0:T(8,128)(2,1)S(1)} collective-permute-done((bf16[4,128,128]{2,1,0:T(8,128)(2,1)S(1)}, bf16[4,128,128]{2,1,0:T(8,128)(2,1)S(1)}, u32[]{:S(2)}, u32[]{:S(2)}) %collective-permute-start.27) | collective-permute-done | bytes 131104 | tf_op jit(solution)/shard_map/ppermute | solution.py:225
  90.0 2.3 %input_grad.1 = bf16[128,2048]{1,0:T(8,128)(2,1)} custom-call(bf16[4,128,128]{2,1,0:T(8,128)(2,1)S(1)} %pad_maximum_fusion.1.own_ref, bf16[4,128,128]{2,1,0:T(8,128)(2,1)S(1)} %collective-permute-done.27.other_ref, bf16[4096,512]{1,0:T(8,128)(2,1)S(1)} %copy-done, bf16[1024,512]{1,0:T(8,128)(2,1)S(1)} %collective-permute-done.4.w_near, ...), custom_call_target="tpu_custom_call" | custom-call | flops 8000000000 | bytes 5242880 | tf_op jit(solution)/shard_map/input_grad/pallas_call | solution.py:746
  92.2 2.2 %collective-permute-done.29.refs_3_ = bf16[128,512]{1,0:T(8,128)(2,1)S(1)} collective-permute-done((bf16[128,512]{1,0:T(8,128)(2,1)S(1)}, bf16[128,512]{1,0:T(8,128)(2,1)S(1)}, u32[]{:S(2)}, u32[]{:S(2)}) %collective-permute-start.29) | collective-permute-done | bytes 131104 | tf_op jit(solution)/shard_map/ppermute | solution.py:221
  (75 shorter events, 20.6 us)
Async XLA Ops:
  9.8 6.5 %collective-permute-start.3 = (bf16[144,256]{1,0:T(8,128)(2,1)}, bf16[144,256]{1,0:T(8,128)(2,1)S(1)}, u32[]{:S(2)}, u32[]{:S(2)}) collective-permute-start(bf16[144,256]{1,0:T(8,128)(2,1)} %get-tuple-element.65), channel_id=1, source_target_pairs={{0,12},{2,14},{4,8},{6,10},{8,4},{10,6},{12,0},{14,2},{16,28},{18,... | collective-permute-start | bytes 221192 | tf_op jit(solution)/shard_map/ppermute | solution.py:221
  10.8 13.3 %collective-permute-start.7 = (bf16[288,256]{1,0:T(8,128)(2,1)S(1)}, bf16[288,256]{1,0:T(8,128)(2,1)S(1)}, u32[]{:S(2)}, u32[]{:S(2)}) collective-permute-start(bf16[288,256]{1,0:T(8,128)(2,1)S(1)} %get-tuple-element.113.refs_3_), channel_id=1, source_target_pairs={{0,16},{2,18},{4,20},{6,22},{8,24},{10,26},{12,28},{14,30},{16,0},... | collective-permute-start | bytes 442376 | tf_op jit(solution)/shard_map/ppermute | solution.py:221
  16.3 10.2 %collective-permute-start.8 = (bf16[288,256]{1,0:T(8,128)(2,1)S(1)}, bf16[288,256]{1,0:T(8,128)(2,1)S(1)}, u32[]{:S(2)}, u32[]{:S(2)}) collective-permute-start(bf16[288,256]{1,0:T(8,128)(2,1)S(1)} %get-tuple-element.109.refs_4_), channel_id=1, source_target_pairs={{0,16},{2,18},{4,20},{6,22},{8,24},{10,26},{12,28},{14,30},{16,0},... | collective-permute-start | bytes 442376 | tf_op jit(solution)/shard_map/ppermute | solution.py:221
  18.7 7.9 %collective-permute-start.5 = (bf16[128,1024]{1,0:T(8,128)(2,1)S(1)}, bf16[128,1024]{1,0:T(8,128)(2,1)S(1)}, u32[]{:S(2)}, u32[]{:S(2)}) collective-permute-start(bf16[128,1024]{1,0:T(8,128)(2,1)S(1)} %get-tuple-element.68), channel_id=1, source_target_pairs={{0,4},{2,6},{4,0},{6,2},{8,12},{10,14},{12,8},{14,10},{16,20},{18,... | collective-permute-start | bytes 786440 | tf_op jit(solution)/shard_map/ppermute | solution.py:221
  19.3 9.6 %collective-permute-start.6 = (bf16[128,1024]{1,0:T(8,128)(2,1)S(1)}, bf16[128,1024]{1,0:T(8,128)(2,1)S(1)}, u32[]{:S(2)}, u32[]{:S(2)}) collective-permute-start(bf16[128,1024]{1,0:T(8,128)(2,1)S(1)} %get-tuple-element.69), channel_id=1, source_target_pairs={{0,8},{2,10},{4,12},{6,14},{8,0},{10,2},{12,4},{14,6},{16,24},{18,... | collective-permute-start | bytes 786440 | tf_op jit(solution)/shard_map/ppermute | solution.py:221
  21.8 22.8 %collective-permute-start.4 = (bf16[1024,512]{1,0:T(8,128)(2,1)}, bf16[1024,512]{1,0:T(8,128)(2,1)S(1)}, u32[]{:S(2)}, u32[]{:S(2)}) collective-permute-start(bf16[1024,512]{1,0:T(8,128)(2,1)} %pack_weights.1), channel_id=1, source_target_pairs={{0,1},{1,0},{2,3},{3,2},{4,5},{5,4},{6,7},{7,6},{8,9},{9,8},{10,11... | collective-permute-start | bytes 3145736 | tf_op jit(solution)/shard_map/ppermute | solution.py:225
  28.9 14.6 %collective-permute-start.1 = (bf16[128,1024]{1,0:T(8,128)(2,1)S(1)}, bf16[128,1024]{1,0:T(8,128)(2,1)S(1)}, u32[]{:S(2)}, u32[]{:S(2)}) collective-permute-start(bf16[128,1024]{1,0:T(8,128)(2,1)S(1)} %get-tuple-element.63), channel_id=1, source_target_pairs={{0,12},{2,14},{4,8},{6,10},{8,4},{10,6},{12,0},{14,2},{16,28},{18,... | collective-permute-start | bytes 786440 | tf_op jit(solution)/shard_map/ppermute | solution.py:221
  29.4 18.4 %collective-permute-start.10 = (bf16[4,128,256]{2,1,0:T(8,128)(2,1)S(1)}, bf16[4,128,256]{2,1,0:T(8,128)(2,1)S(1)}, u32[]{:S(2)}, u32[]{:S(2)}) collective-permute-start(bf16[4,128,256]{2,1,0:T(8,128)(2,1)S(1)} %get-tuple-element.78), channel_id=1, source_target_pairs={{0,16},{2,18},{4,20},{6,22},{8,24},{10,26},{12,28},{14,30},{16,0},... | collective-permute-start | bytes 786440 | tf_op jit(solution)/shard_map/ppermute | solution.py:221
  39.5 8.4 %collective-permute-start.11 = (bf16[128,512]{1,0:T(8,128)(2,1)S(1)}, bf16[128,512]{1,0:T(8,128)(2,1)S(1)}, u32[]{:S(2)}, u32[]{:S(2)}) collective-permute-start(bf16[128,512]{1,0:T(8,128)(2,1)S(1)} %get-tuple-element.80), channel_id=1, source_target_pairs={{0,4},{2,6},{4,0},{6,2},{8,12},{10,14},{12,8},{14,10},{16,20},{18,... | collective-permute-start | bytes 393224 | tf_op jit(solution)/shard_map/ppermute | solution.py:221
  40.3 7.5 %collective-permute-start.12 = (bf16[128,512]{1,0:T(8,128)(2,1)S(1)}, bf16[128,512]{1,0:T(8,128)(2,1)S(1)}, u32[]{:S(2)}, u32[]{:S(2)}) collective-permute-start(bf16[128,512]{1,0:T(8,128)(2,1)S(1)} %get-tuple-element.81), channel_id=1, source_target_pairs={{0,8},{2,10},{4,12},{6,14},{8,0},{10,2},{12,4},{14,6},{16,24},{18,... | collective-permute-start | bytes 393224 | tf_op jit(solution)/shard_map/ppermute | solution.py:221
  47.9 20.1 %collective-permute-start.21 = (bf16[1024,512]{1,0:T(8,128)(2,1)S(1)}, bf16[1024,512]{1,0:T(8,128)(2,1)S(1)}, u32[]{:S(2)}, u32[]{:S(2)}) collective-permute-start(bf16[1024,512]{1,0:T(8,128)(2,1)S(1)} %collective-permute-done.4.w_near), channel_id=1, source_target_pairs={{0,2},{2,0},{4,6},{6,4},{8,10},{10,8},{12,14},{14,12},{16,18},{18,... | collective-permute-start | bytes 3145736 | tf_op jit(solution)/shard_map/ppermute | solution.py:221
  50.0 9.5 %collective-permute-start.14 = (bf16[2,128,256]{2,1,0:T(8,128)(2,1)S(1)}, bf16[2,128,256]{2,1,0:T(8,128)(2,1)S(1)}, u32[]{:S(2)}, u32[]{:S(2)}) collective-permute-start(bf16[2,128,256]{2,1,0:T(8,128)(2,1)S(1)} %get-tuple-element.86), channel_id=1, source_target_pairs={{0,8},{2,10},{4,12},{6,14},{8,0},{10,2},{12,4},{14,6},{16,24},{18,... | collective-permute-start | bytes 393224 | tf_op jit(solution)/shard_map/ppermute | solution.py:221
  50.8 10.4 %collective-permute-start.15 = (bf16[2,128,256]{2,1,0:T(8,128)(2,1)S(1)}, bf16[2,128,256]{2,1,0:T(8,128)(2,1)S(1)}, u32[]{:S(2)}, u32[]{:S(2)}) collective-permute-start(bf16[2,128,256]{2,1,0:T(8,128)(2,1)S(1)} %get-tuple-element.87), channel_id=1, source_target_pairs={{0,12},{2,14},{4,8},{6,10},{8,4},{10,6},{12,0},{14,2},{16,28},{18,... | collective-permute-start | bytes 393224 | tf_op jit(solution)/shard_map/ppermute | solution.py:221
  52.2 15.8 %collective-permute-start.20 = (bf16[1024,128]{1,0:T(8,128)(2,1)S(1)}, bf16[1024,128]{1,0:T(8,128)(2,1)S(1)}, u32[]{:S(2)}, u32[]{:S(2)}) collective-permute-start(bf16[1024,128]{1,0:T(8,128)(2,1)S(1)} %get-tuple-element.94), channel_id=1, source_target_pairs={{0,16},{2,18},{4,20},{6,22},{8,24},{10,26},{12,28},{14,30},{16,0},... | collective-permute-start | bytes 786440 | tf_op jit(solution)/shard_map/ppermute | solution.py:221
  54.0 7.4 %collective-permute-start.17 = (bf16[2,128,128]{2,1,0:T(8,128)(2,1)S(1)}, bf16[2,128,128]{2,1,0:T(8,128)(2,1)S(1)}, u32[]{:S(2)}, u32[]{:S(2)}) collective-permute-start(bf16[2,128,128]{2,1,0:T(8,128)(2,1)S(1)} %get-tuple-element.90), channel_id=1, source_target_pairs={{0,4},{2,6},{4,0},{6,2},{8,12},{10,14},{12,8},{14,10},{16,20},{18,... | collective-permute-start | bytes 196616 | tf_op jit(solution)/shard_map/ppermute | solution.py:221
  59.6 7.0 %collective-permute-start.18 = (bf16[2,128,128]{2,1,0:T(8,128)(2,1)S(1)}, bf16[2,128,128]{2,1,0:T(8,128)(2,1)S(1)}, u32[]{:S(2)}, u32[]{:S(2)}) collective-permute-start(bf16[2,128,128]{2,1,0:T(8,128)(2,1)S(1)} %get-tuple-element.91), channel_id=1, source_target_pairs={{0,8},{2,10},{4,12},{6,14},{8,0},{10,2},{12,4},{14,6},{16,24},{18,... | collective-permute-start | bytes 196616 | tf_op jit(solution)/shard_map/ppermute | solution.py:221
  61.2 6.7 %collective-permute-start.19 = (bf16[2,128,128]{2,1,0:T(8,128)(2,1)S(1)}, bf16[2,128,128]{2,1,0:T(8,128)(2,1)S(1)}, u32[]{:S(2)}, u32[]{:S(2)}) collective-permute-start(bf16[2,128,128]{2,1,0:T(8,128)(2,1)S(1)} %get-tuple-element.92), channel_id=1, source_target_pairs={{0,12},{2,14},{4,8},{6,10},{8,4},{10,6},{12,0},{14,2},{16,28},{18,... | collective-permute-start | bytes 196616 | tf_op jit(solution)/shard_map/ppermute | solution.py:221
  68.0 12.7 %collective-permute-start.26 = (bf16[1024,128]{1,0:T(8,128)(2,1)S(1)}, bf16[1024,128]{1,0:T(8,128)(2,1)S(1)}, u32[]{:S(2)}, u32[]{:S(2)}) collective-permute-start(bf16[1024,128]{1,0:T(8,128)(2,1)S(1)} %sum_halves.1.refs_0_), channel_id=1, source_target_pairs={{0,12},{2,14},{4,8},{6,10},{8,4},{10,6},{12,0},{14,2},{16,28},{18,... | collective-permute-start | bytes 786440 | tf_op jit(solution)/shard_map/ppermute | solution.py:221
  68.4 18.2 %collective-permute-start.23 = (bf16[256,1024]{1,0:T(8,128)(2,1)S(1)}, bf16[256,1024]{1,0:T(8,128)(2,1)S(1)}, u32[]{:S(2)}, u32[]{:S(2)}) collective-permute-start(bf16[256,1024]{1,0:T(8,128)(2,1)S(1)} %turn_features.1.own_ref), channel_id=1, source_target_pairs={{0,1},{1,0},{2,3},{3,2},{4,5},{5,4},{6,7},{7,6},{8,9},{9,8},{10,11... | collective-permute-start | bytes 1572872 | tf_op jit(solution)/shard_map/ppermute | solution.py:225
  69.9 15.0 %collective-permute-start.25 = (bf16[1024,128]{1,0:T(8,128)(2,1)S(1)}, bf16[1024,128]{1,0:T(8,128)(2,1)S(1)}, u32[]{:S(2)}, u32[]{:S(2)}) collective-permute-start(bf16[1024,128]{1,0:T(8,128)(2,1)S(1)} %sum_halves.1.refs_0_), channel_id=1, source_target_pairs={{0,8},{2,10},{4,12},{6,14},{8,0},{10,2},{12,4},{14,6},{16,24},{18,... | collective-permute-start | bytes 786440 | tf_op jit(solution)/shard_map/ppermute | solution.py:221
  72.1 12.8 %collective-permute-start.24 = (bf16[1024,128]{1,0:T(8,128)(2,1)S(1)}, bf16[1024,128]{1,0:T(8,128)(2,1)S(1)}, u32[]{:S(2)}, u32[]{:S(2)}) collective-permute-start(bf16[1024,128]{1,0:T(8,128)(2,1)S(1)} %sum_halves.1.refs_0_), channel_id=1, source_target_pairs={{0,4},{2,6},{4,0},{6,2},{8,12},{10,14},{12,8},{14,10},{16,20},{18,... | collective-permute-start | bytes 786440 | tf_op jit(solution)/shard_map/ppermute | solution.py:221
  73.1 13.5 %collective-permute-start.22 = (bf16[4,128,128]{2,1,0:T(8,128)(2,1)S(1)}, bf16[4,128,128]{2,1,0:T(8,128)(2,1)S(1)}, u32[]{:S(2)}, u32[]{:S(2)}) collective-permute-start(bf16[4,128,128]{2,1,0:T(8,128)(2,1)S(1)} %pad_maximum_fusion), channel_id=1, source_target_pairs={{0,16},{2,18},{4,20},{6,22},{8,24},{10,26},{12,28},{14,30},{16,0},... | collective-permute-start | bytes 393224 | tf_op jit(solution)/shard_map/ppermute | solution.py:221
  87.5 6.9 %collective-permute-start.28 = (f32[256,512]{1,0:T(8,128)S(1)}, f32[256,512]{1,0:T(8,128)S(1)}, u32[]{:S(2)}, u32[]{:S(2)}) collective-permute-start(f32[256,512]{1,0:T(8,128)S(1)} %get-tuple-element.100), channel_id=1, source_target_pairs={{0,2},{2,0},{4,6},{6,4},{8,10},{10,8},{12,14},{14,12},{16,18},{18,... | collective-permute-start | bytes 1572872 | tf_op jit(solution)/shard_map/ppermute | solution.py:221
  87.6 6.8 %collective-permute-start.29 = (bf16[128,512]{1,0:T(8,128)(2,1)S(1)}, bf16[128,512]{1,0:T(8,128)(2,1)S(1)}, u32[]{:S(2)}, u32[]{:S(2)}) collective-permute-start(bf16[128,512]{1,0:T(8,128)(2,1)S(1)} %get-tuple-element.104), channel_id=1, source_target_pairs={{0,12},{2,14},{4,8},{6,10},{8,4},{10,6},{12,0},{14,2},{16,28},{18,... | collective-permute-start | bytes 393224 | tf_op jit(solution)/shard_map/ppermute | solution.py:221
  (11 other events, 104.0 us)

commit v8 on v7

--- a/solution.py
+++ b/solution.py
@@ -351,63 +351,83 @@
             found = jnp.where(start <= position, start, found)
         return found
 
-    @pl.loop(0, 2 * parts)
-    def _(block):
-        first = first_row(2 * first_part + block)
+    zeros = jnp.zeros((8, GROUP * BLK), jnp.float32)
+    last_tile = keys.shape[0] - TILE
+
+    @pl.loop(0, parts)
+    def _(part):
+        blocks = [2 * part, 2 * part + 1]
+        firsts = [first_row(2 * first_part + block) for block in blocks]
         lanes = lax.broadcasted_iota(jnp.int32, (1, GROUP * BLK), 1)
-        position = first + (lanes & (BLK - 1))
-        start = document_start(position)
-        low = document_start(first) // HD * HD
-        count = (first + BLK - low + TILE - 1) // TILE
-
-        def rows_of(k):
-            return pl.ds(pl.multiple_of(low + k * TILE, HD), TILE)
+        positions = [first + (lanes & (BLK - 1)) for first in firsts]
+        row_starts = [document_start(position) for position in positions]
+        lows = [document_start(first) // HD * HD for first in firsts]
+        counts = [
+            (first + BLK - low + TILE - 1) // TILE for first, low in zip(firsts, lows)
+        ]
+        count = jnp.maximum(*counts)
+
+        def rows_of(j, k):
+            offset = jnp.minimum(lows[j] + k * TILE, last_tile)
+            return pl.ds(pl.multiple_of(offset, HD), TILE)
 
         def run(over_tiles):
-            query = q_rows[block]
-            grad = g_rows[block]
-            zeros = jnp.zeros((8, GROUP * BLK), jnp.float32)
+            query = [q_rows[block] for block in blocks]
+            grad = [g_rows[block] for block in blocks]
 
             def visit_scores(k, row_max):
-                here = rows_of(k)
-                raw = dot_nt(keys[here], query)
-                row = low + k * TILE + lax.broadcasted_iota(jnp.int32, raw.shape, 0)
-                raw = jnp.where((row <= position) & (row >= start), raw, masked_fill)
-                scores[k] = raw
-                d_prob[k] = dot_nt(values[here], grad)
-                return jnp.maximum(row_max, folded(raw, jnp.max))
-
-            row_max = over_tiles(visit_scores, zeros + masked_fill)
-            row_max = jnp.max(row_max, axis=0, keepdims=True)
+                seen = []
+                for j in range(2):
+                    here = rows_of(j, k)
+                    raw = dot_nt(keys[here], query[j])
+                    row = lows[j] + k * TILE + lax.broadcasted_iota(jnp.int32, raw.shape, 0)
+                    allowed = (row <= positions[j]) & (row >= row_starts[j])
+                    raw = jnp.where(allowed, raw, masked_fill)
+                    scores[j, k] = raw
+                    d_prob[j, k] = dot_nt(values[here], grad[j])
+                    seen.append(jnp.maximum(row_max[j], folded(raw, jnp.max)))
+                return seen
+
+            row_max = over_tiles(visit_scores, [zeros + masked_fill] * 2)
+            row_max = [jnp.max(part_max, axis=0, keepdims=True) for part_max in row_max]
 
             def visit_sums(k, running):
-                terms = jnp.exp2((scores[k] - row_max) * base_two)
-                scores[k] = terms
-                return (
-                    running[0] + folded(terms, jnp.sum),
-                    running[1] + folded(terms * d_prob[k], jnp.sum),
-                )
-
-            row_sum, weighted = over_tiles(visit_sums, (zeros, zeros))
-            inverse = 1.0 / jnp.sum(row_sum, axis=0, keepdims=True)
-            delta = jnp.sum(weighted, axis=0, keepdims=True) * inverse
+                sums = []
+                for j in range(2):
+                    terms = jnp.exp2((scores[j, k] - row_max[j]) * base_two)
+                    scores[j, k] = terms
+                    sums.append(running[2 * j] + folded(terms, jnp.sum))
+                    sums.append(running[2 * j + 1] + folded(terms * d_prob[j, k], jnp.sum))
+                return sums
+
+            sums = over_tiles(visit_sums, [zeros] * 4)
+            sums = [jnp.sum(part_sum, axis=0, keepdims=True) for part_sum in sums]
+            inverse = [1.0 / sums[2 * j] for j in range(2)]
+            delta = [sums[2 * j + 1] * inverse[j] for j in range(2)]
 
             def visit_grads(k, dq):
-                here = rows_of(k)
-                prob = scores[k] * inverse
-                score_bf = (prob * (d_prob[k] - delta)).astype(jnp.bfloat16)
-                dk[here] += jnp.dot(score_bf, query, preferred_element_type=jnp.float32)
-                dv[here] += jnp.dot(
-                    prob.astype(jnp.bfloat16), grad, preferred_element_type=jnp.float32
-                )
-                return dq + jnp.dot(
-                    keys_t[:, here], score_bf, preferred_element_type=jnp.float32
-                )
-
-            dq = over_tiles(visit_grads, jnp.zeros((HD, GROUP * BLK), jnp.float32))
-            dq = (dq * score_scale).T.astype(jnp.bfloat16)
-            for h in range(GROUP):
-                dq_all[block, :, h * HD : (h + 1) * HD] = dq[h * BLK : (h + 1) * BLK]
+                added = []
+                for j in range(2):
+                    here = rows_of(j, k)
+                    prob = scores[j, k] * inverse[j]
+                    score_bf = (prob * (d_prob[j, k] - delta[j])).astype(jnp.bfloat16)
+                    dk[here] += jnp.dot(score_bf, query[j], preferred_element_type=jnp.float32)
+                    dv[here] += jnp.dot(
+                        prob.astype(jnp.bfloat16), grad[j], preferred_element_type=jnp.float32
+                    )
+                    added.append(
+                        dq[j]
+                        + jnp.dot(
+                            keys_t[:, here], score_bf, preferred_element_type=jnp.float32
+                        )
+                    )
+                return added
+
+            dq = over_tiles(visit_grads, [jnp.zeros((HD, GROUP * BLK), jnp.float32)] * 2)
+            for j in range(2):
+                turned = (dq[j] * score_scale).T.astype(jnp.bfloat16)
+                for h in range(GROUP):
+                    dq_all[blocks[j], :, h * HD : (h + 1) * HD] = turned[h * BLK : (h + 1) * BLK]
 
         for fixed in range(1, UNROLLED + 1):
 
@@ -643,7 +663,7 @@
 
     def attend_scratch(blocks):
         stacked = VMEM((blocks, GROUP * BLK, HD), jnp.bfloat16)
-        tiles = VMEM((total_rows // TILE, TILE, GROUP * BLK), jnp.float32)
+        tiles = VMEM((2, total_rows // TILE, TILE, GROUP * BLK), jnp.float32)
         return [
             stacked,
             stacked,
@@ -662,7 +682,7 @@
         in_specs=[smem] + [vmem] * (GROUP + 4),
         out_specs=[vmem] * (GROUP + 5),
         scratch_shapes=attend_scratch(Q_BLOCKS - 2),
-        compiler_params=limits(20),
+        compiler_params=limits(24),
         cost_estimate=pl.CostEstimate(flops=ATTEND_COST, bytes_accessed=0, transcendentals=0),
         name="attend_first",
     )(doc_lens, *rows[:-1], own_a, own_b, far_a, far_b, core_pairs)
@@ -672,7 +692,7 @@
         in_specs=[smem] + [vmem] * 7,
         out_specs=[vmem] * 3,
         scratch_shapes=[VMEM((padded_rows, HD), jnp.float32)] * 2 + attend_scratch(2),
-        compiler_params=limits(20),
+        compiler_params=limits(24),
         cost_estimate=pl.CostEstimate(flops=ATTEND_COST, bytes_accessed=0, transcendentals=0),
         name="attend_last",
     )(doc_lens, after(rows[-1], w_near), keys, keys_t, all_values, dk_first, dv_first, marks)

time: 95.9 us -> 95.2 us (level)
  waiting for transfers between devices: 40.4 us -> 39.4 us
  transfers between devices with their start and end apart: 30 -> 30, of which waited for: 15 -> 15; matrix products, arithmetic and copies ran while one was open for 1% -> 1% of each run, Pallas kernels for 17% -> 16%
where the time goes in v8:
time: 95.2 us; the launch traced here: 94.5 us
  waiting for transfers between devices  39.4 us (41%)
  starting transfers between devices  32.2 us (34%)
  Pallas kernels  21 us (22%)
  local copies, waits for them, and re-layouts  1.01 us (1%)
    ppermute x27, waiting for transfers between devices, swap(): return lax.ppermute(array, 'dp', [(i, i ^ mask) for i in range(16)])  36.3 us
    ppermute x27, starting transfers between devices, swap(): return lax.ppermute(array, 'dp', [(i, i ^ mask) for i in range(16)])  27.5 us
    pallas_call x1, Pallas kernels, on_device_by_heads(): pl.pallas_call(attend_first, out_shape=[row_grad] * (GROUP - 1) + [sorted...  6.38 us
    ppermute x3, starting transfers between devices, swap_tensor(): return lax.ppermute(array, 'tensor', [(0, 1), (1, 0)])  4.75 us
    pallas_call x1, Pallas kernels, on_device_by_heads(): pl.pallas_call(project_keys, out_shape=[shaped((MARKED, 2 * HD))] * GROUP...  4.51 us
    ppermute x3, waiting for transfers between devices, swap_tensor(): return lax.ppermute(array, 'tensor', [(0, 1), (1, 0)])  3.11 us
    pallas_call x1, Pallas kernels, on_device_by_heads(): pl.pallas_call(attend_last, out_shape=[row_grad, half_sums, half_sums], i...  2.93 us
    pallas_call x1, Pallas kernels, on_device_by_heads(): pl.pallas_call(input_grad, out_shape=shaped((ROWS, features // 2)), in_sp...  2.27 us
  transfers between devices with their start and end apart: 30, of which 15 were waited for; matrix products, arithmetic and copies ran while one was open for 1% of the time, Pallas kernels for 16%

profile of v8, /device:TPU:0, one launch (start us, length us, event | category | flops | bytes accessed | tf_op | source)
XLA Modules:
  0.0 94.5 jit_solution(8181130746922504578)
XLA Ops:
  0.7 4.5 %project_keys.1 = (bf16[144,256]{1,0:T(8,128)(2,1)}, bf16[144,256]{1,0:T(8,128)(2,1)}, bf16[144,256]{1,0:T(8,128)(2,1)}, bf16[144,256]{1,0:T(8,128)(2,1)}) custom-call(s32[2]{0:T(128)} %pos_ref.1, bf16[128,4096]{1,0:T(8,128)(2,1)} %inputs_ref.2, bf16[128,512]{1,0:T(8,128)(2,1)} %values_ref.1, bf16[4096,512]{1,0:T(8,128)(2,1)} %w_own.1), custom_call_target="tpu_custom_call" | custom-call | flops 536870912 | bytes 4194304 | tf_op jit(solution)/shard_map/project_keys/pallas_call | solution.py:599
  5.2 3.0 %collective-permute-start = (bf16[144,256]{1,0:T(8,128)(2,1)}, bf16[144,256]{1,0:T(8,128)(2,1)S(1)}, u32[]{:S(2)}, u32[]{:S(2)}) collective-permute-start(bf16[144,256]{1,0:T(8,128)(2,1)} %get-tuple-element.60), channel_id=1, source_target_pairs={{0,4},{2,6},{4,0},{6,2},{8,12},{10,14},{12,8},{14,10},{16,20},{18,... | collective-permute-start | bytes 221192 | tf_op jit(solution)/shard_map/ppermute | solution.py:221
  10.8 3.1 %collective-permute-start.7 = (bf16[288,256]{1,0:T(8,128)(2,1)S(1)}, bf16[288,256]{1,0:T(8,128)(2,1)S(1)}, u32[]{:S(2)}, u32[]{:S(2)}) collective-permute-start(bf16[288,256]{1,0:T(8,128)(2,1)S(1)} %get-tuple-element.113.refs_3_), channel_id=1, source_target_pairs={{0,16},{2,18},{4,20},{6,22},{8,24},{10,26},{12,28},{14,30},{16,0},... | collective-permute-start | bytes 442376 | tf_op jit(solution)/shard_map/ppermute | solution.py:221
  13.9 2.4 %collective-permute-done.3 = bf16[144,256]{1,0:T(8,128)(2,1)S(1)} collective-permute-done((bf16[144,256]{1,0:T(8,128)(2,1)}, bf16[144,256]{1,0:T(8,128)(2,1)S(1)}, u32[]{:S(2)}, u32[]{:S(2)}) %collective-permute-start.3) | collective-permute-done | bytes 73760 | tf_op jit(solution)/shard_map/ppermute | solution.py:221
  16.3 2.3 %collective-permute-start.8 = (bf16[288,256]{1,0:T(8,128)(2,1)S(1)}, bf16[288,256]{1,0:T(8,128)(2,1)S(1)}, u32[]{:S(2)}, u32[]{:S(2)}) collective-permute-start(bf16[288,256]{1,0:T(8,128)(2,1)S(1)} %get-tuple-element.109.refs_4_), channel_id=1, source_target_pairs={{0,16},{2,18},{4,20},{6,22},{8,24},{10,26},{12,28},{14,30},{16,0},... | collective-permute-start | bytes 442376 | tf_op jit(solution)/shard_map/ppermute | solution.py:221
  19.5 2.3 %pack_weights.1 = bf16[1024,512]{1,0:T(8,128)(2,1)} custom-call(bf16[4096,512]{1,0:T(8,128)(2,1)} %w_own.1), custom_call_target="tpu_custom_call" | custom-call | tf_op jit(solution)/shard_map/pack_weights/pallas_call | solution.py:644
  24.2 2.4 %collective-permute-done.8.refs_6_ = bf16[288,256]{1,0:T(8,128)(2,1)S(1)} collective-permute-done((bf16[288,256]{1,0:T(8,128)(2,1)S(1)}, bf16[288,256]{1,0:T(8,128)(2,1)S(1)}, u32[]{:S(2)}, u32[]{:S(2)}) %collective-permute-start.8) | collective-permute-done | bytes 147488 | tf_op jit(solution)/shard_map/ppermute | solution.py:221
  26.6 2.3 %collective-permute-done.6.refs_2_ = bf16[128,1024]{1,0:T(8,128)(2,1)S(1)} collective-permute-done((bf16[128,1024]{1,0:T(8,128)(2,1)S(1)}, bf16[128,1024]{1,0:T(8,128)(2,1)S(1)}, u32[]{:S(2)}, u32[]{:S(2)}) %collective-permute-start.6) | collective-permute-done | bytes 262176 | tf_op jit(solution)/shard_map/ppermute | solution.py:221
  29.4 3.2 %collective-permute-start.10 = (bf16[4,128,256]{2,1,0:T(8,128)(2,1)S(1)}, bf16[4,128,256]{2,1,0:T(8,128)(2,1)S(1)}, u32[]{:S(2)}, u32[]{:S(2)}) collective-permute-start(bf16[4,128,256]{2,1,0:T(8,128)(2,1)S(1)} %get-tuple-element.78), channel_id=1, source_target_pairs={{0,16},{2,18},{4,20},{6,22},{8,24},{10,26},{12,28},{14,30},{16,0},... | collective-permute-start | bytes 786440 | tf_op jit(solution)/shard_map/ppermute | solution.py:221
  32.6 6.4 %attend_first.1 = (bf16[128,512]{1,0:T(8,128)(2,1)S(1)}, bf16[128,512]{1,0:T(8,128)(2,1)S(1)}, bf16[128,512]{1,0:T(8,128)(2,1)S(1)}, bf16[2176,128]{1,0:T(8,128)...) custom-call(s32[4]{0:T(128)S(1)} %copy-done.4, ...), custom_call_target="tpu_custom_call" | custom-call | flops 4000000000 | tf_op jit(solution)/shard_map/attend_first/pallas_call | solution.py:677
  40.1 3.7 %collective-permute-done.1.row_ref = bf16[128,1024]{1,0:T(8,128)(2,1)S(1)} collective-permute-done((bf16[128,1024]{1,0:T(8,128)(2,1)S(1)}, bf16[128,1024]{1,0:T(8,128)(2,1)S(1)}, u32[]{:S(2)}, u32[]{:S(2)}) %collective-permute-start.1) | collective-permute-done | bytes 262176 | tf_op jit(solution)/shard_map/ppermute | solution.py:221
  44.6 2.9 %attend_last.1 = (bf16[128,512]{1,0:T(8,128)(2,1)S(1)}, f32[1024,256]{1,0:T(8,128)S(1)}, f32[1024,256]{1,0:T(8,128)S(1)}) custom-call(s32[4]{0:T(128)S(1)} %copy-done.4, bf16[128,1024]{1,0:T(8,128)(2,1)S(1)} %collective-permute-done.1.row_ref, bf16[2176,128]{1,0:T(8,128)(2,1)S(1)} %get-tuple-element.71.keys, bf16[128,2176]{1,0:T(8,128)(2,1)S(1)} %get-tuple-element.72.keys_t, ...), custom_call_target="tpu_custom_call" | custom-call | flops 4000000000 | tf_op jit(solution)/shard_map/attend_last/pallas_call | solution.py:689
  55.0 3.4 %collective-permute-done.14.refs_2_ = bf16[2,128,256]{2,1,0:T(8,128)(2,1)S(1)} collective-permute-done((bf16[2,128,256]{2,1,0:T(8,128)(2,1)S(1)}, bf16[2,128,256]{2,1,0:T(8,128)(2,1)S(1)}, u32[]{:S(2)}, u32[]{:S(2)}) %collective-permute-start.14) | collective-permute-done | bytes 131104 | tf_op jit(solution)/shard_map/ppermute | solution.py:221
  58.3 3.4 %collective-permute-done.15.refs_3_ = bf16[2,128,256]{2,1,0:T(8,128)(2,1)S(1)} collective-permute-done((bf16[2,128,256]{2,1,0:T(8,128)(2,1)S(1)}, bf16[2,128,256]{2,1,0:T(8,128)(2,1)S(1)}, u32[]{:S(2)}, u32[]{:S(2)}) %collective-permute-start.15) | collective-permute-done | bytes 131104 | tf_op jit(solution)/shard_map/ppermute | solution.py:221
  62.0 1.8 %collective-permute-done.18.refs_6_ = bf16[2,128,128]{2,1,0:T(8,128)(2,1)S(1)} collective-permute-done((bf16[2,128,128]{2,1,0:T(8,128)(2,1)S(1)}, bf16[2,128,128]{2,1,0:T(8,128)(2,1)S(1)}, u32[]{:S(2)}, u32[]{:S(2)}) %collective-permute-start.18) | collective-permute-done | bytes 65568 | tf_op jit(solution)/shard_map/ppermute | solution.py:221
  63.9 3.5 %collective-permute-done.19.refs_7_ = bf16[2,128,128]{2,1,0:T(8,128)(2,1)S(1)} collective-permute-done((bf16[2,128,128]{2,1,0:T(8,128)(2,1)S(1)}, bf16[2,128,128]{2,1,0:T(8,128)(2,1)S(1)}, u32[]{:S(2)}, u32[]{:S(2)}) %collective-permute-start.19) | collective-permute-done | bytes 65568 | tf_op jit(solution)/shard_map/ppermute | solution.py:221
  69.7 2.0 %collective-permute-start.25 = (bf16[1024,128]{1,0:T(8,128)(2,1)S(1)}, bf16[1024,128]{1,0:T(8,128)(2,1)S(1)}, u32[]{:S(2)}, u32[]{:S(2)}) collective-permute-start(bf16[1024,128]{1,0:T(8,128)(2,1)S(1)} %sum_halves.1.refs_0_), channel_id=1, source_target_pairs={{0,8},{2,10},{4,12},{6,14},{8,0},{10,2},{12,4},{14,6},{16,24},{18,... | collective-permute-start | bytes 786440 | tf_op jit(solution)/shard_map/ppermute | solution.py:221
  72.6 1.8 %collective-permute-start.22 = (bf16[4,128,128]{2,1,0:T(8,128)(2,1)S(1)}, bf16[4,128,128]{2,1,0:T(8,128)(2,1)S(1)}, u32[]{:S(2)}, u32[]{:S(2)}) collective-permute-start(bf16[4,128,128]{2,1,0:T(8,128)(2,1)S(1)} %pad_maximum_fusion), channel_id=1, source_target_pairs={{0,16},{2,18},{4,20},{6,22},{8,24},{10,26},{12,28},{14,30},{16,0},... | collective-permute-start | bytes 393224 | tf_op jit(solution)/shard_map/ppermute | solution.py:221
  74.4 5.8 %collective-permute-done.26.refs_3_ = bf16[1024,128]{1,0:T(8,128)(2,1)S(1)} collective-permute-done((bf16[1024,128]{1,0:T(8,128)(2,1)S(1)}, bf16[1024,128]{1,0:T(8,128)(2,1)S(1)}, u32[]{:S(2)}, u32[]{:S(2)}) %collective-permute-start.26) | collective-permute-done | bytes 262176 | tf_op jit(solution)/shard_map/ppermute | solution.py:221
  80.2 3.7 %collective-permute-done.25.refs_2_ = bf16[1024,128]{1,0:T(8,128)(2,1)S(1)} collective-permute-done((bf16[1024,128]{1,0:T(8,128)(2,1)S(1)}, bf16[1024,128]{1,0:T(8,128)(2,1)S(1)}, u32[]{:S(2)}, u32[]{:S(2)}) %collective-permute-start.25) | collective-permute-done | bytes 262176 | tf_op jit(solution)/shard_map/ppermute | solution.py:221
  83.9 1.6 %collective-permute-start.27 = (bf16[4,128,128]{2,1,0:T(8,128)(2,1)S(1)}, bf16[4,128,128]{2,1,0:T(8,128)(2,1)S(1)}, u32[]{:S(2)}, u32[]{:S(2)}) collective-permute-start(bf16[4,128,128]{2,1,0:T(8,128)(2,1)S(1)} %pad_maximum_fusion.1.own_ref), channel_id=1, source_target_pairs={{0,1},{1,0},{2,3},{3,2},{4,5},{5,4},{6,7},{7,6},{8,9},{9,8},{10,11... | collective-permute-start | bytes 393224 | tf_op jit(solution)/shard_map/ppermute | solution.py:225
  86.7 2.3 %collective-permute-done.27.other_ref = bf16[4,128,128]{2,1,0:T(8,128)(2,1)S(1)} collective-permute-done((bf16[4,128,128]{2,1,0:T(8,128)(2,1)S(1)}, bf16[4,128,128]{2,1,0:T(8,128)(2,1)S(1)}, u32[]{:S(2)}, u32[]{:S(2)}) %collective-permute-start.27) | collective-permute-done | bytes 131104 | tf_op jit(solution)/shard_map/ppermute | solution.py:225
  89.0 2.3 %input_grad.1 = bf16[128,2048]{1,0:T(8,128)(2,1)} custom-call(bf16[4,128,128]{2,1,0:T(8,128)(2,1)S(1)} %pad_maximum_fusion.1.own_ref, bf16[4,128,128]{2,1,0:T(8,128)(2,1)S(1)} %collective-permute-done.27.other_ref, bf16[4096,512]{1,0:T(8,128)(2,1)S(1)} %copy-done, bf16[1024,512]{1,0:T(8,128)(2,1)S(1)} %collective-permute-done.4.w_near, ...), custom_call_target="tpu_custom_call" | custom-call | flops 8000000000 | bytes 5242880 | tf_op jit(solution)/shard_map/input_grad/pallas_call | solution.py:766
  91.2 2.2 %collective-permute-done.29.refs_3_ = bf16[128,512]{1,0:T(8,128)(2,1)S(1)} collective-permute-done((bf16[128,512]{1,0:T(8,128)(2,1)S(1)}, bf16[128,512]{1,0:T(8,128)(2,1)S(1)}, u32[]{:S(2)}, u32[]{:S(2)}) %collective-permute-start.29) | collective-permute-done | bytes 131104 | tf_op jit(solution)/shard_map/ppermute | solution.py:221
  (75 shorter events, 21.3 us)
Async XLA Ops:
  8.2 5.7 %collective-permute-start.2 = (bf16[144,256]{1,0:T(8,128)(2,1)}, bf16[144,256]{1,0:T(8,128)(2,1)S(1)}, u32[]{:S(2)}, u32[]{:S(2)}) collective-permute-start(bf16[144,256]{1,0:T(8,128)(2,1)} %get-tuple-element.64), channel_id=1, source_target_pairs={{0,8},{2,10},{4,12},{6,14},{8,0},{10,2},{12,4},{14,6},{16,24},{18,... | collective-permute-start | bytes 221192 | tf_op jit(solution)/shard_map/ppermute | solution.py:221
  9.8 6.5 %collective-permute-start.3 = (bf16[144,256]{1,0:T(8,128)(2,1)}, bf16[144,256]{1,0:T(8,128)(2,1)S(1)}, u32[]{:S(2)}, u32[]{:S(2)}) collective-permute-start(bf16[144,256]{1,0:T(8,128)(2,1)} %get-tuple-element.65), channel_id=1, source_target_pairs={{0,12},{2,14},{4,8},{6,10},{8,4},{10,6},{12,0},{14,2},{16,28},{18,... | collective-permute-start | bytes 221192 | tf_op jit(solution)/shard_map/ppermute | solution.py:221
  10.8 13.3 %collective-permute-start.7 = (bf16[288,256]{1,0:T(8,128)(2,1)S(1)}, bf16[288,256]{1,0:T(8,128)(2,1)S(1)}, u32[]{:S(2)}, u32[]{:S(2)}) collective-permute-start(bf16[288,256]{1,0:T(8,128)(2,1)S(1)} %get-tuple-element.113.refs_3_), channel_id=1, source_target_pairs={{0,16},{2,18},{4,20},{6,22},{8,24},{10,26},{12,28},{14,30},{16,0},... | collective-permute-start | bytes 442376 | tf_op jit(solution)/shard_map/ppermute | solution.py:221
  16.3 10.2 %collective-permute-start.8 = (bf16[288,256]{1,0:T(8,128)(2,1)S(1)}, bf16[288,256]{1,0:T(8,128)(2,1)S(1)}, u32[]{:S(2)}, u32[]{:S(2)}) collective-permute-start(bf16[288,256]{1,0:T(8,128)(2,1)S(1)} %get-tuple-element.109.refs_4_), channel_id=1, source_target_pairs={{0,16},{2,18},{4,20},{6,22},{8,24},{10,26},{12,28},{14,30},{16,0},... | collective-permute-start | bytes 442376 | tf_op jit(solution)/shard_map/ppermute | solution.py:221
  18.7 7.9 %collective-permute-start.5 = (bf16[128,1024]{1,0:T(8,128)(2,1)S(1)}, bf16[128,1024]{1,0:T(8,128)(2,1)S(1)}, u32[]{:S(2)}, u32[]{:S(2)}) collective-permute-start(bf16[128,1024]{1,0:T(8,128)(2,1)S(1)} %get-tuple-element.68), channel_id=1, source_target_pairs={{0,4},{2,6},{4,0},{6,2},{8,12},{10,14},{12,8},{14,10},{16,20},{18,... | collective-permute-start | bytes 786440 | tf_op jit(solution)/shard_map/ppermute | solution.py:221
  19.3 9.6 %collective-permute-start.6 = (bf16[128,1024]{1,0:T(8,128)(2,1)S(1)}, bf16[128,1024]{1,0:T(8,128)(2,1)S(1)}, u32[]{:S(2)}, u32[]{:S(2)}) collective-permute-start(bf16[128,1024]{1,0:T(8,128)(2,1)S(1)} %get-tuple-element.69), channel_id=1, source_target_pairs={{0,8},{2,10},{4,12},{6,14},{8,0},{10,2},{12,4},{14,6},{16,24},{18,... | collective-permute-start | bytes 786440 | tf_op jit(solution)/shard_map/ppermute | solution.py:221
  21.8 22.8 %collective-permute-start.4 = (bf16[1024,512]{1,0:T(8,128)(2,1)}, bf16[1024,512]{1,0:T(8,128)(2,1)S(1)}, u32[]{:S(2)}, u32[]{:S(2)}) collective-permute-start(bf16[1024,512]{1,0:T(8,128)(2,1)} %pack_weights.1), channel_id=1, source_target_pairs={{0,1},{1,0},{2,3},{3,2},{4,5},{5,4},{6,7},{7,6},{8,9},{9,8},{10,11... | collective-permute-start | bytes 3145736 | tf_op jit(solution)/shard_map/ppermute | solution.py:225
  28.9 14.9 %collective-permute-start.1 = (bf16[128,1024]{1,0:T(8,128)(2,1)S(1)}, bf16[128,1024]{1,0:T(8,128)(2,1)S(1)}, u32[]{:S(2)}, u32[]{:S(2)}) collective-permute-start(bf16[128,1024]{1,0:T(8,128)(2,1)S(1)} %get-tuple-element.63), channel_id=1, source_target_pairs={{0,12},{2,14},{4,8},{6,10},{8,4},{10,6},{12,0},{14,2},{16,28},{18,... | collective-permute-start | bytes 786440 | tf_op jit(solution)/shard_map/ppermute | solution.py:221
  29.4 18.1 %collective-permute-start.10 = (bf16[4,128,256]{2,1,0:T(8,128)(2,1)S(1)}, bf16[4,128,256]{2,1,0:T(8,128)(2,1)S(1)}, u32[]{:S(2)}, u32[]{:S(2)}) collective-permute-start(bf16[4,128,256]{2,1,0:T(8,128)(2,1)S(1)} %get-tuple-element.78), channel_id=1, source_target_pairs={{0,16},{2,18},{4,20},{6,22},{8,24},{10,26},{12,28},{14,30},{16,0},... | collective-permute-start | bytes 786440 | tf_op jit(solution)/shard_map/ppermute | solution.py:221
  39.0 8.5 %collective-permute-start.11 = (bf16[128,512]{1,0:T(8,128)(2,1)S(1)}, bf16[128,512]{1,0:T(8,128)(2,1)S(1)}, u32[]{:S(2)}, u32[]{:S(2)}) collective-permute-start(bf16[128,512]{1,0:T(8,128)(2,1)S(1)} %get-tuple-element.80), channel_id=1, source_target_pairs={{0,4},{2,6},{4,0},{6,2},{8,12},{10,14},{12,8},{14,10},{16,20},{18,... | collective-permute-start | bytes 393224 | tf_op jit(solution)/shard_map/ppermute | solution.py:221
  40.1 7.4 %collective-permute-start.12 = (bf16[128,512]{1,0:T(8,128)(2,1)S(1)}, bf16[128,512]{1,0:T(8,128)(2,1)S(1)}, u32[]{:S(2)}, u32[]{:S(2)}) collective-permute-start(bf16[128,512]{1,0:T(8,128)(2,1)S(1)} %get-tuple-element.81), channel_id=1, source_target_pairs={{0,8},{2,10},{4,12},{6,14},{8,0},{10,2},{12,4},{14,6},{16,24},{18,... | collective-permute-start | bytes 393224 | tf_op jit(solution)/shard_map/ppermute | solution.py:221
  47.7 19.9 %collective-permute-start.21 = (bf16[1024,512]{1,0:T(8,128)(2,1)S(1)}, bf16[1024,512]{1,0:T(8,128)(2,1)S(1)}, u32[]{:S(2)}, u32[]{:S(2)}) collective-permute-start(bf16[1024,512]{1,0:T(8,128)(2,1)S(1)} %collective-permute-done.4.w_near), channel_id=1, source_target_pairs={{0,2},{2,0},{4,6},{6,4},{8,10},{10,8},{12,14},{14,12},{16,18},{18,... | collective-permute-start | bytes 3145736 | tf_op jit(solution)/shard_map/ppermute | solution.py:221
  49.5 8.8 %collective-permute-start.14 = (bf16[2,128,256]{2,1,0:T(8,128)(2,1)S(1)}, bf16[2,128,256]{2,1,0:T(8,128)(2,1)S(1)}, u32[]{:S(2)}, u32[]{:S(2)}) collective-permute-start(bf16[2,128,256]{2,1,0:T(8,128)(2,1)S(1)} %get-tuple-element.86), channel_id=1, source_target_pairs={{0,8},{2,10},{4,12},{6,14},{8,0},{10,2},{12,4},{14,6},{16,24},{18,... | collective-permute-start | bytes 393224 | tf_op jit(solution)/shard_map/ppermute | solution.py:221
  50.6 11.2 %collective-permute-start.15 = (bf16[2,128,256]{2,1,0:T(8,128)(2,1)S(1)}, bf16[2,128,256]{2,1,0:T(8,128)(2,1)S(1)}, u32[]{:S(2)}, u32[]{:S(2)}) collective-permute-start(bf16[2,128,256]{2,1,0:T(8,128)(2,1)S(1)} %get-tuple-element.87), channel_id=1, source_target_pairs={{0,12},{2,14},{4,8},{6,10},{8,4},{10,6},{12,0},{14,2},{16,28},{18,... | collective-permute-start | bytes 393224 | tf_op jit(solution)/shard_map/ppermute | solution.py:221
  51.9 15.6 %collective-permute-start.20 = (bf16[1024,128]{1,0:T(8,128)(2,1)S(1)}, bf16[1024,128]{1,0:T(8,128)(2,1)S(1)}, u32[]{:S(2)}, u32[]{:S(2)}) collective-permute-start(bf16[1024,128]{1,0:T(8,128)(2,1)S(1)} %get-tuple-element.94), channel_id=1, source_target_pairs={{0,16},{2,18},{4,20},{6,22},{8,24},{10,26},{12,28},{14,30},{16,0},... | collective-permute-start | bytes 786440 | tf_op jit(solution)/shard_map/ppermute | solution.py:221
  53.7 8.3 %collective-permute-start.17 = (bf16[2,128,128]{2,1,0:T(8,128)(2,1)S(1)}, bf16[2,128,128]{2,1,0:T(8,128)(2,1)S(1)}, u32[]{:S(2)}, u32[]{:S(2)}) collective-permute-start(bf16[2,128,128]{2,1,0:T(8,128)(2,1)S(1)} %get-tuple-element.90), channel_id=1, source_target_pairs={{0,4},{2,6},{4,0},{6,2},{8,12},{10,14},{12,8},{14,10},{16,20},{18,... | collective-permute-start | bytes 196616 | tf_op jit(solution)/shard_map/ppermute | solution.py:221
  61.8 5.7 %collective-permute-start.19 = (bf16[2,128,128]{2,1,0:T(8,128)(2,1)S(1)}, bf16[2,128,128]{2,1,0:T(8,128)(2,1)S(1)}, u32[]{:S(2)}, u32[]{:S(2)}) collective-permute-start(bf16[2,128,128]{2,1,0:T(8,128)(2,1)S(1)} %get-tuple-element.92), channel_id=1, source_target_pairs={{0,12},{2,14},{4,8},{6,10},{8,4},{10,6},{12,0},{14,2},{16,28},{18,... | collective-permute-start | bytes 196616 | tf_op jit(solution)/shard_map/ppermute | solution.py:221
  67.5 12.6 %collective-permute-start.26 = (bf16[1024,128]{1,0:T(8,128)(2,1)S(1)}, bf16[1024,128]{1,0:T(8,128)(2,1)S(1)}, u32[]{:S(2)}, u32[]{:S(2)}) collective-permute-start(bf16[1024,128]{1,0:T(8,128)(2,1)S(1)} %sum_halves.1.refs_0_), channel_id=1, source_target_pairs={{0,12},{2,14},{4,8},{6,10},{8,4},{10,6},{12,0},{14,2},{16,28},{18,... | collective-permute-start | bytes 786440 | tf_op jit(solution)/shard_map/ppermute | solution.py:221
  68.1 17.4 %collective-permute-start.23 = (bf16[256,1024]{1,0:T(8,128)(2,1)S(1)}, bf16[256,1024]{1,0:T(8,128)(2,1)S(1)}, u32[]{:S(2)}, u32[]{:S(2)}) collective-permute-start(bf16[256,1024]{1,0:T(8,128)(2,1)S(1)} %turn_features.1.own_ref), channel_id=1, source_target_pairs={{0,1},{1,0},{2,3},{3,2},{4,5},{5,4},{6,7},{7,6},{8,9},{9,8},{10,11... | collective-permute-start | bytes 1572872 | tf_op jit(solution)/shard_map/ppermute | solution.py:225
  69.7 14.2 %collective-permute-start.25 = (bf16[1024,128]{1,0:T(8,128)(2,1)S(1)}, bf16[1024,128]{1,0:T(8,128)(2,1)S(1)}, u32[]{:S(2)}, u32[]{:S(2)}) collective-permute-start(bf16[1024,128]{1,0:T(8,128)(2,1)S(1)} %sum_halves.1.refs_0_), channel_id=1, source_target_pairs={{0,8},{2,10},{4,12},{6,14},{8,0},{10,2},{12,4},{14,6},{16,24},{18,... | collective-permute-start | bytes 786440 | tf_op jit(solution)/shard_map/ppermute | solution.py:221
  71.7 12.2 %collective-permute-start.24 = (bf16[1024,128]{1,0:T(8,128)(2,1)S(1)}, bf16[1024,128]{1,0:T(8,128)(2,1)S(1)}, u32[]{:S(2)}, u32[]{:S(2)}) collective-permute-start(bf16[1024,128]{1,0:T(8,128)(2,1)S(1)} %sum_halves.1.refs_0_), channel_id=1, source_target_pairs={{0,4},{2,6},{4,0},{6,2},{8,12},{10,14},{12,8},{14,10},{16,20},{18,... | collective-permute-start | bytes 786440 | tf_op jit(solution)/shard_map/ppermute | solution.py:221
  72.6 13.0 %collective-permute-start.22 = (bf16[4,128,128]{2,1,0:T(8,128)(2,1)S(1)}, bf16[4,128,128]{2,1,0:T(8,128)(2,1)S(1)}, u32[]{:S(2)}, u32[]{:S(2)}) collective-permute-start(bf16[4,128,128]{2,1,0:T(8,128)(2,1)S(1)} %pad_maximum_fusion), channel_id=1, source_target_pairs={{0,16},{2,18},{4,20},{6,22},{8,24},{10,26},{12,28},{14,30},{16,0},... | collective-permute-start | bytes 393224 | tf_op jit(solution)/shard_map/ppermute | solution.py:221
  86.5 6.9 %collective-permute-start.28 = (f32[256,512]{1,0:T(8,128)S(1)}, f32[256,512]{1,0:T(8,128)S(1)}, u32[]{:S(2)}, u32[]{:S(2)}) collective-permute-start(f32[256,512]{1,0:T(8,128)S(1)} %get-tuple-element.100), channel_id=1, source_target_pairs={{0,2},{2,0},{4,6},{6,4},{8,10},{10,8},{12,14},{14,12},{16,18},{18,... | collective-permute-start | bytes 1572872 | tf_op jit(solution)/shard_map/ppermute | solution.py:221
  86.6 6.8 %collective-permute-start.29 = (bf16[128,512]{1,0:T(8,128)(2,1)S(1)}, bf16[128,512]{1,0:T(8,128)(2,1)S(1)}, u32[]{:S(2)}, u32[]{:S(2)}) collective-permute-start(bf16[128,512]{1,0:T(8,128)(2,1)S(1)} %get-tuple-element.104), channel_id=1, source_target_pairs={{0,12},{2,14},{4,8},{6,10},{8,4},{10,6},{12,0},{14,2},{16,28},{18,... | collective-permute-start | bytes 393224 | tf_op jit(solution)/shard_map/ppermute | solution.py:221
  (11 other events, 102.3 us)

commit v9 on v8

--- a/solution.py
+++ b/solution.py
@@ -327,7 +327,7 @@
 
 
 def attend_rows(
-    first_part, first_row, lens_ref, row_refs, dq_refs, keys, keys_t, values, dk, dv, scratch
+    member_of, first_row, lens_ref, row_refs, dq_refs, keys, keys_t, values, dk, dv, scratch
 ):
     q_rows, g_rows, dq_all, scores, d_prob = scratch
     score_scale = 1.0 / math.sqrt(HD)
@@ -357,7 +357,7 @@
     @pl.loop(0, parts)
     def _(part):
         blocks = [2 * part, 2 * part + 1]
-        firsts = [first_row(2 * first_part + block) for block in blocks]
+        firsts = [first_row(2 * member_of(part) + j) for j in range(2)]
         lanes = lax.broadcasted_iota(jnp.int32, (1, GROUP * BLK), 1)
         positions = [first + (lanes & (BLK - 1)) for first in firsts]
         row_starts = [document_start(position) for position in positions]
@@ -483,7 +483,17 @@
         here = pl.ds(tile * TILE, TILE)
         keys_t[:, here] = keys[here].astype(jnp.float32).T.astype(jnp.bfloat16)
     attend_rows(
-        0, first_row, lens_ref, row_refs, dq_refs, keys, keys_t, values, dk, dv, scratch
+        lambda part: part + jnp.minimum(part, 1),
+        first_row,
+        lens_ref,
+        row_refs,
+        dq_refs,
+        keys,
+        keys_t,
+        values,
+        dk,
+        dv,
+        scratch,
     )
 
 
@@ -498,7 +508,17 @@
     to_scalars.wait()
     first_row = first_row_of(positions)
     attend_rows(
-        GROUP - 1, first_row, lens_ref, [row_ref], [dq_ref], keys, keys_t, values, dk, dv, scratch
+        lambda part: part + 1,
+        first_row,
+        lens_ref,
+        [row_ref],
+        [dq_ref],
+        keys,
+        keys_t,
+        values,
+        dk,
+        dv,
+        scratch,
     )
     for block in range(4 * Q_BLOCKS):
         quarter = block // Q_BLOCKS
@@ -652,7 +672,7 @@
     )(after(w_key, own_b))
     w_near = swap_tensor(leaving)
     near_pairs = jnp.concatenate([own_a, own_b, far_a, far_b], axis=0)
-    core_pairs = swap(after(near_pairs, near_features, leaving, rows[1], rows[2]), CORE)
+    core_pairs = swap(after(near_pairs, near_features, leaving, rows[2], rows[3]), CORE)
     far_features = swap(far_features, Z_HI)
 
     row_grad = shaped((ROWS, GROUP * HD))
@@ -685,7 +705,7 @@
         compiler_params=limits(24),
         cost_estimate=pl.CostEstimate(flops=ATTEND_COST, bytes_accessed=0, transcendentals=0),
         name="attend_first",
-    )(doc_lens, *rows[:-1], own_a, own_b, far_a, far_b, core_pairs)
+    )(doc_lens, rows[0], *rows[2:], own_a, own_b, far_a, far_b, core_pairs)
     last_grad, kept, sent = pl.pallas_call(
         attend_last,
         out_shape=[row_grad, half_sums, half_sums],
@@ -695,9 +715,9 @@
         compiler_params=limits(24),
         cost_estimate=pl.CostEstimate(flops=ATTEND_COST, bytes_accessed=0, transcendentals=0),
         name="attend_last",
-    )(doc_lens, after(rows[-1], w_near), keys, keys_t, all_values, dk_first, dv_first, marks)
-
-    row_grads = with_partners(row_grads)
+    )(doc_lens, after(rows[1], w_near), keys, keys_t, all_values, dk_first, dv_first, marks)
+
+    row_grads = [row_grads[0], swap(row_grads[1], 4), swap(row_grads[2], 6)]
     sent = after(sent, far_features, *row_grads)
     dk_sum, dk_near, *value_grads = pl.pallas_call(
         sum_cores,
@@ -741,13 +761,13 @@
         cost_estimate=pl.CostEstimate(flops=1_000_000, bytes_accessed=0, transcendentals=0),
         name="sum_halves",
     )(dk_sum, dk_far)
-    key_grad = after(key_grad, own_features, value_far, w_far)
+    key_grad = after(key_grad, own_features, w_far)
     key_grads = with_partners([key_grad] * GROUP)
     own_key_grad = jnp.stack([key_grads[m][m * ROWS : (m + 1) * ROWS] for m in range(GROUP)])
     other_key_grad = swap_tensor(own_key_grad)
 
     value_far = swap(after(value_far, key_grad), Z_HI)
-    last_grad = swap(after(last_grad, own_key_grad), 6)
+    last_grad = swap(after(last_grad, own_key_grad), 2)
 
     keep, send = pl.pallas_call(
         weight_grad,
@@ -787,7 +807,7 @@
         out_specs=[vmem] * 3,
         compiler_params=limits(16),
         name="finish",
-    )(after(keep, d_input), arrived, value_far, *row_grads, last_grad, *value_grads)
+    )(after(keep, d_input), arrived, value_far, row_grads[0], last_grad, *row_grads[1:], *value_grads)
     return (d_query, d_value, d_input, d_wkey)
 
 

time: 95.2 us -> 105 us (1.10)
  waiting for transfers between devices: 39.4 us -> 46.6 us
  Pallas kernels: 21 us -> 22.5 us
    ppermute x27, waiting for transfers between devices: 36.3 us -> 46.2 us  [swap(): return lax.ppermute(array, 'dp', [(i, i ^ mask) for i in range(16)])]
    ppermute x3, waiting for transfers between devices: 3.11 us -> 0.38 us  [swap_tensor(): return lax.ppermute(array, 'tensor', [(0, 1), (1, 0)])]
    pallas_call x1, Pallas kernels: 6.38 us -> 8.34 us  [on_device_by_heads(): pl.pallas_call(attend_first, out_shape=[row_grad] * (GROUP - 1) + [sorted...]
  transfers between devices with their start and end apart: 30 -> 30, of which waited for: 15 -> 17; matrix products, arithmetic and copies ran while one was open for 1% -> 1% of each run, Pallas kernels for 16% -> 16%
where the time goes in v9:
time: 105 us; the launch traced here: 104 us
  waiting for transfers between devices  46.6 us (44%)
  starting transfers between devices  33 us (31%)
  Pallas kernels  22.5 us (21%)
    ppermute x27, waiting for transfers between devices, swap(): return lax.ppermute(array, 'dp', [(i, i ^ mask) for i in range(16)])  46.2 us
    ppermute x27, starting transfers between devices, swap(): return lax.ppermute(array, 'dp', [(i, i ^ mask) for i in range(16)])  28.3 us
    pallas_call x1, Pallas kernels, on_device_by_heads(): pl.pallas_call(attend_first, out_shape=[row_grad] * (GROUP - 1) + [sorted...  8.34 us
    ppermute x3, starting transfers between devices, swap_tensor(): return lax.ppermute(array, 'tensor', [(0, 1), (1, 0)])  4.75 us
    pallas_call x1, Pallas kernels, on_device_by_heads(): pl.pallas_call(project_keys, out_shape=[shaped((MARKED, 2 * HD))] * GROUP...  4.51 us
    pallas_call x1, Pallas kernels, on_device_by_heads(): pl.pallas_call(attend_last, out_shape=[row_grad, half_sums, half_sums], i...  2.47 us
    pallas_call x1, Pallas kernels, on_device_by_heads(): pl.pallas_call(input_grad, out_shape=shaped((ROWS, features // 2)), in_sp...  2.27 us
    pallas_call x1, Pallas kernels, on_device_by_heads(): pl.pallas_call(pack_weights, out_shape=shaped((2 * PART, kv_columns)), in...  2.25 us
  transfers between devices with their start and end apart: 30, of which 17 were waited for; matrix products, arithmetic and copies ran while one was open for 1% of the time, Pallas kernels for 16%

profile of v9, /device:TPU:0, one launch (start us, length us, event | category | flops | bytes accessed | tf_op | source)
XLA Modules:
  0.0 104.0 jit_solution(10171433786056754223)
XLA Ops:
  0.7 4.5 %project_keys.1 = (bf16[144,256]{1,0:T(8,128)(2,1)}, bf16[144,256]{1,0:T(8,128)(2,1)}, bf16[144,256]{1,0:T(8,128)(2,1)}, bf16[144,256]{1,0:T(8,128)(2,1)}) custom-call(s32[2]{0:T(128)} %pos_ref.1, bf16[128,4096]{1,0:T(8,128)(2,1)} %inputs_ref.2, bf16[128,512]{1,0:T(8,128)(2,1)} %values_ref.1, bf16[4096,512]{1,0:T(8,128)(2,1)} %w_own.1), custom_call_target="tpu_custom_call" | custom-call | flops 536870912 | bytes 4194304 | tf_op jit(solution)/shard_map/project_keys/pallas_call | solution.py:619
  5.2 3.0 %collective-permute-start = (bf16[144,256]{1,0:T(8,128)(2,1)}, bf16[144,256]{1,0:T(8,128)(2,1)S(1)}, u32[]{:S(2)}, u32[]{:S(2)}) collective-permute-start(bf16[144,256]{1,0:T(8,128)(2,1)} %get-tuple-element.60), channel_id=1, source_target_pairs={{0,4},{2,6},{4,0},{6,2},{8,12},{10,14},{12,8},{14,10},{16,20},{18,... | collective-permute-start | bytes 221192 | tf_op jit(solution)/shard_map/ppermute | solution.py:221
  10.8 3.1 %collective-permute-start.7 = (bf16[288,256]{1,0:T(8,128)(2,1)S(1)}, bf16[288,256]{1,0:T(8,128)(2,1)S(1)}, u32[]{:S(2)}, u32[]{:S(2)}) collective-permute-start(bf16[288,256]{1,0:T(8,128)(2,1)S(1)} %get-tuple-element.113.refs_3_), channel_id=1, source_target_pairs={{0,16},{2,18},{4,20},{6,22},{8,24},{10,26},{12,28},{14,30},{16,0},... | collective-permute-start | bytes 442376 | tf_op jit(solution)/shard_map/ppermute | solution.py:221
  13.9 2.4 %collective-permute-done.3 = bf16[144,256]{1,0:T(8,128)(2,1)S(1)} collective-permute-done((bf16[144,256]{1,0:T(8,128)(2,1)}, bf16[144,256]{1,0:T(8,128)(2,1)S(1)}, u32[]{:S(2)}, u32[]{:S(2)}) %collective-permute-start.3) | collective-permute-done | bytes 73760 | tf_op jit(solution)/shard_map/ppermute | solution.py:221
  16.3 2.3 %collective-permute-start.8 = (bf16[288,256]{1,0:T(8,128)(2,1)S(1)}, bf16[288,256]{1,0:T(8,128)(2,1)S(1)}, u32[]{:S(2)}, u32[]{:S(2)}) collective-permute-start(bf16[288,256]{1,0:T(8,128)(2,1)S(1)} %get-tuple-element.109.refs_4_), channel_id=1, source_target_pairs={{0,16},{2,18},{4,20},{6,22},{8,24},{10,26},{12,28},{14,30},{16,0},... | collective-permute-start | bytes 442376 | tf_op jit(solution)/shard_map/ppermute | solution.py:221
  18.7 2.1 %collective-permute-start.6 = (bf16[128,1024]{1,0:T(8,128)(2,1)S(1)}, bf16[128,1024]{1,0:T(8,128)(2,1)S(1)}, u32[]{:S(2)}, u32[]{:S(2)}) collective-permute-start(bf16[128,1024]{1,0:T(8,128)(2,1)S(1)} %get-tuple-element.69), channel_id=1, source_target_pairs={{0,12},{2,14},{4,8},{6,10},{8,4},{10,6},{12,0},{14,2},{16,28},{18,... | collective-permute-start | bytes 786440 | tf_op jit(solution)/shard_map/ppermute | solution.py:221
  20.8 2.3 %pack_weights.1 = bf16[1024,512]{1,0:T(8,128)(2,1)} custom-call(bf16[4096,512]{1,0:T(8,128)(2,1)} %w_own.1), custom_call_target="tpu_custom_call" | custom-call | tf_op jit(solution)/shard_map/pack_weights/pallas_call | solution.py:664
  26.5 4.0 %collective-permute-done.5.refs_1_ = bf16[128,1024]{1,0:T(8,128)(2,1)S(1)} collective-permute-done((bf16[128,1024]{1,0:T(8,128)(2,1)S(1)}, bf16[128,1024]{1,0:T(8,128)(2,1)S(1)}, u32[]{:S(2)}, u32[]{:S(2)}) %collective-permute-start.5) | collective-permute-done | bytes 262176 | tf_op jit(solution)/shard_map/ppermute | solution.py:221
  30.6 4.2 %collective-permute-done.6.refs_2_ = bf16[128,1024]{1,0:T(8,128)(2,1)S(1)} collective-permute-done((bf16[128,1024]{1,0:T(8,128)(2,1)S(1)}, bf16[128,1024]{1,0:T(8,128)(2,1)S(1)}, u32[]{:S(2)}, u32[]{:S(2)}) %collective-permute-start.6) | collective-permute-done | bytes 262176 | tf_op jit(solution)/shard_map/ppermute | solution.py:221
  36.7 8.3 %attend_first.1 = (bf16[128,512]{1,0:T(8,128)(2,1)S(1)}, bf16[128,512]{1,0:T(8,128)(2,1)S(1)}, bf16[128,512]{1,0:T(8,128)(2,1)S(1)}, bf16[2176,128]{1,0:T(8,128)...) custom-call(s32[4]{0:T(128)S(1)} %copy-done.4, ...), custom_call_target="tpu_custom_call" | custom-call | flops 4000000000 | tf_op jit(solution)/shard_map/attend_first/pallas_call | solution.py:697
  46.4 2.5 %attend_last.1 = (bf16[128,512]{1,0:T(8,128)(2,1)S(1)}, f32[1024,256]{1,0:T(8,128)S(1)}, f32[1024,256]{1,0:T(8,128)S(1)}) custom-call(s32[4]{0:T(128)S(1)} %copy-done.4, bf16[128,1024]{1,0:T(8,128)(2,1)S(1)} %collective-permute-done.1.row_ref, bf16[2176,128]{1,0:T(8,128)(2,1)S(1)} %get-tuple-element.71.keys, bf16[128,2176]{1,0:T(8,128)(2,1)S(1)} %get-tuple-element.72.keys_t, ...), custom_call_target="tpu_custom_call" | custom-call | flops 4000000000 | tf_op jit(solution)/shard_map/attend_last/pallas_call | solution.py:709
  50.1 2.8 %collective-permute-done.11.refs_2_ = bf16[128,512]{1,0:T(8,128)(2,1)S(1)} collective-permute-done((bf16[128,512]{1,0:T(8,128)(2,1)S(1)}, bf16[128,512]{1,0:T(8,128)(2,1)S(1)}, u32[]{:S(2)}, u32[]{:S(2)}) %collective-permute-start.11) | collective-permute-done | bytes 131104 | tf_op jit(solution)/shard_map/ppermute | solution.py:221
  52.9 3.8 %collective-permute-done.12.refs_3_ = bf16[128,512]{1,0:T(8,128)(2,1)S(1)} collective-permute-done((bf16[128,512]{1,0:T(8,128)(2,1)S(1)}, bf16[128,512]{1,0:T(8,128)(2,1)S(1)}, u32[]{:S(2)}, u32[]{:S(2)}) %collective-permute-start.12) | collective-permute-done | bytes 131104 | tf_op jit(solution)/shard_map/ppermute | solution.py:221
  57.2 2.1 %collective-permute-done.16.arrived_ref = f32[1024,256]{1,0:T(8,128)S(1)} collective-permute-done((f32[1024,256]{1,0:T(8,128)S(1)}, f32[1024,256]{1,0:T(8,128)S(1)}, u32[]{:S(2)}, u32[]{:S(2)}) %collective-permute-start.16) | collective-permute-done | bytes 1048608 | tf_op jit(solution)/shard_map/ppermute | solution.py:221
  60.1 2.3 %collective-permute-start.14 = (bf16[2,128,256]{2,1,0:T(8,128)(2,1)S(1)}, bf16[2,128,256]{2,1,0:T(8,128)(2,1)S(1)}, u32[]{:S(2)}, u32[]{:S(2)}) collective-permute-start(bf16[2,128,256]{2,1,0:T(8,128)(2,1)S(1)} %get-tuple-element.86), channel_id=1, source_target_pairs={{0,8},{2,10},{4,12},{6,14},{8,0},{10,2},{12,4},{14,6},{16,24},{18,... | collective-permute-start | bytes 393224 | tf_op jit(solution)/shard_map/ppermute | solution.py:221
  63.2 2.0 %collective-permute-done.13.refs_1_ = bf16[2,128,256]{2,1,0:T(8,128)(2,1)S(1)} collective-permute-done((bf16[2,128,256]{2,1,0:T(8,128)(2,1)S(1)}, bf16[2,128,256]{2,1,0:T(8,128)(2,1)S(1)}, u32[]{:S(2)}, u32[]{:S(2)}) %collective-permute-start.13) | collective-permute-done | bytes 131104 | tf_op jit(solution)/shard_map/ppermute | solution.py:221
  65.6 3.5 %collective-permute-done.14.refs_2_ = bf16[2,128,256]{2,1,0:T(8,128)(2,1)S(1)} collective-permute-done((bf16[2,128,256]{2,1,0:T(8,128)(2,1)S(1)}, bf16[2,128,256]{2,1,0:T(8,128)(2,1)S(1)}, u32[]{:S(2)}, u32[]{:S(2)}) %collective-permute-start.14) | collective-permute-done | bytes 131104 | tf_op jit(solution)/shard_map/ppermute | solution.py:221
  69.1 2.5 %collective-permute-start.18 = (bf16[2,128,128]{2,1,0:T(8,128)(2,1)S(1)}, bf16[2,128,128]{2,1,0:T(8,128)(2,1)S(1)}, u32[]{:S(2)}, u32[]{:S(2)}) collective-permute-start(bf16[2,128,128]{2,1,0:T(8,128)(2,1)S(1)} %get-tuple-element.91), channel_id=1, source_target_pairs={{0,8},{2,10},{4,12},{6,14},{8,0},{10,2},{12,4},{14,6},{16,24},{18,... | collective-permute-start | bytes 196616 | tf_op jit(solution)/shard_map/ppermute | solution.py:221
  71.6 3.9 %collective-permute-done.15.refs_3_ = bf16[2,128,256]{2,1,0:T(8,128)(2,1)S(1)} collective-permute-done((bf16[2,128,256]{2,1,0:T(8,128)(2,1)S(1)}, bf16[2,128,256]{2,1,0:T(8,128)(2,1)S(1)}, u32[]{:S(2)}, u32[]{:S(2)}) %collective-permute-start.15) | collective-permute-done | bytes 131104 | tf_op jit(solution)/shard_map/ppermute | solution.py:221
  77.3 3.3 %collective-permute-done.19.refs_7_ = bf16[2,128,128]{2,1,0:T(8,128)(2,1)S(1)} collective-permute-done((bf16[2,128,128]{2,1,0:T(8,128)(2,1)S(1)}, bf16[2,128,128]{2,1,0:T(8,128)(2,1)S(1)}, u32[]{:S(2)}, u32[]{:S(2)}) %collective-permute-start.19) | collective-permute-done | bytes 65568 | tf_op jit(solution)/shard_map/ppermute | solution.py:221
  80.8 3.1 %collective-permute-start.25 = (bf16[1024,128]{1,0:T(8,128)(2,1)S(1)}, bf16[1024,128]{1,0:T(8,128)(2,1)S(1)}, u32[]{:S(2)}, u32[]{:S(2)}) collective-permute-start(bf16[1024,128]{1,0:T(8,128)(2,1)S(1)} %sum_halves.1.refs_0_), channel_id=1, source_target_pairs={{0,8},{2,10},{4,12},{6,14},{8,0},{10,2},{12,4},{14,6},{16,24},{18,... | collective-permute-start | bytes 786440 | tf_op jit(solution)/shard_map/ppermute | solution.py:221
  85.3 7.2 %collective-permute-done.26.refs_3_ = bf16[1024,128]{1,0:T(8,128)(2,1)S(1)} collective-permute-done((bf16[1024,128]{1,0:T(8,128)(2,1)S(1)}, bf16[1024,128]{1,0:T(8,128)(2,1)S(1)}, u32[]{:S(2)}, u32[]{:S(2)}) %collective-permute-start.26) | collective-permute-done | bytes 262176 | tf_op jit(solution)/shard_map/ppermute | solution.py:221
  96.8 2.1 %collective-permute-start.29 = (bf16[128,512]{1,0:T(8,128)(2,1)S(1)}, bf16[128,512]{1,0:T(8,128)(2,1)S(1)}, u32[]{:S(2)}, u32[]{:S(2)}) collective-permute-start(bf16[128,512]{1,0:T(8,128)(2,1)S(1)} %get-tuple-element.104), channel_id=1, source_target_pairs={{0,4},{2,6},{4,0},{6,2},{8,12},{10,14},{12,8},{14,10},{16,20},{18,... | collective-permute-start | bytes 393224 | tf_op jit(solution)/shard_map/ppermute | solution.py:221
  99.2 2.3 %input_grad.1 = bf16[128,2048]{1,0:T(8,128)(2,1)} custom-call(bf16[4,128,128]{2,1,0:T(8,128)(2,1)S(1)} %pad_maximum_fusion.1.own_ref, bf16[4,128,128]{2,1,0:T(8,128)(2,1)S(1)} %collective-permute-done.27.other_ref, bf16[4096,512]{1,0:T(8,128)(2,1)S(1)} %copy-done, bf16[1024,512]{1,0:T(8,128)(2,1)S(1)} %collective-permute-done.4.w_near, ...), custom_call_target="tpu_custom_call" | custom-call | flops 8000000000 | bytes 5242880 | tf_op jit(solution)/shard_map/input_grad/pallas_call | solution.py:786
  (75 shorter events, 23.5 us)
Async XLA Ops:
  8.2 5.7 %collective-permute-start.2 = (bf16[144,256]{1,0:T(8,128)(2,1)}, bf16[144,256]{1,0:T(8,128)(2,1)S(1)}, u32[]{:S(2)}, u32[]{:S(2)}) collective-permute-start(bf16[144,256]{1,0:T(8,128)(2,1)} %get-tuple-element.64), channel_id=1, source_target_pairs={{0,8},{2,10},{4,12},{6,14},{8,0},{10,2},{12,4},{14,6},{16,24},{18,... | collective-permute-start | bytes 221192 | tf_op jit(solution)/shard_map/ppermute | solution.py:221
  9.8 6.5 %collective-permute-start.3 = (bf16[144,256]{1,0:T(8,128)(2,1)}, bf16[144,256]{1,0:T(8,128)(2,1)S(1)}, u32[]{:S(2)}, u32[]{:S(2)}) collective-permute-start(bf16[144,256]{1,0:T(8,128)(2,1)} %get-tuple-element.65), channel_id=1, source_target_pairs={{0,12},{2,14},{4,8},{6,10},{8,4},{10,6},{12,0},{14,2},{16,28},{18,... | collective-permute-start | bytes 221192 | tf_op jit(solution)/shard_map/ppermute | solution.py:221
  10.8 13.8 %collective-permute-start.7 = (bf16[288,256]{1,0:T(8,128)(2,1)S(1)}, bf16[288,256]{1,0:T(8,128)(2,1)S(1)}, u32[]{:S(2)}, u32[]{:S(2)}) collective-permute-start(bf16[288,256]{1,0:T(8,128)(2,1)S(1)} %get-tuple-element.113.refs_3_), channel_id=1, source_target_pairs={{0,16},{2,18},{4,20},{6,22},{8,24},{10,26},{12,28},{14,30},{16,0},... | collective-permute-start | bytes 442376 | tf_op jit(solution)/shard_map/ppermute | solution.py:221
  16.3 10.2 %collective-permute-start.8 = (bf16[288,256]{1,0:T(8,128)(2,1)S(1)}, bf16[288,256]{1,0:T(8,128)(2,1)S(1)}, u32[]{:S(2)}, u32[]{:S(2)}) collective-permute-start(bf16[288,256]{1,0:T(8,128)(2,1)S(1)} %get-tuple-element.109.refs_4_), channel_id=1, source_target_pairs={{0,16},{2,18},{4,20},{6,22},{8,24},{10,26},{12,28},{14,30},{16,0},... | collective-permute-start | bytes 442376 | tf_op jit(solution)/shard_map/ppermute | solution.py:221
  18.7 11.9 %collective-permute-start.5 = (bf16[128,1024]{1,0:T(8,128)(2,1)S(1)}, bf16[128,1024]{1,0:T(8,128)(2,1)S(1)}, u32[]{:S(2)}, u32[]{:S(2)}) collective-permute-start(bf16[128,1024]{1,0:T(8,128)(2,1)S(1)} %get-tuple-element.68), channel_id=1, source_target_pairs={{0,8},{2,10},{4,12},{6,14},{8,0},{10,2},{12,4},{14,6},{16,24},{18,... | collective-permute-start | bytes 786440 | tf_op jit(solution)/shard_map/ppermute | solution.py:221
  18.7 16.1 %collective-permute-start.6 = (bf16[128,1024]{1,0:T(8,128)(2,1)S(1)}, bf16[128,1024]{1,0:T(8,128)(2,1)S(1)}, u32[]{:S(2)}, u32[]{:S(2)}) collective-permute-start(bf16[128,1024]{1,0:T(8,128)(2,1)S(1)} %get-tuple-element.69), channel_id=1, source_target_pairs={{0,12},{2,14},{4,8},{6,10},{8,4},{10,6},{12,0},{14,2},{16,28},{18,... | collective-permute-start | bytes 786440 | tf_op jit(solution)/shard_map/ppermute | solution.py:221
  23.1 23.3 %collective-permute-start.4 = (bf16[1024,512]{1,0:T(8,128)(2,1)}, bf16[1024,512]{1,0:T(8,128)(2,1)S(1)}, u32[]{:S(2)}, u32[]{:S(2)}) collective-permute-start(bf16[1024,512]{1,0:T(8,128)(2,1)} %pack_weights.1), channel_id=1, source_target_pairs={{0,1},{1,0},{2,3},{3,2},{4,5},{5,4},{6,7},{7,6},{8,9},{9,8},{10,11... | collective-permute-start | bytes 3145736 | tf_op jit(solution)/shard_map/ppermute | solution.py:225
  34.7 11.7 %collective-permute-start.1 = (bf16[128,1024]{1,0:T(8,128)(2,1)S(1)}, bf16[128,1024]{1,0:T(8,128)(2,1)S(1)}, u32[]{:S(2)}, u32[]{:S(2)}) collective-permute-start(bf16[128,1024]{1,0:T(8,128)(2,1)S(1)} %get-tuple-element.63), channel_id=1, source_target_pairs={{0,4},{2,6},{4,0},{6,2},{8,12},{10,14},{12,8},{14,10},{16,20},{18,... | collective-permute-start | bytes 786440 | tf_op jit(solution)/shard_map/ppermute | solution.py:221
  34.8 15.3 %collective-permute-start.10 = (bf16[4,128,256]{2,1,0:T(8,128)(2,1)S(1)}, bf16[4,128,256]{2,1,0:T(8,128)(2,1)S(1)}, u32[]{:S(2)}, u32[]{:S(2)}) collective-permute-start(bf16[4,128,256]{2,1,0:T(8,128)(2,1)S(1)} %get-tuple-element.78), channel_id=1, source_target_pairs={{0,16},{2,18},{4,20},{6,22},{8,24},{10,26},{12,28},{14,30},{16,0},... | collective-permute-start | bytes 786440 | tf_op jit(solution)/shard_map/ppermute | solution.py:221
  45.1 7.8 %collective-permute-start.11 = (bf16[128,512]{1,0:T(8,128)(2,1)S(1)}, bf16[128,512]{1,0:T(8,128)(2,1)S(1)}, u32[]{:S(2)}, u32[]{:S(2)}) collective-permute-start(bf16[128,512]{1,0:T(8,128)(2,1)S(1)} %get-tuple-element.80), channel_id=1, source_target_pairs={{0,8},{2,10},{4,12},{6,14},{8,0},{10,2},{12,4},{14,6},{16,24},{18,... | collective-permute-start | bytes 393224 | tf_op jit(solution)/shard_map/ppermute | solution.py:221
  45.8 10.9 %collective-permute-start.12 = (bf16[128,512]{1,0:T(8,128)(2,1)S(1)}, bf16[128,512]{1,0:T(8,128)(2,1)S(1)}, u32[]{:S(2)}, u32[]{:S(2)}) collective-permute-start(bf16[128,512]{1,0:T(8,128)(2,1)S(1)} %get-tuple-element.81), channel_id=1, source_target_pairs={{0,12},{2,14},{4,8},{6,10},{8,4},{10,6},{12,0},{14,2},{16,28},{18,... | collective-permute-start | bytes 393224 | tf_op jit(solution)/shard_map/ppermute | solution.py:221
  56.8 23.9 %collective-permute-start.21 = (bf16[1024,512]{1,0:T(8,128)(2,1)S(1)}, bf16[1024,512]{1,0:T(8,128)(2,1)S(1)}, u32[]{:S(2)}, u32[]{:S(2)}) collective-permute-start(bf16[1024,512]{1,0:T(8,128)(2,1)S(1)} %collective-permute-done.4.w_near), channel_id=1, source_target_pairs={{0,2},{2,0},{4,6},{6,4},{8,10},{10,8},{12,14},{14,12},{16,18},{18,... | collective-permute-start | bytes 3145736 | tf_op jit(solution)/shard_map/ppermute | solution.py:221
  59.5 21.2 %collective-permute-start.20 = (bf16[1024,128]{1,0:T(8,128)(2,1)S(1)}, bf16[1024,128]{1,0:T(8,128)(2,1)S(1)}, u32[]{:S(2)}, u32[]{:S(2)}) collective-permute-start(bf16[1024,128]{1,0:T(8,128)(2,1)S(1)} %get-tuple-element.94), channel_id=1, source_target_pairs={{0,16},{2,18},{4,20},{6,22},{8,24},{10,26},{12,28},{14,30},{16,0},... | collective-permute-start | bytes 786440 | tf_op jit(solution)/shard_map/ppermute | solution.py:221
  60.1 9.0 %collective-permute-start.14 = (bf16[2,128,256]{2,1,0:T(8,128)(2,1)S(1)}, bf16[2,128,256]{2,1,0:T(8,128)(2,1)S(1)}, u32[]{:S(2)}, u32[]{:S(2)}) collective-permute-start(bf16[2,128,256]{2,1,0:T(8,128)(2,1)S(1)} %get-tuple-element.86), channel_id=1, source_target_pairs={{0,8},{2,10},{4,12},{6,14},{8,0},{10,2},{12,4},{14,6},{16,24},{18,... | collective-permute-start | bytes 393224 | tf_op jit(solution)/shard_map/ppermute | solution.py:221
  62.4 13.1 %collective-permute-start.15 = (bf16[2,128,256]{2,1,0:T(8,128)(2,1)S(1)}, bf16[2,128,256]{2,1,0:T(8,128)(2,1)S(1)}, u32[]{:S(2)}, u32[]{:S(2)}) collective-permute-start(bf16[2,128,256]{2,1,0:T(8,128)(2,1)S(1)} %get-tuple-element.87), channel_id=1, source_target_pairs={{0,12},{2,14},{4,8},{6,10},{8,4},{10,6},{12,0},{14,2},{16,28},{18,... | collective-permute-start | bytes 393224 | tf_op jit(solution)/shard_map/ppermute | solution.py:221
  65.2 10.5 %collective-permute-start.17 = (bf16[2,128,128]{2,1,0:T(8,128)(2,1)S(1)}, bf16[2,128,128]{2,1,0:T(8,128)(2,1)S(1)}, u32[]{:S(2)}, u32[]{:S(2)}) collective-permute-start(bf16[2,128,128]{2,1,0:T(8,128)(2,1)S(1)} %get-tuple-element.90), channel_id=1, source_target_pairs={{0,4},{2,6},{4,0},{6,2},{8,12},{10,14},{12,8},{14,10},{16,20},{18,... | collective-permute-start | bytes 196616 | tf_op jit(solution)/shard_map/ppermute | solution.py:221
  69.1 8.3 %collective-permute-start.18 = (bf16[2,128,128]{2,1,0:T(8,128)(2,1)S(1)}, bf16[2,128,128]{2,1,0:T(8,128)(2,1)S(1)}, u32[]{:S(2)}, u32[]{:S(2)}) collective-permute-start(bf16[2,128,128]{2,1,0:T(8,128)(2,1)S(1)} %get-tuple-element.91), channel_id=1, source_target_pairs={{0,8},{2,10},{4,12},{6,14},{8,0},{10,2},{12,4},{14,6},{16,24},{18,... | collective-permute-start | bytes 196616 | tf_op jit(solution)/shard_map/ppermute | solution.py:221
  75.7 20.0 %collective-permute-start.23 = (bf16[256,1024]{1,0:T(8,128)(2,1)S(1)}, bf16[256,1024]{1,0:T(8,128)(2,1)S(1)}, u32[]{:S(2)}, u32[]{:S(2)}) collective-permute-start(bf16[256,1024]{1,0:T(8,128)(2,1)S(1)} %turn_features.1.own_ref), channel_id=1, source_target_pairs={{0,1},{1,0},{2,3},{3,2},{4,5},{5,4},{6,7},{7,6},{8,9},{9,8},{10,11... | collective-permute-start | bytes 1572872 | tf_op jit(solution)/shard_map/ppermute | solution.py:225
  80.7 11.8 %collective-permute-start.26 = (bf16[1024,128]{1,0:T(8,128)(2,1)S(1)}, bf16[1024,128]{1,0:T(8,128)(2,1)S(1)}, u32[]{:S(2)}, u32[]{:S(2)}) collective-permute-start(bf16[1024,128]{1,0:T(8,128)(2,1)S(1)} %sum_halves.1.refs_0_), channel_id=1, source_target_pairs={{0,12},{2,14},{4,8},{6,10},{8,4},{10,6},{12,0},{14,2},{16,28},{18,... | collective-permute-start | bytes 786440 | tf_op jit(solution)/shard_map/ppermute | solution.py:221
  80.8 13.3 %collective-permute-start.25 = (bf16[1024,128]{1,0:T(8,128)(2,1)S(1)}, bf16[1024,128]{1,0:T(8,128)(2,1)S(1)}, u32[]{:S(2)}, u32[]{:S(2)}) collective-permute-start(bf16[1024,128]{1,0:T(8,128)(2,1)S(1)} %sum_halves.1.refs_0_), channel_id=1, source_target_pairs={{0,8},{2,10},{4,12},{6,14},{8,0},{10,2},{12,4},{14,6},{16,24},{18,... | collective-permute-start | bytes 786440 | tf_op jit(solution)/shard_map/ppermute | solution.py:221
  84.0 10.1 %collective-permute-start.24 = (bf16[1024,128]{1,0:T(8,128)(2,1)S(1)}, bf16[1024,128]{1,0:T(8,128)(2,1)S(1)}, u32[]{:S(2)}, u32[]{:S(2)}) collective-permute-start(bf16[1024,128]{1,0:T(8,128)(2,1)S(1)} %sum_halves.1.refs_0_), channel_id=1, source_target_pairs={{0,4},{2,6},{4,0},{6,2},{8,12},{10,14},{12,8},{14,10},{16,20},{18,... | collective-permute-start | bytes 786440 | tf_op jit(solution)/shard_map/ppermute | solution.py:221
  84.4 11.4 %collective-permute-start.22 = (bf16[4,128,128]{2,1,0:T(8,128)(2,1)S(1)}, bf16[4,128,128]{2,1,0:T(8,128)(2,1)S(1)}, u32[]{:S(2)}, u32[]{:S(2)}) collective-permute-start(bf16[4,128,128]{2,1,0:T(8,128)(2,1)S(1)} %pad_maximum_fusion), channel_id=1, source_target_pairs={{0,16},{2,18},{4,20},{6,22},{8,24},{10,26},{12,28},{14,30},{16,0},... | collective-permute-start | bytes 393224 | tf_op jit(solution)/shard_map/ppermute | solution.py:221
  96.7 6.2 %collective-permute-start.28 = (f32[256,512]{1,0:T(8,128)S(1)}, f32[256,512]{1,0:T(8,128)S(1)}, u32[]{:S(2)}, u32[]{:S(2)}) collective-permute-start(f32[256,512]{1,0:T(8,128)S(1)} %get-tuple-element.100), channel_id=1, source_target_pairs={{0,2},{2,0},{4,6},{6,4},{8,10},{10,8},{12,14},{14,12},{16,18},{18,... | collective-permute-start | bytes 1572872 | tf_op jit(solution)/shard_map/ppermute | solution.py:221
  96.8 6.1 %collective-permute-start.29 = (bf16[128,512]{1,0:T(8,128)(2,1)S(1)}, bf16[128,512]{1,0:T(8,128)(2,1)S(1)}, u32[]{:S(2)}, u32[]{:S(2)}) collective-permute-start(bf16[128,512]{1,0:T(8,128)(2,1)S(1)} %get-tuple-element.104), channel_id=1, source_target_pairs={{0,4},{2,6},{4,0},{6,2},{8,12},{10,14},{12,8},{14,10},{16,20},{18,... | collective-permute-start | bytes 393224 | tf_op jit(solution)/shard_map/ppermute | solution.py:221
  (11 other events, 99.5 us)

commit v10 on v8

--- a/solution.py
+++ b/solution.py
@@ -548,33 +548,21 @@
         out_ref[:, columns(chunk, PART)] = part.astype(jnp.bfloat16)
 
 
-def sum_cores(kept_ref, arrived_ref, dk_ref, dk_bf_ref, *dv_refs):
-    dk = kept_ref[:, :HD] + arrived_ref[:, :HD]
-    dk_ref[...] = dk
-    dk_bf_ref[...] = dk.astype(jnp.bfloat16)
-    for m, dv_ref in enumerate(dv_refs):
-        for far in range(2):
-            here = pl.ds((far * GROUP + m) * ROWS, ROWS)
-            dv_ref[far] = (kept_ref[here, HD:] + arrived_ref[here, HD:]).astype(jnp.bfloat16)
-
-
-def sum_halves(near_ref, far_ref, out_ref):
-    quarter = GROUP * ROWS
-    for k in range(2):
-        here, there = pl.ds(k * quarter, quarter), pl.ds((1 - k) * quarter, quarter)
-        total = near_ref[here] + far_ref[there].astype(jnp.float32)
-        out_ref[here] = total.astype(jnp.bfloat16)
-
-
-def finish(keep_ref, arrived_ref, far_ref, *refs):
-    row_refs, value_refs, refs = refs[:GROUP], refs[GROUP : 2 * GROUP], refs[2 * GROUP :]
+def pack_grads(value_ref, row_ref, *refs):
+    for m, out_ref in enumerate(refs):
+        out_ref[:, :HD] = value_ref[m * ROWS : (m + 1) * ROWS]
+    refs[-1][:, HD:] = row_ref[...]
+
+
+def finish(keep_ref, arrived_ref, *refs):
+    row_refs, grad_refs, refs = refs[: GROUP - 1], refs[GROUP - 1 : 2 * GROUP - 1], refs[2 * GROUP - 1 :]
     weight_out, query_out, value_out = refs
     head = own_head()
     weight_out[...] = keep_ref[...] + arrived_ref[...]
     for m in range(GROUP):
-        query_out[:, columns(head ^ m, GROUP * HD)] = row_refs[m][...]
-        value = value_refs[m][0].astype(jnp.float32) + far_ref[m].astype(jnp.float32)
-        value_out[:, columns(head ^ m, HD)] = value.astype(jnp.bfloat16)
+        row = row_refs[m][...] if m < GROUP - 1 else grad_refs[m][:, HD:]
+        query_out[:, columns(head ^ m, GROUP * HD)] = row
+        value_out[:, columns(head ^ m, HD)] = grad_refs[m][:, :HD]
 
 
 def shaped(shape, dtype=jnp.bfloat16):
@@ -593,7 +581,7 @@
     features = inputs.shape[1]
     kv_columns = values.shape[1]
     total_rows = 16 * ROWS
-    half = total_rows // 2
+    half, quarter = total_rows // 2, total_rows // 4
     vmem, smem, hbm = whole_spec(), whole_spec(SMEM), whole_spec(HBM)
 
     pairs = pl.pallas_call(
@@ -699,19 +687,10 @@
 
     row_grads = with_partners(row_grads)
     sent = after(sent, far_features, *row_grads)
-    dk_sum, dk_near, *value_grads = pl.pallas_call(
-        sum_cores,
-        out_shape=[shaped((half, HD), jnp.float32), shaped((half, HD))]
-        + [shaped((2, ROWS, HD))] * GROUP,
-        in_specs=[vmem] * 2,
-        out_specs=[vmem] * (2 + GROUP),
-        compiler_params=limits(16),
-        name="sum_cores",
-    )(kept, swap(sent, CORE))
-    dk_far = swap(dk_near, Z_HI)
-    w_far = swap(after(w_near, sent), CORE)
-    value_grads = with_partners(value_grads)
-    value_far = jnp.stack([grad[1] for grad in value_grads])
+    grads = kept + swap(sent, CORE)
+    dk_sum, dv_sum = grads[:, :HD], grads[:, HD:]
+    dk_far = swap(dk_sum.astype(jnp.bfloat16), Z_HI)
+    w_far = swap(after(w_near, dk_sum), CORE)
 
     feature_parts = pl.pallas_call(
         join_features,
@@ -727,27 +706,31 @@
         in_specs=[vmem] * GROUP,
         out_specs=vmem,
         compiler_params=limits(16),
-        cost_estimate=pl.CostEstimate(flops=1_000_000_000, bytes_accessed=0, transcendentals=0),
+        cost_estimate=pl.CostEstimate(flops=4_000_000_000, bytes_accessed=0, transcendentals=0),
         name="turn_features",
     )(*with_partners(feature_parts))
     other_features = swap_tensor(own_features)
 
-    key_grad = pl.pallas_call(
-        sum_halves,
-        out_shape=shaped((half, HD)),
-        in_specs=[vmem] * 2,
-        out_specs=vmem,
-        compiler_params=limits(8),
-        cost_estimate=pl.CostEstimate(flops=1_000_000, bytes_accessed=0, transcendentals=0),
-        name="sum_halves",
-    )(dk_sum, dk_far)
-    key_grad = after(key_grad, own_features, value_far, w_far)
+    dk_far = jnp.concatenate([dk_far[quarter:], dk_far[:quarter]], axis=0)
+    key_grad = (dk_sum + dk_far.astype(jnp.float32)).astype(jnp.bfloat16)
+    key_grad = after(key_grad, own_features, w_far)
     key_grads = with_partners([key_grad] * GROUP)
     own_key_grad = jnp.stack([key_grads[m][m * ROWS : (m + 1) * ROWS] for m in range(GROUP)])
     other_key_grad = swap_tensor(own_key_grad)
 
-    value_far = swap(after(value_far, key_grad), Z_HI)
-    last_grad = swap(after(last_grad, own_key_grad), 6)
+    dv_far = swap(after(dv_sum[quarter:].astype(jnp.bfloat16), key_grad), Z_HI)
+    value_grad = (dv_sum[:quarter] + dv_far.astype(jnp.float32)).astype(jnp.bfloat16)
+    packed_grads = pl.pallas_call(
+        pack_grads,
+        out_shape=[shaped((ROWS, HD))] * (GROUP - 1) + [shaped((ROWS, (GROUP + 1) * HD))],
+        in_specs=[vmem] * 2,
+        out_specs=[vmem] * GROUP,
+        compiler_params=limits(16),
+        name="pack_grads",
+    )(value_grad, last_grad)
+    packed_grads = [after(packed_grads[0], own_key_grad)] + [
+        after(grad, own_key_grad) for grad in packed_grads[1:]
+    ]
 
     keep, send = pl.pallas_call(
         weight_grad,
@@ -760,7 +743,7 @@
             flops=4 * 256 * half * kv_columns, bytes_accessed=4 << 20, transcendentals=0
         ),
         name="weight_grad",
-    )(after(own_features, value_far), other_features, *key_grads)
+    )(own_features, other_features, *key_grads)
     arrived = swap(send, CORE)
 
     d_input = pl.pallas_call(
@@ -783,11 +766,11 @@
             shaped(queries.shape),
             shaped(values.shape),
         ],
-        in_specs=[vmem] * (3 + 2 * GROUP),
+        in_specs=[vmem] * (1 + 2 * GROUP),
         out_specs=[vmem] * 3,
         compiler_params=limits(16),
         name="finish",
-    )(after(keep, d_input), arrived, value_far, *row_grads, last_grad, *value_grads)
+    )(keep, arrived, *row_grads, *with_partners(packed_grads))
     return (d_query, d_value, d_input, d_wkey)
 
 

time: 95.2 us -> 95.2 us (level); the launches traced: 94.5 us -> 95.5 us
    ppermute x27 -> x26, waiting for transfers between devices: 36.3 us -> 38.6 us  [swap(): return lax.ppermute(array, 'dp', [(i, i ^ mask) for i in range(16)])]
    ppermute x3, waiting for transfers between devices: 3.11 us -> 1.21 us  [swap_tensor(): return lax.ppermute(array, 'tensor', [(0, 1), (1, 0)])]
    ppermute x27 -> x26, starting transfers between devices: 27.5 us -> 27.4 us  [swap(): return lax.ppermute(array, 'dp', [(i, i ^ mask) for i in range(16)])]
  transfers between devices with their start and end apart: 30 -> 29, of which waited for: 15 -> 14; matrix products, arithmetic and copies ran while one was open for 1% -> 1% of each run, Pallas kernels for 16% -> 16%
where the time goes in v10:
time: 95.2 us; the launch traced here: 95.5 us
  waiting for transfers between devices  39.8 us (42%)
  starting transfers between devices  32.2 us (34%)
  Pallas kernels  21.3 us (22%)
  local copies, waits for them, and re-layouts  1.06 us (1%)
    ppermute x26, waiting for transfers between devices, swap(): return lax.ppermute(array, 'dp', [(i, i ^ mask) for i in range(16)])  38.6 us
    ppermute x26, starting transfers between devices, swap(): return lax.ppermute(array, 'dp', [(i, i ^ mask) for i in range(16)])  27.4 us
    pallas_call x1, Pallas kernels, on_device_by_heads(): pl.pallas_call(attend_first, out_shape=[row_grad] * (GROUP - 1) + [sorted...  6.83 us
    ppermute x3, starting transfers between devices, swap_tensor(): return lax.ppermute(array, 'tensor', [(0, 1), (1, 0)])  4.75 us
    pallas_call x1, Pallas kernels, on_device_by_heads(): pl.pallas_call(project_keys, out_shape=[shaped((MARKED, 2 * HD))] * GROUP...  4.51 us
    pallas_call x1, Pallas kernels, on_device_by_heads(): pl.pallas_call(attend_last, out_shape=[row_grad, half_sums, half_sums], i...  2.93 us
    pallas_call x1, Pallas kernels, on_device_by_heads(): pl.pallas_call(pack_weights, out_shape=shaped((2 * PART, kv_columns)), in...  2.32 us
    pallas_call x1, Pallas kernels, on_device_by_heads(): pl.pallas_call(input_grad, out_shape=shaped((ROWS, features // 2)), in_sp...  2.27 us
  transfers between devices with their start and end apart: 29, of which 14 were waited for; matrix products, arithmetic and copies ran while one was open for 1% of the time, Pallas kernels for 16%

profile of v10, /device:TPU:0, one launch (start us, length us, event | category | flops | bytes accessed | tf_op | source)
XLA Modules:
  0.0 95.5 jit_solution(9063594332471062801)
XLA Ops:
  0.7 4.5 %project_keys.1 = (bf16[144,256]{1,0:T(8,128)(2,1)}, bf16[144,256]{1,0:T(8,128)(2,1)}, bf16[144,256]{1,0:T(8,128)(2,1)}, bf16[144,256]{1,0:T(8,128)(2,1)}) custom-call(s32[2]{0:T(128)} %pos_ref.1, bf16[128,4096]{1,0:T(8,128)(2,1)} %inputs_ref.2, bf16[128,512]{1,0:T(8,128)(2,1)} %values_ref.1, bf16[4096,512]{1,0:T(8,128)(2,1)} %w_own.1), custom_call_target="tpu_custom_call" | custom-call | flops 536870912 | bytes 4194304 | tf_op jit(solution)/shard_map/project_keys/pallas_call | solution.py:587
  5.2 3.0 %collective-permute-start = (bf16[144,256]{1,0:T(8,128)(2,1)}, bf16[144,256]{1,0:T(8,128)(2,1)S(1)}, u32[]{:S(2)}, u32[]{:S(2)}) collective-permute-start(bf16[144,256]{1,0:T(8,128)(2,1)} %get-tuple-element.59), channel_id=1, source_target_pairs={{0,4},{2,6},{4,0},{6,2},{8,12},{10,14},{12,8},{14,10},{16,20},{18,... | collective-permute-start | bytes 221192 | tf_op jit(solution)/shard_map/ppermute | solution.py:221
  10.8 3.1 %collective-permute-start.7 = (bf16[288,256]{1,0:T(8,128)(2,1)S(1)}, bf16[288,256]{1,0:T(8,128)(2,1)S(1)}, u32[]{:S(2)}, u32[]{:S(2)}) collective-permute-start(bf16[288,256]{1,0:T(8,128)(2,1)S(1)} %get-tuple-element.113.refs_3_), channel_id=1, source_target_pairs={{0,16},{2,18},{4,20},{6,22},{8,24},{10,26},{12,28},{14,30},{16,0},... | collective-permute-start | bytes 442376 | tf_op jit(solution)/shard_map/ppermute | solution.py:221
  13.9 2.4 %collective-permute-done.3 = bf16[144,256]{1,0:T(8,128)(2,1)S(1)} collective-permute-done((bf16[144,256]{1,0:T(8,128)(2,1)}, bf16[144,256]{1,0:T(8,128)(2,1)S(1)}, u32[]{:S(2)}, u32[]{:S(2)}) %collective-permute-start.3) | collective-permute-done | bytes 73760 | tf_op jit(solution)/shard_map/ppermute | solution.py:221
  16.3 2.3 %collective-permute-start.8 = (bf16[288,256]{1,0:T(8,128)(2,1)S(1)}, bf16[288,256]{1,0:T(8,128)(2,1)S(1)}, u32[]{:S(2)}, u32[]{:S(2)}) collective-permute-start(bf16[288,256]{1,0:T(8,128)(2,1)S(1)} %get-tuple-element.109.refs_4_), channel_id=1, source_target_pairs={{0,16},{2,18},{4,20},{6,22},{8,24},{10,26},{12,28},{14,30},{16,0},... | collective-permute-start | bytes 442376 | tf_op jit(solution)/shard_map/ppermute | solution.py:221
  19.4 2.3 %pack_weights.1 = bf16[1024,512]{1,0:T(8,128)(2,1)} custom-call(bf16[4096,512]{1,0:T(8,128)(2,1)} %w_own.1), custom_call_target="tpu_custom_call" | custom-call | tf_op jit(solution)/shard_map/pack_weights/pallas_call | solution.py:632
  21.9 1.6 %collective-permute-start.4 = (bf16[1024,512]{1,0:T(8,128)(2,1)}, bf16[1024,512]{1,0:T(8,128)(2,1)S(1)}, u32[]{:S(2)}, u32[]{:S(2)}) collective-permute-start(bf16[1024,512]{1,0:T(8,128)(2,1)} %pack_weights.1), channel_id=1, source_target_pairs={{0,1},{1,0},{2,3},{3,2},{4,5},{5,4},{6,7},{7,6},{8,9},{9,8},{10,11... | collective-permute-start | bytes 3145736 | tf_op jit(solution)/shard_map/ppermute | solution.py:225
  24.2 2.4 %collective-permute-done.8.refs_6_ = bf16[288,256]{1,0:T(8,128)(2,1)S(1)} collective-permute-done((bf16[288,256]{1,0:T(8,128)(2,1)S(1)}, bf16[288,256]{1,0:T(8,128)(2,1)S(1)}, u32[]{:S(2)}, u32[]{:S(2)}) %collective-permute-start.8) | collective-permute-done | bytes 147488 | tf_op jit(solution)/shard_map/ppermute | solution.py:221
  26.5 2.3 %collective-permute-done.6.refs_2_ = bf16[128,1024]{1,0:T(8,128)(2,1)S(1)} collective-permute-done((bf16[128,1024]{1,0:T(8,128)(2,1)S(1)}, bf16[128,1024]{1,0:T(8,128)(2,1)S(1)}, u32[]{:S(2)}, u32[]{:S(2)}) %collective-permute-start.6) | collective-permute-done | bytes 262176 | tf_op jit(solution)/shard_map/ppermute | solution.py:221
  29.4 3.2 %collective-permute-start.10 = (bf16[4,128,256]{2,1,0:T(8,128)(2,1)S(1)}, bf16[4,128,256]{2,1,0:T(8,128)(2,1)S(1)}, u32[]{:S(2)}, u32[]{:S(2)}) collective-permute-start(bf16[4,128,256]{2,1,0:T(8,128)(2,1)S(1)} %get-tuple-element.77), channel_id=1, source_target_pairs={{0,16},{2,18},{4,20},{6,22},{8,24},{10,26},{12,28},{14,30},{16,0},... | collective-permute-start | bytes 786440 | tf_op jit(solution)/shard_map/ppermute | solution.py:221
  32.6 6.8 %attend_first.1 = (bf16[128,512]{1,0:T(8,128)(2,1)S(1)}, bf16[128,512]{1,0:T(8,128)(2,1)S(1)}, bf16[128,512]{1,0:T(8,128)(2,1)S(1)}, bf16[2176,128]{1,0:T(8,128)...) custom-call(s32[4]{0:T(128)S(1)} %copy-done.4, ...), custom_call_target="tpu_custom_call" | custom-call | flops 4000000000 | tf_op jit(solution)/shard_map/attend_first/pallas_call | solution.py:665
  40.6 2.9 %collective-permute-done.1.row_ref = bf16[128,1024]{1,0:T(8,128)(2,1)S(1)} collective-permute-done((bf16[128,1024]{1,0:T(8,128)(2,1)S(1)}, bf16[128,1024]{1,0:T(8,128)(2,1)S(1)}, u32[]{:S(2)}, u32[]{:S(2)}) %collective-permute-start.1) | collective-permute-done | bytes 262176 | tf_op jit(solution)/shard_map/ppermute | solution.py:221
  44.6 2.9 %attend_last.1 = (bf16[128,512]{1,0:T(8,128)(2,1)S(1)}, f32[1024,256]{1,0:T(8,128)S(1)}, f32[1024,256]{1,0:T(8,128)S(1)}) custom-call(s32[4]{0:T(128)S(1)} %copy-done.4, bf16[128,1024]{1,0:T(8,128)(2,1)S(1)} %collective-permute-done.1.row_ref, bf16[2176,128]{1,0:T(8,128)(2,1)S(1)} %get-tuple-element.70.keys, bf16[128,2176]{1,0:T(8,128)(2,1)S(1)} %get-tuple-element.71.keys_t, ...), custom_call_target="tpu_custom_call" | custom-call | flops 4000000000 | tf_op jit(solution)/shard_map/attend_last/pallas_call | solution.py:677
  48.2 2.2 %collective-permute-start.13 = (bf16[2,128,256]{2,1,0:T(8,128)(2,1)S(1)}, bf16[2,128,256]{2,1,0:T(8,128)(2,1)S(1)}, u32[]{:S(2)}, u32[]{:S(2)}) collective-permute-start(bf16[2,128,256]{2,1,0:T(8,128)(2,1)S(1)} %get-tuple-element.84), channel_id=1, source_target_pairs={{0,4},{2,6},{4,0},{6,2},{8,12},{10,14},{12,8},{14,10},{16,20},{18,... | collective-permute-start | bytes 393224 | tf_op jit(solution)/shard_map/ppermute | solution.py:221
  52.5 1.7 %collective-permute-done.13.refs_1_ = bf16[2,128,256]{2,1,0:T(8,128)(2,1)S(1)} collective-permute-done((bf16[2,128,256]{2,1,0:T(8,128)(2,1)S(1)}, bf16[2,128,256]{2,1,0:T(8,128)(2,1)S(1)}, u32[]{:S(2)}, u32[]{:S(2)}) %collective-permute-start.13) | collective-permute-done | bytes 131104 | tf_op jit(solution)/shard_map/ppermute | solution.py:221
  54.2 5.2 %collective-permute-done.14.refs_2_ = bf16[2,128,256]{2,1,0:T(8,128)(2,1)S(1)} collective-permute-done((bf16[2,128,256]{2,1,0:T(8,128)(2,1)S(1)}, bf16[2,128,256]{2,1,0:T(8,128)(2,1)S(1)}, u32[]{:S(2)}, u32[]{:S(2)}) %collective-permute-start.14) | collective-permute-done | bytes 131104 | tf_op jit(solution)/shard_map/ppermute | solution.py:221
  59.9 6.6 %collective-permute-done.18 = bf16[1024,128]{1,0:T(8,128)(2,1)S(1)} collective-permute-done((bf16[1024,128]{1,0:T(8,128)(2,1)S(1)}, bf16[1024,128]{1,0:T(8,128)(2,1)S(1)}, u32[]{:S(2)}, u32[]{:S(2)}) %collective-permute-start.18) | collective-permute-done | bytes 262176 | tf_op jit(solution)/shard_map/ppermute | solution.py:221
  66.7 1.6 %collective-permute-start.16 = (bf16[256,1024]{1,0:T(8,128)(2,1)S(1)}, bf16[256,1024]{1,0:T(8,128)(2,1)S(1)}, u32[]{:S(2)}, u32[]{:S(2)}) collective-permute-start(bf16[256,1024]{1,0:T(8,128)(2,1)S(1)} %turn_features.1.own_ref), channel_id=1, source_target_pairs={{0,1},{1,0},{2,3},{3,2},{4,5},{5,4},{6,7},{7,6},{8,9},{9,8},{10,11... | collective-permute-start | bytes 1572872 | tf_op jit(solution)/shard_map/ppermute | solution.py:225
  68.3 3.1 %collective-permute-start.21 = (bf16[1024,128]{1,0:T(8,128)(2,1)S(1)}, bf16[1024,128]{1,0:T(8,128)(2,1)S(1)}, u32[]{:S(2)}, u32[]{:S(2)}) collective-permute-start(bf16[1024,128]{1,0:T(8,128)(2,1)S(1)} %add_convert_fusion.refs_0_), channel_id=1, source_target_pairs={{0,8},{2,10},{4,12},{6,14},{8,0},{10,2},{12,4},{14,6},{16,24},{18,... | collective-permute-start | bytes 786440 | tf_op jit(solution)/shard_map/ppermute | solution.py:221
  71.8 7.4 %collective-permute-done.22.refs_3_ = bf16[1024,128]{1,0:T(8,128)(2,1)S(1)} collective-permute-done((bf16[1024,128]{1,0:T(8,128)(2,1)S(1)}, bf16[1024,128]{1,0:T(8,128)(2,1)S(1)}, u32[]{:S(2)}, u32[]{:S(2)}) %collective-permute-start.22) | collective-permute-done | bytes 262176 | tf_op jit(solution)/shard_map/ppermute | solution.py:221
  79.2 4.3 %collective-permute-done.21.refs_2_ = bf16[1024,128]{1,0:T(8,128)(2,1)S(1)} collective-permute-done((bf16[1024,128]{1,0:T(8,128)(2,1)S(1)}, bf16[1024,128]{1,0:T(8,128)(2,1)S(1)}, u32[]{:S(2)}, u32[]{:S(2)}) %collective-permute-start.21) | collective-permute-done | bytes 262176 | tf_op jit(solution)/shard_map/ppermute | solution.py:221
  83.5 1.6 %collective-permute-start.28 = (bf16[4,128,128]{2,1,0:T(8,128)(2,1)S(1)}, bf16[4,128,128]{2,1,0:T(8,128)(2,1)S(1)}, u32[]{:S(2)}, u32[]{:S(2)}) collective-permute-start(bf16[4,128,128]{2,1,0:T(8,128)(2,1)S(1)} %pad_maximum_fusion.own_ref), channel_id=1, source_target_pairs={{0,1},{1,0},{2,3},{3,2},{4,5},{5,4},{6,7},{7,6},{8,9},{9,8},{10,11... | collective-permute-start | bytes 393224 | tf_op jit(solution)/shard_map/ppermute | solution.py:225
  87.8 2.0 %collective-permute-start.25 = (bf16[128,128]{1,0:T(8,128)(2,1)S(1)}, bf16[128,128]{1,0:T(8,128)(2,1)S(1)}, u32[]{:S(2)}, u32[]{:S(2)}) collective-permute-start(bf16[128,128]{1,0:T(8,128)(2,1)S(1)} %get-tuple-element.97), channel_id=1, source_target_pairs={{0,4},{2,6},{4,0},{6,2},{8,12},{10,14},{12,8},{14,10},{16,20},{18,... | collective-permute-start | bytes 98312 | tf_op jit(solution)/shard_map/ppermute | solution.py:221
  89.8 2.3 %input_grad.1 = bf16[128,2048]{1,0:T(8,128)(2,1)} custom-call(bf16[4,128,128]{2,1,0:T(8,128)(2,1)S(1)} %pad_maximum_fusion.own_ref, bf16[4,128,128]{2,1,0:T(8,128)(2,1)S(1)} %collective-permute-done.28.other_ref, bf16[4096,512]{1,0:T(8,128)(2,1)S(1)} %copy-done, bf16[1024,512]{1,0:T(8,128)(2,1)S(1)} %collective-permute-done.4.w_near, ...), custom_call_target="tpu_custom_call" | custom-call | flops 8000000000 | bytes 5242880 | tf_op jit(solution)/shard_map/input_grad/pallas_call | solution.py:749
  (73 shorter events, 16.9 us)
Async XLA Ops:
  9.8 6.5 %collective-permute-start.3 = (bf16[144,256]{1,0:T(8,128)(2,1)}, bf16[144,256]{1,0:T(8,128)(2,1)S(1)}, u32[]{:S(2)}, u32[]{:S(2)}) collective-permute-start(bf16[144,256]{1,0:T(8,128)(2,1)} %get-tuple-element.64), channel_id=1, source_target_pairs={{0,12},{2,14},{4,8},{6,10},{8,4},{10,6},{12,0},{14,2},{16,28},{18,... | collective-permute-start | bytes 221192 | tf_op jit(solution)/shard_map/ppermute | solution.py:221
  10.8 13.3 %collective-permute-start.7 = (bf16[288,256]{1,0:T(8,128)(2,1)S(1)}, bf16[288,256]{1,0:T(8,128)(2,1)S(1)}, u32[]{:S(2)}, u32[]{:S(2)}) collective-permute-start(bf16[288,256]{1,0:T(8,128)(2,1)S(1)} %get-tuple-element.113.refs_3_), channel_id=1, source_target_pairs={{0,16},{2,18},{4,20},{6,22},{8,24},{10,26},{12,28},{14,30},{16,0},... | collective-permute-start | bytes 442376 | tf_op jit(solution)/shard_map/ppermute | solution.py:221
  16.3 10.2 %collective-permute-start.8 = (bf16[288,256]{1,0:T(8,128)(2,1)S(1)}, bf16[288,256]{1,0:T(8,128)(2,1)S(1)}, u32[]{:S(2)}, u32[]{:S(2)}) collective-permute-start(bf16[288,256]{1,0:T(8,128)(2,1)S(1)} %get-tuple-element.109.refs_4_), channel_id=1, source_target_pairs={{0,16},{2,18},{4,20},{6,22},{8,24},{10,26},{12,28},{14,30},{16,0},... | collective-permute-start | bytes 442376 | tf_op jit(solution)/shard_map/ppermute | solution.py:221
  18.6 7.9 %collective-permute-start.5 = (bf16[128,1024]{1,0:T(8,128)(2,1)S(1)}, bf16[128,1024]{1,0:T(8,128)(2,1)S(1)}, u32[]{:S(2)}, u32[]{:S(2)}) collective-permute-start(bf16[128,1024]{1,0:T(8,128)(2,1)S(1)} %get-tuple-element.67), channel_id=1, source_target_pairs={{0,4},{2,6},{4,0},{6,2},{8,12},{10,14},{12,8},{14,10},{16,20},{18,... | collective-permute-start | bytes 786440 | tf_op jit(solution)/shard_map/ppermute | solution.py:221
  19.2 9.6 %collective-permute-start.6 = (bf16[128,1024]{1,0:T(8,128)(2,1)S(1)}, bf16[128,1024]{1,0:T(8,128)(2,1)S(1)}, u32[]{:S(2)}, u32[]{:S(2)}) collective-permute-start(bf16[128,1024]{1,0:T(8,128)(2,1)S(1)} %get-tuple-element.68), channel_id=1, source_target_pairs={{0,8},{2,10},{4,12},{6,14},{8,0},{10,2},{12,4},{14,6},{16,24},{18,... | collective-permute-start | bytes 786440 | tf_op jit(solution)/shard_map/ppermute | solution.py:221
  21.9 22.8 %collective-permute-start.4 = (bf16[1024,512]{1,0:T(8,128)(2,1)}, bf16[1024,512]{1,0:T(8,128)(2,1)S(1)}, u32[]{:S(2)}, u32[]{:S(2)}) collective-permute-start(bf16[1024,512]{1,0:T(8,128)(2,1)} %pack_weights.1), channel_id=1, source_target_pairs={{0,1},{1,0},{2,3},{3,2},{4,5},{5,4},{6,7},{7,6},{8,9},{9,8},{10,11... | collective-permute-start | bytes 3145736 | tf_op jit(solution)/shard_map/ppermute | solution.py:225
  28.9 14.6 %collective-permute-start.1 = (bf16[128,1024]{1,0:T(8,128)(2,1)S(1)}, bf16[128,1024]{1,0:T(8,128)(2,1)S(1)}, u32[]{:S(2)}, u32[]{:S(2)}) collective-permute-start(bf16[128,1024]{1,0:T(8,128)(2,1)S(1)} %get-tuple-element.62), channel_id=1, source_target_pairs={{0,12},{2,14},{4,8},{6,10},{8,4},{10,6},{12,0},{14,2},{16,28},{18,... | collective-permute-start | bytes 786440 | tf_op jit(solution)/shard_map/ppermute | solution.py:221
  29.4 18.2 %collective-permute-start.10 = (bf16[4,128,256]{2,1,0:T(8,128)(2,1)S(1)}, bf16[4,128,256]{2,1,0:T(8,128)(2,1)S(1)}, u32[]{:S(2)}, u32[]{:S(2)}) collective-permute-start(bf16[4,128,256]{2,1,0:T(8,128)(2,1)S(1)} %get-tuple-element.77), channel_id=1, source_target_pairs={{0,16},{2,18},{4,20},{6,22},{8,24},{10,26},{12,28},{14,30},{16,0},... | collective-permute-start | bytes 786440 | tf_op jit(solution)/shard_map/ppermute | solution.py:221
  39.5 8.1 %collective-permute-start.11 = (bf16[128,512]{1,0:T(8,128)(2,1)S(1)}, bf16[128,512]{1,0:T(8,128)(2,1)S(1)}, u32[]{:S(2)}, u32[]{:S(2)}) collective-permute-start(bf16[128,512]{1,0:T(8,128)(2,1)S(1)} %get-tuple-element.79), channel_id=1, source_target_pairs={{0,4},{2,6},{4,0},{6,2},{8,12},{10,14},{12,8},{14,10},{16,20},{18,... | collective-permute-start | bytes 393224 | tf_op jit(solution)/shard_map/ppermute | solution.py:221
  39.6 8.0 %collective-permute-start.12 = (bf16[128,512]{1,0:T(8,128)(2,1)S(1)}, bf16[128,512]{1,0:T(8,128)(2,1)S(1)}, u32[]{:S(2)}, u32[]{:S(2)}) collective-permute-start(bf16[128,512]{1,0:T(8,128)(2,1)S(1)} %get-tuple-element.80), channel_id=1, source_target_pairs={{0,8},{2,10},{4,12},{6,14},{8,0},{10,2},{12,4},{14,6},{16,24},{18,... | collective-permute-start | bytes 393224 | tf_op jit(solution)/shard_map/ppermute | solution.py:221
  47.7 19.0 %collective-permute-start.19 = (bf16[1024,512]{1,0:T(8,128)(2,1)S(1)}, bf16[1024,512]{1,0:T(8,128)(2,1)S(1)}, u32[]{:S(2)}, u32[]{:S(2)}) collective-permute-start(bf16[1024,512]{1,0:T(8,128)(2,1)S(1)} %collective-permute-done.4.w_near), channel_id=1, source_target_pairs={{0,2},{2,0},{4,6},{6,4},{8,10},{10,8},{12,14},{14,12},{16,18},{18,... | collective-permute-start | bytes 3145736 | tf_op jit(solution)/shard_map/ppermute | solution.py:221
  50.4 9.0 %collective-permute-start.14 = (bf16[2,128,256]{2,1,0:T(8,128)(2,1)S(1)}, bf16[2,128,256]{2,1,0:T(8,128)(2,1)S(1)}, u32[]{:S(2)}, u32[]{:S(2)}) collective-permute-start(bf16[2,128,256]{2,1,0:T(8,128)(2,1)S(1)} %get-tuple-element.85), channel_id=1, source_target_pairs={{0,8},{2,10},{4,12},{6,14},{8,0},{10,2},{12,4},{14,6},{16,24},{18,... | collective-permute-start | bytes 393224 | tf_op jit(solution)/shard_map/ppermute | solution.py:221
  50.5 9.2 %collective-permute-start.15 = (bf16[2,128,256]{2,1,0:T(8,128)(2,1)S(1)}, bf16[2,128,256]{2,1,0:T(8,128)(2,1)S(1)}, u32[]{:S(2)}, u32[]{:S(2)}) collective-permute-start(bf16[2,128,256]{2,1,0:T(8,128)(2,1)S(1)} %get-tuple-element.86), channel_id=1, source_target_pairs={{0,12},{2,14},{4,8},{6,10},{8,4},{10,6},{12,0},{14,2},{16,28},{18,... | collective-permute-start | bytes 393224 | tf_op jit(solution)/shard_map/ppermute | solution.py:221
  52.2 14.4 %collective-permute-start.18 = (bf16[1024,128]{1,0:T(8,128)(2,1)S(1)}, bf16[1024,128]{1,0:T(8,128)(2,1)S(1)}, u32[]{:S(2)}, u32[]{:S(2)}) collective-permute-start(bf16[1024,128]{1,0:T(8,128)(2,1)S(1)} %slice.59), channel_id=1, source_target_pairs={{0,16},{2,18},{4,20},{6,22},{8,24},{10,26},{12,28},{14,30},{16,0},... | collective-permute-start | bytes 786440 | tf_op jit(solution)/shard_map/ppermute | solution.py:221
  66.7 12.5 %collective-permute-start.22 = (bf16[1024,128]{1,0:T(8,128)(2,1)S(1)}, bf16[1024,128]{1,0:T(8,128)(2,1)S(1)}, u32[]{:S(2)}, u32[]{:S(2)}) collective-permute-start(bf16[1024,128]{1,0:T(8,128)(2,1)S(1)} %add_convert_fusion.refs_0_), channel_id=1, source_target_pairs={{0,12},{2,14},{4,8},{6,10},{8,4},{10,6},{12,0},{14,2},{16,28},{18,... | collective-permute-start | bytes 786440 | tf_op jit(solution)/shard_map/ppermute | solution.py:221
  66.7 18.5 %collective-permute-start.16 = (bf16[256,1024]{1,0:T(8,128)(2,1)S(1)}, bf16[256,1024]{1,0:T(8,128)(2,1)S(1)}, u32[]{:S(2)}, u32[]{:S(2)}) collective-permute-start(bf16[256,1024]{1,0:T(8,128)(2,1)S(1)} %turn_features.1.own_ref), channel_id=1, source_target_pairs={{0,1},{1,0},{2,3},{3,2},{4,5},{5,4},{6,7},{7,6},{8,9},{9,8},{10,11... | collective-permute-start | bytes 1572872 | tf_op jit(solution)/shard_map/ppermute | solution.py:225
  68.3 15.2 %collective-permute-start.21 = (bf16[1024,128]{1,0:T(8,128)(2,1)S(1)}, bf16[1024,128]{1,0:T(8,128)(2,1)S(1)}, u32[]{:S(2)}, u32[]{:S(2)}) collective-permute-start(bf16[1024,128]{1,0:T(8,128)(2,1)S(1)} %add_convert_fusion.refs_0_), channel_id=1, source_target_pairs={{0,8},{2,10},{4,12},{6,14},{8,0},{10,2},{12,4},{14,6},{16,24},{18,... | collective-permute-start | bytes 786440 | tf_op jit(solution)/shard_map/ppermute | solution.py:221
  71.4 12.1 %collective-permute-start.20 = (bf16[1024,128]{1,0:T(8,128)(2,1)S(1)}, bf16[1024,128]{1,0:T(8,128)(2,1)S(1)}, u32[]{:S(2)}, u32[]{:S(2)}) collective-permute-start(bf16[1024,128]{1,0:T(8,128)(2,1)S(1)} %add_convert_fusion.refs_0_), channel_id=1, source_target_pairs={{0,4},{2,6},{4,0},{6,2},{8,12},{10,14},{12,8},{14,10},{16,20},{18,... | collective-permute-start | bytes 786440 | tf_op jit(solution)/shard_map/ppermute | solution.py:221
  71.8 13.3 %collective-permute-start.24 = (bf16[512,128]{1,0:T(8,128)(2,1)S(1)}, bf16[512,128]{1,0:T(8,128)(2,1)S(1)}, u32[]{:S(2)}, u32[]{:S(2)}) collective-permute-start(bf16[512,128]{1,0:T(8,128)(2,1)S(1)} %slice.58), channel_id=1, source_target_pairs={{0,16},{2,18},{4,20},{6,22},{8,24},{10,26},{12,28},{14,30},{16,0},... | collective-permute-start | bytes 393224 | tf_op jit(solution)/shard_map/ppermute | solution.py:221
  83.5 6.2 %collective-permute-start.28 = (bf16[4,128,128]{2,1,0:T(8,128)(2,1)S(1)}, bf16[4,128,128]{2,1,0:T(8,128)(2,1)S(1)}, u32[]{:S(2)}, u32[]{:S(2)}) collective-permute-start(bf16[4,128,128]{2,1,0:T(8,128)(2,1)S(1)} %pad_maximum_fusion.own_ref), channel_id=1, source_target_pairs={{0,1},{1,0},{2,3},{3,2},{4,5},{5,4},{6,7},{7,6},{8,9},{9,8},{10,11... | collective-permute-start | bytes 393224 | tf_op jit(solution)/shard_map/ppermute | solution.py:225
  86.1 8.3 %collective-permute-start.23 = (f32[256,512]{1,0:T(8,128)S(1)}, f32[256,512]{1,0:T(8,128)S(1)}, u32[]{:S(2)}, u32[]{:S(2)}) collective-permute-start(f32[256,512]{1,0:T(8,128)S(1)} %get-tuple-element.91), channel_id=1, source_target_pairs={{0,2},{2,0},{4,6},{6,4},{8,10},{10,8},{12,14},{14,12},{16,18},{18,... | collective-permute-start | bytes 1572872 | tf_op jit(solution)/shard_map/ppermute | solution.py:221
  86.2 8.2 %collective-permute-start.27 = (bf16[128,640]{1,0:T(8,128)(2,1)S(1)}, bf16[128,640]{1,0:T(8,128)(2,1)S(1)}, u32[]{:S(2)}, u32[]{:S(2)}) collective-permute-start(bf16[128,640]{1,0:T(8,128)(2,1)S(1)} %get-tuple-element.101), channel_id=1, source_target_pairs={{0,12},{2,14},{4,8},{6,10},{8,4},{10,6},{12,0},{14,2},{16,28},{18,... | collective-permute-start | bytes 491528 | tf_op jit(solution)/shard_map/ppermute | solution.py:221
  86.3 6.7 %collective-permute-start.26 = (bf16[128,128]{1,0:T(8,128)(2,1)S(1)}, bf16[128,128]{1,0:T(8,128)(2,1)S(1)}, u32[]{:S(2)}, u32[]{:S(2)}) collective-permute-start(bf16[128,128]{1,0:T(8,128)(2,1)S(1)} %get-tuple-element.99), channel_id=1, source_target_pairs={{0,8},{2,10},{4,12},{6,14},{8,0},{10,2},{12,4},{14,6},{16,24},{18,... | collective-permute-start | bytes 98312 | tf_op jit(solution)/shard_map/ppermute | solution.py:221
  87.8 6.7 %collective-permute-start.25 = (bf16[128,128]{1,0:T(8,128)(2,1)S(1)}, bf16[128,128]{1,0:T(8,128)(2,1)S(1)}, u32[]{:S(2)}, u32[]{:S(2)}) collective-permute-start(bf16[128,128]{1,0:T(8,128)(2,1)S(1)} %get-tuple-element.97), channel_id=1, source_target_pairs={{0,4},{2,6},{4,0},{6,2},{8,12},{10,14},{12,8},{14,10},{16,20},{18,... | collective-permute-start | bytes 98312 | tf_op jit(solution)/shard_map/ppermute | solution.py:221
  (10 other events, 80.2 us)

commit v11 on v10

--- a/solution.py
+++ b/solution.py
@@ -548,21 +548,19 @@
         out_ref[:, columns(chunk, PART)] = part.astype(jnp.bfloat16)
 
 
-def pack_grads(value_ref, row_ref, *refs):
+def pack_grads(value_ref, *refs):
     for m, out_ref in enumerate(refs):
-        out_ref[:, :HD] = value_ref[m * ROWS : (m + 1) * ROWS]
-    refs[-1][:, HD:] = row_ref[...]
+        out_ref[...] = value_ref[m * ROWS : (m + 1) * ROWS]
 
 
 def finish(keep_ref, arrived_ref, *refs):
-    row_refs, grad_refs, refs = refs[: GROUP - 1], refs[GROUP - 1 : 2 * GROUP - 1], refs[2 * GROUP - 1 :]
+    row_refs, value_refs, refs = refs[:GROUP], refs[GROUP : 2 * GROUP], refs[2 * GROUP :]
     weight_out, query_out, value_out = refs
     head = own_head()
     weight_out[...] = keep_ref[...] + arrived_ref[...]
     for m in range(GROUP):
-        row = row_refs[m][...] if m < GROUP - 1 else grad_refs[m][:, HD:]
-        query_out[:, columns(head ^ m, GROUP * HD)] = row
-        value_out[:, columns(head ^ m, HD)] = grad_refs[m][:, :HD]
+        query_out[:, columns(head ^ m, GROUP * HD)] = row_refs[m][...]
+        value_out[:, columns(head ^ m, HD)] = value_refs[m][...]
 
 
 def shaped(shape, dtype=jnp.bfloat16):
@@ -690,7 +688,7 @@
     grads = kept + swap(sent, CORE)
     dk_sum, dv_sum = grads[:, :HD], grads[:, HD:]
     dk_far = swap(dk_sum.astype(jnp.bfloat16), Z_HI)
-    w_far = swap(after(w_near, dk_sum), CORE)
+    w_far = swap(after(w_near, sent), CORE)
 
     feature_parts = pl.pallas_call(
         join_features,
@@ -706,14 +704,15 @@
         in_specs=[vmem] * GROUP,
         out_specs=vmem,
         compiler_params=limits(16),
-        cost_estimate=pl.CostEstimate(flops=4_000_000_000, bytes_accessed=0, transcendentals=0),
+        cost_estimate=pl.CostEstimate(flops=2_000_000_000, bytes_accessed=0, transcendentals=0),
         name="turn_features",
     )(*with_partners(feature_parts))
     other_features = swap_tensor(own_features)
 
     dk_far = jnp.concatenate([dk_far[quarter:], dk_far[:quarter]], axis=0)
     key_grad = (dk_sum + dk_far.astype(jnp.float32)).astype(jnp.bfloat16)
-    key_grad = after(key_grad, own_features, w_far)
+    last_grad = swap(after(last_grad, dk_sum), 6)
+    key_grad = after(key_grad, own_features, w_far, last_grad)
     key_grads = with_partners([key_grad] * GROUP)
     own_key_grad = jnp.stack([key_grads[m][m * ROWS : (m + 1) * ROWS] for m in range(GROUP)])
     other_key_grad = swap_tensor(own_key_grad)
@@ -722,12 +721,12 @@
     value_grad = (dv_sum[:quarter] + dv_far.astype(jnp.float32)).astype(jnp.bfloat16)
     packed_grads = pl.pallas_call(
         pack_grads,
-        out_shape=[shaped((ROWS, HD))] * (GROUP - 1) + [shaped((ROWS, (GROUP + 1) * HD))],
-        in_specs=[vmem] * 2,
+        out_shape=[shaped((ROWS, HD))] * GROUP,
+        in_specs=[vmem],
         out_specs=[vmem] * GROUP,
         compiler_params=limits(16),
         name="pack_grads",
-    )(value_grad, last_grad)
+    )(value_grad)
     packed_grads = [after(packed_grads[0], own_key_grad)] + [
         after(grad, own_key_grad) for grad in packed_grads[1:]
     ]
@@ -766,11 +765,11 @@
             shaped(queries.shape),
             shaped(values.shape),
         ],
-        in_specs=[vmem] * (1 + 2 * GROUP),
+        in_specs=[vmem] * (2 + 2 * GROUP),
         out_specs=[vmem] * 3,
         compiler_params=limits(16),
         name="finish",
-    )(keep, arrived, *row_grads, *with_partners(packed_grads))
+    )(keep, arrived, *row_grads, last_grad, *with_partners(packed_grads))
     return (d_query, d_value, d_input, d_wkey)
 
 

time: 95.2 us -> 93.3 us (0.980)
  waiting for transfers between devices: 39.8 us -> 33.5 us
  Pallas kernels: 21.3 us -> 23.8 us
  starting transfers between devices: 32.2 us -> 34 us
    ppermute x26 -> x27, waiting for transfers between devices: 38.6 us -> 32.7 us  [swap(): return lax.ppermute(array, 'dp', [(i, i ^ mask) for i in range(16)])]
    ppermute x26 -> x27, starting transfers between devices: 27.4 us -> 29.3 us  [swap(): return lax.ppermute(array, 'dp', [(i, i ^ mask) for i in range(16)])]
    pallas_call x1, Pallas kernels: 6.83 us -> 8.45 us  [on_device_by_heads(): pl.pallas_call(attend_first, out_shape=[row_grad] * (GROUP - 1) + [sorted...]
    pallas_call x1, Pallas kernels: 2.93 us -> 3.89 us  [on_device_by_heads(): pl.pallas_call(attend_last, out_shape=[row_grad, half_sums, half_sums], i...]
  transfers between devices with their start and end apart: 29 -> 30, of which waited for: 14 -> 12; matrix products, arithmetic and copies ran while one was open for 1% -> 1% of each run, Pallas kernels for 16% -> 19%
where the time goes in v11:
time: 93.3 us; the launch traced here: 93.5 us
  starting transfers between devices  34 us (36%)
  waiting for transfers between devices  33.5 us (36%)
  Pallas kernels  23.8 us (26%)
  local copies, waits for them, and re-layouts  1.07 us (1%)
    ppermute x27, waiting for transfers between devices, swap(): return lax.ppermute(array, 'dp', [(i, i ^ mask) for i in range(16)])  32.7 us
    ppermute x27, starting transfers between devices, swap(): return lax.ppermute(array, 'dp', [(i, i ^ mask) for i in range(16)])  29.3 us
    pallas_call x1, Pallas kernels, on_device_by_heads(): pl.pallas_call(attend_first, out_shape=[row_grad] * (GROUP - 1) + [sorted...  8.45 us
    ppermute x3, starting transfers between devices, swap_tensor(): return lax.ppermute(array, 'tensor', [(0, 1), (1, 0)])  4.69 us
    pallas_call x1, Pallas kernels, on_device_by_heads(): pl.pallas_call(project_keys, out_shape=[shaped((MARKED, 2 * HD))] * GROUP...  4.51 us
    pallas_call x1, Pallas kernels, on_device_by_heads(): pl.pallas_call(attend_last, out_shape=[row_grad, half_sums, half_sums], i...  3.89 us
    pallas_call x1, Pallas kernels, on_device_by_heads(): pl.pallas_call(input_grad, out_shape=shaped((ROWS, features // 2)), in_sp...  2.27 us
    pallas_call x1, Pallas kernels, on_device_by_heads(): pl.pallas_call(pack_weights, out_shape=shaped((2 * PART, kv_columns)), in...  2.25 us
  transfers between devices with their start and end apart: 30, of which 12 were waited for; matrix products, arithmetic and copies ran while one was open for 1% of the time, Pallas kernels for 19%

profile of v11, /device:TPU:0, one launch (start us, length us, event | category | flops | bytes accessed | tf_op | source)
XLA Modules:
  0.0 93.5 jit_solution(8651042829242913869)
XLA Ops:
  0.7 4.5 %project_keys.1 = (bf16[144,256]{1,0:T(8,128)(2,1)}, bf16[144,256]{1,0:T(8,128)(2,1)}, bf16[144,256]{1,0:T(8,128)(2,1)}, bf16[144,256]{1,0:T(8,128)(2,1)}) custom-call(s32[2]{0:T(128)} %pos_ref.1, bf16[128,4096]{1,0:T(8,128)(2,1)} %inputs_ref.2, bf16[128,512]{1,0:T(8,128)(2,1)} %values_ref.1, bf16[4096,512]{1,0:T(8,128)(2,1)} %w_own.1), custom_call_target="tpu_custom_call" | custom-call | flops 536870912 | bytes 4194304 | tf_op jit(solution)/shard_map/project_keys/pallas_call | solution.py:585
  5.2 3.0 %collective-permute-start = (bf16[144,256]{1,0:T(8,128)(2,1)}, bf16[144,256]{1,0:T(8,128)(2,1)S(1)}, u32[]{:S(2)}, u32[]{:S(2)}) collective-permute-start(bf16[144,256]{1,0:T(8,128)(2,1)} %get-tuple-element.60), channel_id=1, source_target_pairs={{0,4},{2,6},{4,0},{6,2},{8,12},{10,14},{12,8},{14,10},{16,20},{18,... | collective-permute-start | bytes 221192 | tf_op jit(solution)/shard_map/ppermute | solution.py:221
  8.2 1.6 %collective-permute-start.2 = (bf16[144,256]{1,0:T(8,128)(2,1)}, bf16[144,256]{1,0:T(8,128)(2,1)S(1)}, u32[]{:S(2)}, u32[]{:S(2)}) collective-permute-start(bf16[144,256]{1,0:T(8,128)(2,1)} %get-tuple-element.64), channel_id=1, source_target_pairs={{0,8},{2,10},{4,12},{6,14},{8,0},{10,2},{12,4},{14,6},{16,24},{18,... | collective-permute-start | bytes 221192 | tf_op jit(solution)/shard_map/ppermute | solution.py:221
  10.8 3.1 %collective-permute-start.7 = (bf16[288,256]{1,0:T(8,128)(2,1)S(1)}, bf16[288,256]{1,0:T(8,128)(2,1)S(1)}, u32[]{:S(2)}, u32[]{:S(2)}) collective-permute-start(bf16[288,256]{1,0:T(8,128)(2,1)S(1)} %get-tuple-element.115.refs_3_), channel_id=1, source_target_pairs={{0,16},{2,18},{4,20},{6,22},{8,24},{10,26},{12,28},{14,30},{16,0},... | collective-permute-start | bytes 442376 | tf_op jit(solution)/shard_map/ppermute | solution.py:221
  13.9 2.4 %collective-permute-done.3 = bf16[144,256]{1,0:T(8,128)(2,1)S(1)} collective-permute-done((bf16[144,256]{1,0:T(8,128)(2,1)}, bf16[144,256]{1,0:T(8,128)(2,1)S(1)}, u32[]{:S(2)}, u32[]{:S(2)}) %collective-permute-start.3) | collective-permute-done | bytes 73760 | tf_op jit(solution)/shard_map/ppermute | solution.py:221
  16.3 2.3 %collective-permute-start.8 = (bf16[288,256]{1,0:T(8,128)(2,1)S(1)}, bf16[288,256]{1,0:T(8,128)(2,1)S(1)}, u32[]{:S(2)}, u32[]{:S(2)}) collective-permute-start(bf16[288,256]{1,0:T(8,128)(2,1)S(1)} %get-tuple-element.111.refs_4_), channel_id=1, source_target_pairs={{0,16},{2,18},{4,20},{6,22},{8,24},{10,26},{12,28},{14,30},{16,0},... | collective-permute-start | bytes 442376 | tf_op jit(solution)/shard_map/ppermute | solution.py:221
  19.5 2.2 %pack_weights.1 = bf16[1024,512]{1,0:T(8,128)(2,1)} custom-call(bf16[4096,512]{1,0:T(8,128)(2,1)} %w_own.1), custom_call_target="tpu_custom_call" | custom-call | tf_op jit(solution)/shard_map/pack_weights/pallas_call | solution.py:630
  21.8 1.6 %collective-permute-start.4 = (bf16[1024,512]{1,0:T(8,128)(2,1)}, bf16[1024,512]{1,0:T(8,128)(2,1)S(1)}, u32[]{:S(2)}, u32[]{:S(2)}) collective-permute-start(bf16[1024,512]{1,0:T(8,128)(2,1)} %pack_weights.1), channel_id=1, source_target_pairs={{0,1},{1,0},{2,3},{3,2},{4,5},{5,4},{6,7},{7,6},{8,9},{9,8},{10,11... | collective-permute-start | bytes 3145736 | tf_op jit(solution)/shard_map/ppermute | solution.py:225
  24.2 2.4 %collective-permute-done.8.refs_6_ = bf16[288,256]{1,0:T(8,128)(2,1)S(1)} collective-permute-done((bf16[288,256]{1,0:T(8,128)(2,1)S(1)}, bf16[288,256]{1,0:T(8,128)(2,1)S(1)}, u32[]{:S(2)}, u32[]{:S(2)}) %collective-permute-start.8) | collective-permute-done | bytes 147488 | tf_op jit(solution)/shard_map/ppermute | solution.py:221
  26.6 2.3 %collective-permute-done.6.refs_2_ = bf16[128,1024]{1,0:T(8,128)(2,1)S(1)} collective-permute-done((bf16[128,1024]{1,0:T(8,128)(2,1)S(1)}, bf16[128,1024]{1,0:T(8,128)(2,1)S(1)}, u32[]{:S(2)}, u32[]{:S(2)}) %collective-permute-start.6) | collective-permute-done | bytes 262176 | tf_op jit(solution)/shard_map/ppermute | solution.py:221
  29.4 3.2 %collective-permute-start.10 = (bf16[4,128,256]{2,1,0:T(8,128)(2,1)S(1)}, bf16[4,128,256]{2,1,0:T(8,128)(2,1)S(1)}, u32[]{:S(2)}, u32[]{:S(2)}) collective-permute-start(bf16[4,128,256]{2,1,0:T(8,128)(2,1)S(1)} %get-tuple-element.78), channel_id=1, source_target_pairs={{0,16},{2,18},{4,20},{6,22},{8,24},{10,26},{12,28},{14,30},{16,0},... | collective-permute-start | bytes 786440 | tf_op jit(solution)/shard_map/ppermute | solution.py:221
  32.6 8.5 %attend_first.1 = (bf16[128,512]{1,0:T(8,128)(2,1)S(1)}, bf16[128,512]{1,0:T(8,128)(2,1)S(1)}, bf16[128,512]{1,0:T(8,128)(2,1)S(1)}, bf16[2176,128]{1,0:T(8,128)...) custom-call(s32[4]{0:T(128)S(1)} %copy-done.4, ...), custom_call_target="tpu_custom_call" | custom-call | flops 4000000000 | tf_op jit(solution)/shard_map/attend_first/pallas_call | solution.py:663
  41.1 1.6 %collective-permute-start.11 = (bf16[128,512]{1,0:T(8,128)(2,1)S(1)}, bf16[128,512]{1,0:T(8,128)(2,1)S(1)}, u32[]{:S(2)}, u32[]{:S(2)}) collective-permute-start(bf16[128,512]{1,0:T(8,128)(2,1)S(1)} %get-tuple-element.80), channel_id=1, source_target_pairs={{0,4},{2,6},{4,0},{6,2},{8,12},{10,14},{12,8},{14,10},{16,20},{18,... | collective-permute-start | bytes 393224 | tf_op jit(solution)/shard_map/ppermute | solution.py:221
  44.6 3.9 %attend_last.1 = (bf16[128,512]{1,0:T(8,128)(2,1)S(1)}, f32[1024,256]{1,0:T(8,128)S(1)}, f32[1024,256]{1,0:T(8,128)S(1)}) custom-call(s32[4]{0:T(128)S(1)} %copy-done.4, bf16[128,1024]{1,0:T(8,128)(2,1)S(1)} %collective-permute-done.1.row_ref, bf16[2176,128]{1,0:T(8,128)(2,1)S(1)} %get-tuple-element.71.keys, bf16[128,2176]{1,0:T(8,128)(2,1)S(1)} %get-tuple-element.72.keys_t, ...), custom_call_target="tpu_custom_call" | custom-call | flops 4000000000 | tf_op jit(solution)/shard_map/attend_last/pallas_call | solution.py:675
  53.0 1.7 %collective-permute-done.13.refs_1_ = bf16[2,128,256]{2,1,0:T(8,128)(2,1)S(1)} collective-permute-done((bf16[2,128,256]{2,1,0:T(8,128)(2,1)S(1)}, bf16[2,128,256]{2,1,0:T(8,128)(2,1)S(1)}, u32[]{:S(2)}, u32[]{:S(2)}) %collective-permute-start.13) | collective-permute-done | bytes 131104 | tf_op jit(solution)/shard_map/ppermute | solution.py:221
  54.7 1.7 %collective-permute-start.20 = (bf16[128,512]{1,0:T(8,128)(2,1)S(1)}, bf16[128,512]{1,0:T(8,128)(2,1)S(1)}, u32[]{:S(2)}, u32[]{:S(2)}) collective-permute-start(bf16[128,512]{1,0:T(8,128)(2,1)S(1)} %get-tuple-element.91), channel_id=1, source_target_pairs={{0,12},{2,14},{4,8},{6,10},{8,4},{10,6},{12,0},{14,2},{16,28},{18,... | collective-permute-start | bytes 393224 | tf_op jit(solution)/shard_map/ppermute | solution.py:221
  56.4 5.5 %collective-permute-done.15.refs_3_ = bf16[2,128,256]{2,1,0:T(8,128)(2,1)S(1)} collective-permute-done((bf16[2,128,256]{2,1,0:T(8,128)(2,1)S(1)}, bf16[2,128,256]{2,1,0:T(8,128)(2,1)S(1)}, u32[]{:S(2)}, u32[]{:S(2)}) %collective-permute-start.15) | collective-permute-done | bytes 131104 | tf_op jit(solution)/shard_map/ppermute | solution.py:221
  62.1 5.1 %collective-permute-done.18 = bf16[1024,128]{1,0:T(8,128)(2,1)S(1)} collective-permute-done((bf16[1024,128]{1,0:T(8,128)(2,1)S(1)}, bf16[1024,128]{1,0:T(8,128)(2,1)S(1)}, u32[]{:S(2)}, u32[]{:S(2)}) %collective-permute-start.18) | collective-permute-done | bytes 262176 | tf_op jit(solution)/shard_map/ppermute | solution.py:221
  67.4 1.6 %collective-permute-start.23 = (bf16[1024,128]{1,0:T(8,128)(2,1)S(1)}, bf16[1024,128]{1,0:T(8,128)(2,1)S(1)}, u32[]{:S(2)}, u32[]{:S(2)}) collective-permute-start(bf16[1024,128]{1,0:T(8,128)(2,1)S(1)} %add_convert_fusion.refs_0_), channel_id=1, source_target_pairs={{0,12},{2,14},{4,8},{6,10},{8,4},{10,6},{12,0},{14,2},{16,28},{18,... | collective-permute-start | bytes 786440 | tf_op jit(solution)/shard_map/ppermute | solution.py:221
  72.6 7.8 %collective-permute-done.23.refs_3_ = bf16[1024,128]{1,0:T(8,128)(2,1)S(1)} collective-permute-done((bf16[1024,128]{1,0:T(8,128)(2,1)S(1)}, bf16[1024,128]{1,0:T(8,128)(2,1)S(1)}, u32[]{:S(2)}, u32[]{:S(2)}) %collective-permute-start.23) | collective-permute-done | bytes 262176 | tf_op jit(solution)/shard_map/ppermute | solution.py:221
  80.4 2.6 %collective-permute-done.22.refs_2_ = bf16[1024,128]{1,0:T(8,128)(2,1)S(1)} collective-permute-done((bf16[1024,128]{1,0:T(8,128)(2,1)S(1)}, bf16[1024,128]{1,0:T(8,128)(2,1)S(1)}, u32[]{:S(2)}, u32[]{:S(2)}) %collective-permute-start.22) | collective-permute-done | bytes 262176 | tf_op jit(solution)/shard_map/ppermute | solution.py:221
  83.0 1.6 %collective-permute-start.29 = (bf16[4,128,128]{2,1,0:T(8,128)(2,1)S(1)}, bf16[4,128,128]{2,1,0:T(8,128)(2,1)S(1)}, u32[]{:S(2)}, u32[]{:S(2)}) collective-permute-start(bf16[4,128,128]{2,1,0:T(8,128)(2,1)S(1)} %pad_maximum_fusion.own_ref), channel_id=1, source_target_pairs={{0,1},{1,0},{2,3},{3,2},{4,5},{5,4},{6,7},{7,6},{8,9},{9,8},{10,11... | collective-permute-start | bytes 393224 | tf_op jit(solution)/shard_map/ppermute | solution.py:225
  87.6 1.6 %collective-permute-start.28 = (bf16[128,128]{1,0:T(8,128)(2,1)S(1)}, bf16[128,128]{1,0:T(8,128)(2,1)S(1)}, u32[]{:S(2)}, u32[]{:S(2)}) collective-permute-start(bf16[128,128]{1,0:T(8,128)(2,1)S(1)} %get-tuple-element.103), channel_id=1, source_target_pairs={{0,12},{2,14},{4,8},{6,10},{8,4},{10,6},{12,0},{14,2},{16,28},{18,... | collective-permute-start | bytes 98312 | tf_op jit(solution)/shard_map/ppermute | solution.py:221
  89.2 2.3 %input_grad.1 = bf16[128,2048]{1,0:T(8,128)(2,1)} custom-call(bf16[4,128,128]{2,1,0:T(8,128)(2,1)S(1)} %pad_maximum_fusion.own_ref, bf16[4,128,128]{2,1,0:T(8,128)(2,1)S(1)} %collective-permute-done.29.other_ref, bf16[4096,512]{1,0:T(8,128)(2,1)S(1)} %copy-done, bf16[1024,512]{1,0:T(8,128)(2,1)S(1)} %collective-permute-done.4.w_near, ...), custom_call_target="tpu_custom_call" | custom-call | flops 8000000000 | bytes 5242880 | tf_op jit(solution)/shard_map/input_grad/pallas_call | solution.py:748
  (75 shorter events, 18.6 us)
Async XLA Ops:
  8.2 5.7 %collective-permute-start.2 = (bf16[144,256]{1,0:T(8,128)(2,1)}, bf16[144,256]{1,0:T(8,128)(2,1)S(1)}, u32[]{:S(2)}, u32[]{:S(2)}) collective-permute-start(bf16[144,256]{1,0:T(8,128)(2,1)} %get-tuple-element.64), channel_id=1, source_target_pairs={{0,8},{2,10},{4,12},{6,14},{8,0},{10,2},{12,4},{14,6},{16,24},{18,... | collective-permute-start | bytes 221192 | tf_op jit(solution)/shard_map/ppermute | solution.py:221
  9.8 6.5 %collective-permute-start.3 = (bf16[144,256]{1,0:T(8,128)(2,1)}, bf16[144,256]{1,0:T(8,128)(2,1)S(1)}, u32[]{:S(2)}, u32[]{:S(2)}) collective-permute-start(bf16[144,256]{1,0:T(8,128)(2,1)} %get-tuple-element.65), channel_id=1, source_target_pairs={{0,12},{2,14},{4,8},{6,10},{8,4},{10,6},{12,0},{14,2},{16,28},{18,... | collective-permute-start | bytes 221192 | tf_op jit(solution)/shard_map/ppermute | solution.py:221
  10.8 13.3 %collective-permute-start.7 = (bf16[288,256]{1,0:T(8,128)(2,1)S(1)}, bf16[288,256]{1,0:T(8,128)(2,1)S(1)}, u32[]{:S(2)}, u32[]{:S(2)}) collective-permute-start(bf16[288,256]{1,0:T(8,128)(2,1)S(1)} %get-tuple-element.115.refs_3_), channel_id=1, source_target_pairs={{0,16},{2,18},{4,20},{6,22},{8,24},{10,26},{12,28},{14,30},{16,0},... | collective-permute-start | bytes 442376 | tf_op jit(solution)/shard_map/ppermute | solution.py:221
  16.3 10.2 %collective-permute-start.8 = (bf16[288,256]{1,0:T(8,128)(2,1)S(1)}, bf16[288,256]{1,0:T(8,128)(2,1)S(1)}, u32[]{:S(2)}, u32[]{:S(2)}) collective-permute-start(bf16[288,256]{1,0:T(8,128)(2,1)S(1)} %get-tuple-element.111.refs_4_), channel_id=1, source_target_pairs={{0,16},{2,18},{4,20},{6,22},{8,24},{10,26},{12,28},{14,30},{16,0},... | collective-permute-start | bytes 442376 | tf_op jit(solution)/shard_map/ppermute | solution.py:221
  18.7 7.9 %collective-permute-start.5 = (bf16[128,1024]{1,0:T(8,128)(2,1)S(1)}, bf16[128,1024]{1,0:T(8,128)(2,1)S(1)}, u32[]{:S(2)}, u32[]{:S(2)}) collective-permute-start(bf16[128,1024]{1,0:T(8,128)(2,1)S(1)} %get-tuple-element.68), channel_id=1, source_target_pairs={{0,4},{2,6},{4,0},{6,2},{8,12},{10,14},{12,8},{14,10},{16,20},{18,... | collective-permute-start | bytes 786440 | tf_op jit(solution)/shard_map/ppermute | solution.py:221
  19.3 9.6 %collective-permute-start.6 = (bf16[128,1024]{1,0:T(8,128)(2,1)S(1)}, bf16[128,1024]{1,0:T(8,128)(2,1)S(1)}, u32[]{:S(2)}, u32[]{:S(2)}) collective-permute-start(bf16[128,1024]{1,0:T(8,128)(2,1)S(1)} %get-tuple-element.69), channel_id=1, source_target_pairs={{0,8},{2,10},{4,12},{6,14},{8,0},{10,2},{12,4},{14,6},{16,24},{18,... | collective-permute-start | bytes 786440 | tf_op jit(solution)/shard_map/ppermute | solution.py:221
  21.8 22.8 %collective-permute-start.4 = (bf16[1024,512]{1,0:T(8,128)(2,1)}, bf16[1024,512]{1,0:T(8,128)(2,1)S(1)}, u32[]{:S(2)}, u32[]{:S(2)}) collective-permute-start(bf16[1024,512]{1,0:T(8,128)(2,1)} %pack_weights.1), channel_id=1, source_target_pairs={{0,1},{1,0},{2,3},{3,2},{4,5},{5,4},{6,7},{7,6},{8,9},{9,8},{10,11... | collective-permute-start | bytes 3145736 | tf_op jit(solution)/shard_map/ppermute | solution.py:225
  28.9 14.9 %collective-permute-start.1 = (bf16[128,1024]{1,0:T(8,128)(2,1)S(1)}, bf16[128,1024]{1,0:T(8,128)(2,1)S(1)}, u32[]{:S(2)}, u32[]{:S(2)}) collective-permute-start(bf16[128,1024]{1,0:T(8,128)(2,1)S(1)} %get-tuple-element.63), channel_id=1, source_target_pairs={{0,12},{2,14},{4,8},{6,10},{8,4},{10,6},{12,0},{14,2},{16,28},{18,... | collective-permute-start | bytes 786440 | tf_op jit(solution)/shard_map/ppermute | solution.py:221
  29.4 19.1 %collective-permute-start.10 = (bf16[4,128,256]{2,1,0:T(8,128)(2,1)S(1)}, bf16[4,128,256]{2,1,0:T(8,128)(2,1)S(1)}, u32[]{:S(2)}, u32[]{:S(2)}) collective-permute-start(bf16[4,128,256]{2,1,0:T(8,128)(2,1)S(1)} %get-tuple-element.78), channel_id=1, source_target_pairs={{0,16},{2,18},{4,20},{6,22},{8,24},{10,26},{12,28},{14,30},{16,0},... | collective-permute-start | bytes 786440 | tf_op jit(solution)/shard_map/ppermute | solution.py:221
  41.1 7.4 %collective-permute-start.11 = (bf16[128,512]{1,0:T(8,128)(2,1)S(1)}, bf16[128,512]{1,0:T(8,128)(2,1)S(1)}, u32[]{:S(2)}, u32[]{:S(2)}) collective-permute-start(bf16[128,512]{1,0:T(8,128)(2,1)S(1)} %get-tuple-element.80), channel_id=1, source_target_pairs={{0,4},{2,6},{4,0},{6,2},{8,12},{10,14},{12,8},{14,10},{16,20},{18,... | collective-permute-start | bytes 393224 | tf_op jit(solution)/shard_map/ppermute | solution.py:221
  42.6 5.9 %collective-permute-start.12 = (bf16[128,512]{1,0:T(8,128)(2,1)S(1)}, bf16[128,512]{1,0:T(8,128)(2,1)S(1)}, u32[]{:S(2)}, u32[]{:S(2)}) collective-permute-start(bf16[128,512]{1,0:T(8,128)(2,1)S(1)} %get-tuple-element.81), channel_id=1, source_target_pairs={{0,8},{2,10},{4,12},{6,14},{8,0},{10,2},{12,4},{14,6},{16,24},{18,... | collective-permute-start | bytes 393224 | tf_op jit(solution)/shard_map/ppermute | solution.py:221
  48.6 18.7 %collective-permute-start.19 = (bf16[1024,512]{1,0:T(8,128)(2,1)S(1)}, bf16[1024,512]{1,0:T(8,128)(2,1)S(1)}, u32[]{:S(2)}, u32[]{:S(2)}) collective-permute-start(bf16[1024,512]{1,0:T(8,128)(2,1)S(1)} %collective-permute-done.4.w_near), channel_id=1, source_target_pairs={{0,2},{2,0},{4,6},{6,4},{8,10},{10,8},{12,14},{14,12},{16,18},{18,... | collective-permute-start | bytes 3145736 | tf_op jit(solution)/shard_map/ppermute | solution.py:221
  50.0 6.4 %collective-permute-start.14 = (bf16[2,128,256]{2,1,0:T(8,128)(2,1)S(1)}, bf16[2,128,256]{2,1,0:T(8,128)(2,1)S(1)}, u32[]{:S(2)}, u32[]{:S(2)}) collective-permute-start(bf16[2,128,256]{2,1,0:T(8,128)(2,1)S(1)} %get-tuple-element.86), channel_id=1, source_target_pairs={{0,8},{2,10},{4,12},{6,14},{8,0},{10,2},{12,4},{14,6},{16,24},{18,... | collective-permute-start | bytes 393224 | tf_op jit(solution)/shard_map/ppermute | solution.py:221
  51.3 10.6 %collective-permute-start.15 = (bf16[2,128,256]{2,1,0:T(8,128)(2,1)S(1)}, bf16[2,128,256]{2,1,0:T(8,128)(2,1)S(1)}, u32[]{:S(2)}, u32[]{:S(2)}) collective-permute-start(bf16[2,128,256]{2,1,0:T(8,128)(2,1)S(1)} %get-tuple-element.87), channel_id=1, source_target_pairs={{0,12},{2,14},{4,8},{6,10},{8,4},{10,6},{12,0},{14,2},{16,28},{18,... | collective-permute-start | bytes 393224 | tf_op jit(solution)/shard_map/ppermute | solution.py:221
  52.9 14.3 %collective-permute-start.18 = (bf16[1024,128]{1,0:T(8,128)(2,1)S(1)}, bf16[1024,128]{1,0:T(8,128)(2,1)S(1)}, u32[]{:S(2)}, u32[]{:S(2)}) collective-permute-start(bf16[1024,128]{1,0:T(8,128)(2,1)S(1)} %slice.59), channel_id=1, source_target_pairs={{0,16},{2,18},{4,20},{6,22},{8,24},{10,26},{12,28},{14,30},{16,0},... | collective-permute-start | bytes 786440 | tf_op jit(solution)/shard_map/ppermute | solution.py:221
  54.7 12.7 %collective-permute-start.20 = (bf16[128,512]{1,0:T(8,128)(2,1)S(1)}, bf16[128,512]{1,0:T(8,128)(2,1)S(1)}, u32[]{:S(2)}, u32[]{:S(2)}) collective-permute-start(bf16[128,512]{1,0:T(8,128)(2,1)S(1)} %get-tuple-element.91), channel_id=1, source_target_pairs={{0,12},{2,14},{4,8},{6,10},{8,4},{10,6},{12,0},{14,2},{16,28},{18,... | collective-permute-start | bytes 393224 | tf_op jit(solution)/shard_map/ppermute | solution.py:221
  67.4 13.0 %collective-permute-start.23 = (bf16[1024,128]{1,0:T(8,128)(2,1)S(1)}, bf16[1024,128]{1,0:T(8,128)(2,1)S(1)}, u32[]{:S(2)}, u32[]{:S(2)}) collective-permute-start(bf16[1024,128]{1,0:T(8,128)(2,1)S(1)} %add_convert_fusion.refs_0_), channel_id=1, source_target_pairs={{0,12},{2,14},{4,8},{6,10},{8,4},{10,6},{12,0},{14,2},{16,28},{18,... | collective-permute-start | bytes 786440 | tf_op jit(solution)/shard_map/ppermute | solution.py:221
  69.0 15.7 %collective-permute-start.16 = (bf16[256,1024]{1,0:T(8,128)(2,1)S(1)}, bf16[256,1024]{1,0:T(8,128)(2,1)S(1)}, u32[]{:S(2)}, u32[]{:S(2)}) collective-permute-start(bf16[256,1024]{1,0:T(8,128)(2,1)S(1)} %turn_features.1.own_ref), channel_id=1, source_target_pairs={{0,1},{1,0},{2,3},{3,2},{4,5},{5,4},{6,7},{7,6},{8,9},{9,8},{10,11... | collective-permute-start | bytes 1572872 | tf_op jit(solution)/shard_map/ppermute | solution.py:225
  70.5 12.5 %collective-permute-start.22 = (bf16[1024,128]{1,0:T(8,128)(2,1)S(1)}, bf16[1024,128]{1,0:T(8,128)(2,1)S(1)}, u32[]{:S(2)}, u32[]{:S(2)}) collective-permute-start(bf16[1024,128]{1,0:T(8,128)(2,1)S(1)} %add_convert_fusion.refs_0_), channel_id=1, source_target_pairs={{0,8},{2,10},{4,12},{6,14},{8,0},{10,2},{12,4},{14,6},{16,24},{18,... | collective-permute-start | bytes 786440 | tf_op jit(solution)/shard_map/ppermute | solution.py:221
  71.1 11.8 %collective-permute-start.21 = (bf16[1024,128]{1,0:T(8,128)(2,1)S(1)}, bf16[1024,128]{1,0:T(8,128)(2,1)S(1)}, u32[]{:S(2)}, u32[]{:S(2)}) collective-permute-start(bf16[1024,128]{1,0:T(8,128)(2,1)S(1)} %add_convert_fusion.refs_0_), channel_id=1, source_target_pairs={{0,4},{2,6},{4,0},{6,2},{8,12},{10,14},{12,8},{14,10},{16,20},{18,... | collective-permute-start | bytes 786440 | tf_op jit(solution)/shard_map/ppermute | solution.py:221
  72.5 12.1 %collective-permute-start.25 = (bf16[512,128]{1,0:T(8,128)(2,1)S(1)}, bf16[512,128]{1,0:T(8,128)(2,1)S(1)}, u32[]{:S(2)}, u32[]{:S(2)}) collective-permute-start(bf16[512,128]{1,0:T(8,128)(2,1)S(1)} %slice.58), channel_id=1, source_target_pairs={{0,16},{2,18},{4,20},{6,22},{8,24},{10,26},{12,28},{14,30},{16,0},... | collective-permute-start | bytes 393224 | tf_op jit(solution)/shard_map/ppermute | solution.py:221
  83.0 6.2 %collective-permute-start.29 = (bf16[4,128,128]{2,1,0:T(8,128)(2,1)S(1)}, bf16[4,128,128]{2,1,0:T(8,128)(2,1)S(1)}, u32[]{:S(2)}, u32[]{:S(2)}) collective-permute-start(bf16[4,128,128]{2,1,0:T(8,128)(2,1)S(1)} %pad_maximum_fusion.own_ref), channel_id=1, source_target_pairs={{0,1},{1,0},{2,3},{3,2},{4,5},{5,4},{6,7},{7,6},{8,9},{9,8},{10,11... | collective-permute-start | bytes 393224 | tf_op jit(solution)/shard_map/ppermute | solution.py:225
  85.6 6.8 %collective-permute-start.24 = (f32[256,512]{1,0:T(8,128)S(1)}, f32[256,512]{1,0:T(8,128)S(1)}, u32[]{:S(2)}, u32[]{:S(2)}) collective-permute-start(f32[256,512]{1,0:T(8,128)S(1)} %get-tuple-element.94), channel_id=1, source_target_pairs={{0,2},{2,0},{4,6},{6,4},{8,10},{10,8},{12,14},{14,12},{16,18},{18,... | collective-permute-start | bytes 1572872 | tf_op jit(solution)/shard_map/ppermute | solution.py:221
  85.7 5.8 %collective-permute-start.26 = (bf16[128,128]{1,0:T(8,128)(2,1)S(1)}, bf16[128,128]{1,0:T(8,128)(2,1)S(1)}, u32[]{:S(2)}, u32[]{:S(2)}) collective-permute-start(bf16[128,128]{1,0:T(8,128)(2,1)S(1)} %get-tuple-element.99), channel_id=1, source_target_pairs={{0,4},{2,6},{4,0},{6,2},{8,12},{10,14},{12,8},{14,10},{16,20},{18,... | collective-permute-start | bytes 98312 | tf_op jit(solution)/shard_map/ppermute | solution.py:221
  (11 other events, 96.0 us)

commit v12 on v11

--- a/solution.py
+++ b/solution.py
@@ -688,7 +688,7 @@
     grads = kept + swap(sent, CORE)
     dk_sum, dv_sum = grads[:, :HD], grads[:, HD:]
     dk_far = swap(dk_sum.astype(jnp.bfloat16), Z_HI)
-    w_far = swap(after(w_near, sent), CORE)
+    w_far = swap(after(w_near, dk_sum), CORE)
 
     feature_parts = pl.pallas_call(
         join_features,
@@ -704,7 +704,7 @@
         in_specs=[vmem] * GROUP,
         out_specs=vmem,
         compiler_params=limits(16),
-        cost_estimate=pl.CostEstimate(flops=2_000_000_000, bytes_accessed=0, transcendentals=0),
+        cost_estimate=pl.CostEstimate(flops=8_000_000_000, bytes_accessed=0, transcendentals=0),
         name="turn_features",
     )(*with_partners(feature_parts))
     other_features = swap_tensor(own_features)

time: 93.3 us -> 96.8 us (1.038)
  waiting for transfers between devices: 33.5 us -> 40 us
  Pallas kernels: 23.8 us -> 20.8 us
    ppermute x27, waiting for transfers between devices: 32.7 us -> 38.9 us  [swap(): return lax.ppermute(array, 'dp', [(i, i ^ mask) for i in range(16)])]
    pallas_call x1, Pallas kernels: 8.45 us -> 6.88 us  [on_device_by_heads(): pl.pallas_call(attend_first, out_shape=[row_grad] * (GROUP - 1) + [sorted...]
    pallas_call x1, Pallas kernels: 3.89 us -> 2.47 us  [on_device_by_heads(): pl.pallas_call(attend_last, out_shape=[row_grad, half_sums, half_sums], i...]
  transfers between devices with their start and end apart: 30 -> 30, of which waited for: 12 -> 14; matrix products, arithmetic and copies ran while one was open for 1% -> 1% of each run, Pallas kernels for 19% -> 16%
where the time goes in v12:
time: 96.8 us; the launch traced here: 96.3 us
  waiting for transfers between devices  40 us (41%)
  starting transfers between devices  33.3 us (34%)
  Pallas kernels  20.8 us (21%)
  local copies, waits for them, and re-layouts  1.07 us (1%)
    ppermute x27, waiting for transfers between devices, swap(): return lax.ppermute(array, 'dp', [(i, i ^ mask) for i in range(16)])  38.9 us
    ppermute x27, starting transfers between devices, swap(): return lax.ppermute(array, 'dp', [(i, i ^ mask) for i in range(16)])  28.6 us
    pallas_call x1, Pallas kernels, on_device_by_heads(): pl.pallas_call(attend_first, out_shape=[row_grad] * (GROUP - 1) + [sorted...  6.88 us
    ppermute x3, starting transfers between devices, swap_tensor(): return lax.ppermute(array, 'tensor', [(0, 1), (1, 0)])  4.72 us
    pallas_call x1, Pallas kernels, on_device_by_heads(): pl.pallas_call(project_keys, out_shape=[shaped((MARKED, 2 * HD))] * GROUP...  4.51 us
    pallas_call x1, Pallas kernels, on_device_by_heads(): pl.pallas_call(attend_last, out_shape=[row_grad, half_sums, half_sums], i...  2.47 us
    pallas_call x1, Pallas kernels, on_device_by_heads(): pl.pallas_call(input_grad, out_shape=shaped((ROWS, features // 2)), in_sp...  2.27 us
    pallas_call x1, Pallas kernels, on_device_by_heads(): pl.pallas_call(pack_weights, out_shape=shaped((2 * PART, kv_columns)), in...  2.25 us
  transfers between devices with their start and end apart: 30, of which 14 were waited for; matrix products, arithmetic and copies ran while one was open for 1% of the time, Pallas kernels for 16%

profile of v12, /device:TPU:0, one launch (start us, length us, event | category | flops | bytes accessed | tf_op | source)
XLA Modules:
  0.0 96.3 jit_solution(15197112921621720326)
XLA Ops:
  0.7 4.5 %project_keys.1 = (bf16[144,256]{1,0:T(8,128)(2,1)}, bf16[144,256]{1,0:T(8,128)(2,1)}, bf16[144,256]{1,0:T(8,128)(2,1)}, bf16[144,256]{1,0:T(8,128)(2,1)}) custom-call(s32[2]{0:T(128)} %pos_ref.1, bf16[128,4096]{1,0:T(8,128)(2,1)} %inputs_ref.2, bf16[128,512]{1,0:T(8,128)(2,1)} %values_ref.1, bf16[4096,512]{1,0:T(8,128)(2,1)} %w_own.1), custom_call_target="tpu_custom_call" | custom-call | flops 536870912 | bytes 4194304 | tf_op jit(solution)/shard_map/project_keys/pallas_call | solution.py:585
  5.2 3.0 %collective-permute-start = (bf16[144,256]{1,0:T(8,128)(2,1)}, bf16[144,256]{1,0:T(8,128)(2,1)S(1)}, u32[]{:S(2)}, u32[]{:S(2)}) collective-permute-start(bf16[144,256]{1,0:T(8,128)(2,1)} %get-tuple-element.60), channel_id=1, source_target_pairs={{0,4},{2,6},{4,0},{6,2},{8,12},{10,14},{12,8},{14,10},{16,20},{18,... | collective-permute-start | bytes 221192 | tf_op jit(solution)/shard_map/ppermute | solution.py:221
  10.8 3.1 %collective-permute-start.7 = (bf16[288,256]{1,0:T(8,128)(2,1)S(1)}, bf16[288,256]{1,0:T(8,128)(2,1)S(1)}, u32[]{:S(2)}, u32[]{:S(2)}) collective-permute-start(bf16[288,256]{1,0:T(8,128)(2,1)S(1)} %get-tuple-element.117.refs_3_), channel_id=1, source_target_pairs={{0,16},{2,18},{4,20},{6,22},{8,24},{10,26},{12,28},{14,30},{16,0},... | collective-permute-start | bytes 442376 | tf_op jit(solution)/shard_map/ppermute | solution.py:221
  13.9 2.4 %collective-permute-done.3 = bf16[144,256]{1,0:T(8,128)(2,1)S(1)} collective-permute-done((bf16[144,256]{1,0:T(8,128)(2,1)}, bf16[144,256]{1,0:T(8,128)(2,1)S(1)}, u32[]{:S(2)}, u32[]{:S(2)}) %collective-permute-start.3) | collective-permute-done | bytes 73760 | tf_op jit(solution)/shard_map/ppermute | solution.py:221
  16.3 2.3 %collective-permute-start.8 = (bf16[288,256]{1,0:T(8,128)(2,1)S(1)}, bf16[288,256]{1,0:T(8,128)(2,1)S(1)}, u32[]{:S(2)}, u32[]{:S(2)}) collective-permute-start(bf16[288,256]{1,0:T(8,128)(2,1)S(1)} %get-tuple-element.113.refs_4_), channel_id=1, source_target_pairs={{0,16},{2,18},{4,20},{6,22},{8,24},{10,26},{12,28},{14,30},{16,0},... | collective-permute-start | bytes 442376 | tf_op jit(solution)/shard_map/ppermute | solution.py:221
  19.5 2.2 %pack_weights.1 = bf16[1024,512]{1,0:T(8,128)(2,1)} custom-call(bf16[4096,512]{1,0:T(8,128)(2,1)} %w_own.1), custom_call_target="tpu_custom_call" | custom-call | tf_op jit(solution)/shard_map/pack_weights/pallas_call | solution.py:630
  21.8 1.6 %collective-permute-start.4 = (bf16[1024,512]{1,0:T(8,128)(2,1)}, bf16[1024,512]{1,0:T(8,128)(2,1)S(1)}, u32[]{:S(2)}, u32[]{:S(2)}) collective-permute-start(bf16[1024,512]{1,0:T(8,128)(2,1)} %pack_weights.1), channel_id=1, source_target_pairs={{0,1},{1,0},{2,3},{3,2},{4,5},{5,4},{6,7},{7,6},{8,9},{9,8},{10,11... | collective-permute-start | bytes 3145736 | tf_op jit(solution)/shard_map/ppermute | solution.py:225
  24.2 2.4 %collective-permute-done.8.refs_6_ = bf16[288,256]{1,0:T(8,128)(2,1)S(1)} collective-permute-done((bf16[288,256]{1,0:T(8,128)(2,1)S(1)}, bf16[288,256]{1,0:T(8,128)(2,1)S(1)}, u32[]{:S(2)}, u32[]{:S(2)}) %collective-permute-start.8) | collective-permute-done | bytes 147488 | tf_op jit(solution)/shard_map/ppermute | solution.py:221
  26.6 2.3 %collective-permute-done.6.refs_2_ = bf16[128,1024]{1,0:T(8,128)(2,1)S(1)} collective-permute-done((bf16[128,1024]{1,0:T(8,128)(2,1)S(1)}, bf16[128,1024]{1,0:T(8,128)(2,1)S(1)}, u32[]{:S(2)}, u32[]{:S(2)}) %collective-permute-start.6) | collective-permute-done | bytes 262176 | tf_op jit(solution)/shard_map/ppermute | solution.py:221
  29.4 3.2 %collective-permute-start.10 = (bf16[4,128,256]{2,1,0:T(8,128)(2,1)S(1)}, bf16[4,128,256]{2,1,0:T(8,128)(2,1)S(1)}, u32[]{:S(2)}, u32[]{:S(2)}) collective-permute-start(bf16[4,128,256]{2,1,0:T(8,128)(2,1)S(1)} %get-tuple-element.78), channel_id=1, source_target_pairs={{0,16},{2,18},{4,20},{6,22},{8,24},{10,26},{12,28},{14,30},{16,0},... | collective-permute-start | bytes 786440 | tf_op jit(solution)/shard_map/ppermute | solution.py:221
  32.6 6.9 %attend_first.1 = (bf16[128,512]{1,0:T(8,128)(2,1)S(1)}, bf16[128,512]{1,0:T(8,128)(2,1)S(1)}, bf16[128,512]{1,0:T(8,128)(2,1)S(1)}, bf16[2176,128]{1,0:T(8,128)...) custom-call(s32[4]{0:T(128)S(1)} %copy-done.4, ...), custom_call_target="tpu_custom_call" | custom-call | flops 4000000000 | tf_op jit(solution)/shard_map/attend_first/pallas_call | solution.py:663
  40.6 2.9 %collective-permute-done.1.row_ref = bf16[128,1024]{1,0:T(8,128)(2,1)S(1)} collective-permute-done((bf16[128,1024]{1,0:T(8,128)(2,1)S(1)}, bf16[128,1024]{1,0:T(8,128)(2,1)S(1)}, u32[]{:S(2)}, u32[]{:S(2)}) %collective-permute-start.1) | collective-permute-done | bytes 262176 | tf_op jit(solution)/shard_map/ppermute | solution.py:221
  44.6 2.5 %attend_last.1 = (bf16[128,512]{1,0:T(8,128)(2,1)S(1)}, f32[1024,256]{1,0:T(8,128)S(1)}, f32[1024,256]{1,0:T(8,128)S(1)}) custom-call(s32[4]{0:T(128)S(1)} %copy-done.4, bf16[128,1024]{1,0:T(8,128)(2,1)S(1)} %collective-permute-done.1.row_ref, bf16[2176,128]{1,0:T(8,128)(2,1)S(1)} %get-tuple-element.71.keys, bf16[128,2176]{1,0:T(8,128)(2,1)S(1)} %get-tuple-element.72.keys_t, ...), custom_call_target="tpu_custom_call" | custom-call | flops 4000000000 | tf_op jit(solution)/shard_map/attend_last/pallas_call | solution.py:675
  48.5 2.1 %collective-permute-start.14 = (bf16[2,128,256]{2,1,0:T(8,128)(2,1)S(1)}, bf16[2,128,256]{2,1,0:T(8,128)(2,1)S(1)}, u32[]{:S(2)}, u32[]{:S(2)}) collective-permute-start(bf16[2,128,256]{2,1,0:T(8,128)(2,1)S(1)} %get-tuple-element.86), channel_id=1, source_target_pairs={{0,8},{2,10},{4,12},{6,14},{8,0},{10,2},{12,4},{14,6},{16,24},{18,... | collective-permute-start | bytes 393224 | tf_op jit(solution)/shard_map/ppermute | solution.py:221
  54.7 6.9 %collective-permute-done.15.refs_3_ = bf16[2,128,256]{2,1,0:T(8,128)(2,1)S(1)} collective-permute-done((bf16[2,128,256]{2,1,0:T(8,128)(2,1)S(1)}, bf16[2,128,256]{2,1,0:T(8,128)(2,1)S(1)}, u32[]{:S(2)}, u32[]{:S(2)}) %collective-permute-start.15) | collective-permute-done | bytes 131104 | tf_op jit(solution)/shard_map/ppermute | solution.py:221
  61.9 4.8 %collective-permute-done.18 = bf16[1024,128]{1,0:T(8,128)(2,1)S(1)} collective-permute-done((bf16[1024,128]{1,0:T(8,128)(2,1)S(1)}, bf16[1024,128]{1,0:T(8,128)(2,1)S(1)}, u32[]{:S(2)}, u32[]{:S(2)}) %collective-permute-start.18) | collective-permute-done | bytes 262176 | tf_op jit(solution)/shard_map/ppermute | solution.py:221
  66.8 2.6 %collective-permute-done.20.refs_3_ = bf16[128,512]{1,0:T(8,128)(2,1)S(1)} collective-permute-done((bf16[128,512]{1,0:T(8,128)(2,1)S(1)}, bf16[128,512]{1,0:T(8,128)(2,1)S(1)}, u32[]{:S(2)}, u32[]{:S(2)}) %collective-permute-start.20) | collective-permute-done | bytes 131104 | tf_op jit(solution)/shard_map/ppermute | solution.py:221
  71.0 2.4 %collective-permute-start.22 = (bf16[1024,128]{1,0:T(8,128)(2,1)S(1)}, bf16[1024,128]{1,0:T(8,128)(2,1)S(1)}, u32[]{:S(2)}, u32[]{:S(2)}) collective-permute-start(bf16[1024,128]{1,0:T(8,128)(2,1)S(1)} %add_convert_fusion.refs_0_), channel_id=1, source_target_pairs={{0,8},{2,10},{4,12},{6,14},{8,0},{10,2},{12,4},{14,6},{16,24},{18,... | collective-permute-start | bytes 786440 | tf_op jit(solution)/shard_map/ppermute | solution.py:221
  74.6 7.7 %collective-permute-done.23.refs_3_ = bf16[1024,128]{1,0:T(8,128)(2,1)S(1)} collective-permute-done((bf16[1024,128]{1,0:T(8,128)(2,1)S(1)}, bf16[1024,128]{1,0:T(8,128)(2,1)S(1)}, u32[]{:S(2)}, u32[]{:S(2)}) %collective-permute-start.23) | collective-permute-done | bytes 262176 | tf_op jit(solution)/shard_map/ppermute | solution.py:221
  82.3 3.4 %collective-permute-done.22.refs_2_ = bf16[1024,128]{1,0:T(8,128)(2,1)S(1)} collective-permute-done((bf16[1024,128]{1,0:T(8,128)(2,1)S(1)}, bf16[1024,128]{1,0:T(8,128)(2,1)S(1)}, u32[]{:S(2)}, u32[]{:S(2)}) %collective-permute-start.22) | collective-permute-done | bytes 262176 | tf_op jit(solution)/shard_map/ppermute | solution.py:221
  85.8 1.6 %collective-permute-start.29 = (bf16[4,128,128]{2,1,0:T(8,128)(2,1)S(1)}, bf16[4,128,128]{2,1,0:T(8,128)(2,1)S(1)}, u32[]{:S(2)}, u32[]{:S(2)}) collective-permute-start(bf16[4,128,128]{2,1,0:T(8,128)(2,1)S(1)} %pad_maximum_fusion.own_ref), channel_id=1, source_target_pairs={{0,1},{1,0},{2,3},{3,2},{4,5},{5,4},{6,7},{7,6},{8,9},{9,8},{10,11... | collective-permute-start | bytes 393224 | tf_op jit(solution)/shard_map/ppermute | solution.py:225
  88.5 1.9 %collective-permute-start.26 = (bf16[128,128]{1,0:T(8,128)(2,1)S(1)}, bf16[128,128]{1,0:T(8,128)(2,1)S(1)}, u32[]{:S(2)}, u32[]{:S(2)}) collective-permute-start(bf16[128,128]{1,0:T(8,128)(2,1)S(1)} %get-tuple-element.99), channel_id=1, source_target_pairs={{0,4},{2,6},{4,0},{6,2},{8,12},{10,14},{12,8},{14,10},{16,20},{18,... | collective-permute-start | bytes 98312 | tf_op jit(solution)/shard_map/ppermute | solution.py:221
  90.4 1.6 %collective-permute-start.28 = (bf16[128,128]{1,0:T(8,128)(2,1)S(1)}, bf16[128,128]{1,0:T(8,128)(2,1)S(1)}, u32[]{:S(2)}, u32[]{:S(2)}) collective-permute-start(bf16[128,128]{1,0:T(8,128)(2,1)S(1)} %get-tuple-element.103), channel_id=1, source_target_pairs={{0,12},{2,14},{4,8},{6,10},{8,4},{10,6},{12,0},{14,2},{16,28},{18,... | collective-permute-start | bytes 98312 | tf_op jit(solution)/shard_map/ppermute | solution.py:221
  92.0 2.3 %input_grad.1 = bf16[128,2048]{1,0:T(8,128)(2,1)} custom-call(bf16[4,128,128]{2,1,0:T(8,128)(2,1)S(1)} %pad_maximum_fusion.own_ref, bf16[4,128,128]{2,1,0:T(8,128)(2,1)S(1)} %collective-permute-done.29.other_ref, bf16[4096,512]{1,0:T(8,128)(2,1)S(1)} %copy-done, bf16[1024,512]{1,0:T(8,128)(2,1)S(1)} %collective-permute-done.4.w_near, ...), custom_call_target="tpu_custom_call" | custom-call | flops 8000000000 | bytes 5242880 | tf_op jit(solution)/shard_map/input_grad/pallas_call | solution.py:748
  (75 shorter events, 18.7 us)
Async XLA Ops:
  9.8 6.5 %collective-permute-start.3 = (bf16[144,256]{1,0:T(8,128)(2,1)}, bf16[144,256]{1,0:T(8,128)(2,1)S(1)}, u32[]{:S(2)}, u32[]{:S(2)}) collective-permute-start(bf16[144,256]{1,0:T(8,128)(2,1)} %get-tuple-element.65), channel_id=1, source_target_pairs={{0,12},{2,14},{4,8},{6,10},{8,4},{10,6},{12,0},{14,2},{16,28},{18,... | collective-permute-start | bytes 221192 | tf_op jit(solution)/shard_map/ppermute | solution.py:221
  10.8 13.3 %collective-permute-start.7 = (bf16[288,256]{1,0:T(8,128)(2,1)S(1)}, bf16[288,256]{1,0:T(8,128)(2,1)S(1)}, u32[]{:S(2)}, u32[]{:S(2)}) collective-permute-start(bf16[288,256]{1,0:T(8,128)(2,1)S(1)} %get-tuple-element.117.refs_3_), channel_id=1, source_target_pairs={{0,16},{2,18},{4,20},{6,22},{8,24},{10,26},{12,28},{14,30},{16,0},... | collective-permute-start | bytes 442376 | tf_op jit(solution)/shard_map/ppermute | solution.py:221
  16.3 10.2 %collective-permute-start.8 = (bf16[288,256]{1,0:T(8,128)(2,1)S(1)}, bf16[288,256]{1,0:T(8,128)(2,1)S(1)}, u32[]{:S(2)}, u32[]{:S(2)}) collective-permute-start(bf16[288,256]{1,0:T(8,128)(2,1)S(1)} %get-tuple-element.113.refs_4_), channel_id=1, source_target_pairs={{0,16},{2,18},{4,20},{6,22},{8,24},{10,26},{12,28},{14,30},{16,0},... | collective-permute-start | bytes 442376 | tf_op jit(solution)/shard_map/ppermute | solution.py:221
  18.7 7.9 %collective-permute-start.5 = (bf16[128,1024]{1,0:T(8,128)(2,1)S(1)}, bf16[128,1024]{1,0:T(8,128)(2,1)S(1)}, u32[]{:S(2)}, u32[]{:S(2)}) collective-permute-start(bf16[128,1024]{1,0:T(8,128)(2,1)S(1)} %get-tuple-element.68), channel_id=1, source_target_pairs={{0,4},{2,6},{4,0},{6,2},{8,12},{10,14},{12,8},{14,10},{16,20},{18,... | collective-permute-start | bytes 786440 | tf_op jit(solution)/shard_map/ppermute | solution.py:221
  19.3 9.6 %collective-permute-start.6 = (bf16[128,1024]{1,0:T(8,128)(2,1)S(1)}, bf16[128,1024]{1,0:T(8,128)(2,1)S(1)}, u32[]{:S(2)}, u32[]{:S(2)}) collective-permute-start(bf16[128,1024]{1,0:T(8,128)(2,1)S(1)} %get-tuple-element.69), channel_id=1, source_target_pairs={{0,8},{2,10},{4,12},{6,14},{8,0},{10,2},{12,4},{14,6},{16,24},{18,... | collective-permute-start | bytes 786440 | tf_op jit(solution)/shard_map/ppermute | solution.py:221
  21.8 22.8 %collective-permute-start.4 = (bf16[1024,512]{1,0:T(8,128)(2,1)}, bf16[1024,512]{1,0:T(8,128)(2,1)S(1)}, u32[]{:S(2)}, u32[]{:S(2)}) collective-permute-start(bf16[1024,512]{1,0:T(8,128)(2,1)} %pack_weights.1), channel_id=1, source_target_pairs={{0,1},{1,0},{2,3},{3,2},{4,5},{5,4},{6,7},{7,6},{8,9},{9,8},{10,11... | collective-permute-start | bytes 3145736 | tf_op jit(solution)/shard_map/ppermute | solution.py:225
  28.9 14.6 %collective-permute-start.1 = (bf16[128,1024]{1,0:T(8,128)(2,1)S(1)}, bf16[128,1024]{1,0:T(8,128)(2,1)S(1)}, u32[]{:S(2)}, u32[]{:S(2)}) collective-permute-start(bf16[128,1024]{1,0:T(8,128)(2,1)S(1)} %get-tuple-element.63), channel_id=1, source_target_pairs={{0,12},{2,14},{4,8},{6,10},{8,4},{10,6},{12,0},{14,2},{16,28},{18,... | collective-permute-start | bytes 786440 | tf_op jit(solution)/shard_map/ppermute | solution.py:221
  29.4 17.7 %collective-permute-start.10 = (bf16[4,128,256]{2,1,0:T(8,128)(2,1)S(1)}, bf16[4,128,256]{2,1,0:T(8,128)(2,1)S(1)}, u32[]{:S(2)}, u32[]{:S(2)}) collective-permute-start(bf16[4,128,256]{2,1,0:T(8,128)(2,1)S(1)} %get-tuple-element.78), channel_id=1, source_target_pairs={{0,16},{2,18},{4,20},{6,22},{8,24},{10,26},{12,28},{14,30},{16,0},... | collective-permute-start | bytes 786440 | tf_op jit(solution)/shard_map/ppermute | solution.py:221
  39.5 7.6 %collective-permute-start.11 = (bf16[128,512]{1,0:T(8,128)(2,1)S(1)}, bf16[128,512]{1,0:T(8,128)(2,1)S(1)}, u32[]{:S(2)}, u32[]{:S(2)}) collective-permute-start(bf16[128,512]{1,0:T(8,128)(2,1)S(1)} %get-tuple-element.80), channel_id=1, source_target_pairs={{0,4},{2,6},{4,0},{6,2},{8,12},{10,14},{12,8},{14,10},{16,20},{18,... | collective-permute-start | bytes 393224 | tf_op jit(solution)/shard_map/ppermute | solution.py:221
  40.6 6.5 %collective-permute-start.12 = (bf16[128,512]{1,0:T(8,128)(2,1)S(1)}, bf16[128,512]{1,0:T(8,128)(2,1)S(1)}, u32[]{:S(2)}, u32[]{:S(2)}) collective-permute-start(bf16[128,512]{1,0:T(8,128)(2,1)S(1)} %get-tuple-element.81), channel_id=1, source_target_pairs={{0,8},{2,10},{4,12},{6,14},{8,0},{10,2},{12,4},{14,6},{16,24},{18,... | collective-permute-start | bytes 393224 | tf_op jit(solution)/shard_map/ppermute | solution.py:221
  47.2 6.0 %collective-permute-start.13 = (bf16[2,128,256]{2,1,0:T(8,128)(2,1)S(1)}, bf16[2,128,256]{2,1,0:T(8,128)(2,1)S(1)}, u32[]{:S(2)}, u32[]{:S(2)}) collective-permute-start(bf16[2,128,256]{2,1,0:T(8,128)(2,1)S(1)} %get-tuple-element.85), channel_id=1, source_target_pairs={{0,4},{2,6},{4,0},{6,2},{8,12},{10,14},{12,8},{14,10},{16,20},{18,... | collective-permute-start | bytes 393224 | tf_op jit(solution)/shard_map/ppermute | solution.py:221
  48.5 6.2 %collective-permute-start.14 = (bf16[2,128,256]{2,1,0:T(8,128)(2,1)S(1)}, bf16[2,128,256]{2,1,0:T(8,128)(2,1)S(1)}, u32[]{:S(2)}, u32[]{:S(2)}) collective-permute-start(bf16[2,128,256]{2,1,0:T(8,128)(2,1)S(1)} %get-tuple-element.86), channel_id=1, source_target_pairs={{0,8},{2,10},{4,12},{6,14},{8,0},{10,2},{12,4},{14,6},{16,24},{18,... | collective-permute-start | bytes 393224 | tf_op jit(solution)/shard_map/ppermute | solution.py:221
  50.6 11.0 %collective-permute-start.15 = (bf16[2,128,256]{2,1,0:T(8,128)(2,1)S(1)}, bf16[2,128,256]{2,1,0:T(8,128)(2,1)S(1)}, u32[]{:S(2)}, u32[]{:S(2)}) collective-permute-start(bf16[2,128,256]{2,1,0:T(8,128)(2,1)S(1)} %get-tuple-element.87), channel_id=1, source_target_pairs={{0,12},{2,14},{4,8},{6,10},{8,4},{10,6},{12,0},{14,2},{16,28},{18,... | collective-permute-start | bytes 393224 | tf_op jit(solution)/shard_map/ppermute | solution.py:221
  51.8 14.9 %collective-permute-start.18 = (bf16[1024,128]{1,0:T(8,128)(2,1)S(1)}, bf16[1024,128]{1,0:T(8,128)(2,1)S(1)}, u32[]{:S(2)}, u32[]{:S(2)}) collective-permute-start(bf16[1024,128]{1,0:T(8,128)(2,1)S(1)} %slice.64), channel_id=1, source_target_pairs={{0,16},{2,18},{4,20},{6,22},{8,24},{10,26},{12,28},{14,30},{16,0},... | collective-permute-start | bytes 786440 | tf_op jit(solution)/shard_map/ppermute | solution.py:221
  52.9 16.5 %collective-permute-start.19 = (bf16[1024,512]{1,0:T(8,128)(2,1)S(1)}, bf16[1024,512]{1,0:T(8,128)(2,1)S(1)}, u32[]{:S(2)}, u32[]{:S(2)}) collective-permute-start(bf16[1024,512]{1,0:T(8,128)(2,1)S(1)} %collective-permute-done.4.w_near), channel_id=1, source_target_pairs={{0,2},{2,0},{4,6},{6,4},{8,10},{10,8},{12,14},{14,12},{16,18},{18,... | collective-permute-start | bytes 3145736 | tf_op jit(solution)/shard_map/ppermute | solution.py:221
  61.8 7.6 %collective-permute-start.20 = (bf16[128,512]{1,0:T(8,128)(2,1)S(1)}, bf16[128,512]{1,0:T(8,128)(2,1)S(1)}, u32[]{:S(2)}, u32[]{:S(2)}) collective-permute-start(bf16[128,512]{1,0:T(8,128)(2,1)S(1)} %get-tuple-element.91), channel_id=1, source_target_pairs={{0,12},{2,14},{4,8},{6,10},{8,4},{10,6},{12,0},{14,2},{16,28},{18,... | collective-permute-start | bytes 393224 | tf_op jit(solution)/shard_map/ppermute | solution.py:221
  69.4 12.9 %collective-permute-start.23 = (bf16[1024,128]{1,0:T(8,128)(2,1)S(1)}, bf16[1024,128]{1,0:T(8,128)(2,1)S(1)}, u32[]{:S(2)}, u32[]{:S(2)}) collective-permute-start(bf16[1024,128]{1,0:T(8,128)(2,1)S(1)} %add_convert_fusion.refs_0_), channel_id=1, source_target_pairs={{0,12},{2,14},{4,8},{6,10},{8,4},{10,6},{12,0},{14,2},{16,28},{18,... | collective-permute-start | bytes 786440 | tf_op jit(solution)/shard_map/ppermute | solution.py:221
  69.4 18.0 %collective-permute-start.16 = (bf16[256,1024]{1,0:T(8,128)(2,1)S(1)}, bf16[256,1024]{1,0:T(8,128)(2,1)S(1)}, u32[]{:S(2)}, u32[]{:S(2)}) collective-permute-start(bf16[256,1024]{1,0:T(8,128)(2,1)S(1)} %turn_features.1.own_ref), channel_id=1, source_target_pairs={{0,1},{1,0},{2,3},{3,2},{4,5},{5,4},{6,7},{7,6},{8,9},{9,8},{10,11... | collective-permute-start | bytes 1572872 | tf_op jit(solution)/shard_map/ppermute | solution.py:225
  71.0 14.8 %collective-permute-start.22 = (bf16[1024,128]{1,0:T(8,128)(2,1)S(1)}, bf16[1024,128]{1,0:T(8,128)(2,1)S(1)}, u32[]{:S(2)}, u32[]{:S(2)}) collective-permute-start(bf16[1024,128]{1,0:T(8,128)(2,1)S(1)} %add_convert_fusion.refs_0_), channel_id=1, source_target_pairs={{0,8},{2,10},{4,12},{6,14},{8,0},{10,2},{12,4},{14,6},{16,24},{18,... | collective-permute-start | bytes 786440 | tf_op jit(solution)/shard_map/ppermute | solution.py:221
  73.4 12.4 %collective-permute-start.21 = (bf16[1024,128]{1,0:T(8,128)(2,1)S(1)}, bf16[1024,128]{1,0:T(8,128)(2,1)S(1)}, u32[]{:S(2)}, u32[]{:S(2)}) collective-permute-start(bf16[1024,128]{1,0:T(8,128)(2,1)S(1)} %add_convert_fusion.refs_0_), channel_id=1, source_target_pairs={{0,4},{2,6},{4,0},{6,2},{8,12},{10,14},{12,8},{14,10},{16,20},{18,... | collective-permute-start | bytes 786440 | tf_op jit(solution)/shard_map/ppermute | solution.py:221
  74.5 12.9 %collective-permute-start.25 = (bf16[512,128]{1,0:T(8,128)(2,1)S(1)}, bf16[512,128]{1,0:T(8,128)(2,1)S(1)}, u32[]{:S(2)}, u32[]{:S(2)}) collective-permute-start(bf16[512,128]{1,0:T(8,128)(2,1)S(1)} %slice.58), channel_id=1, source_target_pairs={{0,16},{2,18},{4,20},{6,22},{8,24},{10,26},{12,28},{14,30},{16,0},... | collective-permute-start | bytes 393224 | tf_op jit(solution)/shard_map/ppermute | solution.py:221
  85.8 6.2 %collective-permute-start.29 = (bf16[4,128,128]{2,1,0:T(8,128)(2,1)S(1)}, bf16[4,128,128]{2,1,0:T(8,128)(2,1)S(1)}, u32[]{:S(2)}, u32[]{:S(2)}) collective-permute-start(bf16[4,128,128]{2,1,0:T(8,128)(2,1)S(1)} %pad_maximum_fusion.own_ref), channel_id=1, source_target_pairs={{0,1},{1,0},{2,3},{3,2},{4,5},{5,4},{6,7},{7,6},{8,9},{9,8},{10,11... | collective-permute-start | bytes 393224 | tf_op jit(solution)/shard_map/ppermute | solution.py:225
  88.4 6.8 %collective-permute-start.24 = (f32[256,512]{1,0:T(8,128)S(1)}, f32[256,512]{1,0:T(8,128)S(1)}, u32[]{:S(2)}, u32[]{:S(2)}) collective-permute-start(f32[256,512]{1,0:T(8,128)S(1)} %get-tuple-element.94), channel_id=1, source_target_pairs={{0,2},{2,0},{4,6},{6,4},{8,10},{10,8},{12,14},{14,12},{16,18},{18,... | collective-permute-start | bytes 1572872 | tf_op jit(solution)/shard_map/ppermute | solution.py:221
  88.5 5.8 %collective-permute-start.26 = (bf16[128,128]{1,0:T(8,128)(2,1)S(1)}, bf16[128,128]{1,0:T(8,128)(2,1)S(1)}, u32[]{:S(2)}, u32[]{:S(2)}) collective-permute-start(bf16[128,128]{1,0:T(8,128)(2,1)S(1)} %get-tuple-element.99), channel_id=1, source_target_pairs={{0,4},{2,6},{4,0},{6,2},{8,12},{10,14},{12,8},{14,10},{16,20},{18,... | collective-permute-start | bytes 98312 | tf_op jit(solution)/shard_map/ppermute | solution.py:221
  (11 other events, 99.3 us)
